TPU v7x, 256 devices: a whole 4x4x8 slice. The times are simulated.
256 devices in a mesh: seq: 64 (over x_hi, z, y), head: 4 (over x_lo, core).
Axes of the slice: x: 4 (x_hi: 2, x_lo: 2; x = x_hi * 2 + x_lo), y: 4, z: 8, core: 2. Of those that a mesh axis runs over, the one named last changes fastest.
Arguments:
- queries: bfloat16 [8192, 2560], P('seq', 'head'), may hold values from -240 to 240
- keys: bfloat16 [8192, 2560], P('seq', 'head'), may hold values from -6 to 6
- values: bfloat16 [8192, 2560], P('seq', 'head'), may hold values from -6 to 6
- frame_mask: int32 [64, 64], replicated, may hold values from 0 to 1, as said below
- w_out: bfloat16 [2560, 5120], P('head'), may hold values from -0.125 to 0.125
Outputs:
- projected: bfloat16 [8192, 5120], P('seq', 'head')
Inputs may be any that keep to these rules, and one draw needn't show every extreme that they name: `frame_mask`: every frame block may attend to itself and to the blocks one away; blocks 0 and 32 may attend to each other; no block attends to a block more than 32 blocks away.
All inputs are finite; a program needn't handle non-finite values.
Results may differ from a plain program's by a relative error of at most 0.015.
Values may be sent and summed in bfloat16 or wider, within the bound.
No kernel may reach another device: no remote copies, remote signals or barrier semaphores. Data moves between devices by JAX's collectives and lax.ppermute only.
A program may use at most 128 MiB of HBM per device.

v0:
```python
import jax
import jax.numpy as jnp
from jax import lax
from jax.sharding import PartitionSpec as P

HEAD_DIM = 128


def local(queries, keys, values, frame_mask, w_out):
    rows, width = queries.shape
    head_size = HEAD_DIM
    local_heads = width // head_size
    count_blocks = frame_mask.shape[0]
    scale = head_size ** (-0.5)
    block_id = lax.axis_index("seq")
    mask_row = lax.dynamic_slice_in_dim(frame_mask, block_id, 1, 0)[0]
    block_ids = jnp.arange(count_blocks, dtype=jnp.int32)

    def compute_with(live, key_rows, value_rows):

        def compute(state):
            top_all, total_all, accum_all = state
            tops, totals, accums = ([], [], [])
            for head in range(local_heads):
                first = head * head_size
                query_head = queries[:, first : first + head_size]
                key_head = key_rows[:, first : first + head_size]
                value_head = value_rows[:, first : first + head_size]
                scores = (
                    lax.dot_general(
                        query_head,
                        key_head,
                        (((1,), (1,)), ((), ())),
                        preferred_element_type=jnp.float32,
                    )
                    * scale
                )
                scores = jnp.where(live[None, :], scores, -1e30)
                top = top_all[head]
                new_top = jnp.maximum(top, jnp.max(scores, axis=1, keepdims=True))
                weights = jnp.where(live[None, :], jnp.exp(scores - new_top), 0.0)
                tops.append(new_top)
                totals.append(jnp.sum(weights, axis=1, keepdims=True))
                accums.append(
                    jnp.dot(
                        weights.astype(jnp.bfloat16), value_head, preferred_element_type=jnp.float32
                    )
                )
            return (jnp.stack(tops), jnp.stack(totals), jnp.stack(accums))

        return compute

    def unchanged(state):
        return state

    start_state = (
        jnp.full((local_heads, rows, 1), -1e30, jnp.float32),
        jnp.zeros((local_heads, rows, 1), jnp.float32),
        jnp.zeros((local_heads, rows, head_size), jnp.float32),
    )
    key_rows = lax.all_gather(keys, "seq", axis=0, tiled=True)
    value_rows = lax.all_gather(values, "seq", axis=0, tiled=True)
    length = key_rows.shape[0]
    owner = jnp.arange(length, dtype=jnp.int32) // rows
    hits = (owner[:, None] == block_ids[None, :]) & (mask_row[None, :] > 0)
    live = jnp.any(hits, axis=1)
    top, total, accum = lax.cond(
        jnp.any(live), compute_with(live, key_rows, value_rows), unchanged, start_state
    )
    attended = jnp.concatenate(
        [(accum[head] / total[head]).astype(jnp.bfloat16) for head in range(local_heads)], axis=1
    )
    partial_rows = jnp.dot(attended, w_out, preferred_element_type=jnp.float32)
    summed = lax.psum_scatter(
        partial_rows.astype(jnp.bfloat16), "head", scatter_dimension=1, tiled=True
    )
    return summed


def solution(mesh):
    in_specs = (P("seq", "head"), P("seq", "head"), P("seq", "head"), P(), P("head", None))
    out_specs = P("seq", "head")
    return jax.shard_map(local, mesh=mesh, in_specs=in_specs, out_specs=out_specs, check_vma=False)
```

profile of v0, /device:TPU:1, one launch (start us, length us, event | category | flops | bytes accessed | tf_op | source)
XLA Modules:
  0.0 410.4 jit_solution(8088942128619084983)
XLA Ops:
  6.5 0.7 all-gather.3.cloned.1.call-update
  8.8 4.4 %fusion.110 = (pred[8192,64]{1,0:T(8,128)(4,1)S(1)}, pred[]{:T(512)}) fusion(s32[8192]{0:T(1024)S(1)} %add_select_fusion, pred[64]{0:T(512)(128)(4,1)S(1)} %compare_bitcast_fusion), kind=kLoop, calls=%fused_computation.87 | loop fusion | flops 1572863 | bytes 557121 | tf_op jit(solution)/shard_map/and | solution.py:65
  13.8 164.6 %all-gather.3.cloned.1.call-done = bf16[8192,640]{1,0:T(8,128)(2,1)} async-done(((bf16[128,640]{1,0:T(8,128)(2,1)}), bf16[8192,640]{1,0:T(8,128)(2,1)}) %all-gather.3.cloned.1.call-update) | async-done | bytes 10485776 | tf_op jit(solution)/shard_map/all_gather | solution.py:61
  178.3 164.4 %all-gather.5.cloned.1.call-done = bf16[8192,640]{1,0:T(8,128)(2,1)} async-done(((bf16[128,640]{1,0:T(8,128)(2,1)}), bf16[8192,640]{1,0:T(8,128)(2,1)}) %all-gather.5.cloned.1.call-update) | async-done | bytes 10485776 | tf_op jit(solution)/shard_map/all_gather | solution.py:62
  342.7 29.2 %conditional.1 = (f32[5,128,1]{1,2,0:T(1,128)S(1)}, f32[5,128,128]{2,1,0:T(8,128)}) conditional(s32[]{:T(128)} %convert_element_type.36, () %tuple.13, (pred[8192,64]{1,0:T(8,128)(4,1)S(1)}, bf16[128,640]{1,0:T(8,128)(2,1)}, bf16[8192,640]{1,0:T(8,128)(2,1)}, bf16[8192,640]{1,0:T(8,128)(2,1)}, pred[]{:T(512)}) %tuple.14), branch_computations={%region_2.3_spmd, %region_3.14_spmd} | conditional | flops 2732056064 | bytes 127639688 | solution.py:67
  342.7 1.2 reduce_or.20
  343.9 2.6 fusion.125
  346.5 3.0 fusion.129
  349.6 0.9 fusion.126
  350.5 0.9 fusion.127
  351.4 0.9 fusion.128
  352.3 4.1 fusion.14
  356.5 3.1 fusion.55
  359.5 3.0 fusion.65
  362.6 3.1 fusion.75
  365.7 3.1 fusion.85
  368.8 3.1 fusion.95
  372.0 0.9 fusion.118
  372.9 0.9 fusion.119
  373.8 0.9 fusion.120
  374.8 0.9 fusion.121
  375.7 0.9 fusion.122
  376.7 5.2 %convolution_convert_fusion = bf16[128,5120]{1,0:T(8,128)(2,1)} fusion(bf16[128,640]{1,0:T(8,128)(2,1)S(1)} %fusion.122, bf16[640,5120]{1,0:T(8,128)(2,1)} %param.11), kind=kOutput, calls=%fused_computation.85 | convolution fusion | flops 839516160 | bytes 8028160 | tf_op jit(solution)/shard_map/dot_general | solution.py:73
  381.9 22.0 %reduce-scatter.2.cloned.1.call-done = bf16[128,1280]{1,0:T(8,128)(2,1)} async-done(((bf16[128,5120]{1,0:T(8,128)(2,1)}), bf16[128,1280]{1,0:T(8,128)(2,1)}) %reduce-scatter.2.cloned.1.call-update) | async-done | bytes 327696 | tf_op jit(solution)/shard_map/reduce_scatter | solution.py:74
  (24 shorter events, 1.6 us)
Async XLA Ops:
  6.5 171.8 %all-gather.3.cloned.1.call-start = ((), (), s32[]{:S(2)}) async-start(), calls=%async_computation.1 | async-start | bytes 10649600 | tf_op jit(solution)/shard_map/all_gather | solution.py:61
  7.3 335.5 %all-gather.5.cloned.1.call-start = ((), (), s32[]{:S(2)}) async-start(), calls=%async_computation.2 | async-start | bytes 10649600 | tf_op jit(solution)/shard_map/all_gather | solution.py:62
  8.0 395.9 %reduce-scatter.2.cloned.1.call-start = ((), (), s32[]{:S(2)}) async-start(), calls=%async_computation.3 | async-start | bytes 1638400 | tf_op jit(solution)/shard_map/reduce_scatter | solution.py:74
  342.7 3.8 copy-start.1
  343.9 5.6 %copy-start = (bf16[8192,640]{1,0:T(8,128)(2,1)S(1)}, bf16[8192,640]{1,0:T(8,128)(2,1)}, u32[]{:S(2)}) copy-start(bf16[8192,640]{1,0:T(8,128)(2,1)} %get-tuple-element.15) | copy-start | bytes 31457284 | tf_op jit(solution)/shard_map/cond
  356.5 6.1 %copy-start.2 = (f32[5,128,1]{1,2,0:T(1,128)}, f32[5,128,1]{1,2,0:T(1,128)S(1)}, u32[]{:S(2)}) copy-start(f32[5,128,1]{1,2,0:T(1,128)S(1)} %constant_dynamic-update-slice_fusion) | copy-start | bytes 7684 | tf_op jit(solution)/shard_map/cond
  368.8 3.1 copy-start.3
Sparse Core Ops, SparseCore 0:
  11.0 167.3 all-gather.2
  182.0 160.7 all-gather.4
  382.0 21.8 reduce-scatter.1
where the time goes:
time: 411 us; the launch traced here: 410 us
  waiting for transfers between devices  352 us (86%)
  matrix products  29 us (7%)
  other arithmetic  15 us (4%)
  between operations  13.8 us (3%)
    all_gather x1, waiting for transfers between devices, local(): key_rows = lax.all_gather(keys, 'seq', axis=0, tiled=True)  165 us
    all_gather x1, waiting for transfers between devices, local(): value_rows = lax.all_gather(values, 'seq', axis=0, tiled=True)  164 us
    reduce_scatter x1, waiting for transfers between devices, local(): lax.psum_scatter(partial_rows.astype(jnp.bfloat16), 'head', scatter_dimen...  22 us
    dot_general x5, matrix products, compute(): jnp.dot(weights.astype(jnp.bfloat16), value_head, preferred_element_type=...  15.5 us
    dot_general x5, matrix products, compute(): lax.dot_general(query_head, key_head, (((1,), (1,)), ((), ())), preferred...  8.34 us
  transfers between devices with their start and end apart: 3, of which 3 were waited for; matrix products, arithmetic and copies ran while one was open for 1% of the time, Pallas kernels for 0%

commit v1 on v0

v1 whole, which is shorter than its diff:
```python
import jax
import jax.numpy as jnp
from jax import lax
from jax.experimental import pallas as pl
from jax.experimental.pallas import tpu as pltpu
from jax.sharding import Mesh
from jax.sharding import PartitionSpec as P

HEAD_DIM = 128
BLOCK = 128
HEADS = 5
XH, NZ, NY, XL, NC = 2, 8, 4, 2, 2
ROW = NZ
KEYS = XH * NZ * NY
CHUNK = 4
LOW = -1e30
EXP2_SCALE = HEAD_DIM ** (-0.5) * 1.4426950408889634


def shift(size, by):
    return [(i, (i + by) % size) for i in range(size)]


def swap_planes(x):
    pairs = [((0, 0), (0, 0)), ((1, 1), (1, 1)), ((0, 1), (1, 0)), ((1, 0), (0, 1))]
    return lax.ppermute(x, ("xh", "c"), [(a * 2 + b, d * 2 + e) for (a, b), (d, e) in pairs])


def attend_kernel(count_ref, list_ref, q_ref, *refs):
    sources, out_ref, kv_ref, s_ref, sems = refs[:8], refs[8], refs[9], refs[10], refs[11]
    copies = [
        pltpu.make_async_copy(sources[i], kv_ref.at[pl.ds(i * NZ, NZ)], sems.at[i])
        for i in range(8)
    ]
    for copy in copies:
        copy.start()
    for copy in copies:
        copy.wait()

    def one_query_block(index, carry):
        query = q_ref[index]
        live = count_ref[index]
        steps = (live + (CHUNK - 1)) // CHUNK

        def score(step, top):
            for u in range(CHUNK):
                i = step * CHUNK + u
                key = kv_ref[list_ref[index, i], 0:BLOCK, :]
                s = lax.dot_general(
                    query, key, (((1,), (1,)), ((), ())), preferred_element_type=jnp.float32
                )
                s = jnp.where(i < live, s, LOW)
                s_ref[i] = s
                top = jnp.maximum(top, s)
            return top

        top = lax.fori_loop(0, steps, score, jnp.full((BLOCK, BLOCK), LOW, jnp.float32))
        top = jnp.max(top, axis=1, keepdims=True)

        def mix(step, state):
            total, accum = state
            for u in range(CHUNK):
                i = step * CHUNK + u
                value = kv_ref[list_ref[index, i], BLOCK : 2 * BLOCK, :]
                weight = jnp.exp2((s_ref[i] - top) * EXP2_SCALE)
                total = total + weight
                accum = accum + jnp.dot(
                    weight.astype(jnp.bfloat16), value, preferred_element_type=jnp.float32
                )
            return total, accum

        zero = jnp.zeros((BLOCK, BLOCK), jnp.float32)
        total, accum = lax.fori_loop(0, steps, mix, (zero, zero))
        total = jnp.sum(total, axis=1, keepdims=True)
        out_ref[index] = (accum / total).astype(jnp.bfloat16)
        return carry

    lax.fori_loop(0, ROW, one_query_block, 0)


def attend(count, live_list, query, parts):
    return pl.pallas_call(
        attend_kernel,
        out_shape=jax.ShapeDtypeStruct((ROW, BLOCK, HEAD_DIM), jnp.bfloat16),
        in_specs=[
            pl.BlockSpec(memory_space=pltpu.SMEM),
            pl.BlockSpec(memory_space=pltpu.SMEM),
            pl.BlockSpec(memory_space=pltpu.VMEM),
        ]
        + [pl.BlockSpec(memory_space=pl.ANY)] * 8,
        out_specs=pl.BlockSpec(memory_space=pltpu.VMEM),
        scratch_shapes=[
            pltpu.VMEM((KEYS, 2 * BLOCK, HEAD_DIM), jnp.bfloat16),
            pltpu.VMEM((KEYS, BLOCK, BLOCK), jnp.float32),
            pltpu.SemaphoreType.DMA((8,)),
        ],
        compiler_params=pltpu.CompilerParams(vmem_limit_bytes=24 * 1024 * 1024),
    )(count, live_list, query, *parts)


def live_lists(frame_mask):
    y, c = lax.axis_index("y"), lax.axis_index("c")
    z = jnp.arange(NZ, dtype=jnp.int32)
    own = 32 * c + 4 * z + y
    order = []
    for back in range(NY):
        for plane in (c, 1 - c):
            order.append(32 * plane + 4 * z + (y - back) % NY)
    order = jnp.concatenate(order)
    ids = jnp.arange(KEYS, dtype=jnp.int32)
    rows = jnp.sum(jnp.where(own[:, None, None] == ids[None, :, None], frame_mask[None], 0), axis=1)
    hit = jnp.sum(jnp.where(order[:, None] == ids[None, :], 1, 0)[None] * rows[:, None, :], axis=2)
    hit = jnp.where(hit > 0, 1, 0)
    before = jnp.sum(
        jnp.where(ids[None, None, :] < ids[None, :, None], 1, 0) * hit[:, None, :], axis=2
    )
    place = (before[:, None, :] == ids[None, :, None]) & (hit[:, None, :] > 0)
    lists = jnp.sum(jnp.where(place, ids[None, None, :], 0), axis=2)
    return jnp.sum(hit, axis=1).astype(jnp.int32), lists.astype(jnp.int32)


def heads_first(x):
    return jnp.transpose(x.reshape(BLOCK, HEADS, HEAD_DIM), (1, 0, 2))


def local(queries, keys, values, frame_mask, w_out):
    xl, c = lax.axis_index("xl"), lax.axis_index("c")
    count, lists = live_lists(frame_mask)
    qkv = jnp.concatenate([heads_first(queries), heads_first(keys), heads_first(values)], axis=1)
    qkv = swap_planes(qkv)
    qkv = jnp.concatenate([qkv, jnp.zeros((NZ - HEADS,) + qkv.shape[1:], qkv.dtype)], axis=0)
    qkv = lax.all_to_all(qkv, "z", 0, 0, tiled=True)
    query, kv = qkv[:, :BLOCK], qkv[:, BLOCK:]
    columns = [kv] + [lax.ppermute(kv, "y", shift(NY, by)) for by in (1, 2, 3)]
    parts = []
    for column in columns:
        parts += [column, lax.ppermute(column, "c", shift(NC, 1))]
    attended = attend(count, lists, query, parts)
    attended = lax.all_to_all(attended, "z", 0, 0, tiled=True)[:HEADS]
    attended = swap_planes(attended)
    attended = jnp.transpose(attended, (1, 0, 2)).reshape(BLOCK, HEADS * HEAD_DIM)

    width = w_out.shape[1] // 4

    def project(to_xl, to_c):
        w = lax.dynamic_slice(
            w_out, (0, (to_xl * 2 + to_c) * width), (HEADS * HEAD_DIM, width)
        )
        return jnp.dot(attended, w, preferred_element_type=jnp.float32)

    def over_cores(to_xl):
        sent = lax.ppermute(project(to_xl, 1 - c).astype(jnp.bfloat16), "c", shift(NC, 1))
        return project(to_xl, c) + sent.astype(jnp.float32)

    far = lax.ppermute(over_cores(1 - xl).astype(jnp.bfloat16), "xl", shift(XL, 1))
    near = over_cores(xl)
    return (near + far.astype(jnp.float32)).astype(jnp.bfloat16)


def solution(mesh):
    fine = Mesh(mesh.devices.reshape(XH, NZ, NY, XL, NC), ("xh", "z", "y", "xl", "c"))
    seq, head = ("xh", "z", "y"), ("xl", "c")
    in_specs = (P(seq, head), P(seq, head), P(seq, head), P(), P(head, None))
    return jax.shard_map(
        local, mesh=fine, in_specs=in_specs, out_specs=P(seq, head), check_vma=False
    )
```

time: 411 us -> 114 us (0.28)
  waiting for transfers between devices: 352 us -> 46.3 us
  starting transfers between devices: 0.08 us -> 27.3 us
  matrix products: 29 us -> 8.28 us
  blocking collectives: 0 us -> 14.6 us
  between operations: 13.8 us -> 0.2 us
  other arithmetic: 15 us -> 1.88 us
  Pallas kernels: 0 us -> 10.7 us
  local copies, waits for them, and re-layouts: 0.06 us -> 5.05 us
    all_gather x2 -> x0, waiting for transfers between devices: 329 us -> none  [the longest x1 165 us: local(): key_rows = lax.all_gather(keys, 'seq', axis=0, tiled=True)]
    ppermute x0 -> x12, waiting for transfers between devices: none -> 32.4 us  [the longest x3 13.1 us: local(): columns = [kv] + [lax.ppermute(kv, 'y', shift(NY, by)) for by in (1, 2, 3)]]
    reduce_scatter x1 -> x0, waiting for transfers between devices: 22 us -> none  [local(): lax.psum_scatter(partial_rows.astype(jnp.bfloat16), 'head', scatter_dimen...]
    dot_general x11 -> x4, matrix products: 29 us -> 8.28 us  [project(): return jnp.dot(attended, w, preferred_element_type=jnp.float32)]
    ppermute x0 -> x12, starting transfers between devices: none -> 18.8 us  [the longest x2 11.2 us: swap_planes(): lax.ppermute(x, ('xh', 'c'), [(a * 2 + b, d * 2 + e) for (a, b), (d, e) i...]
    all_to_all x0 -> x1, blocking collectives: none -> 14.6 us  [local(): attended = lax.all_to_all(attended, 'z', 0, 0, tiled=True)[:HEADS]]
    all_to_all x0 -> x1, waiting for transfers between devices: none -> 13.9 us  [local(): qkv = lax.all_to_all(qkv, 'z', 0, 0, tiled=True)]
    pallas_call x0 -> x1, Pallas kernels: none -> 10.7 us  [attend(): pl.pallas_call(attend_kernel, out_shape=jax.ShapeDtypeStruct((ROW, BLOCK,...]
  transfers between devices with their start and end apart: 3 -> 13, of which waited for: 3 -> 8; matrix products, arithmetic and copies ran while one was open for 1% -> 5% of each run, Pallas kernels for 0% -> 0%
where the time goes in v1:
time: 114 us
  waiting for transfers between devices  46.3 us (41%)
  starting transfers between devices  27.3 us (24%)
  blocking collectives  14.6 us (13%)
  Pallas kernels  10.7 us (9%)
  matrix products  8.28 us (7%)
  local copies, waits for them, and re-layouts  5.05 us (4%)
  other arithmetic  1.88 us (2%)
    all_to_all x1, blocking collectives, local(): attended = lax.all_to_all(attended, 'z', 0, 0, tiled=True)[:HEADS]  14.6 us
    all_to_all x1, waiting for transfers between devices, local(): qkv = lax.all_to_all(qkv, 'z', 0, 0, tiled=True)  13.9 us
    ppermute x3, waiting for transfers between devices, local(): columns = [kv] + [lax.ppermute(kv, 'y', shift(NY, by)) for by in (1, 2, 3)]  13.1 us
    ppermute x2, starting transfers between devices, swap_planes(): lax.ppermute(x, ('xh', 'c'), [(a * 2 + b, d * 2 + e) for (a, b), (d, e) i...  11.2 us
    pallas_call x1, Pallas kernels, attend(): pl.pallas_call(attend_kernel, out_shape=jax.ShapeDtypeStruct((ROW, BLOCK,...  10.7 us
    ppermute x2, waiting for transfers between devices, swap_planes(): lax.ppermute(x, ('xh', 'c'), [(a * 2 + b, d * 2 + e) for (a, b), (d, e) i...  9.49 us
    all_to_all x1, starting transfers between devices, local(): qkv = lax.all_to_all(qkv, 'z', 0, 0, tiled=True)  8.48 us
    dot_general x4, matrix products, project(): return jnp.dot(attended, w, preferred_element_type=jnp.float32)  8.28 us
  transfers between devices with their start and end apart: 13, of which 8 were waited for; matrix products, arithmetic and copies ran while one was open for 5% of the time, Pallas kernels for 0%

profile of v1, /device:TPU:1, one launch (start us, length us, event | category | flops | bytes accessed | tf_op | source)
XLA Modules:
  0.0 114.2 jit_solution(3724939186526788365)
XLA Ops:
  0.0 1.1 copy.17
  1.3 1.1 copy.15
  2.5 1.1 copy.13
  3.8 6.0 %collective-permute-start = (bf16[5,384,128]{2,1,0:T(8,128)(2,1)S(1)}, bf16[5,384,128]{2,1,0:T(8,128)(2,1)S(1)}, u32[]{:S(2)}, u32[]{:S(2)}) collective-permute-start(bf16[5,384,128]{2,1,0:T(8,128)(2,1)S(1)} %pad_maximum_fusion), channel_id=1, source_target_pairs={{0,0},{129,129},{1,128},{128,1},{2,2},{131,131},{3,130},{130,3},{4... | collective-permute-start | bytes 1474568 | tf_op jit(solution)/shard_map/ppermute | solution.py:26
  9.9 6.5 %collective-permute-done = bf16[5,384,128]{2,1,0:T(8,128)(2,1)S(1)} collective-permute-done((bf16[5,384,128]{2,1,0:T(8,128)(2,1)S(1)}, bf16[5,384,128]{2,1,0:T(8,128)(2,1)S(1)}, u32[]{:S(2)}, u32[]{:S(2)}) %collective-permute-start) | collective-permute-done | bytes 491552 | tf_op jit(solution)/shard_map/ppermute | solution.py:26
  16.4 1.0 concatenate.11
  17.3 8.5 %all-to-all-start = ((bf16[8,384,128]{2,1,0:T(8,128)(2,1)}), bf16[8,384,128]{2,1,0:T(8,128)(2,1)S(1)}, u32[]{:S(2)}, u32[]{:S(2)}) async-start(bf16[8,384,128]{2,1,0:T(8,128)(2,1)} %concatenate.11), calls=%async_computation | async-start | bytes 1572864 | tf_op jit(solution)/shard_map/all_to_all | solution.py:132
  26.0 0.9 select_reduce_fusion.1
  26.9 13.9 %all-to-all-done = bf16[8,384,128]{2,1,0:T(8,128)(2,1)S(1)} async-done(((bf16[8,384,128]{2,1,0:T(8,128)(2,1)}), bf16[8,384,128]{2,1,0:T(8,128)(2,1)S(1)}, u32[]{:S(2)}, u32[]{:S(2)}) %all-to-all-start) | async-done | bytes 786464 | tf_op jit(solution)/shard_map/all_to_all | solution.py:132
  40.8 1.4 %collective-permute-start.2 = (bf16[8,256,128]{2,1,0:T(8,128)(2,1)S(1)}, bf16[8,256,128]{2,1,0:T(8,128)(2,1)S(1)}, u32[]{:S(2)}, u32[]{:S(2)}) collective-permute-start(bf16[8,256,128]{2,1,0:T(8,128)(2,1)S(1)} %slice.13.refs_0_), channel_id=1, source_target_pairs={{0,4},{4,8},{8,12},{12,0},{1,5},{5,9},{9,13},{13,1},{2,6},{6,10},{... | collective-permute-start | bytes 1572872 | tf_op jit(solution)/shard_map/ppermute | solution.py:134
  42.2 2.6 %collective-permute-start.4 = (bf16[8,256,128]{2,1,0:T(8,128)(2,1)S(1)}, bf16[8,256,128]{2,1,0:T(8,128)(2,1)S(1)}, u32[]{:S(2)}, u32[]{:S(2)}) collective-permute-start(bf16[8,256,128]{2,1,0:T(8,128)(2,1)S(1)} %slice.13.refs_0_), channel_id=1, source_target_pairs={{0,8},{4,12},{8,0},{12,4},{1,9},{5,13},{9,1},{13,5},{2,10},{6,14},... | collective-permute-start | bytes 1572872 | tf_op jit(solution)/shard_map/ppermute | solution.py:134
  44.8 1.1 collective-permute-start.6
  46.4 7.5 %collective-permute-done.2.refs_2_ = bf16[8,256,128]{2,1,0:T(8,128)(2,1)S(1)} collective-permute-done((bf16[8,256,128]{2,1,0:T(8,128)(2,1)S(1)}, bf16[8,256,128]{2,1,0:T(8,128)(2,1)S(1)}, u32[]{:S(2)}, u32[]{:S(2)}) %collective-permute-start.2) | collective-permute-done | bytes 524320 | tf_op jit(solution)/shard_map/ppermute | solution.py:134
  53.9 5.6 %collective-permute-done.4.refs_4_ = bf16[8,256,128]{2,1,0:T(8,128)(2,1)S(1)} collective-permute-done((bf16[8,256,128]{2,1,0:T(8,128)(2,1)S(1)}, bf16[8,256,128]{2,1,0:T(8,128)(2,1)S(1)}, u32[]{:S(2)}, u32[]{:S(2)}) %collective-permute-start.4) | collective-permute-done | bytes 524320 | tf_op jit(solution)/shard_map/ppermute | solution.py:134
  62.2 10.7 %shard_map.55 = bf16[8,128,128]{2,1,0:T(8,128)(2,1)S(1)} custom-call(s32[8]{0:T(128)S(1)} %get-tuple-element.6.count_ref, s32[8,64]{1,0:T(8,128)S(1)} %select_reduce_fusion.list_ref, bf16[8,128,128]{2,1,0:T(8,128)(2,1)S(1)} %slice.12.q_ref, bf16[8,256,128]{2,1,0:T(8,128)(2,1)S(1)} %slice.13.refs_0_, bf16[8,256,128]{2,1,0:T(8,128)(2,1)S(1)} %collective-permute-done.1.refs_1_, ...), custom_call_target="tpu_custom_call" | custom-call | tf_op jit(solution)/shard_map/pallas_call | solution.py:82
  72.9 14.6 %all_to_all.10 = bf16[8,128,128]{2,1,0:T(8,128)(2,1)S(1)} all-to-all(bf16[8,128,128]{2,1,0:T(8,128)(2,1)S(1)} %shard_map.55), channel_id=1, replica_groups=mesh['xh'=2,'z'=8,'y'=4,'xl'=2,'c'=2] {'z'}, dimensions={0} | all-to-all | bytes 524288 | tf_op jit(solution)/shard_map/all_to_all | solution.py:139
  87.5 5.1 %collective-permute-start.8 = (bf16[5,128,128]{2,1,0:T(8,128)(2,1)S(1)}, bf16[5,128,128]{2,1,0:T(8,128)(2,1)S(1)}, u32[]{:S(2)}, u32[]{:S(2)}) collective-permute-start(bf16[5,128,128]{2,1,0:T(8,128)(2,1)S(1)} %slice.14), channel_id=1, source_target_pairs={{0,0},{129,129},{1,128},{128,1},{2,2},{131,131},{3,130},{130,3},{4... | collective-permute-start | bytes 491528 | tf_op jit(solution)/shard_map/ppermute | solution.py:26
  92.7 3.0 %collective-permute-done.8 = bf16[5,128,128]{2,1,0:T(8,128)(2,1)S(1)} collective-permute-done((bf16[5,128,128]{2,1,0:T(8,128)(2,1)S(1)}, bf16[5,128,128]{2,1,0:T(8,128)(2,1)S(1)}, u32[]{:S(2)}, u32[]{:S(2)}) %collective-permute-start.8) | collective-permute-done | bytes 163872 | tf_op jit(solution)/shard_map/ppermute | solution.py:26
  95.8 1.9 %convolution_convert_fusion = bf16[128,1280]{1,0:T(8,128)(2,1)S(1)} fusion(bf16[128,640]{0,1:T(8,128)(2,1)S(1)} %bitcast.12, bf16[640,5120]{1,0:T(8,128)(2,1)} %param.9, s32[]{:T(128)S(6)} %select_n.87), kind=kOutput, calls=%fused_computation.5 | convolution fusion | flops 209879040 | bytes 2129924 | tf_op jit(solution)/shard_map/dot_general | solution.py:149
  97.9 1.9 %convolution_convert_fusion.1 = bf16[128,1280]{1,0:T(8,128)(2,1)S(1)} fusion(bf16[128,640]{0,1:T(8,128)(2,1)S(1)} %bitcast.13, bf16[640,5120]{1,0:T(8,128)(2,1)} %param.9, s32[]{:T(128)S(6)} %select_n.85), kind=kOutput, calls=%fused_computation.6 | convolution fusion | flops 209879040 | bytes 2129924 | tf_op jit(solution)/shard_map/dot_general | solution.py:149
  100.3 1.9 %fusion.2 = bf16[128,1280]{1,0:T(8,128)(2,1)S(1)} fusion(bf16[128,640]{0,1:T(8,128)(2,1)S(1)} %bitcast.14, bf16[640,5120]{1,0:T(8,128)(2,1)} %param.9, s32[]{:T(128)S(6)} %select_n.86, bf16[128,1280]{1,0:T(8,128)(2,1)S(1)} %collective-permute-done.10), kind=kOutput, calls=%fused_computation.4 | convolution fusion | flops 210206720 | bytes 2457604 | tf_op jit(solution)/shard_map/dot_general | solution.py:149
  102.2 1.3 %collective-permute-start.11 = (bf16[128,1280]{1,0:T(8,128)(2,1)S(1)}, bf16[128,1280]{1,0:T(8,128)(2,1)S(1)}, u32[]{:S(2)}, u32[]{:S(2)}) collective-permute-start(bf16[128,1280]{1,0:T(8,128)(2,1)S(1)} %fusion.2), channel_id=1, source_target_pairs={{0,2},{2,0},{1,3},{3,1},{4,6},{6,4},{5,7},{7,5},{8,10},{10,8},{9,1... | collective-permute-start | bytes 983048 | tf_op jit(solution)/shard_map/ppermute | solution.py:155
  103.5 8.1 %collective-permute-done.11 = bf16[128,1280]{1,0:T(8,128)(2,1)S(1)} collective-permute-done((bf16[128,1280]{1,0:T(8,128)(2,1)S(1)}, bf16[128,1280]{1,0:T(8,128)(2,1)S(1)}, u32[]{:S(2)}, u32[]{:S(2)}) %collective-permute-start.11) | collective-permute-done | bytes 327712 | tf_op jit(solution)/shard_map/ppermute | solution.py:155
  111.6 2.6 %fusion.1 = bf16[128,1280]{1,0:T(8,128)(2,1)} fusion(bf16[128,640]{0,1:T(8,128)(2,1)S(1)} %bitcast.15, bf16[640,5120]{1,0:T(8,128)(2,1)} %param.9, s32[]{:T(128)S(6)} %select_n.84, bf16[128,1280]{1,0:T(8,128)(2,1)S(1)} %collective-permute-done.11, bf16[128,1280]{1,0:T(8,128)(2,1)S(1)} %collective-permute-done.9), kind=kOutput, calls=%fused_computation.3 | convolution fusion | flops 210534400 | bytes 2785284 | tf_op jit(solution)/shard_map/dot_general | solution.py:149
  (35 shorter events, 4.8 us)
Async XLA Ops:
  3.8 12.5 %collective-permute-start = (bf16[5,384,128]{2,1,0:T(8,128)(2,1)S(1)}, bf16[5,384,128]{2,1,0:T(8,128)(2,1)S(1)}, u32[]{:S(2)}, u32[]{:S(2)}) collective-permute-start(bf16[5,384,128]{2,1,0:T(8,128)(2,1)S(1)} %pad_maximum_fusion), channel_id=1, source_target_pairs={{0,0},{129,129},{1,128},{128,1},{2,2},{131,131},{3,130},{130,3},{4... | collective-permute-start | bytes 1474568 | tf_op jit(solution)/shard_map/ppermute | solution.py:26
  17.3 23.5 %all-to-all-start = ((bf16[8,384,128]{2,1,0:T(8,128)(2,1)}), bf16[8,384,128]{2,1,0:T(8,128)(2,1)S(1)}, u32[]{:S(2)}, u32[]{:S(2)}) async-start(bf16[8,384,128]{2,1,0:T(8,128)(2,1)} %concatenate.11), calls=%async_computation | async-start | bytes 1572864 | tf_op jit(solution)/shard_map/all_to_all | solution.py:132
  40.8 13.1 %collective-permute-start.2 = (bf16[8,256,128]{2,1,0:T(8,128)(2,1)S(1)}, bf16[8,256,128]{2,1,0:T(8,128)(2,1)S(1)}, u32[]{:S(2)}, u32[]{:S(2)}) collective-permute-start(bf16[8,256,128]{2,1,0:T(8,128)(2,1)S(1)} %slice.13.refs_0_), channel_id=1, source_target_pairs={{0,4},{4,8},{8,12},{12,0},{1,5},{5,9},{9,13},{13,1},{2,6},{6,10},{... | collective-permute-start | bytes 1572872 | tf_op jit(solution)/shard_map/ppermute | solution.py:134
  42.2 17.3 %collective-permute-start.4 = (bf16[8,256,128]{2,1,0:T(8,128)(2,1)S(1)}, bf16[8,256,128]{2,1,0:T(8,128)(2,1)S(1)}, u32[]{:S(2)}, u32[]{:S(2)}) collective-permute-start(bf16[8,256,128]{2,1,0:T(8,128)(2,1)S(1)} %slice.13.refs_0_), channel_id=1, source_target_pairs={{0,8},{4,12},{8,0},{12,4},{1,9},{5,13},{9,1},{13,5},{2,10},{6,14},... | collective-permute-start | bytes 1572872 | tf_op jit(solution)/shard_map/ppermute | solution.py:134
  44.8 14.7 %collective-permute-start.6 = (bf16[8,256,128]{2,1,0:T(8,128)(2,1)S(1)}, bf16[8,256,128]{2,1,0:T(8,128)(2,1)S(1)}, u32[]{:S(2)}, u32[]{:S(2)}) collective-permute-start(bf16[8,256,128]{2,1,0:T(8,128)(2,1)S(1)} %slice.13.refs_0_), channel_id=1, source_target_pairs={{0,12},{4,0},{8,4},{12,8},{1,13},{5,1},{9,5},{13,9},{2,14},{6,2},{... | collective-permute-start | bytes 1572872 | tf_op jit(solution)/shard_map/ppermute | solution.py:134
  46.3 14.2 %collective-permute-start.1 = (bf16[8,256,128]{2,1,0:T(8,128)(2,1)S(1)}, bf16[8,256,128]{2,1,0:T(8,128)(2,1)S(1)}, u32[]{:S(2)}, u32[]{:S(2)}) collective-permute-start(bf16[8,256,128]{2,1,0:T(8,128)(2,1)S(1)} %slice.13.refs_0_), channel_id=1, source_target_pairs={{0,1},{1,0},{2,3},{3,2},{4,5},{5,4},{6,7},{7,6},{8,9},{9,8},{10,11... | collective-permute-start | bytes 1572872 | tf_op jit(solution)/shard_map/ppermute | solution.py:137
  53.9 6.6 %collective-permute-start.3 = (bf16[8,256,128]{2,1,0:T(8,128)(2,1)S(1)}, bf16[8,256,128]{2,1,0:T(8,128)(2,1)S(1)}, u32[]{:S(2)}, u32[]{:S(2)}) collective-permute-start(bf16[8,256,128]{2,1,0:T(8,128)(2,1)S(1)} %collective-permute-done.2.refs_2_), channel_id=1, source_target_pairs={{0,1},{1,0},{2,3},{3,2},{4,5},{5,4},{6,7},{7,6},{8,9},{9,8},{10,11... | collective-permute-start | bytes 1572872 | tf_op jit(solution)/shard_map/ppermute | solution.py:137
  59.6 1.9 %collective-permute-start.5 = (bf16[8,256,128]{2,1,0:T(8,128)(2,1)S(1)}, bf16[8,256,128]{2,1,0:T(8,128)(2,1)S(1)}, u32[]{:S(2)}, u32[]{:S(2)}) collective-permute-start(bf16[8,256,128]{2,1,0:T(8,128)(2,1)S(1)} %collective-permute-done.4.refs_4_), channel_id=1, source_target_pairs={{0,1},{1,0},{2,3},{3,2},{4,5},{5,4},{6,7},{7,6},{8,9},{9,8},{10,11... | collective-permute-start | bytes 1572872 | tf_op jit(solution)/shard_map/ppermute | solution.py:137
  59.6 2.7 %collective-permute-start.7 = (bf16[8,256,128]{2,1,0:T(8,128)(2,1)S(1)}, bf16[8,256,128]{2,1,0:T(8,128)(2,1)S(1)}, u32[]{:S(2)}, u32[]{:S(2)}) collective-permute-start(bf16[8,256,128]{2,1,0:T(8,128)(2,1)S(1)} %collective-permute-done.6.refs_6_), channel_id=1, source_target_pairs={{0,1},{1,0},{2,3},{3,2},{4,5},{5,4},{6,7},{7,6},{8,9},{9,8},{10,11... | collective-permute-start | bytes 1572872 | tf_op jit(solution)/shard_map/ppermute | solution.py:137
  87.5 8.1 %collective-permute-start.8 = (bf16[5,128,128]{2,1,0:T(8,128)(2,1)S(1)}, bf16[5,128,128]{2,1,0:T(8,128)(2,1)S(1)}, u32[]{:S(2)}, u32[]{:S(2)}) collective-permute-start(bf16[5,128,128]{2,1,0:T(8,128)(2,1)S(1)} %slice.14), channel_id=1, source_target_pairs={{0,0},{129,129},{1,128},{128,1},{2,2},{131,131},{3,130},{130,3},{4... | collective-permute-start | bytes 491528 | tf_op jit(solution)/shard_map/ppermute | solution.py:26
  97.7 2.6 %collective-permute-start.10 = (bf16[128,1280]{1,0:T(8,128)(2,1)S(1)}, bf16[128,1280]{1,0:T(8,128)(2,1)S(1)}, u32[]{:S(2)}, u32[]{:S(2)}) collective-permute-start(bf16[128,1280]{1,0:T(8,128)(2,1)S(1)} %convolution_convert_fusion), channel_id=1, source_target_pairs={{0,1},{1,0},{2,3},{3,2},{4,5},{5,4},{6,7},{7,6},{8,9},{9,8},{10,11... | collective-permute-start | bytes 983048 | tf_op jit(solution)/shard_map/ppermute | solution.py:152
  99.7 3.8 %collective-permute-start.9 = (bf16[128,1280]{1,0:T(8,128)(2,1)S(1)}, bf16[128,1280]{1,0:T(8,128)(2,1)S(1)}, u32[]{:S(2)}, u32[]{:S(2)}) collective-permute-start(bf16[128,1280]{1,0:T(8,128)(2,1)S(1)} %convolution_convert_fusion.1), channel_id=1, source_target_pairs={{0,1},{1,0},{2,3},{3,2},{4,5},{5,4},{6,7},{7,6},{8,9},{9,8},{10,11... | collective-permute-start | bytes 983048 | tf_op jit(solution)/shard_map/ppermute | solution.py:152
  102.2 9.4 %collective-permute-start.11 = (bf16[128,1280]{1,0:T(8,128)(2,1)S(1)}, bf16[128,1280]{1,0:T(8,128)(2,1)S(1)}, u32[]{:S(2)}, u32[]{:S(2)}) collective-permute-start(bf16[128,1280]{1,0:T(8,128)(2,1)S(1)} %fusion.2), channel_id=1, source_target_pairs={{0,2},{2,0},{1,3},{3,1},{4,6},{6,4},{5,7},{7,5},{8,10},{10,8},{9,1... | collective-permute-start | bytes 983048 | tf_op jit(solution)/shard_map/ppermute | solution.py:155

commit v2 on v0

v2 whole, which is shorter than its diff:
```python
import jax
import jax.numpy as jnp
from jax import lax
from jax.experimental import pallas as pl
from jax.experimental.pallas import tpu as pltpu
from jax.sharding import Mesh
from jax.sharding import PartitionSpec as P

HEAD_DIM = 128
BLOCK = 128
HALF = 64
HEADS = 5
XH, NZ, NY, XL, NC = 2, 8, 4, 2, 2
ROWS = XH * NZ
TILES = ROWS * ROWS // 2
UNROLL = 4
TILE_N = 256
LOW = -1e30
EXP2_SCALE = HEAD_DIM ** (-0.5) * 1.4426950408889634
MIB = 1024 * 1024


def shift(size, by):
    return [(i, (i + by) % size) for i in range(size)]


def in_vmem(count):
    return [pl.BlockSpec(memory_space=pltpu.VMEM)] * count


def in_smem(count):
    return [pl.BlockSpec(memory_space=pltpu.SMEM)] * count


def split_kernel(core_ref, q_ref, k_ref, v_ref, keep_ref, send_ref):
    core = core_ref[0]
    mine = pl.ds(pl.multiple_of(core * HALF, HALF), HALF)
    other = pl.ds(pl.multiple_of((1 - core) * HALF, HALF), HALF)
    keep_ref[...] = jnp.zeros_like(keep_ref)
    for head in range(HEADS):
        lanes = slice(head * HEAD_DIM, (head + 1) * HEAD_DIM)
        for t, ref in enumerate((q_ref, k_ref, v_ref)):
            rows = slice(t * HALF, (t + 1) * HALF)
            keep_ref[core * NZ + head, rows, :] = ref[mine, lanes]
            send_ref[head, rows, :] = ref[other, lanes]


def split(core, queries, keys, values):
    return pl.pallas_call(
        split_kernel,
        out_shape=(
            jax.ShapeDtypeStruct((ROWS, 3 * HALF, HEAD_DIM), jnp.bfloat16),
            jax.ShapeDtypeStruct((HEADS, 3 * HALF, HEAD_DIM), jnp.bfloat16),
        ),
        in_specs=in_smem(1) + in_vmem(3),
        out_specs=tuple(in_vmem(2)),
    )(core, queries, keys, values)


def column_kernel(first, count_ref, table_ref, q_ref, kv_ref, *refs):
    if first:
        m_ref, l_ref, a_ref, s_ref, top_ref = refs
    else:
        m_in, l_in, a_in, m_ref, l_ref, a_ref, s_ref, top_ref = refs
    steps = (count_ref[0] + (UNROLL - 1)) // UNROLL
    lane = lax.broadcasted_iota(jnp.int32, (BLOCK, BLOCK), 1)
    top_ref[...] = jnp.full(top_ref.shape, LOW, jnp.float32)

    def score(step, carry):
        tiles = []
        for u in range(UNROLL):
            e = step * UNROLL + u
            key = jnp.concatenate(
                [kv_ref[table_ref[1, e], :HALF, :], kv_ref[table_ref[2, e], :HALF, :]], axis=0
            )
            s = lax.dot_general(
                q_ref[table_ref[0, e]],
                key,
                (((1,), (1,)), ((), ())),
                preferred_element_type=jnp.float32,
            )
            s = jnp.where(lane < table_ref[3, e], s, LOW)
            s_ref[e] = s
            tiles.append(s)
        for u in range(UNROLL):
            block = table_ref[0, step * UNROLL + u]
            top_ref[block] = jnp.maximum(top_ref[block], tiles[u])
        return carry

    lax.fori_loop(0, steps, score, 0)

    for block in range(ROWS):
        top = jnp.max(top_ref[block], axis=1, keepdims=True)
        if first:
            m_ref[block] = jnp.broadcast_to(top, (BLOCK, BLOCK))
            l_ref[block] = jnp.zeros((BLOCK, BLOCK), jnp.float32)
            a_ref[block] = jnp.zeros((BLOCK, HEAD_DIM), jnp.float32)
        else:
            new = jnp.maximum(m_in[block], top)
            fade = jnp.exp2((m_in[block] - new) * EXP2_SCALE)
            m_ref[block] = new
            l_ref[block] = l_in[block] * fade
            a_ref[block] = a_in[block] * fade

    def mix(step, carry):
        weights, products = [], []
        for u in range(UNROLL):
            e = step * UNROLL + u
            value = jnp.concatenate(
                [kv_ref[table_ref[1, e], HALF:, :], kv_ref[table_ref[2, e], HALF:, :]], axis=0
            )
            weight = jnp.exp2((s_ref[e] - m_ref[table_ref[0, e]]) * EXP2_SCALE)
            weights.append(weight)
            products.append(
                jnp.dot(weight.astype(jnp.bfloat16), value, preferred_element_type=jnp.float32)
            )
        for u in range(UNROLL):
            block = table_ref[0, step * UNROLL + u]
            l_ref[block] = l_ref[block] + weights[u]
            a_ref[block] = a_ref[block] + products[u]
        return carry

    lax.fori_loop(0, steps, mix, 0)


def attend_column(count, table, query, kv, state):
    first = state is None
    shape = jax.ShapeDtypeStruct((ROWS, BLOCK, BLOCK), jnp.float32)

    def kernel(*refs):
        column_kernel(first, *refs)

    return pl.pallas_call(
        kernel,
        out_shape=(shape, shape, shape),
        in_specs=in_smem(2) + in_vmem(2 if first else 5),
        out_specs=tuple(in_vmem(3)),
        scratch_shapes=[
            pltpu.VMEM((TILES, BLOCK, BLOCK), jnp.float32),
            pltpu.VMEM((ROWS, BLOCK, BLOCK), jnp.float32),
        ],
        compiler_params=pltpu.CompilerParams(vmem_limit_bytes=24 * MIB),
        cost_estimate=pl.CostEstimate(
            flops=2 * 20 * 2 * 128**3, bytes_accessed=6 * MIB, transcendentals=20 * 128 * 128
        ),
    )(count, table, query, kv, *(() if first else state))


def parcel_kernel(m_ref, l_ref, a_ref, keep_ref, send_ref):
    lane = lax.broadcasted_iota(jnp.int32, (BLOCK, BLOCK), 1)
    stats = jnp.zeros((BLOCK, BLOCK), jnp.float32)
    for block in range(ROWS):
        total = jnp.sum(l_ref[block], axis=1, keepdims=True)
        stats = jnp.where(lane == block, m_ref[block], stats)
        stats = jnp.where(lane == ROWS + block, total, stats)
        keep_ref[block] = a_ref[block, :HALF, :]
        send_ref[block] = a_ref[block, HALF:, :]
    keep_ref[ROWS] = stats[:HALF]
    send_ref[ROWS] = stats[HALF:]


def parcel(state):
    shape = jax.ShapeDtypeStruct((ROWS + 1, HALF, HEAD_DIM), jnp.float32)
    return pl.pallas_call(
        parcel_kernel,
        out_shape=(shape, shape),
        in_specs=in_vmem(3),
        out_specs=tuple(in_vmem(2)),
    )(*state)


def merge_kernel(here_ref, there_ref, out_ref):
    here, there = here_ref[ROWS], there_ref[ROWS]
    for block in range(ROWS):
        m0, m1 = here[:, block : block + 1], there[:, block : block + 1]
        l0 = here[:, ROWS + block : ROWS + block + 1]
        l1 = there[:, ROWS + block : ROWS + block + 1]
        m = jnp.maximum(m0, m1)
        f0 = jnp.exp2((m0 - m) * EXP2_SCALE)
        f1 = jnp.exp2((m1 - m) * EXP2_SCALE)
        mixed = here_ref[block] * f0 + there_ref[block] * f1
        out_ref[block] = (mixed / (l0 * f0 + l1 * f1)).astype(jnp.bfloat16)


def merge(here, there):
    return pl.pallas_call(
        merge_kernel,
        out_shape=jax.ShapeDtypeStruct((ROWS, HALF, HEAD_DIM), jnp.bfloat16),
        in_specs=in_vmem(2),
        out_specs=in_vmem(1)[0],
    )(here, there)


def project_kernel(place_ref, a_ref, b_ref, w_ref, w2_ref, out_ref, rows_ref):
    core = place_ref[0]

    @pl.when(pl.program_id(0) == 0)
    def _():
        mine = pl.ds(pl.multiple_of(core * HALF, HALF), HALF)
        other = pl.ds(pl.multiple_of((1 - core) * HALF, HALF), HALF)
        for which, head_set in enumerate((core, 1 - core)):
            for head in range(HEADS):
                at = (which * HEADS + head) * HEAD_DIM
                rows_ref[mine, at : at + HEAD_DIM] = a_ref[head_set * NZ + head]
                rows_ref[other, at : at + HEAD_DIM] = b_ref[head_set * NZ + head]

    width = HEADS * HEAD_DIM
    out = jnp.dot(rows_ref[:, :width], w_ref[...], preferred_element_type=jnp.float32)
    out = out + jnp.dot(rows_ref[:, width:], w2_ref[0], preferred_element_type=jnp.float32)
    out_ref[...] = out.astype(out_ref.dtype)


def project(place, a, b, w_own, w_other, dtype):
    width = w_own.shape[1] // (XL * NC)
    tiles = width // TILE_N
    deep = HEADS * HEAD_DIM
    whole = pl.BlockSpec((ROWS, HALF, HEAD_DIM), lambda i, place: (0, 0, 0))
    return pl.pallas_call(
        project_kernel,
        out_shape=jax.ShapeDtypeStruct((BLOCK, width), dtype),
        grid_spec=pltpu.PrefetchScalarGridSpec(
            num_scalar_prefetch=1,
            grid=(tiles,),
            in_specs=[
                whole,
                whole,
                pl.BlockSpec(
                    (deep, TILE_N), lambda i, place: (0, (place[1] * NC + place[0]) * tiles + i)
                ),
                pl.BlockSpec((1, deep, TILE_N), lambda i, place: (place[1], 0, i)),
            ],
            out_specs=pl.BlockSpec((BLOCK, TILE_N), lambda i, place: (0, i)),
            scratch_shapes=[pltpu.VMEM((BLOCK, 2 * deep), jnp.bfloat16)],
        ),
        cost_estimate=pl.CostEstimate(
            flops=2 * BLOCK * 2 * deep * width, bytes_accessed=4 * MIB, transcendentals=0
        ),
    )(place, a, b, w_own, w_other)


def live_tiles(frame_mask):
    y = lax.axis_index("y")
    ids = jnp.arange(ROWS, dtype=jnp.int32)
    blocks = jnp.arange(ROWS * NY, dtype=jnp.int32)
    mine = ids * NY + y
    back = jnp.arange(NY, dtype=jnp.int32)
    theirs = ids[None, :] * NY + ((y - back) % NY)[:, None]
    rows = jnp.sum(
        jnp.where(mine[:, None, None] == blocks[None, :, None], frame_mask[None], 0), axis=1
    )
    hit = jnp.sum(
        jnp.where(theirs[:, None, :, None] == blocks, rows[None, :, None, :], 0), axis=3
    )
    hit = jnp.where(hit != 0, 1, 0)
    rank = jnp.sum(jnp.where(ids[None, :] < ids[:, None], hit[:, :, None, :], 0), axis=3)
    count = jnp.sum(hit, axis=2)
    tiles = (count + 1) // 2
    start = jnp.sum(jnp.where(ids[None, :] < ids[:, None], tiles[:, None, :], 0), axis=2)
    e = jnp.arange(TILES, dtype=jnp.int32)
    chosen = (start[:, :, None] <= e) & (e < (start + tiles)[:, :, None])
    pick = lambda x: jnp.sum(jnp.where(chosen, x, 0), axis=1)
    at = 2 * (e[None, :] - pick(start[:, :, None]))
    live = jnp.clip(pick(count[:, :, None]) - at, 0, 2) * HALF
    live = jnp.where(jnp.any(chosen, axis=1), live, 0)

    def key_at(place):
        found = chosen[:, :, None, :] & (hit[:, :, :, None] > 0)
        found = found & (rank[:, :, :, None] == place[:, None, None, :])
        return jnp.sum(jnp.where(found, ids[None, None, :, None], 0), axis=(1, 2))

    table = jnp.stack([pick(ids[None, :, None]), key_at(at), key_at(at + 1), live], axis=1)
    return jnp.sum(tiles, axis=1).astype(jnp.int32), table.astype(jnp.int32)


def local(queries, keys, values, frame_mask, w_out):
    xl, c = lax.axis_index("xl"), lax.axis_index("c")
    core = jnp.stack([c]).astype(jnp.int32)

    slots, sent = split(core, queries, keys, values)
    got = lax.ppermute(sent, "c", shift(NC, 1))
    slots = lax.dynamic_update_slice(slots, got, ((1 - c) * NZ, 0, 0))
    slots, w_out, frame_mask = lax.optimization_barrier((slots, w_out, frame_mask))

    counts, tables = live_tiles(frame_mask)
    width = w_out.shape[1] // (XL * NC)
    traded = jnp.stack(
        [
            lax.dynamic_slice(
                w_out, (0, (part * NC + 1 - c) * width), (HEADS * HEAD_DIM, width)
            )
            for part in range(XL)
        ]
    )
    w_other = lax.ppermute(traded, "c", shift(NC, 1))

    slots = lax.all_to_all(slots, ("xh", "z"), 0, 0, tiled=True)
    own_query, kv = slots[:, :HALF], slots[:, HALF:]
    query = jnp.concatenate([own_query, lax.ppermute(own_query, "c", shift(NC, 1))], axis=1)
    state = None
    for by in (0, 1, 3, 2):
        column = kv if by == 0 else lax.ppermute(kv, "y", shift(NY, by))
        state = attend_column(counts[by : by + 1], tables[by], query, column, state)
    here, sent = parcel(state)
    there = lax.ppermute(sent, "c", shift(NC, 1))
    attended = lax.all_to_all(merge(here, there), ("xh", "z"), 0, 0, tiled=True)
    other_rows = lax.ppermute(attended, "c", shift(NC, 1))

    def columns_of(to_xl, dtype):
        place = jnp.stack([c, to_xl]).astype(jnp.int32)
        return project(place, attended, other_rows, w_out, w_other, dtype)

    far = lax.ppermute(columns_of(1 - xl, jnp.bfloat16), "xl", shift(XL, 1))
    near = columns_of(xl, jnp.float32)
    return (near + far.astype(jnp.float32)).astype(jnp.bfloat16)


def solution(mesh):
    fine = Mesh(mesh.devices.reshape(XH, NZ, NY, XL, NC), ("xh", "z", "y", "xl", "c"))
    seq, head = ("xh", "z", "y"), ("xl", "c")
    in_specs = (P(seq, head), P(seq, head), P(seq, head), P(), P(head, None))
    return jax.shard_map(
        local, mesh=fine, in_specs=in_specs, out_specs=P(seq, head), check_vma=False
    )
```

time: 411 us -> 127 us (0.31)
  the two profiles are of different devices: /device:TPU:1 before, /device:TPU:16 now
where the time goes in v2:
time: 127 us; the launch traced here: 126 us
  waiting for transfers between devices  38.2 us (30%)
  Pallas kernels  34.7 us (27%)
  blocking collectives  18.9 us (15%)
  starting transfers between devices  15.5 us (12%)
  other arithmetic  9.64 us (8%)
  local copies, waits for them, and re-layouts  9.16 us (7%)
    all_to_all x1, blocking collectives, local(): attended = lax.all_to_all(merge(here, there), ('xh', 'z'), 0, 0, tiled=True)  18.9 us
    all_to_all x1, waiting for transfers between devices, local(): slots = lax.all_to_all(slots, ('xh', 'z'), 0, 0, tiled=True)  17 us
    pallas_call x4, Pallas kernels, attend_column(): pl.pallas_call(kernel, out_shape=(shape, shape, shape), in_specs=in_smem(...  15.3 us
    ppermute x3, waiting for transfers between devices, local(): column = kv if by == 0 else lax.ppermute(kv, 'y', shift(NY, by))  11.5 us
    pallas_call x2, Pallas kernels, project(): pl.pallas_call(project_kernel, out_shape=jax.ShapeDtypeStruct((BLOCK, wid...  11.4 us
    all_to_all x1, starting transfers between devices, local(): slots = lax.all_to_all(slots, ('xh', 'z'), 0, 0, tiled=True)  11.1 us
    ppermute x3, starting transfers between devices, local(): column = kv if by == 0 else lax.ppermute(kv, 'y', shift(NY, by))  3.65 us
    unnamed x10, local copies, waits for them, and re-layouts  3.59 us
  transfers between devices with their start and end apart: 10, of which 7 were waited for; matrix products, arithmetic and copies ran while one was open for 8% of the time, Pallas kernels for 21%

profile of v2, /device:TPU:16, one launch (start us, length us, event | category | flops | bytes accessed | tf_op | source)
XLA Modules:
  0.0 126.2 jit_solution(5239511307943910315)
XLA Ops:
  0.0 2.2 %shard_map.55 = (bf16[16,192,128]{2,1,0:T(8,128)(2,1)}, bf16[5,192,128]{2,1,0:T(8,128)(2,1)}) custom-call(s32[1]{0:T(128)} %bitcast.core_ref, bf16[128,640]{1,0:T(8,128)(2,1)} %q_ref.1, bf16[128,640]{1,0:T(8,128)(2,1)} %k_ref.1, bf16[128,640]{1,0:T(8,128)(2,1)} %v_ref.1), custom_call_target="tpu_custom_call" | custom-call | tf_op jit(solution)/shard_map/pallas_call | solution.py:49
  2.5 1.5 %collective-permute-done = bf16[5,192,128]{2,1,0:T(8,128)(2,1)S(1)} collective-permute-done((bf16[5,192,128]{2,1,0:T(8,128)(2,1)}, bf16[5,192,128]{2,1,0:T(8,128)(2,1)S(1)}, u32[]{:S(2)}, u32[]{:S(2)}) %collective-permute-start) | collective-permute-done | bytes 245792 | tf_op jit(solution)/shard_map/ppermute | solution.py:280
  5.6 1.2 select_reduce_fusion.3
  6.9 11.1 %all-to-all-start = ((bf16[16,192,128]{2,1,0:T(8,128)(2,1)}), bf16[16,192,128]{2,1,0:T(8,128)(2,1)}, u32[]{:S(2)}, u32[]{:S(2)}) async-start(bf16[16,192,128]{2,1,0:T(8,128)(2,1)} %constant_dynamic-update-slice_fusion), calls=%async_computation | async-start | bytes 1572864 | tf_op jit(solution)/shard_map/all_to_all | solution.py:296
  18.0 2.1 %dynamic-slice_bitcast_fusion.1 = (bf16[1,640,1280]{2,1,0:T(8,128)(2,1)S(1)}, bf16[1,640,1280]{2,1,0:T(8,128)(2,1)S(1)}) fusion(bf16[640,5120]{1,0:T(8,128)(2,1)} %w_ref.1, s32[]{:T(128)S(6)} %select_n.104, s32[]{:T(128)S(6)} %select_n.105), kind=kLoop, calls=%fused_computation.2 | loop fusion | bytes 6553608 | tf_op jit(solution)/shard_map/stack | solution.py:286
  20.2 2.0 %pad_maximum_fusion = bf16[2,640,1280]{2,1,0:T(8,128)(2,1)} fusion(bf16[1,640,1280]{2,1,0:T(8,128)(2,1)S(1)} %get-tuple-element.51, bf16[1,640,1280]{2,1,0:T(8,128)(2,1)S(1)} %get-tuple-element.50), kind=kLoop, calls=%fused_computation | loop fusion | flops 1638400 | bytes 6553600 | tf_op jit(solution)/shard_map/stack | solution.py:286
  22.6 1.2 select_reduce_fusion.2
  24.3 17.0 %all-to-all-done = bf16[16,192,128]{2,1,0:T(8,128)(2,1)} async-done(((bf16[16,192,128]{2,1,0:T(8,128)(2,1)}), bf16[16,192,128]{2,1,0:T(8,128)(2,1)}, u32[]{:S(2)}, u32[]{:S(2)}) %all-to-all-start) | async-done | bytes 786464 | tf_op jit(solution)/shard_map/all_to_all | solution.py:296
  42.4 1.4 %collective-permute-start.4 = (bf16[16,128,128]{2,1,0:T(8,128)(2,1)S(1)}, bf16[16,128,128]{2,1,0:T(8,128)(2,1)S(1)}, u32[]{:S(2)}, u32[]{:S(2)}) collective-permute-start(bf16[16,128,128]{2,1,0:T(8,128)(2,1)S(1)} %slice.42.refs_3_), channel_id=1, source_target_pairs={{0,4},{4,8},{8,12},{12,0},{1,5},{5,9},{9,13},{13,1},{2,6},{6,10},{... | collective-permute-start | bytes 1572872 | tf_op jit(solution)/shard_map/ppermute | solution.py:301
  44.5 1.5 %collective-permute-start.2 = (bf16[16,128,128]{2,1,0:T(8,128)(2,1)S(1)}, bf16[16,128,128]{2,1,0:T(8,128)(2,1)S(1)}, u32[]{:S(2)}, u32[]{:S(2)}) collective-permute-start(bf16[16,128,128]{2,1,0:T(8,128)(2,1)S(1)} %slice.42.refs_3_), channel_id=1, source_target_pairs={{0,8},{4,12},{8,0},{12,4},{1,9},{5,13},{9,1},{13,5},{2,10},{6,14},... | collective-permute-start | bytes 1572872 | tf_op jit(solution)/shard_map/ppermute | solution.py:301
  47.8 1.5 %collective-permute-done.1 = bf16[16,64,128]{2,1,0:T(8,128)(2,1)S(1)} collective-permute-done((bf16[16,64,128]{2,1,0:T(8,128)(2,1)S(1)}, bf16[16,64,128]{2,1,0:T(8,128)(2,1)S(1)}, u32[]{:S(2)}, u32[]{:S(2)}) %collective-permute-start.1) | collective-permute-done | bytes 262176 | tf_op jit(solution)/shard_map/ppermute | solution.py:298
  49.3 4.2 %shard_map.56 = (f32[16,128,128]{2,1,0:T(8,128)S(1)}, f32[16,128,128]{2,1,0:T(8,128)S(1)}, f32[16,128,128]{2,1,0:T(8,128)S(1)}) custom-call(s32[1]{0:T(128)} %get-tuple-element.62.refs_0_, s32[4,128]{1,0:T(4,128)S(1)} %get-tuple-element.54.refs_1_, bf16[16,128,128]{2,1,0:T(8,128)(2,1)S(1)} %pad_maximum_fusion.1.refs_2_, bf16[16,128,128]{2,1,0:T(8,128)(2,1)S(1)} %slice.42.refs_3_), custom_call_target="tpu_custom_call" | custom-call | flops 167772160 | bytes 6291456 | tf_op jit(solution)/shard_map/pallas_call | solution.py:133
  53.5 11.5 %collective-permute-done.4.refs_3_ = bf16[16,128,128]{2,1,0:T(8,128)(2,1)S(1)} collective-permute-done((bf16[16,128,128]{2,1,0:T(8,128)(2,1)S(1)}, bf16[16,128,128]{2,1,0:T(8,128)(2,1)S(1)}, u32[]{:S(2)}, u32[]{:S(2)}) %collective-permute-start.4) | collective-permute-done | bytes 524320 | tf_op jit(solution)/shard_map/ppermute | solution.py:301
  65.1 3.7 %shard_map.57 = (f32[16,128,128]{2,1,0:T(8,128)S(1)}, f32[16,128,128]{2,1,0:T(8,128)S(1)}, f32[16,128,128]{2,1,0:T(8,128)S(1)}) custom-call(s32[1]{0:T(128)} %get-tuple-element.63.refs_0_, s32[4,128]{1,0:T(4,128)S(1)} %get-tuple-element.55.refs_1_, bf16[16,128,128]{2,1,0:T(8,128)(2,1)S(1)} %pad_maximum_fusion.1.refs_2_, ...), custom_call_target="tpu_custom_call" | custom-call | flops 167772160 | bytes 6291456 | tf_op jit(solution)/shard_map/pallas_call | solution.py:133
  68.8 3.8 %shard_map.58 = (f32[16,128,128]{2,1,0:T(8,128)S(1)}, f32[16,128,128]{2,1,0:T(8,128)S(1)}, f32[16,128,128]{2,1,0:T(8,128)S(1)}) custom-call(s32[1]{0:T(128)} %get-tuple-element.64.refs_0_, s32[4,128]{1,0:T(4,128)S(1)} %get-tuple-element.56.refs_1_, bf16[16,128,128]{2,1,0:T(8,128)(2,1)S(1)} %pad_maximum_fusion.1.refs_2_, ...), custom_call_target="tpu_custom_call" | custom-call | flops 167772160 | bytes 6291456 | tf_op jit(solution)/shard_map/pallas_call | solution.py:133
  72.6 3.6 %shard_map.59 = (f32[16,128,128]{2,1,0:T(8,128)S(1)}, f32[16,128,128]{2,1,0:T(8,128)S(1)}, f32[16,128,128]{2,1,0:T(8,128)S(1)}) custom-call(s32[1]{0:T(128)} %get-tuple-element.65.refs_0_, s32[4,128]{1,0:T(4,128)S(1)} %get-tuple-element.57.refs_1_, bf16[16,128,128]{2,1,0:T(8,128)(2,1)S(1)} %pad_maximum_fusion.1.refs_2_, ...), custom_call_target="tpu_custom_call" | custom-call | flops 167772160 | bytes 6291456 | tf_op jit(solution)/shard_map/pallas_call | solution.py:133
  79.2 3.2 %shard_map.60 = (f32[17,64,128]{2,1,0:T(8,128)}, f32[17,64,128]{2,1,0:T(8,128)}) custom-call(f32[16,128,128]{2,1,0:T(8,128)} %copy-done, f32[16,128,128]{2,1,0:T(8,128)} %copy-done.1, f32[16,128,128]{2,1,0:T(8,128)} %copy-done.2), custom_call_target="tpu_custom_call" | custom-call | tf_op jit(solution)/shard_map/pallas_call | solution.py:164
  82.4 2.3 %collective-permute-done.5.there_ref = f32[17,64,128]{2,1,0:T(8,128)} collective-permute-done((f32[17,64,128]{2,1,0:T(8,128)}, f32[17,64,128]{2,1,0:T(8,128)}, u32[]{:S(2)}, u32[]{:S(2)}) %collective-permute-start.5) | collective-permute-done | bytes 557088 | tf_op jit(solution)/shard_map/ppermute | solution.py:304
  84.7 2.5 %shard_map.61 = bf16[16,64,128]{2,1,0:T(8,128)(2,1)} custom-call(f32[17,64,128]{2,1,0:T(8,128)} %get-tuple-element.40.here_ref, f32[17,64,128]{2,1,0:T(8,128)} %collective-permute-done.5.there_ref), custom_call_target="tpu_custom_call" | custom-call | tf_op jit(solution)/shard_map/pallas_call | solution.py:186
  87.2 18.9 %all_to_all.10.a_ref = bf16[16,64,128]{2,1,0:T(8,128)(2,1)S(1)} all-to-all(bf16[16,64,128]{2,1,0:T(8,128)(2,1)} %shard_map.61), channel_id=1, replica_groups=mesh['xh'=2,'z'=8,'y'=4,'xl'=2,'c'=2] {'xh','z'}, dimensions={0} | all-to-all | bytes 524288 | tf_op jit(solution)/shard_map/all_to_all | solution.py:305
  108.4 5.7 %shard_map.63 = bf16[128,1280]{1,0:T(8,128)(2,1)} custom-call(s32[2]{0:T(128)} %pad_add_fusion.2.place_ref, bf16[16,64,128]{2,1,0:T(8,128)(2,1)} %copy-done.4, bf16[16,64,128]{2,1,0:T(8,128)(2,1)} %collective-permute-done.6.b_ref, bf16[640,5120]{1,0:T(8,128)(2,1)} %w_ref.1, bf16[2,640,1280]{2,1,0:T(8,128)(2,1)} %copy-done.3), custom_call_target="tpu_custom_call" | custom-call | flops 419430400 | bytes 4194304 | tf_op jit(solution)/shard_map/pallas_call | solution.py:218
  115.2 5.8 %shard_map.62 = f32[128,1280]{1,0:T(8,128)} custom-call(s32[2]{0:T(128)} %pad_add_fusion.1.place_ref, bf16[16,64,128]{2,1,0:T(8,128)(2,1)} %copy-done.4, bf16[16,64,128]{2,1,0:T(8,128)(2,1)} %collective-permute-done.6.b_ref, bf16[640,5120]{1,0:T(8,128)(2,1)} %w_ref.1, bf16[2,640,1280]{2,1,0:T(8,128)(2,1)} %copy-done.3), custom_call_target="tpu_custom_call" | custom-call | flops 419430400 | bytes 4194304 | tf_op jit(solution)/shard_map/pallas_call | solution.py:218
  121.0 3.4 %collective-permute-done.8 = bf16[128,1280]{1,0:T(8,128)(2,1)S(1)} collective-permute-done((bf16[128,1280]{1,0:T(8,128)(2,1)}, bf16[128,1280]{1,0:T(8,128)(2,1)S(1)}, u32[]{:S(2)}, u32[]{:S(2)}) %collective-permute-start.8) | collective-permute-done | bytes 327712 | tf_op jit(solution)/shard_map/ppermute | solution.py:312
  124.4 1.9 %add_convert_fusion = bf16[128,1280]{1,0:T(8,128)(2,1)} fusion(f32[128,1280]{1,0:T(8,128)} %shard_map.62, bf16[128,1280]{1,0:T(8,128)(2,1)S(1)} %collective-permute-done.8), kind=kLoop, calls=%fused_computation.5 | loop fusion | flops 491520 | bytes 1310720 | tf_op jit(solution)/shard_map/convert_element_type | solution.py:314
  (48 shorter events, 13.1 us)
Async XLA Ops:
  2.2 1.7 %collective-permute-start = (bf16[5,192,128]{2,1,0:T(8,128)(2,1)}, bf16[5,192,128]{2,1,0:T(8,128)(2,1)S(1)}, u32[]{:S(2)}, u32[]{:S(2)}) collective-permute-start(bf16[5,192,128]{2,1,0:T(8,128)(2,1)} %get-tuple-element.25), channel_id=1, source_target_pairs={{0,1},{1,0},{2,3},{3,2},{4,5},{5,4},{6,7},{7,6},{8,9},{9,8},{10,11... | collective-permute-start | bytes 737288 | tf_op jit(solution)/shard_map/ppermute | solution.py:280
  6.9 34.4 %all-to-all-start = ((bf16[16,192,128]{2,1,0:T(8,128)(2,1)}), bf16[16,192,128]{2,1,0:T(8,128)(2,1)}, u32[]{:S(2)}, u32[]{:S(2)}) async-start(bf16[16,192,128]{2,1,0:T(8,128)(2,1)} %constant_dynamic-update-slice_fusion), calls=%async_computation | async-start | bytes 1572864 | tf_op jit(solution)/shard_map/all_to_all | solution.py:296
  22.3 84.4 %collective-permute-start.7 = (bf16[2,640,1280]{2,1,0:T(8,128)(2,1)}, bf16[2,640,1280]{2,1,0:T(8,128)(2,1)S(1)}, u32[]{:S(2)}, u32[]{:S(2)}) collective-permute-start(bf16[2,640,1280]{2,1,0:T(8,128)(2,1)} %pad_maximum_fusion), channel_id=1, source_target_pairs={{0,1},{1,0},{2,3},{3,2},{4,5},{5,4},{6,7},{7,6},{8,9},{9,8},{10,11... | collective-permute-start | bytes 9830408 | tf_op jit(solution)/shard_map/ppermute | solution.py:294
  42.4 22.7 %collective-permute-start.4 = (bf16[16,128,128]{2,1,0:T(8,128)(2,1)S(1)}, bf16[16,128,128]{2,1,0:T(8,128)(2,1)S(1)}, u32[]{:S(2)}, u32[]{:S(2)}) collective-permute-start(bf16[16,128,128]{2,1,0:T(8,128)(2,1)S(1)} %slice.42.refs_3_), channel_id=1, source_target_pairs={{0,4},{4,8},{8,12},{12,0},{1,5},{5,9},{9,13},{13,1},{2,6},{6,10},{... | collective-permute-start | bytes 1572872 | tf_op jit(solution)/shard_map/ppermute | solution.py:301
  43.8 25.1 %collective-permute-start.3 = (bf16[16,128,128]{2,1,0:T(8,128)(2,1)S(1)}, bf16[16,128,128]{2,1,0:T(8,128)(2,1)S(1)}, u32[]{:S(2)}, u32[]{:S(2)}) collective-permute-start(bf16[16,128,128]{2,1,0:T(8,128)(2,1)S(1)} %slice.42.refs_3_), channel_id=1, source_target_pairs={{0,12},{4,0},{8,4},{12,8},{1,13},{5,1},{9,5},{13,9},{2,14},{6,2},{... | collective-permute-start | bytes 1572872 | tf_op jit(solution)/shard_map/ppermute | solution.py:301
  44.5 28.1 %collective-permute-start.2 = (bf16[16,128,128]{2,1,0:T(8,128)(2,1)S(1)}, bf16[16,128,128]{2,1,0:T(8,128)(2,1)S(1)}, u32[]{:S(2)}, u32[]{:S(2)}) collective-permute-start(bf16[16,128,128]{2,1,0:T(8,128)(2,1)S(1)} %slice.42.refs_3_), channel_id=1, source_target_pairs={{0,8},{4,12},{8,0},{12,4},{1,9},{5,13},{9,1},{13,5},{2,10},{6,14},... | collective-permute-start | bytes 1572872 | tf_op jit(solution)/shard_map/ppermute | solution.py:301
  47.7 1.6 %collective-permute-start.1 = (bf16[16,64,128]{2,1,0:T(8,128)(2,1)S(1)}, bf16[16,64,128]{2,1,0:T(8,128)(2,1)S(1)}, u32[]{:S(2)}, u32[]{:S(2)}) collective-permute-start(bf16[16,64,128]{2,1,0:T(8,128)(2,1)S(1)} %slice.41), channel_id=1, source_target_pairs={{0,1},{1,0},{2,3},{3,2},{4,5},{5,4},{6,7},{7,6},{8,9},{9,8},{10,11... | collective-permute-start | bytes 786440 | tf_op jit(solution)/shard_map/ppermute | solution.py:298
  76.2 1.0 copy-start
  77.2 1.0 copy-start.1
  78.2 1.0 copy-start.2
  82.4 2.3 %collective-permute-start.5 = (f32[17,64,128]{2,1,0:T(8,128)}, f32[17,64,128]{2,1,0:T(8,128)}, u32[]{:S(2)}, u32[]{:S(2)}) collective-permute-start(f32[17,64,128]{2,1,0:T(8,128)} %get-tuple-element.41), channel_id=1, source_target_pairs={{0,1},{1,0},{2,3},{3,2},{4,5},{5,4},{6,7},{7,6},{8,9},{9,8},{10,11... | collective-permute-start | bytes 1671176 | tf_op jit(solution)/shard_map/ppermute | solution.py:304
  106.1 1.7 %copy-start.4 = (bf16[16,64,128]{2,1,0:T(8,128)(2,1)}, bf16[16,64,128]{2,1,0:T(8,128)(2,1)S(1)}, u32[]{:S(2)}) copy-start(bf16[16,64,128]{2,1,0:T(8,128)(2,1)S(1)} %all_to_all.10.a_ref) | copy-start | bytes 786436
  106.1 1.7 %collective-permute-start.6 = (bf16[16,64,128]{2,1,0:T(8,128)(2,1)S(1)}, bf16[16,64,128]{2,1,0:T(8,128)(2,1)}, u32[]{:S(2)}, u32[]{:S(2)}) collective-permute-start(bf16[16,64,128]{2,1,0:T(8,128)(2,1)S(1)} %all_to_all.10.a_ref), channel_id=1, source_target_pairs={{0,1},{1,0},{2,3},{3,2},{4,5},{5,4},{6,7},{7,6},{8,9},{9,8},{10,11... | collective-permute-start | bytes 786440 | tf_op jit(solution)/shard_map/ppermute | solution.py:306
  106.7 1.7 %copy-start.3 = (bf16[2,640,1280]{2,1,0:T(8,128)(2,1)}, bf16[2,640,1280]{2,1,0:T(8,128)(2,1)S(1)}, u32[]{:S(2)}) copy-start(bf16[2,640,1280]{2,1,0:T(8,128)(2,1)S(1)} %collective-permute-done.7.w2_ref) | copy-start | bytes 9830404
  114.1 10.3 %collective-permute-start.8 = (bf16[128,1280]{1,0:T(8,128)(2,1)}, bf16[128,1280]{1,0:T(8,128)(2,1)S(1)}, u32[]{:S(2)}, u32[]{:S(2)}) collective-permute-start(bf16[128,1280]{1,0:T(8,128)(2,1)} %shard_map.63), channel_id=1, source_target_pairs={{0,2},{2,0},{1,3},{3,1},{4,6},{6,4},{5,7},{7,5},{8,10},{10,8},{9,1... | collective-permute-start | bytes 983048 | tf_op jit(solution)/shard_map/ppermute | solution.py:312

commit v3 on v2

v3 whole, which is shorter than its diff:
```python
import jax
import jax.numpy as jnp
from jax import lax
from jax.experimental import pallas as pl
from jax.experimental.pallas import tpu as pltpu
from jax.sharding import Mesh
from jax.sharding import PartitionSpec as P

HEAD_DIM = 128
BLOCK = 128
HALF = 64
HEADS = 5
XH, NZ, NY, XL, NC = 2, 8, 4, 2, 2
ROWS = XH * NZ
UNROLL = 4
TILE_N = 256
LOW = -1e30
EXP2_SCALE = HEAD_DIM ** (-0.5) * 1.4426950408889634
MIB = 1024 * 1024


def shift(size, by):
    return [(i, (i + by) % size) for i in range(size)]


def in_vmem(count):
    return [pl.BlockSpec(memory_space=pltpu.VMEM)] * count


def in_smem(count):
    return [pl.BlockSpec(memory_space=pltpu.SMEM)] * count


def split_kernel(core_ref, q_ref, k_ref, v_ref, keep_ref, send_ref):
    core = core_ref[0]
    mine = pl.ds(pl.multiple_of(core * HALF, HALF), HALF)
    other = pl.ds(pl.multiple_of((1 - core) * HALF, HALF), HALF)
    keep_ref[...] = jnp.zeros_like(keep_ref)
    for head in range(HEADS):
        lanes = slice(head * HEAD_DIM, (head + 1) * HEAD_DIM)
        for t, ref in enumerate((q_ref, k_ref, v_ref)):
            rows = slice(t * HALF, (t + 1) * HALF)
            keep_ref[core * NZ + head, rows, :] = ref[mine, lanes]
            send_ref[head, rows, :] = ref[other, lanes]


def split(core, queries, keys, values):
    return pl.pallas_call(
        split_kernel,
        out_shape=(
            jax.ShapeDtypeStruct((ROWS, 3 * HALF, HEAD_DIM), jnp.bfloat16),
            jax.ShapeDtypeStruct((HEADS, 3 * HALF, HEAD_DIM), jnp.bfloat16),
        ),
        in_specs=in_smem(1) + in_vmem(3),
        out_specs=tuple(in_vmem(2)),
        compiler_params=pltpu.CompilerParams(vmem_limit_bytes=4 * MIB),
    )(core, queries, keys, values)


def score_tiles(steps, table_ref, q_ref, kv_ref, s_ref, top_ref):
    lane = lax.broadcasted_iota(jnp.int32, (BLOCK, BLOCK), 1)

    def score(step, carry):
        tiles = []
        for u in range(UNROLL):
            e = step * UNROLL + u
            key = jnp.concatenate(
                [kv_ref[table_ref[1, e], :HALF, :], kv_ref[table_ref[2, e], :HALF, :]], axis=0
            )
            s = lax.dot_general(
                q_ref[table_ref[0, e]],
                key,
                (((1,), (1,)), ((), ())),
                preferred_element_type=jnp.float32,
            )
            s = jnp.where(lane < table_ref[3, e], s, LOW)
            s_ref[e] = s
            tiles.append(s)
        for u in range(UNROLL):
            block = table_ref[0, step * UNROLL + u]
            top_ref[block] = jnp.maximum(top_ref[block], tiles[u])
        return carry

    lax.fori_loop(0, steps, score, 0)


def mix_tiles(steps, table_ref, kv_ref, s_ref, m_ref, l_ref, a_ref):
    def mix(step, carry):
        weights, products = [], []
        for u in range(UNROLL):
            e = step * UNROLL + u
            value = jnp.concatenate(
                [kv_ref[table_ref[1, e], HALF:, :], kv_ref[table_ref[2, e], HALF:, :]], axis=0
            )
            weight = jnp.exp2((s_ref[e] - m_ref[table_ref[0, e]]) * EXP2_SCALE)
            weights.append(weight)
            products.append(
                jnp.dot(weight.astype(jnp.bfloat16), value, preferred_element_type=jnp.float32)
            )
        for u in range(UNROLL):
            block = table_ref[0, step * UNROLL + u]
            l_ref[block] = l_ref[block] + weights[u]
            a_ref[block] = a_ref[block] + products[u]
        return carry

    lax.fori_loop(0, steps, mix, 0)


def write_parcels(m_ref, l_ref, a_ref, keep_ref, send_ref):
    lane = lax.broadcasted_iota(jnp.int32, (BLOCK, BLOCK), 1)
    stats = jnp.zeros((BLOCK, BLOCK), jnp.float32)
    for block in range(ROWS):
        total = jnp.sum(l_ref[block], axis=1, keepdims=True)
        stats = jnp.where(lane == block, m_ref[block], stats)
        stats = jnp.where(lane == ROWS + block, total, stats)
        keep_ref[block] = a_ref[block, :HALF, :]
        send_ref[block] = a_ref[block, HALF:, :]
    keep_ref[ROWS] = stats[:HALF]
    send_ref[ROWS] = stats[HALF:]


def attend(count, table, query, parts, state, last):
    first = state is None
    slots = sum(part.shape[0] for part in parts)
    most = ROWS * slots // 2
    whole = jax.ShapeDtypeStruct((ROWS, BLOCK, BLOCK), jnp.float32)
    parcel = jax.ShapeDtypeStruct((ROWS + 1, HALF, HEAD_DIM), jnp.float32)

    def kernel(count_ref, table_ref, q_ref, *refs):
        part_refs, refs = refs[: len(parts)], refs[len(parts) :]
        if not first:
            (m_in, l_in, a_in), refs = refs[:3], refs[3:]
        if last:
            keep_ref, send_ref, kv_ref, s_ref, top_ref, m_ref, l_ref, a_ref = refs
        else:
            m_ref, l_ref, a_ref, kv_ref, s_ref, top_ref = refs
        at = 0
        for part in part_refs:
            kv_ref[at : at + part.shape[0]] = part[...]
            at += part.shape[0]
        steps = (count_ref[0] + (UNROLL - 1)) // UNROLL
        top_ref[...] = jnp.full(top_ref.shape, LOW, jnp.float32)
        score_tiles(steps, table_ref, q_ref, kv_ref, s_ref, top_ref)
        for block in range(ROWS):
            top = jnp.max(top_ref[block], axis=1, keepdims=True)
            if first:
                m_ref[block] = jnp.broadcast_to(top, (BLOCK, BLOCK))
                l_ref[block] = jnp.zeros((BLOCK, BLOCK), jnp.float32)
                a_ref[block] = jnp.zeros((BLOCK, HEAD_DIM), jnp.float32)
            else:
                new = jnp.maximum(m_in[block], top)
                fade = jnp.exp2((m_in[block] - new) * EXP2_SCALE)
                m_ref[block] = new
                l_ref[block] = l_in[block] * fade
                a_ref[block] = a_in[block] * fade
        mix_tiles(steps, table_ref, kv_ref, s_ref, m_ref, l_ref, a_ref)
        if last:
            write_parcels(m_ref, l_ref, a_ref, keep_ref, send_ref)

    scratch = [
        pltpu.VMEM((slots, 2 * HALF, HEAD_DIM), jnp.bfloat16),
        pltpu.VMEM((most, BLOCK, BLOCK), jnp.float32),
        pltpu.VMEM((ROWS, BLOCK, BLOCK), jnp.float32),
    ]
    if last:
        scratch += [pltpu.VMEM((ROWS, BLOCK, BLOCK), jnp.float32)] * 3
    return pl.pallas_call(
        kernel,
        out_shape=(parcel, parcel) if last else (whole, whole, whole),
        in_specs=in_smem(2) + in_vmem(1 + len(parts) + (0 if first else 3)),
        out_specs=tuple(in_vmem(2 if last else 3)),
        scratch_shapes=scratch,
        compiler_params=pltpu.CompilerParams(vmem_limit_bytes=28 * MIB),
        cost_estimate=pl.CostEstimate(
            flops=len(parts) * 40 * 2 * 128**3,
            bytes_accessed=6 * MIB,
            transcendentals=20 * 128 * 128,
        ),
    )(count, table, query, *parts, *(() if first else state))


def merge_kernel(here_ref, there_ref, out_ref):
    here, there = here_ref[ROWS], there_ref[ROWS]
    for block in range(ROWS):
        m0, m1 = here[:, block : block + 1], there[:, block : block + 1]
        l0 = here[:, ROWS + block : ROWS + block + 1]
        l1 = there[:, ROWS + block : ROWS + block + 1]
        m = jnp.maximum(m0, m1)
        f0 = jnp.exp2((m0 - m) * EXP2_SCALE)
        f1 = jnp.exp2((m1 - m) * EXP2_SCALE)
        mixed = here_ref[block] * f0 + there_ref[block] * f1
        out_ref[block] = (mixed / (l0 * f0 + l1 * f1)).astype(jnp.bfloat16)


def merge(here, there):
    return pl.pallas_call(
        merge_kernel,
        out_shape=jax.ShapeDtypeStruct((ROWS, HALF, HEAD_DIM), jnp.bfloat16),
        in_specs=in_vmem(2),
        out_specs=in_vmem(1)[0],
        compiler_params=pltpu.CompilerParams(vmem_limit_bytes=4 * MIB),
    )(here, there)


def project_kernel(core_ref, a_ref, b_ref, w_ref, w2_ref, out_ref, rows_ref):
    core = core_ref[0]
    mine = pl.ds(pl.multiple_of(core * HALF, HALF), HALF)
    other = pl.ds(pl.multiple_of((1 - core) * HALF, HALF), HALF)
    for which, head_set in enumerate((core, 1 - core)):
        for head in range(HEADS):
            at = (which * HEADS + head) * HEAD_DIM
            rows_ref[mine, at : at + HEAD_DIM] = a_ref[head_set * NZ + head]
            rows_ref[other, at : at + HEAD_DIM] = b_ref[head_set * NZ + head]
    deep = HEADS * HEAD_DIM
    for at in range(0, out_ref.shape[1], TILE_N):
        lanes = slice(at, at + TILE_N)
        out = jnp.dot(rows_ref[:, :deep], w_ref[:, lanes], preferred_element_type=jnp.float32)
        out = out + jnp.dot(
            rows_ref[:, deep:], w2_ref[:, lanes], preferred_element_type=jnp.float32
        )
        out_ref[:, lanes] = out.astype(out_ref.dtype)


def project(core, a, b, w_own, w_other, dtype):
    deep, width = w_own.shape
    return pl.pallas_call(
        project_kernel,
        out_shape=jax.ShapeDtypeStruct((BLOCK, width), dtype),
        in_specs=in_smem(1) + in_vmem(4),
        out_specs=in_vmem(1)[0],
        scratch_shapes=[pltpu.VMEM((BLOCK, 2 * deep), jnp.bfloat16)],
        compiler_params=pltpu.CompilerParams(vmem_limit_bytes=8 * MIB),
        cost_estimate=pl.CostEstimate(
            flops=2 * BLOCK * 2 * deep * width, bytes_accessed=4 * MIB, transcendentals=0
        ),
    )(core, a, b, w_own, w_other)


def add_kernel(near_ref, far_ref, out_ref):
    out_ref[...] = (near_ref[...] + far_ref[...].astype(jnp.float32)).astype(out_ref.dtype)


def add(near, far):
    return pl.pallas_call(
        add_kernel,
        out_shape=jax.ShapeDtypeStruct(near.shape, jnp.bfloat16),
        in_specs=in_vmem(2),
        out_specs=in_vmem(1)[0],
        compiler_params=pltpu.CompilerParams(vmem_limit_bytes=4 * MIB),
    )(near, far)


def live_tiles(frame_mask, columns):
    y = lax.axis_index("y")
    ids = jnp.arange(ROWS, dtype=jnp.int32)
    blocks = jnp.arange(ROWS * NY, dtype=jnp.int32)
    slots = jnp.arange(ROWS * len(columns), dtype=jnp.int32)
    mine = ids * NY + y
    theirs = jnp.concatenate([ids * NY + (y - back) % NY for back in columns])
    rows = jnp.sum(
        jnp.where(mine[:, None, None] == blocks[None, :, None], frame_mask[None], 0), axis=1
    )
    hit = jnp.sum(jnp.where(theirs[:, None] == blocks, rows[:, None, :], 0), axis=2)
    hit = jnp.where(hit != 0, 1, 0)
    rank = jnp.sum(jnp.where(slots[None, :] < slots[:, None], hit[:, None, :], 0), axis=2)
    count = jnp.sum(hit, axis=1)
    tiles = (count + 1) // 2
    start = jnp.sum(jnp.where(ids[None, :] < ids[:, None], tiles[None, :], 0), axis=1)
    e = jnp.arange(ROWS * ROWS * len(columns) // 2, dtype=jnp.int32)
    chosen = (start[:, None] <= e) & (e < (start + tiles)[:, None])
    pick = lambda x: jnp.sum(jnp.where(chosen, x[:, None], 0), axis=0)
    at = 2 * (e - pick(start))
    live = jnp.where(jnp.any(chosen, axis=0), jnp.clip(pick(count) - at, 0, 2) * HALF, 0)

    def key_at(place):
        found = chosen[:, None, :] & (hit[:, :, None] > 0) & (rank[:, :, None] == place)
        return jnp.sum(jnp.where(found, slots[None, :, None], 0), axis=(0, 1))

    table = jnp.stack([pick(ids), key_at(at), key_at(at + 1), live])
    return jnp.sum(tiles, keepdims=True).astype(jnp.int32), table.astype(jnp.int32)


def local(queries, keys, values, frame_mask, w_out):
    xl, c = lax.axis_index("xl"), lax.axis_index("c")
    core = jnp.stack([c]).astype(jnp.int32)

    groups = [live_tiles(frame_mask, columns) for columns in ((0,), (1, 3), (2,))]
    slots, sent = split(core, queries, keys, values)
    got = lax.ppermute(sent, "c", shift(NC, 1))
    slots = lax.dynamic_update_slice(slots, got, ((1 - c) * NZ, 0, 0))
    slots, w_out = lax.optimization_barrier((slots, w_out))

    width = w_out.shape[1] // (XL * NC)

    def w_columns(to_xl, to_c):
        return lax.dynamic_slice(w_out, (0, (to_xl * NC + to_c) * width), (w_out.shape[0], width))

    w_own = [w_columns(to_xl, c) for to_xl in (1 - xl, xl)]
    w_other = [
        lax.ppermute(w_columns(to_xl, 1 - c), "c", shift(NC, 1)) for to_xl in (1 - xl, xl)
    ]

    slots = lax.all_to_all(slots, ("xh", "z"), 0, 0, tiled=True)
    own_query, kv = slots[:, :HALF], slots[:, HALF:]
    query = jnp.concatenate([own_query, lax.ppermute(own_query, "c", shift(NC, 1))], axis=1)
    before = lax.ppermute(kv, "y", shift(NY, 1))
    after = lax.ppermute(kv, "y", shift(NY, -1))
    low = lax.ppermute(before[: ROWS // 2], "y", shift(NY, 1))
    high = lax.ppermute(after[ROWS // 2 :], "y", shift(NY, -1))
    state = attend(*groups[0], query, [kv], None, False)
    state = attend(*groups[1], query, [before, after], state, False)
    here, sent = attend(*groups[2], query, [low, high], state, True)
    there = lax.ppermute(sent, "c", shift(NC, 1))
    merged = merge(here, there)
    merged, w_own, w_other = lax.optimization_barrier((merged, w_own, w_other))
    attended = lax.all_to_all(merged, ("xh", "z"), 0, 0, tiled=True)
    other_rows = lax.ppermute(attended, "c", shift(NC, 1))
    far = project(core, attended, other_rows, w_own[0], w_other[0], jnp.bfloat16)
    far = lax.ppermute(far, "xl", shift(XL, 1))
    near = project(core, attended, other_rows, w_own[1], w_other[1], jnp.float32)
    return add(near, far)


def solution(mesh):
    fine = Mesh(mesh.devices.reshape(XH, NZ, NY, XL, NC), ("xh", "z", "y", "xl", "c"))
    seq, head = ("xh", "z", "y"), ("xl", "c")
    in_specs = (P(seq, head), P(seq, head), P(seq, head), P(), P(head, None))
    return jax.shard_map(
        local, mesh=fine, in_specs=in_specs, out_specs=P(seq, head), check_vma=False
    )
```

time: 127 us -> 114 us (0.90)
  the two profiles are of different devices: /device:TPU:16 before, /device:TPU:1 now
where the time goes in v3:
time: 114 us; the launch traced here: 113 us
  starting transfers between devices  30 us (26%)
  waiting for transfers between devices  27.8 us (24%)
  Pallas kernels  20.6 us (18%)
  blocking collectives  16.8 us (15%)
  local copies, waits for them, and re-layouts  10.6 us (9%)
  other arithmetic  7.27 us (6%)
    all_to_all x1, blocking collectives, local(): attended = lax.all_to_all(merged, ('xh', 'z'), 0, 0, tiled=True)  16.8 us
    all_to_all x1, waiting for transfers between devices, local(): slots = lax.all_to_all(slots, ('xh', 'z'), 0, 0, tiled=True)  15.2 us
    pallas_call x3, Pallas kernels, attend(): pl.pallas_call(kernel, out_shape=(parcel, parcel) if last else (whole, wh...  13.9 us
    all_to_all x1, starting transfers between devices, local(): slots = lax.all_to_all(slots, ('xh', 'z'), 0, 0, tiled=True)  9.06 us
    ppermute x1, waiting for transfers between devices, local(): far = lax.ppermute(far, 'xl', shift(XL, 1))  6.47 us
    dynamic_slice x1, local copies, waits for them, and re-layouts, w_columns(): lax.dynamic_slice(w_out, (0, (to_xl * NC + to_c) * width), (w_out.shape[0...  5.04 us
    ppermute x1, starting transfers between devices, local(): there = lax.ppermute(sent, 'c', shift(NC, 1))  4.66 us
    pallas_call x2, Pallas kernels, project(): pl.pallas_call(project_kernel, out_shape=jax.ShapeDtypeStruct((BLOCK, wid...  4.27 us
  transfers between devices with their start and end apart: 12, of which 5 were waited for; matrix products, arithmetic and copies ran while one was open for 13% of the time, Pallas kernels for 15%

profile of v3, /device:TPU:1, one launch (start us, length us, event | category | flops | bytes accessed | tf_op | source)
XLA Modules:
  0.0 113.3 jit_solution(12918869813529638218)
XLA Ops:
  0.0 0.9 copy-done
  2.7 1.0 shard_map.55
  3.8 3.2 %collective-permute-start = (bf16[5,192,128]{2,1,0:T(8,128)(2,1)S(1)}, bf16[5,192,128]{2,1,0:T(8,128)(2,1)S(1)}, u32[]{:S(2)}, u32[]{:S(2)}) collective-permute-start(bf16[5,192,128]{2,1,0:T(8,128)(2,1)S(1)} %get-tuple-element.23), channel_id=1, source_target_pairs={{0,1},{1,0},{2,3},{3,2},{4,5},{5,4},{6,7},{7,6},{8,9},{9,8},{10,11... | collective-permute-start | bytes 737288 | tf_op jit(solution)/shard_map/ppermute | solution.py:289
  7.3 1.0 select_reduce_fusion.2
  14.7 9.1 %all-to-all-start = ((bf16[16,192,128]{2,1,0:T(8,128)(2,1)}), bf16[16,192,128]{2,1,0:T(8,128)(2,1)}, u32[]{:S(2)}, u32[]{:S(2)}) async-start(bf16[16,192,128]{2,1,0:T(8,128)(2,1)} %constant_dynamic-update-slice_fusion), calls=%async_computation | async-start | bytes 1572864 | tf_op jit(solution)/shard_map/all_to_all | solution.py:303
  24.0 5.0 %constant_dynamic-slice_fusion = (bf16[640,1280]{1,0:T(8,128)(2,1)}, bf16[640,1280]{1,0:T(8,128)(2,1)}, bf16[640,1280]{1,0:T(8,128)(2,1)S(1)}, bf16[640,1280]{1,0:T(8,128)(2,1)S(1)}) fusion(bf16[640,5120]{1,0:T(8,128)(2,1)} %param.9, s32[]{:T(128)S(6)} %select_n.265, s32[]{:T(128)S(6)} %select_n.264, s32[]{:T(128)S(6)} %select_n.263, s32[]{:T(128)S(6)} %select_n.262), kind=kLoop, calls=%fused_computation.62 | loop fusion | bytes 13107216 | tf_op jit(solution)/shard_map/dynamic_slice | solution.py:296
  29.5 15.2 %all-to-all-done = bf16[16,192,128]{2,1,0:T(8,128)(2,1)} async-done(((bf16[16,192,128]{2,1,0:T(8,128)(2,1)}), bf16[16,192,128]{2,1,0:T(8,128)(2,1)}, u32[]{:S(2)}, u32[]{:S(2)}) %all-to-all-start) | async-done | bytes 786464 | tf_op jit(solution)/shard_map/all_to_all | solution.py:303
  44.8 1.1 slice.17.refs_0_
  45.9 2.8 %collective-permute-start.4 = (bf16[16,128,128]{2,1,0:T(8,128)(2,1)S(1)}, bf16[16,128,128]{2,1,0:T(8,128)(2,1)S(1)}, u32[]{:S(2)}, u32[]{:S(2)}) collective-permute-start(bf16[16,128,128]{2,1,0:T(8,128)(2,1)S(1)} %slice.17.refs_0_), channel_id=1, source_target_pairs={{0,12},{4,0},{8,4},{12,8},{1,13},{5,1},{9,5},{13,9},{2,14},{6,2},{... | collective-permute-start | bytes 1572872 | tf_op jit(solution)/shard_map/ppermute | solution.py:307
  48.7 1.0 slice.16
  49.7 3.6 %collective-permute-start.1 = (bf16[16,64,128]{2,1,0:T(8,128)(2,1)S(1)}, bf16[16,64,128]{2,1,0:T(8,128)(2,1)S(1)}, u32[]{:S(2)}, u32[]{:S(2)}) collective-permute-start(bf16[16,64,128]{2,1,0:T(8,128)(2,1)S(1)} %slice.16), channel_id=1, source_target_pairs={{0,1},{1,0},{2,3},{3,2},{4,5},{5,4},{6,7},{7,6},{8,9},{9,8},{10,11... | collective-permute-start | bytes 786440 | tf_op jit(solution)/shard_map/ppermute | solution.py:305
  53.4 3.3 %collective-permute-done.4.refs_1_ = bf16[16,128,128]{2,1,0:T(8,128)(2,1)S(1)} collective-permute-done((bf16[16,128,128]{2,1,0:T(8,128)(2,1)S(1)}, bf16[16,128,128]{2,1,0:T(8,128)(2,1)S(1)}, u32[]{:S(2)}, u32[]{:S(2)}) %collective-permute-start.4) | collective-permute-done | bytes 524320 | tf_op jit(solution)/shard_map/ppermute | solution.py:307
  56.7 3.5 %collective-permute-start.5 = (bf16[8,128,128]{2,1,0:T(8,128)(2,1)S(1)}, bf16[8,128,128]{2,1,0:T(8,128)(2,1)S(1)}, u32[]{:S(2)}, u32[]{:S(2)}) collective-permute-start(bf16[8,128,128]{2,1,0:T(8,128)(2,1)S(1)} %slice.19), channel_id=1, source_target_pairs={{0,12},{4,0},{8,4},{12,8},{1,13},{5,1},{9,5},{13,9},{2,14},{6,2},{... | collective-permute-start | bytes 786440 | tf_op jit(solution)/shard_map/ppermute | solution.py:309
  60.4 4.3 %shard_map.56 = (f32[16,128,128]{2,1,0:T(8,128)S(1)}, f32[16,128,128]{2,1,0:T(8,128)S(1)}, f32[16,128,128]{2,1,0:T(8,128)S(1)}) custom-call(s32[1]{0:T(128)} %bitcast.14.count_ref, s32[4,128]{1,0:T(4,128)S(1)} %pad_add_fusion.2.table_ref, bf16[16,128,128]{2,1,0:T(8,128)(2,1)S(1)} %pad_maximum_fusion.q_ref, bf16[16,128,128]{2,1,0:T(8,128)(2,1)S(1)} %slice.17.refs_0_), custom_call_target="tpu_custom_call" | custom-call | flops 167772160 | bytes 6291456 | tf_op jit(solution)/shard_map/pallas_call | solution.py:167
  64.7 5.6 %shard_map.57 = (f32[16,128,128]{2,1,0:T(8,128)S(1)}, f32[16,128,128]{2,1,0:T(8,128)S(1)}, f32[16,128,128]{2,1,0:T(8,128)S(1)}) custom-call(s32[1]{0:T(128)} %bitcast.8.count_ref, s32[4,256]{1,0:T(4,128)S(1)} %pad_add_fusion.table_ref, bf16[16,128,128]{2,1,0:T(8,128)(2,1)S(1)} %pad_maximum_fusion.q_ref, ...), custom_call_target="tpu_custom_call" | custom-call | flops 335544320 | bytes 6291456 | tf_op jit(solution)/shard_map/pallas_call | solution.py:167
  70.3 4.0 %shard_map.58 = (f32[17,64,128]{2,1,0:T(8,128)S(1)}, f32[17,64,128]{2,1,0:T(8,128)S(1)}) custom-call(s32[1]{0:T(128)} %bitcast.1.count_ref, s32[4,128]{1,0:T(4,128)S(1)} %pad_add_fusion.1.table_ref, bf16[16,128,128]{2,1,0:T(8,128)(2,1)S(1)} %pad_maximum_fusion.q_ref, bf16[8,128,128]{2,1,0:T(8,128)(2,1)S(1)} %collective-permute-done.3.refs_0_, ...), custom_call_target="tpu_custom_call" | custom-call | flops 335544320 | bytes 6291456 | tf_op jit(solution)/shard_map/pallas_call | solution.py:167
  74.3 4.7 %collective-permute-start.6 = (f32[17,64,128]{2,1,0:T(8,128)S(1)}, f32[17,64,128]{2,1,0:T(8,128)S(1)}, u32[]{:S(2)}, u32[]{:S(2)}) collective-permute-start(f32[17,64,128]{2,1,0:T(8,128)S(1)} %get-tuple-element.32), channel_id=1, source_target_pairs={{0,1},{1,0},{2,3},{3,2},{4,5},{5,4},{6,7},{7,6},{8,9},{9,8},{10,11... | collective-permute-start | bytes 1671176 | tf_op jit(solution)/shard_map/ppermute | solution.py:313
  79.0 1.6 %collective-permute-done.6.there_ref = f32[17,64,128]{2,1,0:T(8,128)S(1)} collective-permute-done((f32[17,64,128]{2,1,0:T(8,128)S(1)}, f32[17,64,128]{2,1,0:T(8,128)S(1)}, u32[]{:S(2)}, u32[]{:S(2)}) %collective-permute-start.6) | collective-permute-done | bytes 557088 | tf_op jit(solution)/shard_map/ppermute | solution.py:313
  81.2 16.8 %all_to_all.10.a_ref = bf16[16,64,128]{2,1,0:T(8,128)(2,1)S(1)} all-to-all(bf16[16,64,128]{2,1,0:T(8,128)(2,1)S(1)} %shard_map.59), channel_id=1, replica_groups=mesh['xh'=2,'z'=8,'y'=4,'xl'=2,'c'=2] {'xh','z'}, dimensions={0} | all-to-all | bytes 524288 | tf_op jit(solution)/shard_map/all_to_all | solution.py:316
  98.0 2.2 %collective-permute-start.9 = (bf16[16,64,128]{2,1,0:T(8,128)(2,1)S(1)}, bf16[16,64,128]{2,1,0:T(8,128)(2,1)S(1)}, u32[]{:S(2)}, u32[]{:S(2)}) collective-permute-start(bf16[16,64,128]{2,1,0:T(8,128)(2,1)S(1)} %all_to_all.10.a_ref), channel_id=1, source_target_pairs={{0,1},{1,0},{2,3},{3,2},{4,5},{5,4},{6,7},{7,6},{8,9},{9,8},{10,11... | collective-permute-start | bytes 786440 | tf_op jit(solution)/shard_map/ppermute | solution.py:317
  100.2 1.2 %collective-permute-done.9.b_ref = bf16[16,64,128]{2,1,0:T(8,128)(2,1)S(1)} collective-permute-done((bf16[16,64,128]{2,1,0:T(8,128)(2,1)S(1)}, bf16[16,64,128]{2,1,0:T(8,128)(2,1)S(1)}, u32[]{:S(2)}, u32[]{:S(2)}) %collective-permute-start.9) | collective-permute-done | bytes 262176 | tf_op jit(solution)/shard_map/ppermute | solution.py:317
  101.3 2.1 %shard_map.61 = bf16[128,1280]{1,0:T(8,128)(2,1)S(1)} custom-call(s32[1]{0:T(128)} %bitcast.core_ref, bf16[16,64,128]{2,1,0:T(8,128)(2,1)S(1)} %all_to_all.10.a_ref, bf16[16,64,128]{2,1,0:T(8,128)(2,1)S(1)} %collective-permute-done.9.b_ref, bf16[640,1280]{1,0:T(8,128)(2,1)S(1)} %get-tuple-element.37.w_ref, bf16[640,1280]{1,0:T(8,128)(2,1)} %collective-permute-done.7.w2_ref), custom_call_target="tpu_custom_call" | custom-call | flops 419430400 | bytes 4194304 | tf_op jit(solution)/shard_map/pallas_call | solution.py:226
  103.9 2.1 %shard_map.60.near_ref = f32[128,1280]{1,0:T(8,128)S(1)} custom-call(s32[1]{0:T(128)} %bitcast.core_ref, bf16[16,64,128]{2,1,0:T(8,128)(2,1)S(1)} %all_to_all.10.a_ref, bf16[16,64,128]{2,1,0:T(8,128)(2,1)S(1)} %collective-permute-done.9.b_ref, bf16[640,1280]{1,0:T(8,128)(2,1)S(1)} %get-tuple-element.35.w_ref, bf16[640,1280]{1,0:T(8,128)(2,1)} %collective-permute-done.8.w2_ref), custom_call_target="tpu_custom_call" | custom-call | flops 419430400 | bytes 4194304 | tf_op jit(solution)/shard_map/pallas_call | solution.py:226
  106.0 6.5 %collective-permute-done.10.far_ref = bf16[128,1280]{1,0:T(8,128)(2,1)S(1)} collective-permute-done((bf16[128,1280]{1,0:T(8,128)(2,1)S(1)}, bf16[128,1280]{1,0:T(8,128)(2,1)S(1)}, u32[]{:S(2)}, u32[]{:S(2)}) %collective-permute-start.10) | collective-permute-done | bytes 327712 | tf_op jit(solution)/shard_map/ppermute | solution.py:319
  (69 shorter events, 11.3 us)
Async XLA Ops:
  0.0 0.9 copy-start
  0.9 0.9 copy-start.1
  1.8 0.9 copy-start.2
  3.8 10.2 %collective-permute-start = (bf16[5,192,128]{2,1,0:T(8,128)(2,1)S(1)}, bf16[5,192,128]{2,1,0:T(8,128)(2,1)S(1)}, u32[]{:S(2)}, u32[]{:S(2)}) collective-permute-start(bf16[5,192,128]{2,1,0:T(8,128)(2,1)S(1)} %get-tuple-element.23), channel_id=1, source_target_pairs={{0,1},{1,0},{2,3},{3,2},{4,5},{5,4},{6,7},{7,6},{8,9},{9,8},{10,11... | collective-permute-start | bytes 737288 | tf_op jit(solution)/shard_map/ppermute | solution.py:289
  14.7 30.1 %all-to-all-start = ((bf16[16,192,128]{2,1,0:T(8,128)(2,1)}), bf16[16,192,128]{2,1,0:T(8,128)(2,1)}, u32[]{:S(2)}, u32[]{:S(2)}) async-start(bf16[16,192,128]{2,1,0:T(8,128)(2,1)} %constant_dynamic-update-slice_fusion), calls=%async_computation | async-start | bytes 1572864 | tf_op jit(solution)/shard_map/all_to_all | solution.py:303
  29.0 52.1 %collective-permute-start.8 = (bf16[640,1280]{1,0:T(8,128)(2,1)}, bf16[640,1280]{1,0:T(8,128)(2,1)}, u32[]{:S(2)}, u32[]{:S(2)}) collective-permute-start(bf16[640,1280]{1,0:T(8,128)(2,1)} %get-tuple-element.64), channel_id=1, source_target_pairs={{0,1},{1,0},{2,3},{3,2},{4,5},{5,4},{6,7},{7,6},{8,9},{9,8},{10,11... | collective-permute-start | bytes 4915208 | tf_op jit(solution)/shard_map/ppermute | solution.py:300
  29.3 51.9 %collective-permute-start.7 = (bf16[640,1280]{1,0:T(8,128)(2,1)}, bf16[640,1280]{1,0:T(8,128)(2,1)}, u32[]{:S(2)}, u32[]{:S(2)}) collective-permute-start(bf16[640,1280]{1,0:T(8,128)(2,1)} %get-tuple-element.65), channel_id=1, source_target_pairs={{0,1},{1,0},{2,3},{3,2},{4,5},{5,4},{6,7},{7,6},{8,9},{9,8},{10,11... | collective-permute-start | bytes 4915208 | tf_op jit(solution)/shard_map/ppermute | solution.py:300
  45.9 10.8 %collective-permute-start.4 = (bf16[16,128,128]{2,1,0:T(8,128)(2,1)S(1)}, bf16[16,128,128]{2,1,0:T(8,128)(2,1)S(1)}, u32[]{:S(2)}, u32[]{:S(2)}) collective-permute-start(bf16[16,128,128]{2,1,0:T(8,128)(2,1)S(1)} %slice.17.refs_0_), channel_id=1, source_target_pairs={{0,12},{4,0},{8,4},{12,8},{1,13},{5,1},{9,5},{13,9},{2,14},{6,2},{... | collective-permute-start | bytes 1572872 | tf_op jit(solution)/shard_map/ppermute | solution.py:307
  48.7 11.5 %collective-permute-start.2 = (bf16[16,128,128]{2,1,0:T(8,128)(2,1)S(1)}, bf16[16,128,128]{2,1,0:T(8,128)(2,1)S(1)}, u32[]{:S(2)}, u32[]{:S(2)}) collective-permute-start(bf16[16,128,128]{2,1,0:T(8,128)(2,1)S(1)} %slice.17.refs_0_), channel_id=1, source_target_pairs={{0,4},{4,8},{8,12},{12,0},{1,5},{5,9},{9,13},{13,1},{2,6},{6,10},{... | collective-permute-start | bytes 1572872 | tf_op jit(solution)/shard_map/ppermute | solution.py:306
  49.7 10.7 %collective-permute-start.1 = (bf16[16,64,128]{2,1,0:T(8,128)(2,1)S(1)}, bf16[16,64,128]{2,1,0:T(8,128)(2,1)S(1)}, u32[]{:S(2)}, u32[]{:S(2)}) collective-permute-start(bf16[16,64,128]{2,1,0:T(8,128)(2,1)S(1)} %slice.16), channel_id=1, source_target_pairs={{0,1},{1,0},{2,3},{3,2},{4,5},{5,4},{6,7},{7,6},{8,9},{9,8},{10,11... | collective-permute-start | bytes 786440 | tf_op jit(solution)/shard_map/ppermute | solution.py:305
  56.7 13.6 %collective-permute-start.5 = (bf16[8,128,128]{2,1,0:T(8,128)(2,1)S(1)}, bf16[8,128,128]{2,1,0:T(8,128)(2,1)S(1)}, u32[]{:S(2)}, u32[]{:S(2)}) collective-permute-start(bf16[8,128,128]{2,1,0:T(8,128)(2,1)S(1)} %slice.19), channel_id=1, source_target_pairs={{0,12},{4,0},{8,4},{12,8},{1,13},{5,1},{9,5},{13,9},{2,14},{6,2},{... | collective-permute-start | bytes 786440 | tf_op jit(solution)/shard_map/ppermute | solution.py:309
  60.2 10.1 %collective-permute-start.3 = (bf16[8,128,128]{2,1,0:T(8,128)(2,1)S(1)}, bf16[8,128,128]{2,1,0:T(8,128)(2,1)S(1)}, u32[]{:S(2)}, u32[]{:S(2)}) collective-permute-start(bf16[8,128,128]{2,1,0:T(8,128)(2,1)S(1)} %slice.18), channel_id=1, source_target_pairs={{0,4},{4,8},{8,12},{12,0},{1,5},{5,9},{9,13},{13,1},{2,6},{6,10},{... | collective-permute-start | bytes 786440 | tf_op jit(solution)/shard_map/ppermute | solution.py:308
  74.3 6.2 %collective-permute-start.6 = (f32[17,64,128]{2,1,0:T(8,128)S(1)}, f32[17,64,128]{2,1,0:T(8,128)S(1)}, u32[]{:S(2)}, u32[]{:S(2)}) collective-permute-start(f32[17,64,128]{2,1,0:T(8,128)S(1)} %get-tuple-element.32), channel_id=1, source_target_pairs={{0,1},{1,0},{2,3},{3,2},{4,5},{5,4},{6,7},{7,6},{8,9},{9,8},{10,11... | collective-permute-start | bytes 1671176 | tf_op jit(solution)/shard_map/ppermute | solution.py:313
  98.0 3.3 %collective-permute-start.9 = (bf16[16,64,128]{2,1,0:T(8,128)(2,1)S(1)}, bf16[16,64,128]{2,1,0:T(8,128)(2,1)S(1)}, u32[]{:S(2)}, u32[]{:S(2)}) collective-permute-start(bf16[16,64,128]{2,1,0:T(8,128)(2,1)S(1)} %all_to_all.10.a_ref), channel_id=1, source_target_pairs={{0,1},{1,0},{2,3},{3,2},{4,5},{5,4},{6,7},{7,6},{8,9},{9,8},{10,11... | collective-permute-start | bytes 786440 | tf_op jit(solution)/shard_map/ppermute | solution.py:317
  103.5 9.0 %collective-permute-start.10 = (bf16[128,1280]{1,0:T(8,128)(2,1)S(1)}, bf16[128,1280]{1,0:T(8,128)(2,1)S(1)}, u32[]{:S(2)}, u32[]{:S(2)}) collective-permute-start(bf16[128,1280]{1,0:T(8,128)(2,1)S(1)} %shard_map.61), channel_id=1, source_target_pairs={{0,2},{2,0},{1,3},{3,1},{4,6},{6,4},{5,7},{7,5},{8,10},{10,8},{9,1... | collective-permute-start | bytes 983048 | tf_op jit(solution)/shard_map/ppermute | solution.py:319

commit v4 on v3

--- a/solution.py
+++ b/solution.py
@@ -31,11 +31,23 @@
     return [pl.BlockSpec(memory_space=pltpu.SMEM)] * count
 
 
-def split_kernel(core_ref, q_ref, k_ref, v_ref, keep_ref, send_ref):
+def split_kernel(core_ref, q_hbm, k_hbm, v_hbm, keep_ref, send_ref, q_ref, k_ref, v_ref, sems):
+    copies = [
+        pltpu.make_async_copy(source, target, sems.at[i])
+        for i, (source, target) in enumerate(
+            ((q_hbm, q_ref), (k_hbm, k_ref), (v_hbm, v_ref))
+        )
+    ]
+    for copy in copies:
+        copy.start()
     core = core_ref[0]
     mine = pl.ds(pl.multiple_of(core * HALF, HALF), HALF)
     other = pl.ds(pl.multiple_of((1 - core) * HALF, HALF), HALF)
-    keep_ref[...] = jnp.zeros_like(keep_ref)
+    for spare in range(HEADS, NZ):
+        for head_set in range(NC):
+            keep_ref[head_set * NZ + spare] = jnp.zeros((3 * HALF, HEAD_DIM), jnp.bfloat16)
+    for copy in copies:
+        copy.wait()
     for head in range(HEADS):
         lanes = slice(head * HEAD_DIM, (head + 1) * HEAD_DIM)
         for t, ref in enumerate((q_ref, k_ref, v_ref)):
@@ -51,9 +63,11 @@
             jax.ShapeDtypeStruct((ROWS, 3 * HALF, HEAD_DIM), jnp.bfloat16),
             jax.ShapeDtypeStruct((HEADS, 3 * HALF, HEAD_DIM), jnp.bfloat16),
         ),
-        in_specs=in_smem(1) + in_vmem(3),
+        in_specs=in_smem(1) + [pl.BlockSpec(memory_space=pl.ANY)] * 3,
         out_specs=tuple(in_vmem(2)),
-        compiler_params=pltpu.CompilerParams(vmem_limit_bytes=4 * MIB),
+        scratch_shapes=[pltpu.VMEM(queries.shape, jnp.bfloat16)] * 3
+        + [pltpu.SemaphoreType.DMA((3,))],
+        compiler_params=pltpu.CompilerParams(vmem_limit_bytes=56 * MIB),
     )(core, queries, keys, values)
 
 
@@ -202,89 +216,102 @@
     )(here, there)
 
 
-def project_kernel(core_ref, a_ref, b_ref, w_ref, w2_ref, out_ref, rows_ref):
-    core = core_ref[0]
-    mine = pl.ds(pl.multiple_of(core * HALF, HALF), HALF)
-    other = pl.ds(pl.multiple_of((1 - core) * HALF, HALF), HALF)
-    for which, head_set in enumerate((core, 1 - core)):
-        for head in range(HEADS):
-            at = (which * HEADS + head) * HEAD_DIM
-            rows_ref[mine, at : at + HEAD_DIM] = a_ref[head_set * NZ + head]
-            rows_ref[other, at : at + HEAD_DIM] = b_ref[head_set * NZ + head]
-    deep = HEADS * HEAD_DIM
-    for at in range(0, out_ref.shape[1], TILE_N):
-        lanes = slice(at, at + TILE_N)
-        out = jnp.dot(rows_ref[:, :deep], w_ref[:, lanes], preferred_element_type=jnp.float32)
-        out = out + jnp.dot(
-            rows_ref[:, deep:], w2_ref[:, lanes], preferred_element_type=jnp.float32
-        )
-        out_ref[:, lanes] = out.astype(out_ref.dtype)
-
-
-def project(core, a, b, w_own, w_other, dtype):
+def project(core, a, b, w_own, w_other, added):
     deep, width = w_own.shape
+    final = added is not None
+
+    def kernel(core_ref, a_ref, b_ref, w_ref, w2_ref, *refs):
+        if final:
+            added_ref, refs = refs[0], refs[1:]
+        out_ref, rows_ref = refs
+        core = core_ref[0]
+        mine = pl.ds(pl.multiple_of(core * HALF, HALF), HALF)
+        other = pl.ds(pl.multiple_of((1 - core) * HALF, HALF), HALF)
+        for which, head_set in enumerate((core, 1 - core)):
+            for head in range(HEADS):
+                at = (which * HEADS + head) * HEAD_DIM
+                rows_ref[mine, at : at + HEAD_DIM] = a_ref[head_set * NZ + head]
+                rows_ref[other, at : at + HEAD_DIM] = b_ref[head_set * NZ + head]
+        for at in range(0, width, TILE_N):
+            lanes = slice(at, at + TILE_N)
+            out = jnp.dot(rows_ref[:, :deep], w_ref[:, lanes], preferred_element_type=jnp.float32)
+            out = out + jnp.dot(
+                rows_ref[:, deep:], w2_ref[:, lanes], preferred_element_type=jnp.float32
+            )
+            if final:
+                out = out + added_ref[:, lanes]
+            out_ref[:, lanes] = out.astype(out_ref.dtype)
+
     return pl.pallas_call(
-        project_kernel,
-        out_shape=jax.ShapeDtypeStruct((BLOCK, width), dtype),
-        in_specs=in_smem(1) + in_vmem(4),
+        kernel,
+        out_shape=jax.ShapeDtypeStruct((BLOCK, width), jnp.bfloat16 if final else jnp.float32),
+        in_specs=in_smem(1) + in_vmem(5 if final else 4),
         out_specs=in_vmem(1)[0],
         scratch_shapes=[pltpu.VMEM((BLOCK, 2 * deep), jnp.bfloat16)],
         compiler_params=pltpu.CompilerParams(vmem_limit_bytes=8 * MIB),
         cost_estimate=pl.CostEstimate(
             flops=2 * BLOCK * 2 * deep * width, bytes_accessed=4 * MIB, transcendentals=0
         ),
-    )(core, a, b, w_own, w_other)
-
-
-def add_kernel(near_ref, far_ref, out_ref):
-    out_ref[...] = (near_ref[...] + far_ref[...].astype(jnp.float32)).astype(out_ref.dtype)
-
-
-def add(near, far):
-    return pl.pallas_call(
-        add_kernel,
-        out_shape=jax.ShapeDtypeStruct(near.shape, jnp.bfloat16),
-        in_specs=in_vmem(2),
-        out_specs=in_vmem(1)[0],
+    )(core, a, b, w_own, w_other, *((added,) if final else ()))
+
+
+GROUPS = ((0,), (1, 3), (2,))
+
+
+def tiles_kernel(place_ref, mask_ref, *refs):
+    y = place_ref[1]
+    for group, columns in enumerate(GROUPS):
+        count_ref, table_ref = refs[2 * group], refs[2 * group + 1]
+
+        def one_query_block(block, start, columns=columns, table_ref=table_ref):
+            row = block * NY + y
+            found = jnp.int32(0)
+            for column, back in enumerate(columns):
+                theirs = lax.rem(y - back + NY, NY)
+                for i in range(ROWS):
+                    table_ref[1 + lax.rem(found, 2), start + lax.div(found, 2)] = column * ROWS + i
+                    found = found + jnp.where(mask_ref[row, i * NY + theirs] != 0, 1, 0)
+            table_ref[1 + lax.rem(found, 2), start + lax.div(found, 2)] = 0
+            tiles = lax.div(found + 1, 2)
+
+            def fill(t, carry):
+                table_ref[0, start + t] = block
+                table_ref[3, start + t] = jnp.minimum(found - 2 * t, 2) * HALF
+                return carry
+
+            lax.fori_loop(0, tiles, fill, 0)
+            return start + tiles
+
+        total = lax.fori_loop(0, ROWS, one_query_block, jnp.int32(0))
+        count_ref[0] = total
+        for u in range(UNROLL):
+            for r in range(4):
+                table_ref[r, total + u] = 0
+
+
+def live_tiles(place, frame_mask):
+    out_shape = []
+    for columns in GROUPS:
+        most = ROWS * ROWS * len(columns) // 2
+        out_shape += [
+            jax.ShapeDtypeStruct((1,), jnp.int32),
+            jax.ShapeDtypeStruct((4, most + 128), jnp.int32),
+        ]
+    flat = pl.pallas_call(
+        tiles_kernel,
+        out_shape=tuple(out_shape),
+        in_specs=in_smem(2),
+        out_specs=tuple(in_smem(len(out_shape))),
         compiler_params=pltpu.CompilerParams(vmem_limit_bytes=4 * MIB),
-    )(near, far)
-
-
-def live_tiles(frame_mask, columns):
-    y = lax.axis_index("y")
-    ids = jnp.arange(ROWS, dtype=jnp.int32)
-    blocks = jnp.arange(ROWS * NY, dtype=jnp.int32)
-    slots = jnp.arange(ROWS * len(columns), dtype=jnp.int32)
-    mine = ids * NY + y
-    theirs = jnp.concatenate([ids * NY + (y - back) % NY for back in columns])
-    rows = jnp.sum(
-        jnp.where(mine[:, None, None] == blocks[None, :, None], frame_mask[None], 0), axis=1
-    )
-    hit = jnp.sum(jnp.where(theirs[:, None] == blocks, rows[:, None, :], 0), axis=2)
-    hit = jnp.where(hit != 0, 1, 0)
-    rank = jnp.sum(jnp.where(slots[None, :] < slots[:, None], hit[:, None, :], 0), axis=2)
-    count = jnp.sum(hit, axis=1)
-    tiles = (count + 1) // 2
-    start = jnp.sum(jnp.where(ids[None, :] < ids[:, None], tiles[None, :], 0), axis=1)
-    e = jnp.arange(ROWS * ROWS * len(columns) // 2, dtype=jnp.int32)
-    chosen = (start[:, None] <= e) & (e < (start + tiles)[:, None])
-    pick = lambda x: jnp.sum(jnp.where(chosen, x[:, None], 0), axis=0)
-    at = 2 * (e - pick(start))
-    live = jnp.where(jnp.any(chosen, axis=0), jnp.clip(pick(count) - at, 0, 2) * HALF, 0)
-
-    def key_at(place):
-        found = chosen[:, None, :] & (hit[:, :, None] > 0) & (rank[:, :, None] == place)
-        return jnp.sum(jnp.where(found, slots[None, :, None], 0), axis=(0, 1))
-
-    table = jnp.stack([pick(ids), key_at(at), key_at(at + 1), live])
-    return jnp.sum(tiles, keepdims=True).astype(jnp.int32), table.astype(jnp.int32)
+        cost_estimate=pl.CostEstimate(flops=10**6, bytes_accessed=10**5, transcendentals=0),
+    )(place, frame_mask)
+    return [(flat[2 * i], flat[2 * i + 1]) for i in range(len(GROUPS))]
 
 
 def local(queries, keys, values, frame_mask, w_out):
     xl, c = lax.axis_index("xl"), lax.axis_index("c")
-    core = jnp.stack([c]).astype(jnp.int32)
-
-    groups = [live_tiles(frame_mask, columns) for columns in ((0,), (1, 3), (2,))]
+    core = jnp.stack([c, lax.axis_index("y")]).astype(jnp.int32)
+
     slots, sent = split(core, queries, keys, values)
     got = lax.ppermute(sent, "c", shift(NC, 1))
     slots = lax.dynamic_update_slice(slots, got, ((1 - c) * NZ, 0, 0))
@@ -295,30 +322,48 @@
     def w_columns(to_xl, to_c):
         return lax.dynamic_slice(w_out, (0, (to_xl * NC + to_c) * width), (w_out.shape[0], width))
 
-    w_own = [w_columns(to_xl, c) for to_xl in (1 - xl, xl)]
-    w_other = [
-        lax.ppermute(w_columns(to_xl, 1 - c), "c", shift(NC, 1)) for to_xl in (1 - xl, xl)
-    ]
+    w_here, w_core, w_next, w_last = (
+        w_columns(xl, c),
+        w_columns(xl, 1 - c),
+        w_columns(1 - xl, c),
+        w_columns(1 - xl, 1 - c),
+    )
+    w_here, w_core, w_next, w_last, frame_mask = lax.optimization_barrier(
+        (w_here, w_core, w_next, w_last, frame_mask)
+    )
+    places = [(x, core_) for x in range(XH * XL) for core_ in range(NC)]
+    along_x = ("xh", "xl", "c")
+    w_next = lax.ppermute(
+        w_next, along_x, [(x * NC + k, (x + 1) % 4 * NC + k) for x, k in places]
+    )
+    w_last = lax.ppermute(
+        w_last, along_x, [(x * NC + k, (x + 3) % 4 * NC + 1 - k) for x, k in places]
+    )
+    w_core = lax.ppermute(w_core, "c", shift(NC, 1))
+    groups = live_tiles(core, frame_mask)
 
     slots = lax.all_to_all(slots, ("xh", "z"), 0, 0, tiled=True)
+    slots, w_here, groups = lax.optimization_barrier((slots, w_here, groups))
     own_query, kv = slots[:, :HALF], slots[:, HALF:]
-    query = jnp.concatenate([own_query, lax.ppermute(own_query, "c", shift(NC, 1))], axis=1)
     before = lax.ppermute(kv, "y", shift(NY, 1))
     after = lax.ppermute(kv, "y", shift(NY, -1))
+    query = jnp.concatenate([own_query, lax.ppermute(own_query, "c", shift(NC, 1))], axis=1)
+    state = attend(*groups[0], query, [kv], None, False)
+    before, after, state = lax.optimization_barrier((before, after, state))
     low = lax.ppermute(before[: ROWS // 2], "y", shift(NY, 1))
     high = lax.ppermute(after[ROWS // 2 :], "y", shift(NY, -1))
-    state = attend(*groups[0], query, [kv], None, False)
     state = attend(*groups[1], query, [before, after], state, False)
+    low, high, w_next, w_last, w_core = lax.optimization_barrier(
+        (low, high, w_next, w_last, w_core)
+    )
     here, sent = attend(*groups[2], query, [low, high], state, True)
     there = lax.ppermute(sent, "c", shift(NC, 1))
-    merged = merge(here, there)
-    merged, w_own, w_other = lax.optimization_barrier((merged, w_own, w_other))
-    attended = lax.all_to_all(merged, ("xh", "z"), 0, 0, tiled=True)
-    other_rows = lax.ppermute(attended, "c", shift(NC, 1))
-    far = project(core, attended, other_rows, w_own[0], w_other[0], jnp.bfloat16)
-    far = lax.ppermute(far, "xl", shift(XL, 1))
-    near = project(core, attended, other_rows, w_own[1], w_other[1], jnp.float32)
-    return add(near, far)
+    rows = lax.all_to_all(merge(here, there), ("xh", "z"), 0, 0, tiled=True)
+    rows_xl = lax.ppermute(rows, "xl", shift(XL, 1))
+    rows_core = lax.ppermute(rows, "c", shift(NC, 1))
+    near = project(core, rows, rows_core, w_here, w_core, None)
+    rows_both = lax.ppermute(rows_xl, "c", shift(NC, 1))
+    return project(core, rows_xl, rows_both, w_next, w_last, near)
 
 
 def solution(mesh):

time: 114 us -> 107 us (0.939)
  Pallas kernels: 20.6 us -> 34 us
  waiting for transfers between devices: 27.8 us -> 16.6 us
  other arithmetic: 7.27 us -> 0.65 us
  local copies, waits for them, and re-layouts: 10.6 us -> 8.12 us
  starting transfers between devices: 30 us -> 32.3 us
  blocking collectives: 16.8 us -> 15 us
    all_to_all x1, waiting for transfers between devices: 15.2 us -> 0.83 us  [local(): slots = lax.all_to_all(slots, ('xh', 'z'), 0, 0, tiled=True)]
    pallas_call x3, Pallas kernels: 5.05 us -> 16.3 us  [the longest x1 11.3 us: live_tiles(): pl.pallas_call(tiles_kernel, out_shape=tuple(out_shape), in_specs=in_smem...]
    ppermute x4 -> x6, starting transfers between devices: 3.07 us -> 9.53 us  [the longest x1 3.18 us: local(): lax.ppermute(w_last, along_x, [(x * NC + k, (x + 3) % 4 * NC + 1 - k) for...]
    reduce_sum x17 -> x0, other arithmetic: 6.21 us -> none  [the longest x3 2.05 us: live_tiles(): jnp.sum(tiles, keepdims=True).astype(jnp.int32)]
    ppermute x4 -> x6, waiting for transfers between devices: 7.64 us -> 2.7 us  [the longest x1 2.69 us: local(): rows_xl = lax.ppermute(rows, 'xl', shift(XL, 1))]
    ppermute x1, waiting for transfers between devices: 3.29 us -> 7.02 us  [local(): after = lax.ppermute(kv, 'y', shift(NY, -1))]
    ppermute x1, waiting for transfers between devices: 0.01 us -> 3.1 us  [local(): before = lax.ppermute(kv, 'y', shift(NY, 1))]
    ppermute x1, starting transfers between devices: 4.66 us -> 1.77 us  [local(): there = lax.ppermute(sent, 'c', shift(NC, 1))]
  transfers between devices with their start and end apart: 12 -> 14, of which waited for: 5 -> 6; matrix products, arithmetic and copies ran while one was open for 13% -> 7% of each run, Pallas kernels for 15% -> 22%
where the time goes in v4:
time: 107 us
  Pallas kernels  34 us (32%)
  starting transfers between devices  32.3 us (30%)
  waiting for transfers between devices  16.6 us (16%)
  blocking collectives  15 us (14%)
  local copies, waits for them, and re-layouts  8.12 us (8%)
    all_to_all x1, blocking collectives, local(): rows = lax.all_to_all(merge(here, there), ('xh', 'z'), 0, 0, tiled=True)  15 us
    pallas_call x3, Pallas kernels, attend(): pl.pallas_call(kernel, out_shape=(parcel, parcel) if last else (whole, wh...  14.3 us
    pallas_call x1, Pallas kernels, live_tiles(): pl.pallas_call(tiles_kernel, out_shape=tuple(out_shape), in_specs=in_smem...  11.3 us
    all_to_all x1, starting transfers between devices, local(): slots = lax.all_to_all(slots, ('xh', 'z'), 0, 0, tiled=True)  9.06 us
    ppermute x1, waiting for transfers between devices, local(): after = lax.ppermute(kv, 'y', shift(NY, -1))  7.02 us
    dynamic_slice x1, local copies, waits for them, and re-layouts, w_columns(): lax.dynamic_slice(w_out, (0, (to_xl * NC + to_c) * width), (w_out.shape[0...  5.31 us
    pallas_call x2, Pallas kernels, project(): pl.pallas_call(kernel, out_shape=jax.ShapeDtypeStruct((BLOCK, width), jnp...  5.06 us
    ppermute x1, starting transfers between devices, local(): got = lax.ppermute(sent, 'c', shift(NC, 1))  3.33 us
  transfers between devices with their start and end apart: 14, of which 6 were waited for; matrix products, arithmetic and copies ran while one was open for 7% of the time, Pallas kernels for 22%

profile of v4, /device:TPU:1, one launch (start us, length us, event | category | flops | bytes accessed | tf_op | source)
XLA Modules:
  0.0 106.8 jit_solution(3934952264223688160)
XLA Ops:
  0.6 2.8 %shard_map.55 = (bf16[16,192,128]{2,1,0:T(8,128)(2,1)}, bf16[5,192,128]{2,1,0:T(8,128)(2,1)}) custom-call(s32[2]{0:T(128)} %pad_add_fusion.core_ref.place_ref, bf16[128,640]{1,0:T(8,128)(2,1)} %q_hbm.1, bf16[128,640]{1,0:T(8,128)(2,1)} %k_hbm.1, bf16[128,640]{1,0:T(8,128)(2,1)} %v_hbm.1), custom_call_target="tpu_custom_call" | custom-call | tf_op jit(solution)/shard_map/pallas_call | solution.py:60
  3.4 3.3 %collective-permute-start = (bf16[5,192,128]{2,1,0:T(8,128)(2,1)}, bf16[5,192,128]{2,1,0:T(8,128)(2,1)S(1)}, u32[]{:S(2)}, u32[]{:S(2)}) collective-permute-start(bf16[5,192,128]{2,1,0:T(8,128)(2,1)} %get-tuple-element.47), channel_id=1, source_target_pairs={{0,1},{1,0},{2,3},{3,2},{4,5},{5,4},{6,7},{7,6},{8,9},{9,8},{10,11... | collective-permute-start | bytes 737288 | tf_op jit(solution)/shard_map/ppermute | solution.py:316
  6.7 1.3 %collective-permute-done = bf16[5,192,128]{2,1,0:T(8,128)(2,1)S(1)} collective-permute-done((bf16[5,192,128]{2,1,0:T(8,128)(2,1)}, bf16[5,192,128]{2,1,0:T(8,128)(2,1)S(1)}, u32[]{:S(2)}, u32[]{:S(2)}) %collective-permute-start) | collective-permute-done | bytes 245792 | tf_op jit(solution)/shard_map/ppermute | solution.py:316
  8.8 9.1 %all-to-all-start = ((bf16[16,192,128]{2,1,0:T(8,128)(2,1)}), bf16[16,192,128]{2,1,0:T(8,128)(2,1)}, u32[]{:S(2)}, u32[]{:S(2)}) async-start(bf16[16,192,128]{2,1,0:T(8,128)(2,1)} %constant_dynamic-update-slice_fusion), calls=%async_computation | async-start | bytes 1572864 | tf_op jit(solution)/shard_map/all_to_all | solution.py:345
  17.9 5.3 %constant_dynamic-slice_fusion = (bf16[640,1280]{1,0:T(8,128)(2,1)}, bf16[640,1280]{1,0:T(8,128)(2,1)}, bf16[640,1280]{1,0:T(8,128)(2,1)}, bf16[640,1280]{1,0:T(8,128)(2,1)S(1)}) fusion(bf16[640,5120]{1,0:T(8,128)(2,1)} %param.9, s32[]{:T(128)S(6)} %select_n.19, s32[]{:T(128)S(6)} %select_n.18, s32[]{:T(128)S(6)} %select_n.17, s32[]{:T(128)S(6)} %select_n.16), kind=kLoop, calls=%fused_computation.1 | loop fusion | bytes 13107216 | tf_op jit(solution)/shard_map/dynamic_slice | solution.py:323
  23.5 3.2 %collective-permute-start.7 = (bf16[640,1280]{1,0:T(8,128)(2,1)}, bf16[640,1280]{1,0:T(8,128)(2,1)}, u32[]{:S(2)}, u32[]{:S(2)}) collective-permute-start(bf16[640,1280]{1,0:T(8,128)(2,1)} %get-tuple-element.69), channel_id=1, source_target_pairs={{0,131},{1,130},{2,1},{3,0},{128,3},{129,2},{130,129},{131,128},{4... | collective-permute-start | bytes 4915208 | tf_op jit(solution)/shard_map/ppermute | solution.py:339
  26.7 11.3 %shard_map.56 = (s32[1]{0:T(128)}, s32[4,256]{1,0:T(4,128)S(1)}, s32[1]{0:T(128)}, s32[4,384]{1,0:T(4,128)S(1)}, s32[1]{0:T(128)}, /*index=5*/s32[4,256]{1,0:T(4,128)S(1)}) custom-call(s32[2]{0:T(128)S(1)} %copy-done.1, s32[64,64]{1,0:T(8,128)S(1)} %copy-done), custom_call_target="tpu_custom_call" | custom-call | flops 1000000 | bytes 100000 | tf_op jit(solution)/shard_map/pallas_call | solution.py:300
  39.8 3.1 %collective-permute-start.1 = (bf16[16,64,128]{2,1,0:T(8,128)(2,1)S(1)}, bf16[16,64,128]{2,1,0:T(8,128)(2,1)S(1)}, u32[]{:S(2)}, u32[]{:S(2)}) collective-permute-start(bf16[16,64,128]{2,1,0:T(8,128)(2,1)S(1)} %slice.12), channel_id=1, source_target_pairs={{0,1},{1,0},{2,3},{3,2},{4,5},{5,4},{6,7},{7,6},{8,9},{9,8},{10,11... | collective-permute-start | bytes 786440 | tf_op jit(solution)/shard_map/ppermute | solution.py:350
  42.9 1.1 %slice.13.refs_0_ = bf16[16,128,128]{2,1,0:T(8,128)(2,1)S(1)} slice(bf16[16,192,128]{2,1,0:T(8,128)(2,1)} %all-to-all-done), slice={[0:16], [64:192], [0:128]} | slice | bytes 1048576 | tf_op jit(solution)/shard_map/slice | solution.py:347
  44.0 2.8 %collective-permute-start.3 = (bf16[16,128,128]{2,1,0:T(8,128)(2,1)S(1)}, bf16[16,128,128]{2,1,0:T(8,128)(2,1)S(1)}, u32[]{:S(2)}, u32[]{:S(2)}) collective-permute-start(bf16[16,128,128]{2,1,0:T(8,128)(2,1)S(1)} %slice.13.refs_0_), channel_id=1, source_target_pairs={{0,12},{4,0},{8,4},{12,8},{1,13},{5,1},{9,5},{13,9},{2,14},{6,2},{... | collective-permute-start | bytes 1572872 | tf_op jit(solution)/shard_map/ppermute | solution.py:349
  46.9 4.3 %shard_map.57 = (f32[16,128,128]{2,1,0:T(8,128)S(1)}, f32[16,128,128]{2,1,0:T(8,128)S(1)}, f32[16,128,128]{2,1,0:T(8,128)S(1)}) custom-call(s32[1]{0:T(128)} %get-tuple-element.61.count_ref, s32[4,256]{1,0:T(4,128)S(1)} %get-tuple-element.62.table_ref, bf16[16,128,128]{2,1,0:T(8,128)(2,1)S(1)} %pad_maximum_fusion.q_ref, bf16[16,128,128]{2,1,0:T(8,128)(2,1)S(1)} %slice.13.refs_0_), custom_call_target="tpu_custom_call" | custom-call | flops 167772160 | bytes 6291456 | tf_op jit(solution)/shard_map/pallas_call | solution.py:181
  51.1 7.0 %collective-permute-done.3.refs_1_ = bf16[16,128,128]{2,1,0:T(8,128)(2,1)S(1)} collective-permute-done((bf16[16,128,128]{2,1,0:T(8,128)(2,1)S(1)}, bf16[16,128,128]{2,1,0:T(8,128)(2,1)S(1)}, u32[]{:S(2)}, u32[]{:S(2)}) %collective-permute-start.3) | collective-permute-done | bytes 524320 | tf_op jit(solution)/shard_map/ppermute | solution.py:349
  58.1 3.1 %collective-permute-done.2.refs_0_ = bf16[16,128,128]{2,1,0:T(8,128)(2,1)S(1)} collective-permute-done((bf16[16,128,128]{2,1,0:T(8,128)(2,1)S(1)}, bf16[16,128,128]{2,1,0:T(8,128)(2,1)S(1)}, u32[]{:S(2)}, u32[]{:S(2)}) %collective-permute-start.2) | collective-permute-done | bytes 524320 | tf_op jit(solution)/shard_map/ppermute | solution.py:348
  61.4 2.7 %collective-permute-start.5 = (bf16[8,128,128]{2,1,0:T(8,128)(2,1)S(1)}, bf16[8,128,128]{2,1,0:T(8,128)(2,1)S(1)}, u32[]{:S(2)}, u32[]{:S(2)}) collective-permute-start(bf16[8,128,128]{2,1,0:T(8,128)(2,1)S(1)} %slice.15), channel_id=1, source_target_pairs={{0,12},{4,0},{8,4},{12,8},{1,13},{5,1},{9,5},{13,9},{2,14},{6,2},{... | collective-permute-start | bytes 786440 | tf_op jit(solution)/shard_map/ppermute | solution.py:354
  64.0 6.3 %shard_map.58 = (f32[16,128,128]{2,1,0:T(8,128)S(1)}, f32[16,128,128]{2,1,0:T(8,128)S(1)}, f32[16,128,128]{2,1,0:T(8,128)S(1)}) custom-call(s32[1]{0:T(128)} %get-tuple-element.73.count_ref, s32[4,384]{1,0:T(4,128)S(1)} %get-tuple-element.74.table_ref, bf16[16,128,128]{2,1,0:T(8,128)(2,1)S(1)} %pad_maximum_fusion.q_ref, ...), custom_call_target="tpu_custom_call" | custom-call | flops 335544320 | bytes 6291456 | tf_op jit(solution)/shard_map/pallas_call | solution.py:181
  70.4 3.7 %shard_map.59 = (f32[17,64,128]{2,1,0:T(8,128)S(1)}, f32[17,64,128]{2,1,0:T(8,128)S(1)}) custom-call(s32[1]{0:T(128)} %get-tuple-element.58.count_ref, s32[4,256]{1,0:T(4,128)S(1)} %get-tuple-element.59.table_ref, bf16[16,128,128]{2,1,0:T(8,128)(2,1)S(1)} %pad_maximum_fusion.q_ref, bf16[8,128,128]{2,1,0:T(8,128)(2,1)S(1)} %collective-permute-done.4.refs_0_, ...), custom_call_target="tpu_custom_call" | custom-call | flops 335544320 | bytes 6291456 | tf_op jit(solution)/shard_map/pallas_call | solution.py:181
  74.1 1.8 %collective-permute-start.9 = (f32[17,64,128]{2,1,0:T(8,128)S(1)}, f32[17,64,128]{2,1,0:T(8,128)S(1)}, u32[]{:S(2)}, u32[]{:S(2)}) collective-permute-start(f32[17,64,128]{2,1,0:T(8,128)S(1)} %get-tuple-element.82), channel_id=1, source_target_pairs={{0,1},{1,0},{2,3},{3,2},{4,5},{5,4},{6,7},{7,6},{8,9},{9,8},{10,11... | collective-permute-start | bytes 1671176 | tf_op jit(solution)/shard_map/ppermute | solution.py:360
  75.9 1.6 %collective-permute-done.9.there_ref = f32[17,64,128]{2,1,0:T(8,128)S(1)} collective-permute-done((f32[17,64,128]{2,1,0:T(8,128)S(1)}, f32[17,64,128]{2,1,0:T(8,128)S(1)}, u32[]{:S(2)}, u32[]{:S(2)}) %collective-permute-start.9) | collective-permute-done | bytes 557088 | tf_op jit(solution)/shard_map/ppermute | solution.py:360
  78.1 15.0 %all_to_all.10.a_ref = bf16[16,64,128]{2,1,0:T(8,128)(2,1)S(1)} all-to-all(bf16[16,64,128]{2,1,0:T(8,128)(2,1)S(1)} %shard_map.60), channel_id=1, replica_groups=mesh['xh'=2,'z'=8,'y'=4,'xl'=2,'c'=2] {'xh','z'}, dimensions={0} | all-to-all | bytes 524288 | tf_op jit(solution)/shard_map/all_to_all | solution.py:361
  93.5 2.4 %collective-permute-start.12 = (bf16[16,64,128]{2,1,0:T(8,128)(2,1)S(1)}, bf16[16,64,128]{2,1,0:T(8,128)(2,1)S(1)}, u32[]{:S(2)}, u32[]{:S(2)}) collective-permute-start(bf16[16,64,128]{2,1,0:T(8,128)(2,1)S(1)} %all_to_all.10.a_ref), channel_id=1, source_target_pairs={{0,1},{1,0},{2,3},{3,2},{4,5},{5,4},{6,7},{7,6},{8,9},{9,8},{10,11... | collective-permute-start | bytes 786440 | tf_op jit(solution)/shard_map/ppermute | solution.py:363
  96.0 2.7 %collective-permute-done.10.a_ref = bf16[16,64,128]{2,1,0:T(8,128)(2,1)S(1)} collective-permute-done((bf16[16,64,128]{2,1,0:T(8,128)(2,1)S(1)}, bf16[16,64,128]{2,1,0:T(8,128)(2,1)S(1)}, u32[]{:S(2)}, u32[]{:S(2)}) %collective-permute-start.10) | collective-permute-done | bytes 262176 | tf_op jit(solution)/shard_map/ppermute | solution.py:362
  98.6 3.1 %collective-permute-start.11 = (bf16[16,64,128]{2,1,0:T(8,128)(2,1)S(1)}, bf16[16,64,128]{2,1,0:T(8,128)(2,1)S(1)}, u32[]{:S(2)}, u32[]{:S(2)}) collective-permute-start(bf16[16,64,128]{2,1,0:T(8,128)(2,1)S(1)} %collective-permute-done.10.a_ref), channel_id=1, source_target_pairs={{0,1},{1,0},{2,3},{3,2},{4,5},{5,4},{6,7},{7,6},{8,9},{9,8},{10,11... | collective-permute-start | bytes 786440 | tf_op jit(solution)/shard_map/ppermute | solution.py:365
  101.7 2.2 %shard_map.61.refs_0_ = f32[128,1280]{1,0:T(8,128)S(1)} custom-call(s32[2]{0:T(128)S(1)} %copy-done.1, bf16[16,64,128]{2,1,0:T(8,128)(2,1)S(1)} %all_to_all.10.a_ref, bf16[16,64,128]{2,1,0:T(8,128)(2,1)S(1)} %collective-permute-done.12.b_ref, bf16[640,1280]{1,0:T(8,128)(2,1)S(1)} %get-tuple-element.85.w_ref, bf16[640,1280]{1,0:T(8,128)(2,1)} %collective-permute-done.8.w2_ref), custom_call_target="tpu_custom_call" | custom-call | flops 419430400 | bytes 4194304 | tf_op jit(solution)/shard_map/pallas_call | solution.py:245
  103.9 2.9 %shard_map.62 = bf16[128,1280]{1,0:T(8,128)(2,1)} custom-call(s32[2]{0:T(128)S(1)} %copy-done.1, bf16[16,64,128]{2,1,0:T(8,128)(2,1)S(1)} %collective-permute-done.10.a_ref, bf16[16,64,128]{2,1,0:T(8,128)(2,1)S(1)} %collective-permute-done.11.b_ref, bf16[640,1280]{1,0:T(8,128)(2,1)S(1)} %collective-permute-done.6.w_ref, ...), custom_call_target="tpu_custom_call" | custom-call | flops 419430400 | bytes 4194304 | tf_op jit(solution)/shard_map/pallas_call | solution.py:245
  (25 shorter events, 4.7 us)
Async XLA Ops:
  3.4 4.7 %collective-permute-start = (bf16[5,192,128]{2,1,0:T(8,128)(2,1)}, bf16[5,192,128]{2,1,0:T(8,128)(2,1)S(1)}, u32[]{:S(2)}, u32[]{:S(2)}) collective-permute-start(bf16[5,192,128]{2,1,0:T(8,128)(2,1)} %get-tuple-element.47), channel_id=1, source_target_pairs={{0,1},{1,0},{2,3},{3,2},{4,5},{5,4},{6,7},{7,6},{8,9},{9,8},{10,11... | collective-permute-start | bytes 737288 | tf_op jit(solution)/shard_map/ppermute | solution.py:316
  8.8 30.0 %all-to-all-start = ((bf16[16,192,128]{2,1,0:T(8,128)(2,1)}), bf16[16,192,128]{2,1,0:T(8,128)(2,1)}, u32[]{:S(2)}, u32[]{:S(2)}) async-start(bf16[16,192,128]{2,1,0:T(8,128)(2,1)} %constant_dynamic-update-slice_fusion), calls=%async_computation | async-start | bytes 1572864 | tf_op jit(solution)/shard_map/all_to_all | solution.py:345
  17.9 8.8 %copy-start = (s32[64,64]{1,0:T(8,128)S(1)}, s32[64,64]{1,0:T(8,128)}, u32[]{:S(2)}) copy-start(s32[64,64]{1,0:T(8,128)} %mask_ref) | copy-start | bytes 49156
  17.9 8.8 %copy-start.1 = (s32[2]{0:T(128)S(1)}, s32[2]{0:T(128)}, u32[]{:S(2)}) copy-start(s32[2]{0:T(128)} %pad_add_fusion.core_ref.place_ref) | copy-start | bytes 28
  23.2 47.2 %collective-permute-start.6 = (bf16[640,1280]{1,0:T(8,128)(2,1)}, bf16[640,1280]{1,0:T(8,128)(2,1)S(1)}, u32[]{:S(2)}, u32[]{:S(2)}) collective-permute-start(bf16[640,1280]{1,0:T(8,128)(2,1)} %get-tuple-element.68), channel_id=1, source_target_pairs={{0,2},{1,3},{2,128},{3,129},{128,130},{129,131},{130,0},{131,1},{4... | collective-permute-start | bytes 4915208 | tf_op jit(solution)/shard_map/ppermute | solution.py:336
  23.5 46.9 %collective-permute-start.7 = (bf16[640,1280]{1,0:T(8,128)(2,1)}, bf16[640,1280]{1,0:T(8,128)(2,1)}, u32[]{:S(2)}, u32[]{:S(2)}) collective-permute-start(bf16[640,1280]{1,0:T(8,128)(2,1)} %get-tuple-element.69), channel_id=1, source_target_pairs={{0,131},{1,130},{2,1},{3,0},{128,3},{129,2},{130,129},{131,128},{4... | collective-permute-start | bytes 4915208 | tf_op jit(solution)/shard_map/ppermute | solution.py:339
  26.7 43.7 %collective-permute-start.8 = (bf16[640,1280]{1,0:T(8,128)(2,1)}, bf16[640,1280]{1,0:T(8,128)(2,1)}, u32[]{:S(2)}, u32[]{:S(2)}) collective-permute-start(bf16[640,1280]{1,0:T(8,128)(2,1)} %get-tuple-element.70), channel_id=1, source_target_pairs={{0,1},{1,0},{2,3},{3,2},{4,5},{5,4},{6,7},{7,6},{8,9},{9,8},{10,11... | collective-permute-start | bytes 4915208 | tf_op jit(solution)/shard_map/ppermute | solution.py:342
  39.8 7.0 %collective-permute-start.1 = (bf16[16,64,128]{2,1,0:T(8,128)(2,1)S(1)}, bf16[16,64,128]{2,1,0:T(8,128)(2,1)S(1)}, u32[]{:S(2)}, u32[]{:S(2)}) collective-permute-start(bf16[16,64,128]{2,1,0:T(8,128)(2,1)S(1)} %slice.12), channel_id=1, source_target_pairs={{0,1},{1,0},{2,3},{3,2},{4,5},{5,4},{6,7},{7,6},{8,9},{9,8},{10,11... | collective-permute-start | bytes 786440 | tf_op jit(solution)/shard_map/ppermute | solution.py:350
  44.0 14.1 %collective-permute-start.3 = (bf16[16,128,128]{2,1,0:T(8,128)(2,1)S(1)}, bf16[16,128,128]{2,1,0:T(8,128)(2,1)S(1)}, u32[]{:S(2)}, u32[]{:S(2)}) collective-permute-start(bf16[16,128,128]{2,1,0:T(8,128)(2,1)S(1)} %slice.13.refs_0_), channel_id=1, source_target_pairs={{0,12},{4,0},{8,4},{12,8},{1,13},{5,1},{9,5},{13,9},{2,14},{6,2},{... | collective-permute-start | bytes 1572872 | tf_op jit(solution)/shard_map/ppermute | solution.py:349
  46.8 14.4 %collective-permute-start.2 = (bf16[16,128,128]{2,1,0:T(8,128)(2,1)S(1)}, bf16[16,128,128]{2,1,0:T(8,128)(2,1)S(1)}, u32[]{:S(2)}, u32[]{:S(2)}) collective-permute-start(bf16[16,128,128]{2,1,0:T(8,128)(2,1)S(1)} %slice.13.refs_0_), channel_id=1, source_target_pairs={{0,4},{4,8},{8,12},{12,0},{1,5},{5,9},{9,13},{13,1},{2,6},{6,10},{... | collective-permute-start | bytes 1572872 | tf_op jit(solution)/shard_map/ppermute | solution.py:348
  61.3 9.1 %collective-permute-start.4 = (bf16[8,128,128]{2,1,0:T(8,128)(2,1)S(1)}, bf16[8,128,128]{2,1,0:T(8,128)(2,1)S(1)}, u32[]{:S(2)}, u32[]{:S(2)}) collective-permute-start(bf16[8,128,128]{2,1,0:T(8,128)(2,1)S(1)} %slice.14), channel_id=1, source_target_pairs={{0,4},{4,8},{8,12},{12,0},{1,5},{5,9},{9,13},{13,1},{2,6},{6,10},{... | collective-permute-start | bytes 786440 | tf_op jit(solution)/shard_map/ppermute | solution.py:353
  61.4 9.1 %collective-permute-start.5 = (bf16[8,128,128]{2,1,0:T(8,128)(2,1)S(1)}, bf16[8,128,128]{2,1,0:T(8,128)(2,1)S(1)}, u32[]{:S(2)}, u32[]{:S(2)}) collective-permute-start(bf16[8,128,128]{2,1,0:T(8,128)(2,1)S(1)} %slice.15), channel_id=1, source_target_pairs={{0,12},{4,0},{8,4},{12,8},{1,13},{5,1},{9,5},{13,9},{2,14},{6,2},{... | collective-permute-start | bytes 786440 | tf_op jit(solution)/shard_map/ppermute | solution.py:354
  74.1 3.4 %collective-permute-start.9 = (f32[17,64,128]{2,1,0:T(8,128)S(1)}, f32[17,64,128]{2,1,0:T(8,128)S(1)}, u32[]{:S(2)}, u32[]{:S(2)}) collective-permute-start(f32[17,64,128]{2,1,0:T(8,128)S(1)} %get-tuple-element.82), channel_id=1, source_target_pairs={{0,1},{1,0},{2,3},{3,2},{4,5},{5,4},{6,7},{7,6},{8,9},{9,8},{10,11... | collective-permute-start | bytes 1671176 | tf_op jit(solution)/shard_map/ppermute | solution.py:360
  93.0 5.6 %collective-permute-start.10 = (bf16[16,64,128]{2,1,0:T(8,128)(2,1)S(1)}, bf16[16,64,128]{2,1,0:T(8,128)(2,1)S(1)}, u32[]{:S(2)}, u32[]{:S(2)}) collective-permute-start(bf16[16,64,128]{2,1,0:T(8,128)(2,1)S(1)} %all_to_all.10.a_ref), channel_id=1, source_target_pairs={{0,2},{2,0},{1,3},{3,1},{4,6},{6,4},{5,7},{7,5},{8,10},{10,8},{9,1... | collective-permute-start | bytes 786440 | tf_op jit(solution)/shard_map/ppermute | solution.py:362
  93.5 8.2 %collective-permute-start.12 = (bf16[16,64,128]{2,1,0:T(8,128)(2,1)S(1)}, bf16[16,64,128]{2,1,0:T(8,128)(2,1)S(1)}, u32[]{:S(2)}, u32[]{:S(2)}) collective-permute-start(bf16[16,64,128]{2,1,0:T(8,128)(2,1)S(1)} %all_to_all.10.a_ref), channel_id=1, source_target_pairs={{0,1},{1,0},{2,3},{3,2},{4,5},{5,4},{6,7},{7,6},{8,9},{9,8},{10,11... | collective-permute-start | bytes 786440 | tf_op jit(solution)/shard_map/ppermute | solution.py:363
  98.6 5.3 %collective-permute-start.11 = (bf16[16,64,128]{2,1,0:T(8,128)(2,1)S(1)}, bf16[16,64,128]{2,1,0:T(8,128)(2,1)S(1)}, u32[]{:S(2)}, u32[]{:S(2)}) collective-permute-start(bf16[16,64,128]{2,1,0:T(8,128)(2,1)S(1)} %collective-permute-done.10.a_ref), channel_id=1, source_target_pairs={{0,1},{1,0},{2,3},{3,2},{4,5},{5,4},{6,7},{7,6},{8,9},{9,8},{10,11... | collective-permute-start | bytes 786440 | tf_op jit(solution)/shard_map/ppermute | solution.py:365

commit v5 on v4

v5 whole, which is shorter than its diff:
```python
import jax
import jax.numpy as jnp
from jax import lax
from jax.experimental import pallas as pl
from jax.experimental.pallas import tpu as pltpu
from jax.sharding import Mesh
from jax.sharding import PartitionSpec as P

HEAD_DIM = 128
BLOCK = 128
HALF = 64
HEADS = 5
XH, NZ, NY, XL, NC = 2, 8, 4, 2, 2
ROWS = XH * NZ
UNROLL = 4
TILE_N = 256
LOW = -1e30
EXP2_SCALE = HEAD_DIM ** (-0.5) * 1.4426950408889634
MIB = 1024 * 1024


def shift(size, by):
    return [(i, (i + by) % size) for i in range(size)]


def in_vmem(count):
    return [pl.BlockSpec(memory_space=pltpu.VMEM)] * count


def in_smem(count):
    return [pl.BlockSpec(memory_space=pltpu.SMEM)] * count


def split_kernel(q_ref, k_ref, v_ref, keep_ref, send_ref, sems):
    core = lax.axis_index("c")
    mine = pl.ds(pl.multiple_of(core * HALF, HALF), HALF)
    other = pl.ds(pl.multiple_of((1 - core) * HALF, HALF), HALF)
    copies = []

    def copy(source, target):
        copies.append(pltpu.make_async_copy(source, target, sems.at[len(copies)]))
        copies[-1].start()

    for head in range(HEADS):
        lanes = slice(head * HEAD_DIM, (head + 1) * HEAD_DIM)
        for t, ref in enumerate((q_ref, k_ref, v_ref)):
            copy(ref.at[other, lanes], send_ref.at[head, pl.ds(t * HALF, HALF)])
    for head in range(HEADS):
        lanes = slice(head * HEAD_DIM, (head + 1) * HEAD_DIM)
        for t, ref in enumerate((q_ref, k_ref, v_ref)):
            copy(ref.at[mine, lanes], keep_ref.at[core * NZ + head, pl.ds(t * HALF, HALF)])
    for each in copies:
        each.wait()


def split(queries, keys, values):
    anywhere = pl.BlockSpec(memory_space=pl.ANY)
    return pl.pallas_call(
        split_kernel,
        out_shape=(
            jax.ShapeDtypeStruct((ROWS, 3 * HALF, HEAD_DIM), jnp.bfloat16),
            jax.ShapeDtypeStruct((HEADS, 3 * HALF, HEAD_DIM), jnp.bfloat16),
        ),
        in_specs=[anywhere] * 3,
        out_specs=(anywhere,) * 2,
        scratch_shapes=[pltpu.SemaphoreType.DMA((6 * HEADS,))],
        compiler_params=pltpu.CompilerParams(vmem_limit_bytes=56 * MIB),
    )(queries, keys, values)


def score_tiles(steps, tables, q_ref, kv_ref, s_ref, top_ref):
    block_ref, slot_ref, live_ref = tables
    lane = lax.broadcasted_iota(jnp.int32, (BLOCK, BLOCK), 1)

    def score(step, carry):
        tiles = []
        for u in range(UNROLL):
            e = step * UNROLL + u
            key = jnp.concatenate(
                [kv_ref[slot_ref[2 * e], :HALF, :], kv_ref[slot_ref[2 * e + 1], :HALF, :]], axis=0
            )
            s = lax.dot_general(
                q_ref[block_ref[e]],
                key,
                (((1,), (1,)), ((), ())),
                preferred_element_type=jnp.float32,
            )
            s = jnp.where(lane < live_ref[e], s, LOW)
            s_ref[e] = s
            tiles.append(s)
        for u in range(UNROLL):
            block = block_ref[step * UNROLL + u]
            top_ref[block] = jnp.maximum(top_ref[block], tiles[u])
        return carry

    lax.fori_loop(0, steps, score, 0)


def mix_tiles(steps, tables, kv_ref, s_ref, m_ref, l_ref, a_ref):
    block_ref, slot_ref, live_ref = tables

    def mix(step, carry):
        weights, products = [], []
        for u in range(UNROLL):
            e = step * UNROLL + u
            value = jnp.concatenate(
                [kv_ref[slot_ref[2 * e], HALF:, :], kv_ref[slot_ref[2 * e + 1], HALF:, :]], axis=0
            )
            weight = jnp.exp2((s_ref[e] - m_ref[block_ref[e]]) * EXP2_SCALE)
            weights.append(weight)
            products.append(
                jnp.dot(weight.astype(jnp.bfloat16), value, preferred_element_type=jnp.float32)
            )
        for u in range(UNROLL):
            block = block_ref[step * UNROLL + u]
            l_ref[block] = l_ref[block] + weights[u]
            a_ref[block] = a_ref[block] + products[u]
        return carry

    lax.fori_loop(0, steps, mix, 0)


def write_parcels(m_ref, l_ref, a_ref, keep_ref, send_ref):
    lane = lax.broadcasted_iota(jnp.int32, (BLOCK, BLOCK), 1)
    stats = jnp.zeros((BLOCK, BLOCK), jnp.float32)
    for block in range(ROWS):
        total = jnp.sum(l_ref[block], axis=1, keepdims=True)
        stats = jnp.where(lane == block, m_ref[block], stats)
        stats = jnp.where(lane == ROWS + block, total, stats)
        keep_ref[block] = a_ref[block, :HALF, :]
        send_ref[block] = a_ref[block, HALF:, :]
    keep_ref[ROWS] = stats[:HALF]
    send_ref[ROWS] = stats[HALF:]


def attend(tables, query, parts, state, last):
    first = state is None
    slots = sum(part.shape[0] for part in parts)
    most = ROWS * slots // 2
    whole = jax.ShapeDtypeStruct((ROWS, BLOCK, BLOCK), jnp.float32)
    parcel = jax.ShapeDtypeStruct((ROWS + 1, HALF, HEAD_DIM), jnp.float32)

    def kernel(count_ref, block_ref, slot_ref, live_ref, own_ref, other_ref, *refs):
        tables = (block_ref, slot_ref, live_ref)
        part_refs, refs = refs[: len(parts)], refs[len(parts) :]
        if not first:
            (m_in, l_in, a_in), refs = refs[:3], refs[3:]
        if last:
            keep_ref, send_ref, q_ref, kv_ref, s_ref, top_ref, m_ref, l_ref, a_ref = refs
        else:
            m_ref, l_ref, a_ref, q_ref, kv_ref, s_ref, top_ref = refs
        q_ref[:, :HALF, :] = own_ref[...]
        q_ref[:, HALF:, :] = other_ref[...]
        at = 0
        for part in part_refs:
            kv_ref[at : at + part.shape[0]] = part[...]
            at += part.shape[0]
        steps = (count_ref[0] + (UNROLL - 1)) // UNROLL
        top_ref[...] = jnp.full(top_ref.shape, LOW, jnp.float32)
        score_tiles(steps, tables, q_ref, kv_ref, s_ref, top_ref)
        for block in range(ROWS):
            top = jnp.max(top_ref[block], axis=1, keepdims=True)
            if first:
                m_ref[block] = jnp.broadcast_to(top, (BLOCK, BLOCK))
                l_ref[block] = jnp.zeros((BLOCK, BLOCK), jnp.float32)
                a_ref[block] = jnp.zeros((BLOCK, HEAD_DIM), jnp.float32)
            else:
                new = jnp.maximum(m_in[block], top)
                fade = jnp.exp2((m_in[block] - new) * EXP2_SCALE)
                m_ref[block] = new
                l_ref[block] = l_in[block] * fade
                a_ref[block] = a_in[block] * fade
        mix_tiles(steps, tables, kv_ref, s_ref, m_ref, l_ref, a_ref)
        if last:
            write_parcels(m_ref, l_ref, a_ref, keep_ref, send_ref)

    scratch = [
        pltpu.VMEM((ROWS, BLOCK, HEAD_DIM), jnp.bfloat16),
        pltpu.VMEM((slots, 2 * HALF, HEAD_DIM), jnp.bfloat16),
        pltpu.VMEM((most, BLOCK, BLOCK), jnp.float32),
        pltpu.VMEM((ROWS, BLOCK, BLOCK), jnp.float32),
    ]
    if last:
        scratch += [pltpu.VMEM((ROWS, BLOCK, BLOCK), jnp.float32)] * 3
    return pl.pallas_call(
        kernel,
        out_shape=(parcel, parcel) if last else (whole, whole, whole),
        in_specs=in_smem(4) + in_vmem(2 + len(parts) + (0 if first else 3)),
        out_specs=tuple(in_vmem(2 if last else 3)),
        scratch_shapes=scratch,
        compiler_params=pltpu.CompilerParams(vmem_limit_bytes=28 * MIB),
        cost_estimate=pl.CostEstimate(
            flops=len(parts) * 40 * 2 * 128**3,
            bytes_accessed=6 * MIB,
            transcendentals=20 * 128 * 128,
        ),
    )(*tables, *query, *parts, *(() if first else state))


def merge_kernel(here_ref, there_ref, out_ref):
    here, there = here_ref[ROWS], there_ref[ROWS]
    for block in range(ROWS):
        m0, m1 = here[:, block : block + 1], there[:, block : block + 1]
        l0 = here[:, ROWS + block : ROWS + block + 1]
        l1 = there[:, ROWS + block : ROWS + block + 1]
        m = jnp.maximum(m0, m1)
        f0 = jnp.exp2((m0 - m) * EXP2_SCALE)
        f1 = jnp.exp2((m1 - m) * EXP2_SCALE)
        mixed = here_ref[block] * f0 + there_ref[block] * f1
        out_ref[block] = (mixed / (l0 * f0 + l1 * f1)).astype(jnp.bfloat16)


def merge(here, there):
    return pl.pallas_call(
        merge_kernel,
        out_shape=jax.ShapeDtypeStruct((ROWS, HALF, HEAD_DIM), jnp.bfloat16),
        in_specs=in_vmem(2),
        out_specs=in_vmem(1)[0],
        compiler_params=pltpu.CompilerParams(vmem_limit_bytes=4 * MIB),
    )(here, there)


def project(a, b, w_own, w_other, added):
    deep, width = w_own.shape
    final = added is not None

    def kernel(a_ref, b_ref, w_ref, w2_ref, *refs):
        if final:
            added_ref, refs = refs[0], refs[1:]
        out_ref, rows_ref = refs
        core = lax.axis_index("c")
        mine = pl.ds(pl.multiple_of(core * HALF, HALF), HALF)
        other = pl.ds(pl.multiple_of((1 - core) * HALF, HALF), HALF)
        for which, head_set in enumerate((core, 1 - core)):
            for head in range(HEADS):
                at = (which * HEADS + head) * HEAD_DIM
                rows_ref[mine, at : at + HEAD_DIM] = a_ref[head_set * NZ + head]
                rows_ref[other, at : at + HEAD_DIM] = b_ref[head_set * NZ + head]
        for at in range(0, width, TILE_N):
            lanes = slice(at, at + TILE_N)
            out = jnp.dot(rows_ref[:, :deep], w_ref[:, lanes], preferred_element_type=jnp.float32)
            out = out + jnp.dot(
                rows_ref[:, deep:], w2_ref[:, lanes], preferred_element_type=jnp.float32
            )
            if final:
                out = out + added_ref[:, lanes]
            out_ref[:, lanes] = out.astype(out_ref.dtype)

    return pl.pallas_call(
        kernel,
        out_shape=jax.ShapeDtypeStruct((BLOCK, width), jnp.bfloat16 if final else jnp.float32),
        in_specs=in_vmem(5 if final else 4),
        out_specs=in_vmem(1)[0],
        scratch_shapes=[pltpu.VMEM((BLOCK, 2 * deep), jnp.bfloat16)],
        compiler_params=pltpu.CompilerParams(vmem_limit_bytes=8 * MIB),
        cost_estimate=pl.CostEstimate(
            flops=2 * BLOCK * 2 * deep * width, bytes_accessed=4 * MIB, transcendentals=0
        ),
    )(a, b, w_own, w_other, *((added,) if final else ()))


GROUPS = ((0,), (1, 3), (2,))


def tiles_kernel(mask_ref, *refs):
    y = lax.axis_index("y")
    for group, columns in enumerate(GROUPS):
        count_ref, block_ref, slot_ref, live_ref = refs[4 * group : 4 * group + 4]

        def one_query_block(block, start, columns=columns, refs=(block_ref, slot_ref, live_ref)):
            block_ref, slot_ref, live_ref = refs
            row = block * NY + y
            first = 2 * start
            at = first
            for column, back in enumerate(columns):
                theirs = (y - back + NY) & (NY - 1)
                for i in range(ROWS):
                    slot_ref[at] = column * ROWS + i
                    at = at + jnp.where(mask_ref[row, i * NY + theirs] != 0, 1, 0)
            slot_ref[at] = 0
            tiles = (at - first + 1) >> 1

            def fill(t, carry):
                block_ref[start + t] = block
                live_ref[start + t] = 2 * HALF
                return carry

            lax.fori_loop(0, tiles, fill, 0)

            @pl.when(((at - first) & 1) == 1)
            def _():
                live_ref[start + tiles - 1] = HALF

            return start + tiles

        total = lax.fori_loop(0, ROWS, one_query_block, jnp.int32(0))
        count_ref[0] = total
        for u in range(UNROLL):
            block_ref[total + u] = 0
            live_ref[total + u] = 0
            slot_ref[2 * (total + u)] = 0
            slot_ref[2 * (total + u) + 1] = 0


def live_tiles(frame_mask):
    out_shape = []
    for columns in GROUPS:
        most = ROWS * ROWS * len(columns) // 2 + 128
        out_shape += [
            jax.ShapeDtypeStruct((size,), jnp.int32) for size in (1, most, 2 * most, most)
        ]
    flat = pl.pallas_call(
        tiles_kernel,
        out_shape=tuple(out_shape),
        in_specs=in_smem(1),
        out_specs=tuple(in_smem(len(out_shape))),
        compiler_params=pltpu.CompilerParams(vmem_limit_bytes=4 * MIB),
        cost_estimate=pl.CostEstimate(flops=10**6, bytes_accessed=10**5, transcendentals=0),
    )(frame_mask)
    return [tuple(flat[4 * i : 4 * i + 4]) for i in range(len(GROUPS))]


def local(queries, keys, values, frame_mask, w_out):
    xl, c = lax.axis_index("xl"), lax.axis_index("c")

    slots, sent = split(queries, keys, values)
    got = lax.ppermute(sent, "c", shift(NC, 1))
    slots = lax.dynamic_update_slice(slots, got, ((1 - c) * NZ, 0, 0))
    slots, w_out = lax.optimization_barrier((slots, w_out))

    width = w_out.shape[1] // (XL * NC)

    def w_columns(to_xl, to_c):
        return lax.dynamic_slice(w_out, (0, (to_xl * NC + to_c) * width), (w_out.shape[0], width))

    w_here, w_core, w_next, w_last = (
        w_columns(xl, c),
        w_columns(xl, 1 - c),
        w_columns(1 - xl, c),
        w_columns(1 - xl, 1 - c),
    )
    w_here, w_core, w_next, w_last, frame_mask = lax.optimization_barrier(
        (w_here, w_core, w_next, w_last, frame_mask)
    )
    places = [(x, core_) for x in range(XH * XL) for core_ in range(NC)]
    along_x = ("xh", "xl", "c")
    w_next = lax.ppermute(
        w_next, along_x, [(x * NC + k, (x + 1) % 4 * NC + k) for x, k in places]
    )
    w_last = lax.ppermute(
        w_last, along_x, [(x * NC + k, (x + 3) % 4 * NC + 1 - k) for x, k in places]
    )
    w_core = lax.ppermute(w_core, "c", shift(NC, 1))
    groups = live_tiles(frame_mask)

    slots = lax.all_to_all(slots, ("xh", "z"), 0, 0, tiled=True)
    slots, w_here, groups = lax.optimization_barrier((slots, w_here, groups))
    slots, kv = lax.optimization_barrier((slots, slots[:, HALF:]))
    before = lax.ppermute(kv, "y", shift(NY, 1))
    after = lax.ppermute(kv, "y", shift(NY, -1))
    query = slots[:, :HALF]
    query = (query, lax.ppermute(query, "c", shift(NC, 1)))
    state = attend(groups[0], query, [kv], None, False)
    before, after, state = lax.optimization_barrier((before, after, state))
    low = lax.ppermute(before[: ROWS // 2], "y", shift(NY, 1))
    high = lax.ppermute(after[ROWS // 2 :], "y", shift(NY, -1))
    state = attend(groups[1], query, [before, after], state, False)
    low, high, w_next, w_last, w_core = lax.optimization_barrier(
        (low, high, w_next, w_last, w_core)
    )
    here, sent = attend(groups[2], query, [low, high], state, True)
    there = lax.ppermute(sent, "c", shift(NC, 1))
    rows = lax.all_to_all(merge(here, there), ("xh", "z"), 0, 0, tiled=True)
    rows_xl = lax.ppermute(rows, "xl", shift(XL, 1))
    rows_core = lax.ppermute(rows, "c", shift(NC, 1))
    near = project(rows, rows_core, w_here, w_core, None)
    rows_xl, near = lax.optimization_barrier((rows_xl, near))
    rows_both = lax.ppermute(rows_xl, "c", shift(NC, 1))
    return project(rows_xl, rows_both, w_next, w_last, near)


def solution(mesh):
    fine = Mesh(mesh.devices.reshape(XH, NZ, NY, XL, NC), ("xh", "z", "y", "xl", "c"))
    seq, head = ("xh", "z", "y"), ("xl", "c")
    in_specs = (P(seq, head), P(seq, head), P(seq, head), P(), P(head, None))
    return jax.shard_map(
        local, mesh=fine, in_specs=in_specs, out_specs=P(seq, head), check_vma=False
    )
```

time: 107 us -> 121 us (1.13)
  Pallas kernels: 34 us -> 43 us
  waiting for transfers between devices: 16.6 us -> 24.6 us
  starting transfers between devices: 32.3 us -> 30 us
    pallas_call x1, Pallas kernels: 2.8 us -> 16.3 us  [split(): pl.pallas_call(split_kernel, out_shape=(jax.ShapeDtypeStruct((ROWS, 3 * H...]
    all_to_all x1, waiting for transfers between devices: 0.83 us -> 5.33 us  [local(): slots = lax.all_to_all(slots, ('xh', 'z'), 0, 0, tiled=True)]
    pallas_call x1, Pallas kernels: 11.3 us -> 6.8 us  [live_tiles(): pl.pallas_call(tiles_kernel, out_shape=tuple(out_shape), in_specs=in_smem...]
    ppermute x1, starting transfers between devices: 3.09 us -> 0.78 us  [local(): rows_both = lax.ppermute(rows_xl, 'c', shift(NC, 1))]
    ppermute x1, waiting for transfers between devices: 2.69 us -> 4.59 us  [local(): rows_xl = lax.ppermute(rows, 'xl', shift(XL, 1))]
  transfers between devices with their start and end apart: 14 -> 14, of which waited for: 6 -> 8; matrix products, arithmetic and copies ran while one was open for 7% -> 6% of each run, Pallas kernels for 22% -> 16%
where the time goes in v5:
time: 121 us
  Pallas kernels  43 us (36%)
  starting transfers between devices  30 us (25%)
  waiting for transfers between devices  24.6 us (20%)
  blocking collectives  15.2 us (13%)
  local copies, waits for them, and re-layouts  8.11 us (7%)
    pallas_call x1, Pallas kernels, split(): pl.pallas_call(split_kernel, out_shape=(jax.ShapeDtypeStruct((ROWS, 3 * H...  16.3 us
    all_to_all x1, blocking collectives, local(): rows = lax.all_to_all(merge(here, there), ('xh', 'z'), 0, 0, tiled=True)  15.2 us
    pallas_call x3, Pallas kernels, attend(): pl.pallas_call(kernel, out_shape=(parcel, parcel) if last else (whole, wh...  14.2 us
    all_to_all x1, starting transfers between devices, local(): slots = lax.all_to_all(slots, ('xh', 'z'), 0, 0, tiled=True)  9.06 us
    ppermute x1, waiting for transfers between devices, local(): after = lax.ppermute(kv, 'y', shift(NY, -1))  7.01 us
    pallas_call x1, Pallas kernels, live_tiles(): pl.pallas_call(tiles_kernel, out_shape=tuple(out_shape), in_specs=in_smem...  6.8 us
    all_to_all x1, waiting for transfers between devices, local(): slots = lax.all_to_all(slots, ('xh', 'z'), 0, 0, tiled=True)  5.33 us
    dynamic_slice x1, local copies, waits for them, and re-layouts, w_columns(): lax.dynamic_slice(w_out, (0, (to_xl * NC + to_c) * width), (w_out.shape[0...  5.29 us
  transfers between devices with their start and end apart: 14, of which 8 were waited for; matrix products, arithmetic and copies ran while one was open for 6% of the time, Pallas kernels for 16%

profile of v5, /device:TPU:1, one launch (start us, length us, event | category | flops | bytes accessed | tf_op | source)
XLA Modules:
  0.0 121.0 jit_solution(4418416395787678994)
XLA Ops:
  0.0 16.3 %shard_map.55 = (bf16[16,192,128]{2,1,0:T(8,128)(2,1)}, bf16[5,192,128]{2,1,0:T(8,128)(2,1)}) custom-call(bf16[128,640]{1,0:T(8,128)(2,1)} %q_ref.1, bf16[128,640]{1,0:T(8,128)(2,1)} %k_ref.1, bf16[128,640]{1,0:T(8,128)(2,1)} %v_ref.1), custom_call_target="tpu_custom_call" | custom-call | tf_op jit(solution)/shard_map/pallas_call | solution.py:58
  16.3 3.3 %collective-permute-start = (bf16[5,192,128]{2,1,0:T(8,128)(2,1)}, bf16[5,192,128]{2,1,0:T(8,128)(2,1)S(1)}, u32[]{:S(2)}, u32[]{:S(2)}) collective-permute-start(bf16[5,192,128]{2,1,0:T(8,128)(2,1)} %get-tuple-element.63), channel_id=1, source_target_pairs={{0,1},{1,0},{2,3},{3,2},{4,5},{5,4},{6,7},{7,6},{8,9},{9,8},{10,11... | collective-permute-start | bytes 737288 | tf_op jit(solution)/shard_map/ppermute | solution.py:327
  19.6 1.3 %collective-permute-done = bf16[5,192,128]{2,1,0:T(8,128)(2,1)S(1)} collective-permute-done((bf16[5,192,128]{2,1,0:T(8,128)(2,1)}, bf16[5,192,128]{2,1,0:T(8,128)(2,1)S(1)}, u32[]{:S(2)}, u32[]{:S(2)}) %collective-permute-start) | collective-permute-done | bytes 245792 | tf_op jit(solution)/shard_map/ppermute | solution.py:327
  21.7 9.1 %all-to-all-start = ((bf16[16,192,128]{2,1,0:T(8,128)(2,1)}), bf16[16,192,128]{2,1,0:T(8,128)(2,1)}, u32[]{:S(2)}, u32[]{:S(2)}) async-start(bf16[16,192,128]{2,1,0:T(8,128)(2,1)} %constant_dynamic-update-slice_fusion), calls=%async_computation | async-start | bytes 1572864 | tf_op jit(solution)/shard_map/all_to_all | solution.py:356
  30.8 5.3 %constant_dynamic-slice_fusion = (bf16[640,1280]{1,0:T(8,128)(2,1)}, bf16[640,1280]{1,0:T(8,128)(2,1)}, bf16[640,1280]{1,0:T(8,128)(2,1)}, bf16[640,1280]{1,0:T(8,128)(2,1)S(1)}) fusion(bf16[640,5120]{1,0:T(8,128)(2,1)} %param.9, s32[]{:T(128)S(6)} %select_n.19, s32[]{:T(128)S(6)} %select_n.18, s32[]{:T(128)S(6)} %select_n.17, s32[]{:T(128)S(6)} %select_n.16), kind=kLoop, calls=%fused_computation | loop fusion | bytes 13107216 | tf_op jit(solution)/shard_map/dynamic_slice | solution.py:334
  36.4 3.2 %collective-permute-start.7 = (bf16[640,1280]{1,0:T(8,128)(2,1)}, bf16[640,1280]{1,0:T(8,128)(2,1)}, u32[]{:S(2)}, u32[]{:S(2)}) collective-permute-start(bf16[640,1280]{1,0:T(8,128)(2,1)} %get-tuple-element.97), channel_id=1, source_target_pairs={{0,131},{1,130},{2,1},{3,0},{128,3},{129,2},{130,129},{131,128},{4... | collective-permute-start | bytes 4915208 | tf_op jit(solution)/shard_map/ppermute | solution.py:350
  39.6 6.8 %shard_map.56 = (s32[1]{0:T(128)}, s32[256]{0:T(256)S(1)}, s32[512]{0:T(512)S(1)}, s32[256]{0:T(256)S(1)}, s32[1]{0:T(128)}, /*index=5*/s32[384]{0:T(512)S(1)}, ...) custom-call(s32[64,64]{1,0:T(8,128)S(1)} %copy-done), custom_call_target="tpu_custom_call" | custom-call | flops 1000000 | bytes 100000 | tf_op jit(solution)/shard_map/pallas_call | solution.py:312
  46.4 5.3 %all-to-all-done = bf16[16,192,128]{2,1,0:T(8,128)(2,1)} async-done(((bf16[16,192,128]{2,1,0:T(8,128)(2,1)}), bf16[16,192,128]{2,1,0:T(8,128)(2,1)}, u32[]{:S(2)}, u32[]{:S(2)}) %all-to-all-start) | async-done | bytes 786464 | tf_op jit(solution)/shard_map/all_to_all | solution.py:356
  53.8 3.1 %collective-permute-start.1 = (bf16[16,64,128]{2,1,0:T(8,128)(2,1)S(1)}, bf16[16,64,128]{2,1,0:T(8,128)(2,1)S(1)}, u32[]{:S(2)}, u32[]{:S(2)}) collective-permute-start(bf16[16,64,128]{2,1,0:T(8,128)(2,1)S(1)} %slice.13.own_ref), channel_id=1, source_target_pairs={{0,1},{1,0},{2,3},{3,2},{4,5},{5,4},{6,7},{7,6},{8,9},{9,8},{10,11... | collective-permute-start | bytes 786440 | tf_op jit(solution)/shard_map/ppermute | solution.py:362
  56.8 2.7 %collective-permute-start.3 = (bf16[16,128,128]{2,1,0:T(8,128)(2,1)S(1)}, bf16[16,128,128]{2,1,0:T(8,128)(2,1)S(1)}, u32[]{:S(2)}, u32[]{:S(2)}) collective-permute-start(bf16[16,128,128]{2,1,0:T(8,128)(2,1)S(1)} %slice.12.refs_0_), channel_id=1, source_target_pairs={{0,12},{4,0},{8,4},{12,8},{1,13},{5,1},{9,5},{13,9},{2,14},{6,2},{... | collective-permute-start | bytes 1572872 | tf_op jit(solution)/shard_map/ppermute | solution.py:360
  59.6 4.2 %shard_map.57 = (f32[16,128,128]{2,1,0:T(8,128)S(1)}, f32[16,128,128]{2,1,0:T(8,128)S(1)}, f32[16,128,128]{2,1,0:T(8,128)S(1)}) custom-call(s32[1]{0:T(128)} %get-tuple-element.87.count_ref, s32[256]{0:T(256)S(1)} %get-tuple-element.88.block_ref, s32[512]{0:T(512)S(1)} %get-tuple-element.89.slot_ref, s32[256]{0:T(256)S(1)} %get-tuple-element.90.live_ref, ...), custom_call_target="tpu_custom_call" | custom-call | flops 167772160 | bytes 6291456 | tf_op jit(solution)/shard_map/pallas_call | solution.py:185
  63.9 7.0 %collective-permute-done.3.refs_1_ = bf16[16,128,128]{2,1,0:T(8,128)(2,1)S(1)} collective-permute-done((bf16[16,128,128]{2,1,0:T(8,128)(2,1)S(1)}, bf16[16,128,128]{2,1,0:T(8,128)(2,1)S(1)}, u32[]{:S(2)}, u32[]{:S(2)}) %collective-permute-start.3) | collective-permute-done | bytes 524320 | tf_op jit(solution)/shard_map/ppermute | solution.py:360
  70.9 3.1 %collective-permute-done.2.refs_0_ = bf16[16,128,128]{2,1,0:T(8,128)(2,1)S(1)} collective-permute-done((bf16[16,128,128]{2,1,0:T(8,128)(2,1)S(1)}, bf16[16,128,128]{2,1,0:T(8,128)(2,1)S(1)}, u32[]{:S(2)}, u32[]{:S(2)}) %collective-permute-start.2) | collective-permute-done | bytes 524320 | tf_op jit(solution)/shard_map/ppermute | solution.py:359
  74.1 2.7 %collective-permute-start.5 = (bf16[8,128,128]{2,1,0:T(8,128)(2,1)S(1)}, bf16[8,128,128]{2,1,0:T(8,128)(2,1)S(1)}, u32[]{:S(2)}, u32[]{:S(2)}) collective-permute-start(bf16[8,128,128]{2,1,0:T(8,128)(2,1)S(1)} %slice.15), channel_id=1, source_target_pairs={{0,12},{4,0},{8,4},{12,8},{1,13},{5,1},{9,5},{13,9},{2,14},{6,2},{... | collective-permute-start | bytes 786440 | tf_op jit(solution)/shard_map/ppermute | solution.py:366
  76.8 5.9 %shard_map.58 = (f32[16,128,128]{2,1,0:T(8,128)S(1)}, f32[16,128,128]{2,1,0:T(8,128)S(1)}, f32[16,128,128]{2,1,0:T(8,128)S(1)}) custom-call(s32[1]{0:T(128)} %get-tuple-element.101.count_ref, s32[384]{0:T(512)S(1)} %get-tuple-element.102.block_ref, s32[768]{0:T(1024)S(1)} %get-tuple-element.103.slot_ref, s32[384]{0:T(512)S(1)} %get-tuple-element.104.live_ref, ...), custom_call_target="tpu_custom_call" | custom-call | flops 335544320 | bytes 6291456 | tf_op jit(solution)/shard_map/pallas_call | solution.py:185
  82.7 4.1 %shard_map.59 = (f32[17,64,128]{2,1,0:T(8,128)S(1)}, f32[17,64,128]{2,1,0:T(8,128)S(1)}) custom-call(s32[1]{0:T(128)} %get-tuple-element.80.count_ref, s32[256]{0:T(256)S(1)} %get-tuple-element.81.block_ref, s32[512]{0:T(512)S(1)} %get-tuple-element.82.slot_ref, s32[256]{0:T(256)S(1)} %get-tuple-element.83.live_ref, bf16[16,64,128]{2,1,0:T(8,128)(2,1)S(1)} %slice.13.own_ref, ...), custom_call_target="tpu_custom_call" | custom-call | flops 335544320 | bytes 6291456 | tf_op jit(solution)/shard_map/pallas_call | solution.py:185
  86.8 1.8 %collective-permute-start.9 = (f32[17,64,128]{2,1,0:T(8,128)S(1)}, f32[17,64,128]{2,1,0:T(8,128)S(1)}, u32[]{:S(2)}, u32[]{:S(2)}) collective-permute-start(f32[17,64,128]{2,1,0:T(8,128)S(1)} %get-tuple-element.112), channel_id=1, source_target_pairs={{0,1},{1,0},{2,3},{3,2},{4,5},{5,4},{6,7},{7,6},{8,9},{9,8},{10,11... | collective-permute-start | bytes 1671176 | tf_op jit(solution)/shard_map/ppermute | solution.py:372
  88.7 1.6 %collective-permute-done.9.there_ref = f32[17,64,128]{2,1,0:T(8,128)S(1)} collective-permute-done((f32[17,64,128]{2,1,0:T(8,128)S(1)}, f32[17,64,128]{2,1,0:T(8,128)S(1)}, u32[]{:S(2)}, u32[]{:S(2)}) %collective-permute-start.9) | collective-permute-done | bytes 557088 | tf_op jit(solution)/shard_map/ppermute | solution.py:372
  90.8 15.2 %all_to_all.10.a_ref = bf16[16,64,128]{2,1,0:T(8,128)(2,1)S(1)} all-to-all(bf16[16,64,128]{2,1,0:T(8,128)(2,1)S(1)} %shard_map.60), channel_id=1, replica_groups=mesh['xh'=2,'z'=8,'y'=4,'xl'=2,'c'=2] {'xh','z'}, dimensions={0} | all-to-all | bytes 524288 | tf_op jit(solution)/shard_map/all_to_all | solution.py:373
  106.1 2.2 %collective-permute-start.11 = (bf16[16,64,128]{2,1,0:T(8,128)(2,1)S(1)}, bf16[16,64,128]{2,1,0:T(8,128)(2,1)S(1)}, u32[]{:S(2)}, u32[]{:S(2)}) collective-permute-start(bf16[16,64,128]{2,1,0:T(8,128)(2,1)S(1)} %all_to_all.10.a_ref), channel_id=1, source_target_pairs={{0,1},{1,0},{2,3},{3,2},{4,5},{5,4},{6,7},{7,6},{8,9},{9,8},{10,11... | collective-permute-start | bytes 786440 | tf_op jit(solution)/shard_map/ppermute | solution.py:375
  109.4 2.2 %shard_map.61.refs_0_ = f32[128,1280]{1,0:T(8,128)S(1)} custom-call(bf16[16,64,128]{2,1,0:T(8,128)(2,1)S(1)} %all_to_all.10.a_ref, bf16[16,64,128]{2,1,0:T(8,128)(2,1)S(1)} %collective-permute-done.11.b_ref, bf16[640,1280]{1,0:T(8,128)(2,1)S(1)} %get-tuple-element.113.w_ref, bf16[640,1280]{1,0:T(8,128)(2,1)} %collective-permute-done.8.w2_ref), custom_call_target="tpu_custom_call" | custom-call | flops 419430400 | bytes 4194304 | tf_op jit(solution)/shard_map/pallas_call | solution.py:249
  111.6 4.6 %collective-permute-done.10.a_ref = bf16[16,64,128]{2,1,0:T(8,128)(2,1)S(1)} collective-permute-done((bf16[16,64,128]{2,1,0:T(8,128)(2,1)S(1)}, bf16[16,64,128]{2,1,0:T(8,128)(2,1)S(1)}, u32[]{:S(2)}, u32[]{:S(2)}) %collective-permute-start.10) | collective-permute-done | bytes 262176 | tf_op jit(solution)/shard_map/ppermute | solution.py:374
  117.0 1.2 collective-permute-done.12.b_ref
  118.1 2.9 %shard_map.62 = bf16[128,1280]{1,0:T(8,128)(2,1)} custom-call(bf16[16,64,128]{2,1,0:T(8,128)(2,1)S(1)} %collective-permute-done.10.a_ref, bf16[16,64,128]{2,1,0:T(8,128)(2,1)S(1)} %collective-permute-done.12.b_ref, bf16[640,1280]{1,0:T(8,128)(2,1)S(1)} %collective-permute-done.6.w_ref, bf16[640,1280]{1,0:T(8,128)(2,1)} %collective-permute-done.7.w2_ref, ...), custom_call_target="tpu_custom_call" | custom-call | flops 419430400 | bytes 4194304 | tf_op jit(solution)/shard_map/pallas_call | solution.py:249
  (21 shorter events, 5.8 us)
Async XLA Ops:
  16.3 4.7 %collective-permute-start = (bf16[5,192,128]{2,1,0:T(8,128)(2,1)}, bf16[5,192,128]{2,1,0:T(8,128)(2,1)S(1)}, u32[]{:S(2)}, u32[]{:S(2)}) collective-permute-start(bf16[5,192,128]{2,1,0:T(8,128)(2,1)} %get-tuple-element.63), channel_id=1, source_target_pairs={{0,1},{1,0},{2,3},{3,2},{4,5},{5,4},{6,7},{7,6},{8,9},{9,8},{10,11... | collective-permute-start | bytes 737288 | tf_op jit(solution)/shard_map/ppermute | solution.py:327
  21.7 30.0 %all-to-all-start = ((bf16[16,192,128]{2,1,0:T(8,128)(2,1)}), bf16[16,192,128]{2,1,0:T(8,128)(2,1)}, u32[]{:S(2)}, u32[]{:S(2)}) async-start(bf16[16,192,128]{2,1,0:T(8,128)(2,1)} %constant_dynamic-update-slice_fusion), calls=%async_computation | async-start | bytes 1572864 | tf_op jit(solution)/shard_map/all_to_all | solution.py:356
  30.7 8.8 %copy-start = (s32[64,64]{1,0:T(8,128)S(1)}, s32[64,64]{1,0:T(8,128)}, u32[]{:S(2)}) copy-start(s32[64,64]{1,0:T(8,128)} %mask_ref) | copy-start | bytes 49156
  36.0 46.6 %collective-permute-start.6 = (bf16[640,1280]{1,0:T(8,128)(2,1)}, bf16[640,1280]{1,0:T(8,128)(2,1)S(1)}, u32[]{:S(2)}, u32[]{:S(2)}) collective-permute-start(bf16[640,1280]{1,0:T(8,128)(2,1)} %get-tuple-element.96), channel_id=1, source_target_pairs={{0,2},{1,3},{2,128},{3,129},{128,130},{129,131},{130,0},{131,1},{4... | collective-permute-start | bytes 4915208 | tf_op jit(solution)/shard_map/ppermute | solution.py:347
  36.4 46.3 %collective-permute-start.7 = (bf16[640,1280]{1,0:T(8,128)(2,1)}, bf16[640,1280]{1,0:T(8,128)(2,1)}, u32[]{:S(2)}, u32[]{:S(2)}) collective-permute-start(bf16[640,1280]{1,0:T(8,128)(2,1)} %get-tuple-element.97), channel_id=1, source_target_pairs={{0,131},{1,130},{2,1},{3,0},{128,3},{129,2},{130,129},{131,128},{4... | collective-permute-start | bytes 4915208 | tf_op jit(solution)/shard_map/ppermute | solution.py:350
  39.6 43.1 %collective-permute-start.8 = (bf16[640,1280]{1,0:T(8,128)(2,1)}, bf16[640,1280]{1,0:T(8,128)(2,1)}, u32[]{:S(2)}, u32[]{:S(2)}) collective-permute-start(bf16[640,1280]{1,0:T(8,128)(2,1)} %get-tuple-element.98), channel_id=1, source_target_pairs={{0,1},{1,0},{2,3},{3,2},{4,5},{5,4},{6,7},{7,6},{8,9},{9,8},{10,11... | collective-permute-start | bytes 4915208 | tf_op jit(solution)/shard_map/ppermute | solution.py:353
  53.8 5.8 %collective-permute-start.1 = (bf16[16,64,128]{2,1,0:T(8,128)(2,1)S(1)}, bf16[16,64,128]{2,1,0:T(8,128)(2,1)S(1)}, u32[]{:S(2)}, u32[]{:S(2)}) collective-permute-start(bf16[16,64,128]{2,1,0:T(8,128)(2,1)S(1)} %slice.13.own_ref), channel_id=1, source_target_pairs={{0,1},{1,0},{2,3},{3,2},{4,5},{5,4},{6,7},{7,6},{8,9},{9,8},{10,11... | collective-permute-start | bytes 786440 | tf_op jit(solution)/shard_map/ppermute | solution.py:362
  56.8 14.0 %collective-permute-start.3 = (bf16[16,128,128]{2,1,0:T(8,128)(2,1)S(1)}, bf16[16,128,128]{2,1,0:T(8,128)(2,1)S(1)}, u32[]{:S(2)}, u32[]{:S(2)}) collective-permute-start(bf16[16,128,128]{2,1,0:T(8,128)(2,1)S(1)} %slice.12.refs_0_), channel_id=1, source_target_pairs={{0,12},{4,0},{8,4},{12,8},{1,13},{5,1},{9,5},{13,9},{2,14},{6,2},{... | collective-permute-start | bytes 1572872 | tf_op jit(solution)/shard_map/ppermute | solution.py:360
  59.6 14.4 %collective-permute-start.2 = (bf16[16,128,128]{2,1,0:T(8,128)(2,1)S(1)}, bf16[16,128,128]{2,1,0:T(8,128)(2,1)S(1)}, u32[]{:S(2)}, u32[]{:S(2)}) collective-permute-start(bf16[16,128,128]{2,1,0:T(8,128)(2,1)S(1)} %slice.12.refs_0_), channel_id=1, source_target_pairs={{0,4},{4,8},{8,12},{12,0},{1,5},{5,9},{9,13},{13,1},{2,6},{6,10},{... | collective-permute-start | bytes 1572872 | tf_op jit(solution)/shard_map/ppermute | solution.py:359
  74.0 8.7 %collective-permute-start.4 = (bf16[8,128,128]{2,1,0:T(8,128)(2,1)S(1)}, bf16[8,128,128]{2,1,0:T(8,128)(2,1)S(1)}, u32[]{:S(2)}, u32[]{:S(2)}) collective-permute-start(bf16[8,128,128]{2,1,0:T(8,128)(2,1)S(1)} %slice.14), channel_id=1, source_target_pairs={{0,4},{4,8},{8,12},{12,0},{1,5},{5,9},{9,13},{13,1},{2,6},{6,10},{... | collective-permute-start | bytes 786440 | tf_op jit(solution)/shard_map/ppermute | solution.py:365
  74.1 8.6 %collective-permute-start.5 = (bf16[8,128,128]{2,1,0:T(8,128)(2,1)S(1)}, bf16[8,128,128]{2,1,0:T(8,128)(2,1)S(1)}, u32[]{:S(2)}, u32[]{:S(2)}) collective-permute-start(bf16[8,128,128]{2,1,0:T(8,128)(2,1)S(1)} %slice.15), channel_id=1, source_target_pairs={{0,12},{4,0},{8,4},{12,8},{1,13},{5,1},{9,5},{13,9},{2,14},{6,2},{... | collective-permute-start | bytes 786440 | tf_op jit(solution)/shard_map/ppermute | solution.py:366
  86.8 3.4 %collective-permute-start.9 = (f32[17,64,128]{2,1,0:T(8,128)S(1)}, f32[17,64,128]{2,1,0:T(8,128)S(1)}, u32[]{:S(2)}, u32[]{:S(2)}) collective-permute-start(f32[17,64,128]{2,1,0:T(8,128)S(1)} %get-tuple-element.112), channel_id=1, source_target_pairs={{0,1},{1,0},{2,3},{3,2},{4,5},{5,4},{6,7},{7,6},{8,9},{9,8},{10,11... | collective-permute-start | bytes 1671176 | tf_op jit(solution)/shard_map/ppermute | solution.py:372
  106.1 3.3 %collective-permute-start.11 = (bf16[16,64,128]{2,1,0:T(8,128)(2,1)S(1)}, bf16[16,64,128]{2,1,0:T(8,128)(2,1)S(1)}, u32[]{:S(2)}, u32[]{:S(2)}) collective-permute-start(bf16[16,64,128]{2,1,0:T(8,128)(2,1)S(1)} %all_to_all.10.a_ref), channel_id=1, source_target_pairs={{0,1},{1,0},{2,3},{3,2},{4,5},{5,4},{6,7},{7,6},{8,9},{9,8},{10,11... | collective-permute-start | bytes 786440 | tf_op jit(solution)/shard_map/ppermute | solution.py:375
  108.2 7.9 %collective-permute-start.10 = (bf16[16,64,128]{2,1,0:T(8,128)(2,1)S(1)}, bf16[16,64,128]{2,1,0:T(8,128)(2,1)S(1)}, u32[]{:S(2)}, u32[]{:S(2)}) collective-permute-start(bf16[16,64,128]{2,1,0:T(8,128)(2,1)S(1)} %all_to_all.10.a_ref), channel_id=1, source_target_pairs={{0,2},{2,0},{1,3},{3,1},{4,6},{6,4},{5,7},{7,5},{8,10},{10,8},{9,1... | collective-permute-start | bytes 786440 | tf_op jit(solution)/shard_map/ppermute | solution.py:374
  116.2 1.9 %collective-permute-start.12 = (bf16[16,64,128]{2,1,0:T(8,128)(2,1)S(1)}, bf16[16,64,128]{2,1,0:T(8,128)(2,1)S(1)}, u32[]{:S(2)}, u32[]{:S(2)}) collective-permute-start(bf16[16,64,128]{2,1,0:T(8,128)(2,1)S(1)} %collective-permute-done.10.a_ref), channel_id=1, source_target_pairs={{0,1},{1,0},{2,3},{3,2},{4,5},{5,4},{6,7},{7,6},{8,9},{9,8},{10,11... | collective-permute-start | bytes 786440 | tf_op jit(solution)/shard_map/ppermute | solution.py:378

commit v6 on v5

--- a/solution.py
+++ b/solution.py
@@ -31,39 +31,48 @@
     return [pl.BlockSpec(memory_space=pltpu.SMEM)] * count
 
 
-def split_kernel(q_ref, k_ref, v_ref, keep_ref, send_ref, sems):
+def split_kernel(q_hbm, k_hbm, v_hbm, keep_hbm, send_hbm, whole_ref, keep_ref, send_ref, sems):
     core = lax.axis_index("c")
     mine = pl.ds(pl.multiple_of(core * HALF, HALF), HALF)
     other = pl.ds(pl.multiple_of((1 - core) * HALF, HALF), HALF)
-    copies = []
-
-    def copy(source, target):
-        copies.append(pltpu.make_async_copy(source, target, sems.at[len(copies)]))
-        copies[-1].start()
-
-    for head in range(HEADS):
-        lanes = slice(head * HEAD_DIM, (head + 1) * HEAD_DIM)
-        for t, ref in enumerate((q_ref, k_ref, v_ref)):
-            copy(ref.at[other, lanes], send_ref.at[head, pl.ds(t * HALF, HALF)])
-    for head in range(HEADS):
-        lanes = slice(head * HEAD_DIM, (head + 1) * HEAD_DIM)
-        for t, ref in enumerate((q_ref, k_ref, v_ref)):
-            copy(ref.at[mine, lanes], keep_ref.at[core * NZ + head, pl.ds(t * HALF, HALF)])
-    for each in copies:
-        each.wait()
+    loads = [
+        pltpu.make_async_copy(source, whole_ref.at[t], sems.at[t])
+        for t, source in enumerate((q_hbm, k_hbm, v_hbm))
+    ]
+    for load in loads:
+        load.start()
+    for t, load in enumerate(loads):
+        load.wait()
+        rows = slice(t * HALF, (t + 1) * HALF)
+        for head in range(HEADS):
+            lanes = slice(head * HEAD_DIM, (head + 1) * HEAD_DIM)
+            send_ref[head, rows, :] = whole_ref[t, other, lanes]
+            keep_ref[head, rows, :] = whole_ref[t, mine, lanes]
+    send = pltpu.make_async_copy(send_ref, send_hbm, sems.at[3])
+    keep = pltpu.make_async_copy(keep_ref, keep_hbm.at[pl.ds(core * NZ, HEADS)], sems.at[4])
+    send.start()
+    keep.start()
+    send.wait()
+    keep.wait()
 
 
 def split(queries, keys, values):
     anywhere = pl.BlockSpec(memory_space=pl.ANY)
+    part = (HEADS, 3 * HALF, HEAD_DIM)
     return pl.pallas_call(
         split_kernel,
         out_shape=(
             jax.ShapeDtypeStruct((ROWS, 3 * HALF, HEAD_DIM), jnp.bfloat16),
-            jax.ShapeDtypeStruct((HEADS, 3 * HALF, HEAD_DIM), jnp.bfloat16),
+            jax.ShapeDtypeStruct(part, jnp.bfloat16),
         ),
         in_specs=[anywhere] * 3,
         out_specs=(anywhere,) * 2,
-        scratch_shapes=[pltpu.SemaphoreType.DMA((6 * HEADS,))],
+        scratch_shapes=[
+            pltpu.VMEM((3,) + queries.shape, jnp.bfloat16),
+            pltpu.VMEM(part, jnp.bfloat16),
+            pltpu.VMEM(part, jnp.bfloat16),
+            pltpu.SemaphoreType.DMA((5,)),
+        ],
         compiler_params=pltpu.CompilerParams(vmem_limit_bytes=56 * MIB),
     )(queries, keys, values)
 
@@ -220,22 +229,33 @@
     )(here, there)
 
 
-def project(a, b, w_own, w_other, added):
+def project(a, b, w_own, w_other, added=None, staged=()):
     deep, width = w_own.shape
     final = added is not None
 
     def kernel(a_ref, b_ref, w_ref, w2_ref, *refs):
         if final:
             added_ref, refs = refs[0], refs[1:]
-        out_ref, rows_ref = refs
+        sources, out_ref, targets = (
+            refs[: len(staged)],
+            refs[len(staged)],
+            refs[len(staged) + 1 : 2 * len(staged) + 1],
+        )
+        rows_ref, sems = refs[2 * len(staged) + 1 :]
+        copies = [
+            pltpu.make_async_copy(source, target, sems.at[i])
+            for i, (source, target) in enumerate(zip(sources, targets))
+        ]
+        for copy in copies:
+            copy.start()
         core = lax.axis_index("c")
         mine = pl.ds(pl.multiple_of(core * HALF, HALF), HALF)
         other = pl.ds(pl.multiple_of((1 - core) * HALF, HALF), HALF)
         for which, head_set in enumerate((core, 1 - core)):
             for head in range(HEADS):
                 at = (which * HEADS + head) * HEAD_DIM
-                rows_ref[mine, at : at + HEAD_DIM] = a_ref[head_set * NZ + head]
-                rows_ref[other, at : at + HEAD_DIM] = b_ref[head_set * NZ + head]
+                rows_ref[mine, at : at + HEAD_DIM] = a_ref[head_set * HEADS + head]
+                rows_ref[other, at : at + HEAD_DIM] = b_ref[head_set * HEADS + head]
         for at in range(0, width, TILE_N):
             lanes = slice(at, at + TILE_N)
             out = jnp.dot(rows_ref[:, :deep], w_ref[:, lanes], preferred_element_type=jnp.float32)
@@ -245,18 +265,24 @@
             if final:
                 out = out + added_ref[:, lanes]
             out_ref[:, lanes] = out.astype(out_ref.dtype)
-
+        for copy in copies:
+            copy.wait()
+
+    out = jax.ShapeDtypeStruct((BLOCK, width), jnp.bfloat16 if final else jnp.float32)
     return pl.pallas_call(
         kernel,
-        out_shape=jax.ShapeDtypeStruct((BLOCK, width), jnp.bfloat16 if final else jnp.float32),
-        in_specs=in_vmem(5 if final else 4),
-        out_specs=in_vmem(1)[0],
-        scratch_shapes=[pltpu.VMEM((BLOCK, 2 * deep), jnp.bfloat16)],
+        out_shape=(out,) + tuple(jax.ShapeDtypeStruct(x.shape, x.dtype) for x in staged),
+        in_specs=in_vmem(5 if final else 4) + [pl.BlockSpec(memory_space=pl.ANY)] * len(staged),
+        out_specs=tuple(in_vmem(1 + len(staged))),
+        scratch_shapes=[
+            pltpu.VMEM((BLOCK, 2 * deep), jnp.bfloat16),
+            pltpu.SemaphoreType.DMA((max(len(staged), 1),)),
+        ],
         compiler_params=pltpu.CompilerParams(vmem_limit_bytes=8 * MIB),
         cost_estimate=pl.CostEstimate(
             flops=2 * BLOCK * 2 * deep * width, bytes_accessed=4 * MIB, transcendentals=0
         ),
-    )(a, b, w_own, w_other, *((added,) if final else ()))
+    )(a, b, w_own, w_other, *((added,) if final else ()), *staged)
 
 
 GROUPS = ((0,), (1, 3), (2,))
@@ -323,24 +349,24 @@
 def local(queries, keys, values, frame_mask, w_out):
     xl, c = lax.axis_index("xl"), lax.axis_index("c")
 
+    width = w_out.shape[1] // (XL * NC)
+
+    def w_columns(w, to_xl, to_c):
+        return lax.dynamic_slice(w, (0, (to_xl * NC + to_c) * width), (w.shape[0], width))
+
     slots, sent = split(queries, keys, values)
+    sent, w_out = lax.optimization_barrier((sent, w_out))
     got = lax.ppermute(sent, "c", shift(NC, 1))
+    w_core = lax.ppermute(w_columns(w_out, xl, 1 - c), "c", shift(NC, 1))
     slots = lax.dynamic_update_slice(slots, got, ((1 - c) * NZ, 0, 0))
     slots, w_out = lax.optimization_barrier((slots, w_out))
-
-    width = w_out.shape[1] // (XL * NC)
-
-    def w_columns(to_xl, to_c):
-        return lax.dynamic_slice(w_out, (0, (to_xl * NC + to_c) * width), (w_out.shape[0], width))
-
-    w_here, w_core, w_next, w_last = (
-        w_columns(xl, c),
-        w_columns(xl, 1 - c),
-        w_columns(1 - xl, c),
-        w_columns(1 - xl, 1 - c),
-    )
-    w_here, w_core, w_next, w_last, frame_mask = lax.optimization_barrier(
-        (w_here, w_core, w_next, w_last, frame_mask)
+    w_here, w_next, w_last = (
+        w_columns(w_out, xl, c),
+        w_columns(w_out, 1 - xl, c),
+        w_columns(w_out, 1 - xl, 1 - c),
+    )
+    w_here, w_next, w_last, frame_mask = lax.optimization_barrier(
+        (w_here, w_next, w_last, frame_mask)
     )
     places = [(x, core_) for x in range(XH * XL) for core_ in range(NC)]
     along_x = ("xh", "xl", "c")
@@ -350,33 +376,37 @@
     w_last = lax.ppermute(
         w_last, along_x, [(x * NC + k, (x + 3) % 4 * NC + 1 - k) for x, k in places]
     )
-    w_core = lax.ppermute(w_core, "c", shift(NC, 1))
     groups = live_tiles(frame_mask)
 
     slots = lax.all_to_all(slots, ("xh", "z"), 0, 0, tiled=True)
-    slots, w_here, groups = lax.optimization_barrier((slots, w_here, groups))
-    slots, kv = lax.optimization_barrier((slots, slots[:, HALF:]))
-    before = lax.ppermute(kv, "y", shift(NY, 1))
-    after = lax.ppermute(kv, "y", shift(NY, -1))
+    slots, w_here, w_core, groups = lax.optimization_barrier((slots, w_here, w_core, groups))
+    low, high = slots[: ROWS // 2, HALF:], slots[ROWS // 2 :, HALF:]
+    slots, low, high = lax.optimization_barrier((slots, low, high))
+    before_low = lax.ppermute(low, "y", shift(NY, 1))
+    after_high = lax.ppermute(high, "y", shift(NY, -1))
     query = slots[:, :HALF]
     query = (query, lax.ppermute(query, "c", shift(NC, 1)))
-    state = attend(groups[0], query, [kv], None, False)
-    before, after, state = lax.optimization_barrier((before, after, state))
-    low = lax.ppermute(before[: ROWS // 2], "y", shift(NY, 1))
-    high = lax.ppermute(after[ROWS // 2 :], "y", shift(NY, -1))
-    state = attend(groups[1], query, [before, after], state, False)
-    low, high, w_next, w_last, w_core = lax.optimization_barrier(
-        (low, high, w_next, w_last, w_core)
-    )
-    here, sent = attend(groups[2], query, [low, high], state, True)
+    before_high = lax.ppermute(high, "y", shift(NY, 1))
+    after_low = lax.ppermute(low, "y", shift(NY, -1))
+    state = attend(groups[0], query, [low, high], None, False)
+    before_low, after_high, state = lax.optimization_barrier((before_low, after_high, state))
+    far_low = lax.ppermute(before_low, "y", shift(NY, 1))
+    far_high = lax.ppermute(after_high, "y", shift(NY, -1))
+    state = attend(
+        groups[1], query, [before_low, before_high, after_low, after_high], state, False
+    )
+    here, sent = attend(groups[2], query, [far_low, far_high], state, True)
     there = lax.ppermute(sent, "c", shift(NC, 1))
+    there, w_next, w_last = lax.optimization_barrier((there, w_next, w_last))
     rows = lax.all_to_all(merge(here, there), ("xh", "z"), 0, 0, tiled=True)
+    rows = rows.reshape(XH, NZ, HALF, HEAD_DIM)[:, :HEADS]
+    rows = rows.reshape(XH * HEADS, HALF, HEAD_DIM)
     rows_xl = lax.ppermute(rows, "xl", shift(XL, 1))
     rows_core = lax.ppermute(rows, "c", shift(NC, 1))
-    near = project(rows, rows_core, w_here, w_core, None)
+    near, w_next, w_last = project(rows, rows_core, w_here, w_core, None, (w_next, w_last))
     rows_xl, near = lax.optimization_barrier((rows_xl, near))
     rows_both = lax.ppermute(rows_xl, "c", shift(NC, 1))
-    return project(rows_xl, rows_both, w_next, w_last, near)
+    return project(rows_xl, rows_both, w_next, w_last, near)[0]
 
 
 def solution(mesh):

time: 121 us -> 103 us (0.85)
  Pallas kernels: 43 us -> 27.6 us
  waiting for transfers between devices: 24.6 us -> 17.3 us
  starting transfers between devices: 30 us -> 33.7 us
  local copies, waits for them, and re-layouts: 8.11 us -> 9.95 us
    pallas_call x1, Pallas kernels: 16.3 us -> 1.91 us  [split(): pl.pallas_call(split_kernel, out_shape=(jax.ShapeDtypeStruct((ROWS, 3 * H...]
    ppermute x5 -> x7, waiting for transfers between devices: 10.1 us -> 5.54 us  [the longest x1 5.06 us: local(): before_low = lax.ppermute(low, 'y', shift(NY, 1))]
    ppermute x5 -> x7, starting transfers between devices: 5.5 us -> 8.37 us  [the longest x1 2.34 us: local(): far_high = lax.ppermute(after_high, 'y', shift(NY, -1))]
    ppermute x1, waiting for transfers between devices: 4.59 us -> 2.28 us  [local(): rows_xl = lax.ppermute(rows, 'xl', shift(XL, 1))]
    dynamic_slice x1 -> x2, local copies, waits for them, and re-layouts: 5.29 us -> 7.15 us  [w_columns(): lax.dynamic_slice(w, (0, (to_xl * NC + to_c) * width), (w.shape[0], width))]
    ppermute x1, waiting for transfers between devices: 1.35 us -> 0.01 us  [local(): got = lax.ppermute(sent, 'c', shift(NC, 1))]
  transfers between devices with their start and end apart: 14 -> 16, of which waited for: 8 -> 7; matrix products, arithmetic and copies ran while one was open for 6% -> 10% of each run, Pallas kernels for 16% -> 23%
where the time goes in v6:
time: 103 us
  starting transfers between devices  33.7 us (33%)
  Pallas kernels  27.6 us (27%)
  waiting for transfers between devices  17.3 us (17%)
  blocking collectives  14.5 us (14%)
  local copies, waits for them, and re-layouts  9.95 us (10%)
    all_to_all x1, blocking collectives, local(): rows = lax.all_to_all(merge(here, there), ('xh', 'z'), 0, 0, tiled=True)  14.5 us
    pallas_call x3, Pallas kernels, attend(): pl.pallas_call(kernel, out_shape=(parcel, parcel) if last else (whole, wh...  14.3 us
    all_to_all x1, starting transfers between devices, local(): slots = lax.all_to_all(slots, ('xh', 'z'), 0, 0, tiled=True)  9.06 us
    dynamic_slice x2, local copies, waits for them, and re-layouts, w_columns(): lax.dynamic_slice(w, (0, (to_xl * NC + to_c) * width), (w.shape[0], width))  7.15 us
    pallas_call x1, Pallas kernels, live_tiles(): pl.pallas_call(tiles_kernel, out_shape=tuple(out_shape), in_specs=in_smem...  6.81 us
    all_to_all x1, waiting for transfers between devices, local(): slots = lax.all_to_all(slots, ('xh', 'z'), 0, 0, tiled=True)  6.13 us
    ppermute x1, waiting for transfers between devices, local(): before_low = lax.ppermute(low, 'y', shift(NY, 1))  5.06 us
    pallas_call x2, Pallas kernels, project(): pl.pallas_call(kernel, out_shape=(out,) + tuple((jax.ShapeDtypeStruct(x.s...  3.94 us
  transfers between devices with their start and end apart: 16, of which 7 were waited for; matrix products, arithmetic and copies ran while one was open for 10% of the time, Pallas kernels for 23%

profile of v6, /device:TPU:1, one launch (start us, length us, event | category | flops | bytes accessed | tf_op | source)
XLA Modules:
  0.0 103.3 jit_solution(14475593512897028223)
XLA Ops:
  0.0 1.9 %shard_map.55 = (bf16[16,192,128]{2,1,0:T(8,128)(2,1)}, bf16[5,192,128]{2,1,0:T(8,128)(2,1)}) custom-call(bf16[128,640]{1,0:T(8,128)(2,1)} %q_hbm.1, bf16[128,640]{1,0:T(8,128)(2,1)} %k_hbm.1, bf16[128,640]{1,0:T(8,128)(2,1)} %v_hbm.1), custom_call_target="tpu_custom_call" | custom-call | tf_op jit(solution)/shard_map/pallas_call | solution.py:62
  1.9 3.4 %collective-permute-start = (bf16[5,192,128]{2,1,0:T(8,128)(2,1)}, bf16[5,192,128]{2,1,0:T(8,128)(2,1)S(1)}, u32[]{:S(2)}, u32[]{:S(2)}) collective-permute-start(bf16[5,192,128]{2,1,0:T(8,128)(2,1)} %get-tuple-element.68), channel_id=1, source_target_pairs={{0,1},{1,0},{2,3},{3,2},{4,5},{5,4},{6,7},{7,6},{8,9},{9,8},{10,11... | collective-permute-start | bytes 737288 | tf_op jit(solution)/shard_map/ppermute | solution.py:359
  5.3 2.7 %constant_dynamic-slice_fusion = bf16[640,1280]{1,0:T(8,128)(2,1)} fusion(bf16[640,5120]{1,0:T(8,128)(2,1)} %param.9, s32[]{:T(128)S(6)} %select_n.19), kind=kLoop, calls=%fused_computation | loop fusion | bytes 3276804 | tf_op jit(solution)/shard_map/dynamic_slice | solution.py:355
  8.8 9.1 %all-to-all-start = ((bf16[16,192,128]{2,1,0:T(8,128)(2,1)}), bf16[16,192,128]{2,1,0:T(8,128)(2,1)}, u32[]{:S(2)}, u32[]{:S(2)}) async-start(bf16[16,192,128]{2,1,0:T(8,128)(2,1)} %constant_dynamic-update-slice_fusion), calls=%async_computation | async-start | bytes 1572864 | tf_op jit(solution)/shard_map/all_to_all | solution.py:381
  17.9 4.4 %constant_dynamic-slice_fusion.1 = (bf16[640,1280]{1,0:T(8,128)(2,1)}, bf16[640,1280]{1,0:T(8,128)(2,1)}, bf16[640,1280]{1,0:T(8,128)(2,1)S(1)}) fusion(bf16[640,5120]{1,0:T(8,128)(2,1)} %param.9, s32[]{:T(128)S(6)} %select_n.18, s32[]{:T(128)S(6)} %select_n.17, s32[]{:T(128)S(6)} %select_n.16), kind=kLoop, calls=%fused_computation.1 | loop fusion | bytes 9830412 | tf_op jit(solution)/shard_map/dynamic_slice | solution.py:355
  22.6 3.3 %collective-permute-start.11 = (bf16[640,1280]{1,0:T(8,128)(2,1)}, bf16[640,1280]{1,0:T(8,128)(2,1)}, u32[]{:S(2)}, u32[]{:S(2)}) collective-permute-start(bf16[640,1280]{1,0:T(8,128)(2,1)} %get-tuple-element.116), channel_id=1, source_target_pairs={{0,131},{1,130},{2,1},{3,0},{128,3},{129,2},{130,129},{131,128},{4... | collective-permute-start | bytes 4915208 | tf_op jit(solution)/shard_map/ppermute | solution.py:376
  25.9 6.8 %shard_map.56 = (s32[1]{0:T(128)}, s32[256]{0:T(256)S(1)}, s32[512]{0:T(512)S(1)}, s32[256]{0:T(256)S(1)}, s32[1]{0:T(128)}, /*index=5*/s32[384]{0:T(512)S(1)}, ...) custom-call(s32[64,64]{1,0:T(8,128)S(1)} %copy-done), custom_call_target="tpu_custom_call" | custom-call | flops 1000000 | bytes 100000 | tf_op jit(solution)/shard_map/pallas_call | solution.py:338
  32.7 6.1 %all-to-all-done = bf16[16,192,128]{2,1,0:T(8,128)(2,1)} async-done(((bf16[16,192,128]{2,1,0:T(8,128)(2,1)}), bf16[16,192,128]{2,1,0:T(8,128)(2,1)}, u32[]{:S(2)}, u32[]{:S(2)}) %all-to-all-start) | async-done | bytes 786464 | tf_op jit(solution)/shard_map/all_to_all | solution.py:381
  40.9 3.0 %collective-permute-start.2 = (bf16[16,64,128]{2,1,0:T(8,128)(2,1)S(1)}, bf16[16,64,128]{2,1,0:T(8,128)(2,1)S(1)}, u32[]{:S(2)}, u32[]{:S(2)}) collective-permute-start(bf16[16,64,128]{2,1,0:T(8,128)(2,1)S(1)} %slice.14.own_ref), channel_id=1, source_target_pairs={{0,1},{1,0},{2,3},{3,2},{4,5},{5,4},{6,7},{7,6},{8,9},{9,8},{10,11... | collective-permute-start | bytes 786440 | tf_op jit(solution)/shard_map/ppermute | solution.py:388
  45.2 1.4 %collective-permute-start.4 = (bf16[8,128,128]{2,1,0:T(8,128)(2,1)S(1)}, bf16[8,128,128]{2,1,0:T(8,128)(2,1)S(1)}, u32[]{:S(2)}, u32[]{:S(2)}) collective-permute-start(bf16[8,128,128]{2,1,0:T(8,128)(2,1)S(1)} %get-tuple-element.93.refs_1_), channel_id=1, source_target_pairs={{0,12},{4,0},{8,4},{12,8},{1,13},{5,1},{9,5},{13,9},{2,14},{6,2},{... | collective-permute-start | bytes 786440 | tf_op jit(solution)/shard_map/ppermute | solution.py:386
  46.6 1.5 %collective-permute-start.8 = (bf16[8,128,128]{2,1,0:T(8,128)(2,1)S(1)}, bf16[8,128,128]{2,1,0:T(8,128)(2,1)S(1)}, u32[]{:S(2)}, u32[]{:S(2)}) collective-permute-start(bf16[8,128,128]{2,1,0:T(8,128)(2,1)S(1)} %get-tuple-element.92.refs_0_), channel_id=1, source_target_pairs={{0,12},{4,0},{8,4},{12,8},{1,13},{5,1},{9,5},{13,9},{2,14},{6,2},{... | collective-permute-start | bytes 786440 | tf_op jit(solution)/shard_map/ppermute | solution.py:390
  48.1 5.1 %collective-permute-done.3.refs_0_ = bf16[8,128,128]{2,1,0:T(8,128)(2,1)S(1)} collective-permute-done((bf16[8,128,128]{2,1,0:T(8,128)(2,1)S(1)}, bf16[8,128,128]{2,1,0:T(8,128)(2,1)S(1)}, u32[]{:S(2)}, u32[]{:S(2)}) %collective-permute-start.3) | collective-permute-done | bytes 262176 | tf_op jit(solution)/shard_map/ppermute | solution.py:385
  53.1 3.8 %shard_map.57 = (f32[16,128,128]{2,1,0:T(8,128)S(1)}, f32[16,128,128]{2,1,0:T(8,128)S(1)}, f32[16,128,128]{2,1,0:T(8,128)S(1)}) custom-call(s32[1]{0:T(128)} %get-tuple-element.94.count_ref, s32[256]{0:T(256)S(1)} %get-tuple-element.95.block_ref, s32[512]{0:T(512)S(1)} %get-tuple-element.96.slot_ref, s32[256]{0:T(256)S(1)} %get-tuple-element.97.live_ref, ...), custom_call_target="tpu_custom_call" | custom-call | flops 335544320 | bytes 6291456 | tf_op jit(solution)/shard_map/pallas_call | solution.py:194
  57.0 1.8 %collective-permute-start.5 = (bf16[8,128,128]{2,1,0:T(8,128)(2,1)S(1)}, bf16[8,128,128]{2,1,0:T(8,128)(2,1)S(1)}, u32[]{:S(2)}, u32[]{:S(2)}) collective-permute-start(bf16[8,128,128]{2,1,0:T(8,128)(2,1)S(1)} %collective-permute-done.3.refs_0_), channel_id=1, source_target_pairs={{0,4},{4,8},{8,12},{12,0},{1,5},{5,9},{9,13},{13,1},{2,6},{6,10},{... | collective-permute-start | bytes 786440 | tf_op jit(solution)/shard_map/ppermute | solution.py:393
  58.8 2.3 %collective-permute-start.6 = (bf16[8,128,128]{2,1,0:T(8,128)(2,1)S(1)}, bf16[8,128,128]{2,1,0:T(8,128)(2,1)S(1)}, u32[]{:S(2)}, u32[]{:S(2)}) collective-permute-start(bf16[8,128,128]{2,1,0:T(8,128)(2,1)S(1)} %collective-permute-done.4.refs_3_), channel_id=1, source_target_pairs={{0,12},{4,0},{8,4},{12,8},{1,13},{5,1},{9,5},{13,9},{2,14},{6,2},{... | collective-permute-start | bytes 786440 | tf_op jit(solution)/shard_map/ppermute | solution.py:394
  61.6 6.3 %shard_map.58 = (f32[16,128,128]{2,1,0:T(8,128)S(1)}, f32[16,128,128]{2,1,0:T(8,128)S(1)}, f32[16,128,128]{2,1,0:T(8,128)S(1)}) custom-call(s32[1]{0:T(128)} %get-tuple-element.103.count_ref, s32[384]{0:T(512)S(1)} %get-tuple-element.104.block_ref, s32[768]{0:T(1024)S(1)} %get-tuple-element.105.slot_ref, s32[384]{0:T(512)S(1)} %get-tuple-element.106.live_ref, ...), custom_call_target="tpu_custom_call" | custom-call | flops 671088640 | bytes 6291456 | tf_op jit(solution)/shard_map/pallas_call | solution.py:194
  67.9 4.2 %shard_map.59 = (f32[17,64,128]{2,1,0:T(8,128)S(1)}, f32[17,64,128]{2,1,0:T(8,128)S(1)}) custom-call(s32[1]{0:T(128)} %get-tuple-element.86.count_ref, s32[256]{0:T(256)S(1)} %get-tuple-element.87.block_ref, s32[512]{0:T(512)S(1)} %get-tuple-element.88.slot_ref, s32[256]{0:T(256)S(1)} %get-tuple-element.89.live_ref, bf16[16,64,128]{2,1,0:T(8,128)(2,1)S(1)} %slice.14.own_ref, ...), custom_call_target="tpu_custom_call" | custom-call | flops 335544320 | bytes 6291456 | tf_op jit(solution)/shard_map/pallas_call | solution.py:194
  72.1 2.9 %collective-permute-start.9 = (f32[17,64,128]{2,1,0:T(8,128)S(1)}, f32[17,64,128]{2,1,0:T(8,128)S(1)}, u32[]{:S(2)}, u32[]{:S(2)}) collective-permute-start(f32[17,64,128]{2,1,0:T(8,128)S(1)} %get-tuple-element.114), channel_id=1, source_target_pairs={{0,1},{1,0},{2,3},{3,2},{4,5},{5,4},{6,7},{7,6},{8,9},{9,8},{10,11... | collective-permute-start | bytes 1671176 | tf_op jit(solution)/shard_map/ppermute | solution.py:399
  75.1 1.6 %collective-permute-done.9.there_ref = f32[17,64,128]{2,1,0:T(8,128)S(1)} collective-permute-done((f32[17,64,128]{2,1,0:T(8,128)S(1)}, f32[17,64,128]{2,1,0:T(8,128)S(1)}, u32[]{:S(2)}, u32[]{:S(2)}) %collective-permute-start.9) | collective-permute-done | bytes 557088 | tf_op jit(solution)/shard_map/ppermute | solution.py:399
  77.2 14.5 %all_to_all.10 = bf16[16,64,128]{2,1,0:T(8,128)(2,1)S(1)} all-to-all(bf16[16,64,128]{2,1,0:T(8,128)(2,1)S(1)} %shard_map.60), channel_id=1, replica_groups=mesh['xh'=2,'z'=8,'y'=4,'xl'=2,'c'=2] {'xh','z'}, dimensions={0} | all-to-all | bytes 524288 | tf_op jit(solution)/shard_map/all_to_all | solution.py:401
  91.7 2.3 %collective-permute-start.13 = (bf16[10,64,128]{2,1,0:T(8,128)(2,1)S(1)}, bf16[10,64,128]{2,1,0:T(8,128)(2,1)S(1)}, u32[]{:S(2)}, u32[]{:S(2)}) collective-permute-start(bf16[10,64,128]{2,1,0:T(8,128)(2,1)S(1)} %bitcast.2), channel_id=1, source_target_pairs={{0,1},{1,0},{2,3},{3,2},{4,5},{5,4},{6,7},{7,6},{8,9},{9,8},{10,11... | collective-permute-start | bytes 491528 | tf_op jit(solution)/shard_map/ppermute | solution.py:405
  95.0 2.4 %shard_map.61 = (f32[128,1280]{1,0:T(8,128)S(1)}, bf16[640,1280]{1,0:T(8,128)(2,1)S(1)}, bf16[640,1280]{1,0:T(8,128)(2,1)S(1)}) custom-call(bf16[10,64,128]{2,1,0:T(8,128)(2,1)S(1)} %bitcast.4, bf16[10,64,128]{2,1,0:T(8,128)(2,1)S(1)} %collective-permute-done.13.b_ref, bf16[640,1280]{1,0:T(8,128)(2,1)S(1)} %get-tuple-element.118.w_ref, ...), custom_call_target="tpu_custom_call" | custom-call | flops 419430400 | bytes 4194304 | tf_op jit(solution)/shard_map/pallas_call | solution.py:272
  97.5 2.3 %collective-permute-done.12.a_ref = bf16[10,64,128]{2,1,0:T(8,128)(2,1)S(1)} collective-permute-done((bf16[10,64,128]{2,1,0:T(8,128)(2,1)S(1)}, bf16[10,64,128]{2,1,0:T(8,128)(2,1)S(1)}, u32[]{:S(2)}, u32[]{:S(2)}) %collective-permute-start.12) | collective-permute-done | bytes 163872 | tf_op jit(solution)/shard_map/ppermute | solution.py:404
  101.7 1.5 %shard_map.62 = bf16[128,1280]{1,0:T(8,128)(2,1)} custom-call(bf16[10,64,128]{2,1,0:T(8,128)(2,1)S(1)} %collective-permute-done.12.a_ref, bf16[10,64,128]{2,1,0:T(8,128)(2,1)S(1)} %collective-permute-done.14.b_ref, bf16[640,1280]{1,0:T(8,128)(2,1)S(1)} %get-tuple-element.124.w_ref, bf16[640,1280]{1,0:T(8,128)(2,1)S(1)} %get-tuple-element.125.w2_ref, ...), custom_call_target="tpu_custom_call" | custom-call | flops 419430400 | bytes 4194304 | tf_op jit(solution)/shard_map/pallas_call | solution.py:272
  (25 shorter events, 8.5 us)
Async XLA Ops:
  1.9 6.1 %collective-permute-start = (bf16[5,192,128]{2,1,0:T(8,128)(2,1)}, bf16[5,192,128]{2,1,0:T(8,128)(2,1)S(1)}, u32[]{:S(2)}, u32[]{:S(2)}) collective-permute-start(bf16[5,192,128]{2,1,0:T(8,128)(2,1)} %get-tuple-element.68), channel_id=1, source_target_pairs={{0,1},{1,0},{2,3},{3,2},{4,5},{5,4},{6,7},{7,6},{8,9},{9,8},{10,11... | collective-permute-start | bytes 737288 | tf_op jit(solution)/shard_map/ppermute | solution.py:359
  8.0 24.7 %collective-permute-start.1 = (bf16[640,1280]{1,0:T(8,128)(2,1)}, bf16[640,1280]{1,0:T(8,128)(2,1)S(1)}, u32[]{:S(2)}, u32[]{:S(2)}) collective-permute-start(bf16[640,1280]{1,0:T(8,128)(2,1)} %constant_dynamic-slice_fusion), channel_id=1, source_target_pairs={{0,1},{1,0},{2,3},{3,2},{4,5},{5,4},{6,7},{7,6},{8,9},{9,8},{10,11... | collective-permute-start | bytes 4915208 | tf_op jit(solution)/shard_map/ppermute | solution.py:360
  8.8 30.1 %all-to-all-start = ((bf16[16,192,128]{2,1,0:T(8,128)(2,1)}), bf16[16,192,128]{2,1,0:T(8,128)(2,1)}, u32[]{:S(2)}, u32[]{:S(2)}) async-start(bf16[16,192,128]{2,1,0:T(8,128)(2,1)} %constant_dynamic-update-slice_fusion), calls=%async_computation | async-start | bytes 1572864 | tf_op jit(solution)/shard_map/all_to_all | solution.py:381
  17.9 8.0 %copy-start = (s32[64,64]{1,0:T(8,128)S(1)}, s32[64,64]{1,0:T(8,128)}, u32[]{:S(2)}) copy-start(s32[64,64]{1,0:T(8,128)} %mask_ref) | copy-start | bytes 49156
  22.3 52.8 %collective-permute-start.10 = (bf16[640,1280]{1,0:T(8,128)(2,1)}, bf16[640,1280]{1,0:T(8,128)(2,1)}, u32[]{:S(2)}, u32[]{:S(2)}) collective-permute-start(bf16[640,1280]{1,0:T(8,128)(2,1)} %get-tuple-element.115), channel_id=1, source_target_pairs={{0,2},{1,3},{2,128},{3,129},{128,130},{129,131},{130,0},{131,1},{4... | collective-permute-start | bytes 4915208 | tf_op jit(solution)/shard_map/ppermute | solution.py:373
  22.6 52.5 %collective-permute-start.11 = (bf16[640,1280]{1,0:T(8,128)(2,1)}, bf16[640,1280]{1,0:T(8,128)(2,1)}, u32[]{:S(2)}, u32[]{:S(2)}) collective-permute-start(bf16[640,1280]{1,0:T(8,128)(2,1)} %get-tuple-element.116), channel_id=1, source_target_pairs={{0,131},{1,130},{2,1},{3,0},{128,3},{129,2},{130,129},{131,128},{4... | collective-permute-start | bytes 4915208 | tf_op jit(solution)/shard_map/ppermute | solution.py:376
  40.9 5.7 %collective-permute-start.2 = (bf16[16,64,128]{2,1,0:T(8,128)(2,1)S(1)}, bf16[16,64,128]{2,1,0:T(8,128)(2,1)S(1)}, u32[]{:S(2)}, u32[]{:S(2)}) collective-permute-start(bf16[16,64,128]{2,1,0:T(8,128)(2,1)S(1)} %slice.14.own_ref), channel_id=1, source_target_pairs={{0,1},{1,0},{2,3},{3,2},{4,5},{5,4},{6,7},{7,6},{8,9},{9,8},{10,11... | collective-permute-start | bytes 786440 | tf_op jit(solution)/shard_map/ppermute | solution.py:388
  43.9 9.3 %collective-permute-start.3 = (bf16[8,128,128]{2,1,0:T(8,128)(2,1)S(1)}, bf16[8,128,128]{2,1,0:T(8,128)(2,1)S(1)}, u32[]{:S(2)}, u32[]{:S(2)}) collective-permute-start(bf16[8,128,128]{2,1,0:T(8,128)(2,1)S(1)} %get-tuple-element.92.refs_0_), channel_id=1, source_target_pairs={{0,4},{4,8},{8,12},{12,0},{1,5},{5,9},{9,13},{13,1},{2,6},{6,10},{... | collective-permute-start | bytes 786440 | tf_op jit(solution)/shard_map/ppermute | solution.py:385
  45.2 11.8 %collective-permute-start.4 = (bf16[8,128,128]{2,1,0:T(8,128)(2,1)S(1)}, bf16[8,128,128]{2,1,0:T(8,128)(2,1)S(1)}, u32[]{:S(2)}, u32[]{:S(2)}) collective-permute-start(bf16[8,128,128]{2,1,0:T(8,128)(2,1)S(1)} %get-tuple-element.93.refs_1_), channel_id=1, source_target_pairs={{0,12},{4,0},{8,4},{12,8},{1,13},{5,1},{9,5},{13,9},{2,14},{6,2},{... | collective-permute-start | bytes 786440 | tf_op jit(solution)/shard_map/ppermute | solution.py:386
  46.6 12.2 %collective-permute-start.8 = (bf16[8,128,128]{2,1,0:T(8,128)(2,1)S(1)}, bf16[8,128,128]{2,1,0:T(8,128)(2,1)S(1)}, u32[]{:S(2)}, u32[]{:S(2)}) collective-permute-start(bf16[8,128,128]{2,1,0:T(8,128)(2,1)S(1)} %get-tuple-element.92.refs_0_), channel_id=1, source_target_pairs={{0,12},{4,0},{8,4},{12,8},{1,13},{5,1},{9,5},{13,9},{2,14},{6,2},{... | collective-permute-start | bytes 786440 | tf_op jit(solution)/shard_map/ppermute | solution.py:390
  53.1 8.4 %collective-permute-start.7 = (bf16[8,128,128]{2,1,0:T(8,128)(2,1)S(1)}, bf16[8,128,128]{2,1,0:T(8,128)(2,1)S(1)}, u32[]{:S(2)}, u32[]{:S(2)}) collective-permute-start(bf16[8,128,128]{2,1,0:T(8,128)(2,1)S(1)} %get-tuple-element.93.refs_1_), channel_id=1, source_target_pairs={{0,4},{4,8},{8,12},{12,0},{1,5},{5,9},{9,13},{13,1},{2,6},{6,10},{... | collective-permute-start | bytes 786440 | tf_op jit(solution)/shard_map/ppermute | solution.py:389
  57.0 10.9 %collective-permute-start.5 = (bf16[8,128,128]{2,1,0:T(8,128)(2,1)S(1)}, bf16[8,128,128]{2,1,0:T(8,128)(2,1)S(1)}, u32[]{:S(2)}, u32[]{:S(2)}) collective-permute-start(bf16[8,128,128]{2,1,0:T(8,128)(2,1)S(1)} %collective-permute-done.3.refs_0_), channel_id=1, source_target_pairs={{0,4},{4,8},{8,12},{12,0},{1,5},{5,9},{9,13},{13,1},{2,6},{6,10},{... | collective-permute-start | bytes 786440 | tf_op jit(solution)/shard_map/ppermute | solution.py:393
  58.8 9.1 %collective-permute-start.6 = (bf16[8,128,128]{2,1,0:T(8,128)(2,1)S(1)}, bf16[8,128,128]{2,1,0:T(8,128)(2,1)S(1)}, u32[]{:S(2)}, u32[]{:S(2)}) collective-permute-start(bf16[8,128,128]{2,1,0:T(8,128)(2,1)S(1)} %collective-permute-done.4.refs_3_), channel_id=1, source_target_pairs={{0,12},{4,0},{8,4},{12,8},{1,13},{5,1},{9,5},{13,9},{2,14},{6,2},{... | collective-permute-start | bytes 786440 | tf_op jit(solution)/shard_map/ppermute | solution.py:394
  72.1 4.5 %collective-permute-start.9 = (f32[17,64,128]{2,1,0:T(8,128)S(1)}, f32[17,64,128]{2,1,0:T(8,128)S(1)}, u32[]{:S(2)}, u32[]{:S(2)}) collective-permute-start(f32[17,64,128]{2,1,0:T(8,128)S(1)} %get-tuple-element.114), channel_id=1, source_target_pairs={{0,1},{1,0},{2,3},{3,2},{4,5},{5,4},{6,7},{7,6},{8,9},{9,8},{10,11... | collective-permute-start | bytes 1671176 | tf_op jit(solution)/shard_map/ppermute | solution.py:399
  91.7 3.3 %collective-permute-start.13 = (bf16[10,64,128]{2,1,0:T(8,128)(2,1)S(1)}, bf16[10,64,128]{2,1,0:T(8,128)(2,1)S(1)}, u32[]{:S(2)}, u32[]{:S(2)}) collective-permute-start(bf16[10,64,128]{2,1,0:T(8,128)(2,1)S(1)} %bitcast.2), channel_id=1, source_target_pairs={{0,1},{1,0},{2,3},{3,2},{4,5},{5,4},{6,7},{7,6},{8,9},{9,8},{10,11... | collective-permute-start | bytes 491528 | tf_op jit(solution)/shard_map/ppermute | solution.py:405
  94.0 5.8 %collective-permute-start.12 = (bf16[10,64,128]{2,1,0:T(8,128)(2,1)S(1)}, bf16[10,64,128]{2,1,0:T(8,128)(2,1)S(1)}, u32[]{:S(2)}, u32[]{:S(2)}) collective-permute-start(bf16[10,64,128]{2,1,0:T(8,128)(2,1)S(1)} %bitcast.3), channel_id=1, source_target_pairs={{0,2},{2,0},{1,3},{3,1},{4,6},{6,4},{5,7},{7,5},{8,10},{10,8},{9,1... | collective-permute-start | bytes 491528 | tf_op jit(solution)/shard_map/ppermute | solution.py:404
  99.8 1.9 %collective-permute-start.14 = (bf16[10,64,128]{2,1,0:T(8,128)(2,1)S(1)}, bf16[10,64,128]{2,1,0:T(8,128)(2,1)S(1)}, u32[]{:S(2)}, u32[]{:S(2)}) collective-permute-start(bf16[10,64,128]{2,1,0:T(8,128)(2,1)S(1)} %collective-permute-done.12.a_ref), channel_id=1, source_target_pairs={{0,1},{1,0},{2,3},{3,2},{4,5},{5,4},{6,7},{7,6},{8,9},{9,8},{10,11... | collective-permute-start | bytes 491528 | tf_op jit(solution)/shard_map/ppermute | solution.py:408

commit v7 on v6

--- a/solution.py
+++ b/solution.py
@@ -31,10 +31,13 @@
     return [pl.BlockSpec(memory_space=pltpu.SMEM)] * count
 
 
-def split_kernel(q_hbm, k_hbm, v_hbm, keep_hbm, send_hbm, whole_ref, keep_ref, send_ref, sems):
-    core = lax.axis_index("c")
-    mine = pl.ds(pl.multiple_of(core * HALF, HALF), HALF)
-    other = pl.ds(pl.multiple_of((1 - core) * HALF, HALF), HALF)
+def swap_planes(x):
+    pairs = [((0, 0), (0, 0)), ((1, 1), (1, 1)), ((0, 1), (1, 0)), ((1, 0), (0, 1))]
+    return lax.ppermute(x, ("xh", "c"), [(a * NC + b, d * NC + e) for (a, b), (d, e) in pairs])
+
+
+def split_kernel(q_hbm, k_hbm, v_hbm, out_hbm, slots_hbm, whole_ref, out_ref, sems):
+    del slots_hbm
     loads = [
         pltpu.make_async_copy(source, whole_ref.at[t], sems.at[t])
         for t, source in enumerate((q_hbm, k_hbm, v_hbm))
@@ -43,58 +46,48 @@
         load.start()
     for t, load in enumerate(loads):
         load.wait()
-        rows = slice(t * HALF, (t + 1) * HALF)
         for head in range(HEADS):
             lanes = slice(head * HEAD_DIM, (head + 1) * HEAD_DIM)
-            send_ref[head, rows, :] = whole_ref[t, other, lanes]
-            keep_ref[head, rows, :] = whole_ref[t, mine, lanes]
-    send = pltpu.make_async_copy(send_ref, send_hbm, sems.at[3])
-    keep = pltpu.make_async_copy(keep_ref, keep_hbm.at[pl.ds(core * NZ, HEADS)], sems.at[4])
-    send.start()
-    keep.start()
-    send.wait()
-    keep.wait()
+            out_ref[head, t * BLOCK : (t + 1) * BLOCK, :] = whole_ref[t, :, lanes]
+    out = pltpu.make_async_copy(out_ref, out_hbm, sems.at[3])
+    out.start()
+    out.wait()
 
 
 def split(queries, keys, values):
     anywhere = pl.BlockSpec(memory_space=pl.ANY)
-    part = (HEADS, 3 * HALF, HEAD_DIM)
+    part = (HEADS, 3 * BLOCK, HEAD_DIM)
     return pl.pallas_call(
         split_kernel,
         out_shape=(
-            jax.ShapeDtypeStruct((ROWS, 3 * HALF, HEAD_DIM), jnp.bfloat16),
             jax.ShapeDtypeStruct(part, jnp.bfloat16),
+            jax.ShapeDtypeStruct((NZ,) + part[1:], jnp.bfloat16),
         ),
         in_specs=[anywhere] * 3,
         out_specs=(anywhere,) * 2,
         scratch_shapes=[
             pltpu.VMEM((3,) + queries.shape, jnp.bfloat16),
             pltpu.VMEM(part, jnp.bfloat16),
-            pltpu.VMEM(part, jnp.bfloat16),
-            pltpu.SemaphoreType.DMA((5,)),
+            pltpu.SemaphoreType.DMA((4,)),
         ],
         compiler_params=pltpu.CompilerParams(vmem_limit_bytes=56 * MIB),
     )(queries, keys, values)
 
 
-def score_tiles(steps, tables, q_ref, kv_ref, s_ref, top_ref):
-    block_ref, slot_ref, live_ref = tables
-    lane = lax.broadcasted_iota(jnp.int32, (BLOCK, BLOCK), 1)
+def score_tiles(count, tables, q_ref, kv_ref, s_ref, top_ref):
+    block_ref, slot_ref = tables
 
     def score(step, carry):
         tiles = []
         for u in range(UNROLL):
             e = step * UNROLL + u
-            key = jnp.concatenate(
-                [kv_ref[slot_ref[2 * e], :HALF, :], kv_ref[slot_ref[2 * e + 1], :HALF, :]], axis=0
-            )
             s = lax.dot_general(
                 q_ref[block_ref[e]],
-                key,
+                kv_ref[slot_ref[e], :BLOCK, :],
                 (((1,), (1,)), ((), ())),
                 preferred_element_type=jnp.float32,
             )
-            s = jnp.where(lane < live_ref[e], s, LOW)
+            s = jnp.where(e < count, s, LOW)
             s_ref[e] = s
             tiles.append(s)
         for u in range(UNROLL):
@@ -102,23 +95,24 @@
             top_ref[block] = jnp.maximum(top_ref[block], tiles[u])
         return carry
 
-    lax.fori_loop(0, steps, score, 0)
-
-
-def mix_tiles(steps, tables, kv_ref, s_ref, m_ref, l_ref, a_ref):
-    block_ref, slot_ref, live_ref = tables
+    lax.fori_loop(0, (count + (UNROLL - 1)) // UNROLL, score, 0)
+
+
+def mix_tiles(count, tables, kv_ref, s_ref, m_ref, l_ref, a_ref):
+    block_ref, slot_ref = tables
 
     def mix(step, carry):
         weights, products = [], []
         for u in range(UNROLL):
             e = step * UNROLL + u
-            value = jnp.concatenate(
-                [kv_ref[slot_ref[2 * e], HALF:, :], kv_ref[slot_ref[2 * e + 1], HALF:, :]], axis=0
-            )
             weight = jnp.exp2((s_ref[e] - m_ref[block_ref[e]]) * EXP2_SCALE)
             weights.append(weight)
             products.append(
-                jnp.dot(weight.astype(jnp.bfloat16), value, preferred_element_type=jnp.float32)
+                jnp.dot(
+                    weight.astype(jnp.bfloat16),
+                    kv_ref[slot_ref[e], BLOCK:, :],
+                    preferred_element_type=jnp.float32,
+                )
             )
         for u in range(UNROLL):
             block = block_ref[step * UNROLL + u]
@@ -126,47 +120,52 @@
             a_ref[block] = a_ref[block] + products[u]
         return carry
 
-    lax.fori_loop(0, steps, mix, 0)
-
-
-def write_parcels(m_ref, l_ref, a_ref, keep_ref, send_ref):
+    lax.fori_loop(0, (count + (UNROLL - 1)) // UNROLL, mix, 0)
+
+
+def write_parcels(m_ref, l_ref, a_ref, stats_ref, keep_ref, send_ref):
+    core = lax.axis_index("c")
+    mine = pl.ds(pl.multiple_of(core * HALF, HALF), HALF)
+    other = pl.ds(pl.multiple_of((1 - core) * HALF, HALF), HALF)
     lane = lax.broadcasted_iota(jnp.int32, (BLOCK, BLOCK), 1)
     stats = jnp.zeros((BLOCK, BLOCK), jnp.float32)
     for block in range(ROWS):
         total = jnp.sum(l_ref[block], axis=1, keepdims=True)
         stats = jnp.where(lane == block, m_ref[block], stats)
         stats = jnp.where(lane == ROWS + block, total, stats)
-        keep_ref[block] = a_ref[block, :HALF, :]
-        send_ref[block] = a_ref[block, HALF:, :]
-    keep_ref[ROWS] = stats[:HALF]
-    send_ref[ROWS] = stats[HALF:]
+        keep_ref[block] = a_ref[block, mine, :]
+        send_ref[block] = a_ref[block, other, :]
+    stats_ref[...] = stats
+    keep_ref[ROWS] = stats_ref[mine, :]
+    send_ref[ROWS] = stats_ref[other, :]
 
 
 def attend(tables, query, parts, state, last):
     first = state is None
     slots = sum(part.shape[0] for part in parts)
-    most = ROWS * slots // 2
+    most = ROWS * slots
     whole = jax.ShapeDtypeStruct((ROWS, BLOCK, BLOCK), jnp.float32)
     parcel = jax.ShapeDtypeStruct((ROWS + 1, HALF, HEAD_DIM), jnp.float32)
 
-    def kernel(count_ref, block_ref, slot_ref, live_ref, own_ref, other_ref, *refs):
-        tables = (block_ref, slot_ref, live_ref)
+    def kernel(count_ref, block_ref, slot_ref, own_ref, other_ref, *refs):
+        tables = (block_ref, slot_ref)
+        core = lax.axis_index("c")
         part_refs, refs = refs[: len(parts)], refs[len(parts) :]
         if not first:
             (m_in, l_in, a_in), refs = refs[:3], refs[3:]
         if last:
-            keep_ref, send_ref, q_ref, kv_ref, s_ref, top_ref, m_ref, l_ref, a_ref = refs
+            keep_ref, send_ref, q_ref, kv_ref, s_ref, top_ref, m_ref, l_ref, a_ref, stats_ref = refs
         else:
             m_ref, l_ref, a_ref, q_ref, kv_ref, s_ref, top_ref = refs
-        q_ref[:, :HALF, :] = own_ref[...]
-        q_ref[:, HALF:, :] = other_ref[...]
+        q_ref[pl.ds(core * NZ, NZ)] = own_ref[...]
+        q_ref[pl.ds((1 - core) * NZ, NZ)] = other_ref[...]
         at = 0
         for part in part_refs:
             kv_ref[at : at + part.shape[0]] = part[...]
             at += part.shape[0]
-        steps = (count_ref[0] + (UNROLL - 1)) // UNROLL
+        count = count_ref[0]
         top_ref[...] = jnp.full(top_ref.shape, LOW, jnp.float32)
-        score_tiles(steps, tables, q_ref, kv_ref, s_ref, top_ref)
+        score_tiles(count, tables, q_ref, kv_ref, s_ref, top_ref)
         for block in range(ROWS):
             top = jnp.max(top_ref[block], axis=1, keepdims=True)
             if first:
@@ -179,22 +178,23 @@
                 m_ref[block] = new
                 l_ref[block] = l_in[block] * fade
                 a_ref[block] = a_in[block] * fade
-        mix_tiles(steps, tables, kv_ref, s_ref, m_ref, l_ref, a_ref)
+        mix_tiles(count, tables, kv_ref, s_ref, m_ref, l_ref, a_ref)
         if last:
-            write_parcels(m_ref, l_ref, a_ref, keep_ref, send_ref)
+            write_parcels(m_ref, l_ref, a_ref, stats_ref, keep_ref, send_ref)
 
     scratch = [
         pltpu.VMEM((ROWS, BLOCK, HEAD_DIM), jnp.bfloat16),
-        pltpu.VMEM((slots, 2 * HALF, HEAD_DIM), jnp.bfloat16),
+        pltpu.VMEM((slots, 2 * BLOCK, HEAD_DIM), jnp.bfloat16),
         pltpu.VMEM((most, BLOCK, BLOCK), jnp.float32),
         pltpu.VMEM((ROWS, BLOCK, BLOCK), jnp.float32),
     ]
     if last:
         scratch += [pltpu.VMEM((ROWS, BLOCK, BLOCK), jnp.float32)] * 3
+        scratch += [pltpu.VMEM((BLOCK, BLOCK), jnp.float32)]
     return pl.pallas_call(
         kernel,
         out_shape=(parcel, parcel) if last else (whole, whole, whole),
-        in_specs=in_smem(4) + in_vmem(2 + len(parts) + (0 if first else 3)),
+        in_specs=in_smem(3) + in_vmem(2 + len(parts) + (0 if first else 3)),
         out_specs=tuple(in_vmem(2 if last else 3)),
         scratch_shapes=scratch,
         compiler_params=pltpu.CompilerParams(vmem_limit_bytes=28 * MIB),
@@ -289,52 +289,33 @@
 
 
 def tiles_kernel(mask_ref, *refs):
-    y = lax.axis_index("y")
+    y, core = lax.axis_index("y"), lax.axis_index("c")
     for group, columns in enumerate(GROUPS):
-        count_ref, block_ref, slot_ref, live_ref = refs[4 * group : 4 * group + 4]
-
-        def one_query_block(block, start, columns=columns, refs=(block_ref, slot_ref, live_ref)):
-            block_ref, slot_ref, live_ref = refs
+        count_ref, block_ref, slot_ref = refs[3 * group : 3 * group + 3]
+
+        def one_query_block(block, at, columns=columns, refs=(block_ref, slot_ref)):
+            block_ref, slot_ref = refs
             row = block * NY + y
-            first = 2 * start
-            at = first
             for column, back in enumerate(columns):
-                theirs = (y - back + NY) & (NY - 1)
-                for i in range(ROWS):
-                    slot_ref[at] = column * ROWS + i
-                    at = at + jnp.where(mask_ref[row, i * NY + theirs] != 0, 1, 0)
-            slot_ref[at] = 0
-            tiles = (at - first + 1) >> 1
-
-            def fill(t, carry):
-                block_ref[start + t] = block
-                live_ref[start + t] = 2 * HALF
-                return carry
-
-            lax.fori_loop(0, tiles, fill, 0)
-
-            @pl.when(((at - first) & 1) == 1)
-            def _():
-                live_ref[start + tiles - 1] = HALF
-
-            return start + tiles
+                first = core * (NZ * NY) + ((y - back + NY) & (NY - 1))
+                for i in range(NZ):
+                    block_ref[at] = block
+                    slot_ref[at] = column * NZ + i
+                    at = at + jnp.where(mask_ref[row, first + i * NY] != 0, 1, 0)
+            return at
 
         total = lax.fori_loop(0, ROWS, one_query_block, jnp.int32(0))
         count_ref[0] = total
         for u in range(UNROLL):
             block_ref[total + u] = 0
-            live_ref[total + u] = 0
-            slot_ref[2 * (total + u)] = 0
-            slot_ref[2 * (total + u) + 1] = 0
+            slot_ref[total + u] = 0
 
 
 def live_tiles(frame_mask):
     out_shape = []
     for columns in GROUPS:
-        most = ROWS * ROWS * len(columns) // 2 + 128
-        out_shape += [
-            jax.ShapeDtypeStruct((size,), jnp.int32) for size in (1, most, 2 * most, most)
-        ]
+        most = ROWS * NZ * len(columns) + 128
+        out_shape += [jax.ShapeDtypeStruct((size,), jnp.int32) for size in (1, most, most)]
     flat = pl.pallas_call(
         tiles_kernel,
         out_shape=tuple(out_shape),
@@ -343,7 +324,7 @@
         compiler_params=pltpu.CompilerParams(vmem_limit_bytes=4 * MIB),
         cost_estimate=pl.CostEstimate(flops=10**6, bytes_accessed=10**5, transcendentals=0),
     )(frame_mask)
-    return [tuple(flat[4 * i : 4 * i + 4]) for i in range(len(GROUPS))]
+    return [tuple(flat[3 * i : 3 * i + 3]) for i in range(len(GROUPS))]
 
 
 def local(queries, keys, values, frame_mask, w_out):
@@ -354,11 +335,11 @@
     def w_columns(w, to_xl, to_c):
         return lax.dynamic_slice(w, (0, (to_xl * NC + to_c) * width), (w.shape[0], width))
 
-    slots, sent = split(queries, keys, values)
+    sent, slots = split(queries, keys, values)
     sent, w_out = lax.optimization_barrier((sent, w_out))
-    got = lax.ppermute(sent, "c", shift(NC, 1))
+    got = swap_planes(sent)
     w_core = lax.ppermute(w_columns(w_out, xl, 1 - c), "c", shift(NC, 1))
-    slots = lax.dynamic_update_slice(slots, got, ((1 - c) * NZ, 0, 0))
+    slots = lax.dynamic_update_slice(slots, got, (0, 0, 0))
     slots, w_out = lax.optimization_barrier((slots, w_out))
     w_here, w_next, w_last = (
         w_columns(w_out, xl, c),
@@ -378,13 +359,13 @@
     )
     groups = live_tiles(frame_mask)
 
-    slots = lax.all_to_all(slots, ("xh", "z"), 0, 0, tiled=True)
+    slots = lax.all_to_all(slots, "z", 0, 0, tiled=True)
     slots, w_here, w_core, groups = lax.optimization_barrier((slots, w_here, w_core, groups))
-    low, high = slots[: ROWS // 2, HALF:], slots[ROWS // 2 :, HALF:]
+    low, high = slots[: NZ // 2, BLOCK:], slots[NZ // 2 :, BLOCK:]
     slots, low, high = lax.optimization_barrier((slots, low, high))
     before_low = lax.ppermute(low, "y", shift(NY, 1))
     after_high = lax.ppermute(high, "y", shift(NY, -1))
-    query = slots[:, :HALF]
+    query = slots[:, :BLOCK]
     query = (query, lax.ppermute(query, "c", shift(NC, 1)))
     before_high = lax.ppermute(high, "y", shift(NY, 1))
     after_low = lax.ppermute(low, "y", shift(NY, -1))

time: 103 us -> 104 us (level)
  waiting for transfers between devices: 17.3 us -> 23.6 us
  Pallas kernels: 27.6 us -> 23.3 us
  blocking collectives: 14.5 us -> 13.3 us
    ppermute x1, waiting for transfers between devices: 0.01 us -> 3.99 us  [swap_planes(): lax.ppermute(x, ('xh', 'c'), [(a * NC + b, d * NC + e) for (a, b), (d, e)...]
    ppermute x1, starting transfers between devices: 2.96 us -> 0.09 us  [local(): query = (query, lax.ppermute(query, 'c', shift(NC, 1)))]
    ppermute x1, starting transfers between devices: 3.35 us -> 6.04 us  [swap_planes(): lax.ppermute(x, ('xh', 'c'), [(a * NC + b, d * NC + e) for (a, b), (d, e)...]
    all_to_all x1, waiting for transfers between devices: 6.13 us -> 8.79 us  [local(): slots = lax.all_to_all(slots, 'z', 0, 0, tiled=True)]
    pallas_call x1, Pallas kernels: 6.81 us -> 4.3 us  [live_tiles(): pl.pallas_call(tiles_kernel, out_shape=tuple(out_shape), in_specs=in_smem...]
    ppermute x1, starting transfers between devices: 2.94 us -> 5.12 us  [local(): there = lax.ppermute(sent, 'c', shift(NC, 1))]
    pallas_call x3, Pallas kernels: 14.3 us -> 12.6 us  [attend(): pl.pallas_call(kernel, out_shape=(parcel, parcel) if last else (whole, wh...]
    all_to_all x1, blocking collectives: 14.5 us -> 13.3 us  [local(): rows = lax.all_to_all(merge(here, there), ('xh', 'z'), 0, 0, tiled=True)]
  transfers between devices with their start and end apart: 16 -> 16, of which waited for: 7 -> 8; matrix products, arithmetic and copies ran while one was open for 10% -> 10% of each run, Pallas kernels for 23% -> 18%
where the time goes in v7:
time: 104 us; the launch traced here: 105 us
  starting transfers between devices  34.5 us (33%)
  waiting for transfers between devices  23.6 us (23%)
  Pallas kernels  23.3 us (22%)
  blocking collectives  13.3 us (13%)
  local copies, waits for them, and re-layouts  10 us (10%)
    all_to_all x1, blocking collectives, local(): rows = lax.all_to_all(merge(here, there), ('xh', 'z'), 0, 0, tiled=True)  13.3 us
    pallas_call x3, Pallas kernels, attend(): pl.pallas_call(kernel, out_shape=(parcel, parcel) if last else (whole, wh...  12.6 us
    all_to_all x1, waiting for transfers between devices, local(): slots = lax.all_to_all(slots, 'z', 0, 0, tiled=True)  8.79 us
    all_to_all x1, starting transfers between devices, local(): slots = lax.all_to_all(slots, 'z', 0, 0, tiled=True)  8.19 us
    dynamic_slice x2, local copies, waits for them, and re-layouts, w_columns(): lax.dynamic_slice(w, (0, (to_xl * NC + to_c) * width), (w.shape[0], width))  7.13 us
    ppermute x1, starting transfers between devices, swap_planes(): lax.ppermute(x, ('xh', 'c'), [(a * NC + b, d * NC + e) for (a, b), (d, e)...  6.04 us
    ppermute x1, starting transfers between devices, local(): there = lax.ppermute(sent, 'c', shift(NC, 1))  5.12 us
    ppermute x1, waiting for transfers between devices, local(): before_low = lax.ppermute(low, 'y', shift(NY, 1))  4.71 us
  transfers between devices with their start and end apart: 16, of which 8 were waited for; matrix products, arithmetic and copies ran while one was open for 10% of the time, Pallas kernels for 18%

profile of v7, /device:TPU:1, one launch (start us, length us, event | category | flops | bytes accessed | tf_op | source)
XLA Modules:
  0.0 105.0 jit_solution(15114085063919474846)
XLA Ops:
  0.0 1.9 %shard_map.55 = (bf16[5,384,128]{2,1,0:T(8,128)(2,1)}, bf16[8,384,128]{2,1,0:T(8,128)(2,1)}) custom-call(bf16[128,640]{1,0:T(8,128)(2,1)} %q_hbm.1, bf16[128,640]{1,0:T(8,128)(2,1)} %k_hbm.1, bf16[128,640]{1,0:T(8,128)(2,1)} %v_hbm.1), custom_call_target="tpu_custom_call" | custom-call | tf_op jit(solution)/shard_map/pallas_call | solution.py:60
  1.9 6.0 %collective-permute-start = (bf16[5,384,128]{2,1,0:T(8,128)(2,1)}, bf16[5,384,128]{2,1,0:T(8,128)(2,1)S(1)}, u32[]{:S(2)}, u32[]{:S(2)}) collective-permute-start(bf16[5,384,128]{2,1,0:T(8,128)(2,1)} %get-tuple-element.62), channel_id=1, source_target_pairs={{0,0},{129,129},{1,128},{128,1},{2,2},{131,131},{3,130},{130,3},{4... | collective-permute-start | bytes 1474568 | tf_op jit(solution)/shard_map/ppermute | solution.py:36
  8.0 2.7 %constant_dynamic-slice_fusion = bf16[640,1280]{1,0:T(8,128)(2,1)} fusion(bf16[640,5120]{1,0:T(8,128)(2,1)} %param.9, s32[]{:T(128)S(6)} %select_n.15), kind=kLoop, calls=%fused_computation | loop fusion | bytes 3276804 | tf_op jit(solution)/shard_map/dynamic_slice | solution.py:336
  10.7 4.0 %collective-permute-done = bf16[5,384,128]{2,1,0:T(8,128)(2,1)S(1)} collective-permute-done((bf16[5,384,128]{2,1,0:T(8,128)(2,1)}, bf16[5,384,128]{2,1,0:T(8,128)(2,1)S(1)}, u32[]{:S(2)}, u32[]{:S(2)}) %collective-permute-start) | collective-permute-done | bytes 491552 | tf_op jit(solution)/shard_map/ppermute | solution.py:36
  15.5 8.2 %all-to-all-start = ((bf16[8,384,128]{2,1,0:T(8,128)(2,1)}), bf16[8,384,128]{2,1,0:T(8,128)(2,1)}, u32[]{:S(2)}, u32[]{:S(2)}) async-start(bf16[8,384,128]{2,1,0:T(8,128)(2,1)} %constant_dynamic-update-slice_fusion), calls=%async_computation | async-start | bytes 1572864 | tf_op jit(solution)/shard_map/all_to_all | solution.py:362
  23.7 4.4 %constant_dynamic-slice_fusion.1 = (bf16[640,1280]{1,0:T(8,128)(2,1)}, bf16[640,1280]{1,0:T(8,128)(2,1)}, bf16[640,1280]{1,0:T(8,128)(2,1)S(1)}) fusion(bf16[640,5120]{1,0:T(8,128)(2,1)} %param.9, s32[]{:T(128)S(6)} %select_n.14, s32[]{:T(128)S(6)} %select_n.13, s32[]{:T(128)S(6)} %select_n.12), kind=kLoop, calls=%fused_computation.1 | loop fusion | bytes 9830412 | tf_op jit(solution)/shard_map/dynamic_slice | solution.py:336
  29.3 2.1 %collective-permute-start.11 = (bf16[640,1280]{1,0:T(8,128)(2,1)}, bf16[640,1280]{1,0:T(8,128)(2,1)}, u32[]{:S(2)}, u32[]{:S(2)}) collective-permute-start(bf16[640,1280]{1,0:T(8,128)(2,1)} %get-tuple-element.104), channel_id=1, source_target_pairs={{0,131},{1,130},{2,1},{3,0},{128,3},{129,2},{130,129},{131,128},{4... | collective-permute-start | bytes 4915208 | tf_op jit(solution)/shard_map/ppermute | solution.py:357
  31.4 4.3 %shard_map.56 = (s32[1]{0:T(128)}, s32[256]{0:T(256)S(1)}, s32[256]{0:T(256)S(1)}, s32[1]{0:T(128)}, s32[384]{0:T(512)S(1)}, /*index=5*/s32[384]{0:T(512)S(1)}, s32[1]{0:T(128)}, s32[256]{0:T(256)S(1)}, s32[256]{0:T(256)S(1)}) custom-call(s32[64,64]{1,0:T(8,128)S(1)} %copy-done), custom_call_target="tpu_custom_call" | custom-call | flops 1000000 | bytes 100000 | tf_op jit(solution)/shard_map/pallas_call | solution.py:319
  35.7 8.8 %all-to-all-done = bf16[8,384,128]{2,1,0:T(8,128)(2,1)} async-done(((bf16[8,384,128]{2,1,0:T(8,128)(2,1)}), bf16[8,384,128]{2,1,0:T(8,128)(2,1)}, u32[]{:S(2)}, u32[]{:S(2)}) %all-to-all-start) | async-done | bytes 786464 | tf_op jit(solution)/shard_map/all_to_all | solution.py:362
  46.6 1.4 %collective-permute-start.3 = (bf16[4,256,128]{2,1,0:T(8,128)(2,1)S(1)}, bf16[4,256,128]{2,1,0:T(8,128)(2,1)S(1)}, u32[]{:S(2)}, u32[]{:S(2)}) collective-permute-start(bf16[4,256,128]{2,1,0:T(8,128)(2,1)S(1)} %get-tuple-element.82.refs_0_), channel_id=1, source_target_pairs={{0,4},{4,8},{8,12},{12,0},{1,5},{5,9},{9,13},{13,1},{2,6},{6,10},{... | collective-permute-start | bytes 786440 | tf_op jit(solution)/shard_map/ppermute | solution.py:366
  48.0 1.5 %collective-permute-start.4 = (bf16[4,256,128]{2,1,0:T(8,128)(2,1)S(1)}, bf16[4,256,128]{2,1,0:T(8,128)(2,1)S(1)}, u32[]{:S(2)}, u32[]{:S(2)}) collective-permute-start(bf16[4,256,128]{2,1,0:T(8,128)(2,1)S(1)} %get-tuple-element.83.refs_1_), channel_id=1, source_target_pairs={{0,12},{4,0},{8,4},{12,8},{1,13},{5,1},{9,5},{13,9},{2,14},{6,2},{... | collective-permute-start | bytes 786440 | tf_op jit(solution)/shard_map/ppermute | solution.py:367
  49.6 1.4 %collective-permute-start.8 = (bf16[4,256,128]{2,1,0:T(8,128)(2,1)S(1)}, bf16[4,256,128]{2,1,0:T(8,128)(2,1)S(1)}, u32[]{:S(2)}, u32[]{:S(2)}) collective-permute-start(bf16[4,256,128]{2,1,0:T(8,128)(2,1)S(1)} %get-tuple-element.82.refs_0_), channel_id=1, source_target_pairs={{0,12},{4,0},{8,4},{12,8},{1,13},{5,1},{9,5},{13,9},{2,14},{6,2},{... | collective-permute-start | bytes 786440 | tf_op jit(solution)/shard_map/ppermute | solution.py:371
  50.9 4.7 %collective-permute-done.3.refs_0_ = bf16[4,256,128]{2,1,0:T(8,128)(2,1)S(1)} collective-permute-done((bf16[4,256,128]{2,1,0:T(8,128)(2,1)S(1)}, bf16[4,256,128]{2,1,0:T(8,128)(2,1)S(1)}, u32[]{:S(2)}, u32[]{:S(2)}) %collective-permute-start.3) | collective-permute-done | bytes 262176 | tf_op jit(solution)/shard_map/ppermute | solution.py:366
  55.6 3.4 %shard_map.57 = (f32[16,128,128]{2,1,0:T(8,128)S(1)}, f32[16,128,128]{2,1,0:T(8,128)S(1)}, f32[16,128,128]{2,1,0:T(8,128)S(1)}) custom-call(s32[1]{0:T(128)} %get-tuple-element.84.count_ref, s32[256]{0:T(256)S(1)} %get-tuple-element.85.block_ref, s32[256]{0:T(256)S(1)} %get-tuple-element.86.slot_ref, bf16[8,128,128]{2,1,0:T(8,128)(2,1)S(1)} %slice.14.own_ref, ...), custom_call_target="tpu_custom_call" | custom-call | flops 335544320 | bytes 6291456 | tf_op jit(solution)/shard_map/pallas_call | solution.py:194
  60.9 2.9 %collective-permute-start.6 = (bf16[4,256,128]{2,1,0:T(8,128)(2,1)S(1)}, bf16[4,256,128]{2,1,0:T(8,128)(2,1)S(1)}, u32[]{:S(2)}, u32[]{:S(2)}) collective-permute-start(bf16[4,256,128]{2,1,0:T(8,128)(2,1)S(1)} %collective-permute-done.4.refs_3_), channel_id=1, source_target_pairs={{0,12},{4,0},{8,4},{12,8},{1,13},{5,1},{9,5},{13,9},{2,14},{6,2},{... | collective-permute-start | bytes 786440 | tf_op jit(solution)/shard_map/ppermute | solution.py:375
  63.8 5.5 %shard_map.58 = (f32[16,128,128]{2,1,0:T(8,128)S(1)}, f32[16,128,128]{2,1,0:T(8,128)S(1)}, f32[16,128,128]{2,1,0:T(8,128)S(1)}) custom-call(s32[1]{0:T(128)} %get-tuple-element.92.count_ref, s32[384]{0:T(512)S(1)} %get-tuple-element.93.block_ref, s32[384]{0:T(512)S(1)} %get-tuple-element.94.slot_ref, bf16[8,128,128]{2,1,0:T(8,128)(2,1)S(1)} %slice.14.own_ref, ...), custom_call_target="tpu_custom_call" | custom-call | flops 671088640 | bytes 6291456 | tf_op jit(solution)/shard_map/pallas_call | solution.py:194
  69.3 3.7 %shard_map.59 = (f32[17,64,128]{2,1,0:T(8,128)S(1)}, f32[17,64,128]{2,1,0:T(8,128)S(1)}) custom-call(s32[1]{0:T(128)} %get-tuple-element.77.count_ref, s32[256]{0:T(256)S(1)} %get-tuple-element.78.block_ref, s32[256]{0:T(256)S(1)} %get-tuple-element.79.slot_ref, bf16[8,128,128]{2,1,0:T(8,128)(2,1)S(1)} %slice.14.own_ref, ...), custom_call_target="tpu_custom_call" | custom-call | flops 335544320 | bytes 6291456 | tf_op jit(solution)/shard_map/pallas_call | solution.py:194
  73.0 5.1 %collective-permute-start.9 = (f32[17,64,128]{2,1,0:T(8,128)S(1)}, f32[17,64,128]{2,1,0:T(8,128)S(1)}, u32[]{:S(2)}, u32[]{:S(2)}) collective-permute-start(f32[17,64,128]{2,1,0:T(8,128)S(1)} %get-tuple-element.102), channel_id=1, source_target_pairs={{0,1},{1,0},{2,3},{3,2},{4,5},{5,4},{6,7},{7,6},{8,9},{9,8},{10,11... | collective-permute-start | bytes 1671176 | tf_op jit(solution)/shard_map/ppermute | solution.py:380
  78.2 1.6 %collective-permute-done.9.there_ref = f32[17,64,128]{2,1,0:T(8,128)S(1)} collective-permute-done((f32[17,64,128]{2,1,0:T(8,128)S(1)}, f32[17,64,128]{2,1,0:T(8,128)S(1)}, u32[]{:S(2)}, u32[]{:S(2)}) %collective-permute-start.9) | collective-permute-done | bytes 557088 | tf_op jit(solution)/shard_map/ppermute | solution.py:380
  80.3 13.3 %all_to_all.10 = bf16[16,64,128]{2,1,0:T(8,128)(2,1)S(1)} all-to-all(bf16[16,64,128]{2,1,0:T(8,128)(2,1)S(1)} %shard_map.60), channel_id=1, replica_groups=mesh['xh'=2,'z'=8,'y'=4,'xl'=2,'c'=2] {'xh','z'}, dimensions={0} | all-to-all | bytes 524288 | tf_op jit(solution)/shard_map/all_to_all | solution.py:382
  93.6 2.1 %collective-permute-start.13 = (bf16[10,64,128]{2,1,0:T(8,128)(2,1)S(1)}, bf16[10,64,128]{2,1,0:T(8,128)(2,1)S(1)}, u32[]{:S(2)}, u32[]{:S(2)}) collective-permute-start(bf16[10,64,128]{2,1,0:T(8,128)(2,1)S(1)} %bitcast.2), channel_id=1, source_target_pairs={{0,1},{1,0},{2,3},{3,2},{4,5},{5,4},{6,7},{7,6},{8,9},{9,8},{10,11... | collective-permute-start | bytes 491528 | tf_op jit(solution)/shard_map/ppermute | solution.py:386
  96.7 2.4 %shard_map.61 = (f32[128,1280]{1,0:T(8,128)S(1)}, bf16[640,1280]{1,0:T(8,128)(2,1)S(1)}, bf16[640,1280]{1,0:T(8,128)(2,1)S(1)}) custom-call(bf16[10,64,128]{2,1,0:T(8,128)(2,1)S(1)} %bitcast.4, bf16[10,64,128]{2,1,0:T(8,128)(2,1)S(1)} %collective-permute-done.13.b_ref, bf16[640,1280]{1,0:T(8,128)(2,1)S(1)} %get-tuple-element.106.w_ref, ...), custom_call_target="tpu_custom_call" | custom-call | flops 419430400 | bytes 4194304 | tf_op jit(solution)/shard_map/pallas_call | solution.py:272
  99.2 2.3 %collective-permute-done.12.a_ref = bf16[10,64,128]{2,1,0:T(8,128)(2,1)S(1)} collective-permute-done((bf16[10,64,128]{2,1,0:T(8,128)(2,1)S(1)}, bf16[10,64,128]{2,1,0:T(8,128)(2,1)S(1)}, u32[]{:S(2)}, u32[]{:S(2)}) %collective-permute-start.12) | collective-permute-done | bytes 163872 | tf_op jit(solution)/shard_map/ppermute | solution.py:385
  103.4 1.5 %shard_map.62 = bf16[128,1280]{1,0:T(8,128)(2,1)} custom-call(bf16[10,64,128]{2,1,0:T(8,128)(2,1)S(1)} %collective-permute-done.12.a_ref, bf16[10,64,128]{2,1,0:T(8,128)(2,1)S(1)} %collective-permute-done.14.b_ref, bf16[640,1280]{1,0:T(8,128)(2,1)S(1)} %get-tuple-element.112.w_ref, bf16[640,1280]{1,0:T(8,128)(2,1)S(1)} %get-tuple-element.113.w2_ref, ...), custom_call_target="tpu_custom_call" | custom-call | flops 419430400 | bytes 4194304 | tf_op jit(solution)/shard_map/pallas_call | solution.py:272
  (25 shorter events, 9.5 us)
Async XLA Ops:
  1.9 12.8 %collective-permute-start = (bf16[5,384,128]{2,1,0:T(8,128)(2,1)}, bf16[5,384,128]{2,1,0:T(8,128)(2,1)S(1)}, u32[]{:S(2)}, u32[]{:S(2)}) collective-permute-start(bf16[5,384,128]{2,1,0:T(8,128)(2,1)} %get-tuple-element.62), channel_id=1, source_target_pairs={{0,0},{129,129},{1,128},{128,1},{2,2},{131,131},{3,130},{130,3},{4... | collective-permute-start | bytes 1474568 | tf_op jit(solution)/shard_map/ppermute | solution.py:36
  10.7 25.0 %collective-permute-start.1 = (bf16[640,1280]{1,0:T(8,128)(2,1)}, bf16[640,1280]{1,0:T(8,128)(2,1)S(1)}, u32[]{:S(2)}, u32[]{:S(2)}) collective-permute-start(bf16[640,1280]{1,0:T(8,128)(2,1)} %constant_dynamic-slice_fusion), channel_id=1, source_target_pairs={{0,1},{1,0},{2,3},{3,2},{4,5},{5,4},{6,7},{7,6},{8,9},{9,8},{10,11... | collective-permute-start | bytes 4915208 | tf_op jit(solution)/shard_map/ppermute | solution.py:341
  15.5 29.0 %all-to-all-start = ((bf16[8,384,128]{2,1,0:T(8,128)(2,1)}), bf16[8,384,128]{2,1,0:T(8,128)(2,1)}, u32[]{:S(2)}, u32[]{:S(2)}) async-start(bf16[8,384,128]{2,1,0:T(8,128)(2,1)} %constant_dynamic-update-slice_fusion), calls=%async_computation | async-start | bytes 1572864 | tf_op jit(solution)/shard_map/all_to_all | solution.py:362
  23.7 7.7 %copy-start = (s32[64,64]{1,0:T(8,128)S(1)}, s32[64,64]{1,0:T(8,128)}, u32[]{:S(2)}) copy-start(s32[64,64]{1,0:T(8,128)} %mask_ref) | copy-start | bytes 49156
  28.1 50.0 %collective-permute-start.10 = (bf16[640,1280]{1,0:T(8,128)(2,1)}, bf16[640,1280]{1,0:T(8,128)(2,1)}, u32[]{:S(2)}, u32[]{:S(2)}) collective-permute-start(bf16[640,1280]{1,0:T(8,128)(2,1)} %get-tuple-element.103), channel_id=1, source_target_pairs={{0,2},{1,3},{2,128},{3,129},{128,130},{129,131},{130,0},{131,1},{4... | collective-permute-start | bytes 4915208 | tf_op jit(solution)/shard_map/ppermute | solution.py:354
  29.3 48.9 %collective-permute-start.11 = (bf16[640,1280]{1,0:T(8,128)(2,1)}, bf16[640,1280]{1,0:T(8,128)(2,1)}, u32[]{:S(2)}, u32[]{:S(2)}) collective-permute-start(bf16[640,1280]{1,0:T(8,128)(2,1)} %get-tuple-element.104), channel_id=1, source_target_pairs={{0,131},{1,130},{2,1},{3,0},{128,3},{129,2},{130,129},{131,128},{4... | collective-permute-start | bytes 4915208 | tf_op jit(solution)/shard_map/ppermute | solution.py:357
  46.5 3.0 %collective-permute-start.2 = (bf16[8,128,128]{2,1,0:T(8,128)(2,1)S(1)}, bf16[8,128,128]{2,1,0:T(8,128)(2,1)S(1)}, u32[]{:S(2)}, u32[]{:S(2)}) collective-permute-start(bf16[8,128,128]{2,1,0:T(8,128)(2,1)S(1)} %slice.14.own_ref), channel_id=1, source_target_pairs={{0,1},{1,0},{2,3},{3,2},{4,5},{5,4},{6,7},{7,6},{8,9},{9,8},{10,11... | collective-permute-start | bytes 786440 | tf_op jit(solution)/shard_map/ppermute | solution.py:369
  46.6 9.0 %collective-permute-start.3 = (bf16[4,256,128]{2,1,0:T(8,128)(2,1)S(1)}, bf16[4,256,128]{2,1,0:T(8,128)(2,1)S(1)}, u32[]{:S(2)}, u32[]{:S(2)}) collective-permute-start(bf16[4,256,128]{2,1,0:T(8,128)(2,1)S(1)} %get-tuple-element.82.refs_0_), channel_id=1, source_target_pairs={{0,4},{4,8},{8,12},{12,0},{1,5},{5,9},{9,13},{13,1},{2,6},{6,10},{... | collective-permute-start | bytes 786440 | tf_op jit(solution)/shard_map/ppermute | solution.py:366
  48.0 11.0 %collective-permute-start.4 = (bf16[4,256,128]{2,1,0:T(8,128)(2,1)S(1)}, bf16[4,256,128]{2,1,0:T(8,128)(2,1)S(1)}, u32[]{:S(2)}, u32[]{:S(2)}) collective-permute-start(bf16[4,256,128]{2,1,0:T(8,128)(2,1)S(1)} %get-tuple-element.83.refs_1_), channel_id=1, source_target_pairs={{0,12},{4,0},{8,4},{12,8},{1,13},{5,1},{9,5},{13,9},{2,14},{6,2},{... | collective-permute-start | bytes 786440 | tf_op jit(solution)/shard_map/ppermute | solution.py:367
  49.6 11.3 %collective-permute-start.8 = (bf16[4,256,128]{2,1,0:T(8,128)(2,1)S(1)}, bf16[4,256,128]{2,1,0:T(8,128)(2,1)S(1)}, u32[]{:S(2)}, u32[]{:S(2)}) collective-permute-start(bf16[4,256,128]{2,1,0:T(8,128)(2,1)S(1)} %get-tuple-element.82.refs_0_), channel_id=1, source_target_pairs={{0,12},{4,0},{8,4},{12,8},{1,13},{5,1},{9,5},{13,9},{2,14},{6,2},{... | collective-permute-start | bytes 786440 | tf_op jit(solution)/shard_map/ppermute | solution.py:371
  55.6 8.2 %collective-permute-start.7 = (bf16[4,256,128]{2,1,0:T(8,128)(2,1)S(1)}, bf16[4,256,128]{2,1,0:T(8,128)(2,1)S(1)}, u32[]{:S(2)}, u32[]{:S(2)}) collective-permute-start(bf16[4,256,128]{2,1,0:T(8,128)(2,1)S(1)} %get-tuple-element.83.refs_1_), channel_id=1, source_target_pairs={{0,4},{4,8},{8,12},{12,0},{1,5},{5,9},{9,13},{13,1},{2,6},{6,10},{... | collective-permute-start | bytes 786440 | tf_op jit(solution)/shard_map/ppermute | solution.py:370
  59.1 10.2 %collective-permute-start.5 = (bf16[4,256,128]{2,1,0:T(8,128)(2,1)S(1)}, bf16[4,256,128]{2,1,0:T(8,128)(2,1)S(1)}, u32[]{:S(2)}, u32[]{:S(2)}) collective-permute-start(bf16[4,256,128]{2,1,0:T(8,128)(2,1)S(1)} %collective-permute-done.3.refs_0_), channel_id=1, source_target_pairs={{0,4},{4,8},{8,12},{12,0},{1,5},{5,9},{9,13},{13,1},{2,6},{6,10},{... | collective-permute-start | bytes 786440 | tf_op jit(solution)/shard_map/ppermute | solution.py:374
  60.9 8.4 %collective-permute-start.6 = (bf16[4,256,128]{2,1,0:T(8,128)(2,1)S(1)}, bf16[4,256,128]{2,1,0:T(8,128)(2,1)S(1)}, u32[]{:S(2)}, u32[]{:S(2)}) collective-permute-start(bf16[4,256,128]{2,1,0:T(8,128)(2,1)S(1)} %collective-permute-done.4.refs_3_), channel_id=1, source_target_pairs={{0,12},{4,0},{8,4},{12,8},{1,13},{5,1},{9,5},{13,9},{2,14},{6,2},{... | collective-permute-start | bytes 786440 | tf_op jit(solution)/shard_map/ppermute | solution.py:375
  73.0 6.7 %collective-permute-start.9 = (f32[17,64,128]{2,1,0:T(8,128)S(1)}, f32[17,64,128]{2,1,0:T(8,128)S(1)}, u32[]{:S(2)}, u32[]{:S(2)}) collective-permute-start(f32[17,64,128]{2,1,0:T(8,128)S(1)} %get-tuple-element.102), channel_id=1, source_target_pairs={{0,1},{1,0},{2,3},{3,2},{4,5},{5,4},{6,7},{7,6},{8,9},{9,8},{10,11... | collective-permute-start | bytes 1671176 | tf_op jit(solution)/shard_map/ppermute | solution.py:380
  93.6 3.1 %collective-permute-start.13 = (bf16[10,64,128]{2,1,0:T(8,128)(2,1)S(1)}, bf16[10,64,128]{2,1,0:T(8,128)(2,1)S(1)}, u32[]{:S(2)}, u32[]{:S(2)}) collective-permute-start(bf16[10,64,128]{2,1,0:T(8,128)(2,1)S(1)} %bitcast.2), channel_id=1, source_target_pairs={{0,1},{1,0},{2,3},{3,2},{4,5},{5,4},{6,7},{7,6},{8,9},{9,8},{10,11... | collective-permute-start | bytes 491528 | tf_op jit(solution)/shard_map/ppermute | solution.py:386
  95.7 5.8 %collective-permute-start.12 = (bf16[10,64,128]{2,1,0:T(8,128)(2,1)S(1)}, bf16[10,64,128]{2,1,0:T(8,128)(2,1)S(1)}, u32[]{:S(2)}, u32[]{:S(2)}) collective-permute-start(bf16[10,64,128]{2,1,0:T(8,128)(2,1)S(1)} %bitcast.3), channel_id=1, source_target_pairs={{0,2},{2,0},{1,3},{3,1},{4,6},{6,4},{5,7},{7,5},{8,10},{10,8},{9,1... | collective-permute-start | bytes 491528 | tf_op jit(solution)/shard_map/ppermute | solution.py:385
  101.5 1.9 %collective-permute-start.14 = (bf16[10,64,128]{2,1,0:T(8,128)(2,1)S(1)}, bf16[10,64,128]{2,1,0:T(8,128)(2,1)S(1)}, u32[]{:S(2)}, u32[]{:S(2)}) collective-permute-start(bf16[10,64,128]{2,1,0:T(8,128)(2,1)S(1)} %collective-permute-done.12.a_ref), channel_id=1, source_target_pairs={{0,1},{1,0},{2,3},{3,2},{4,5},{5,4},{6,7},{7,6},{8,9},{9,8},{10,11... | collective-permute-start | bytes 491528 | tf_op jit(solution)/shard_map/ppermute | solution.py:389

commit v8 on v7

--- a/solution.py
+++ b/solution.py
@@ -8,7 +8,6 @@
 
 HEAD_DIM = 128
 BLOCK = 128
-HALF = 64
 HEADS = 5
 XH, NZ, NY, XL, NC = 2, 8, 4, 2, 2
 ROWS = XH * NZ
@@ -31,13 +30,7 @@
     return [pl.BlockSpec(memory_space=pltpu.SMEM)] * count
 
 
-def swap_planes(x):
-    pairs = [((0, 0), (0, 0)), ((1, 1), (1, 1)), ((0, 1), (1, 0)), ((1, 0), (0, 1))]
-    return lax.ppermute(x, ("xh", "c"), [(a * NC + b, d * NC + e) for (a, b), (d, e) in pairs])
-
-
-def split_kernel(q_hbm, k_hbm, v_hbm, out_hbm, slots_hbm, whole_ref, out_ref, sems):
-    del slots_hbm
+def split_kernel(q_hbm, k_hbm, v_hbm, slots_hbm, whole_ref, out_ref, sems):
     loads = [
         pltpu.make_async_copy(source, whole_ref.at[t], sems.at[t])
         for t, source in enumerate((q_hbm, k_hbm, v_hbm))
@@ -49,25 +42,22 @@
         for head in range(HEADS):
             lanes = slice(head * HEAD_DIM, (head + 1) * HEAD_DIM)
             out_ref[head, t * BLOCK : (t + 1) * BLOCK, :] = whole_ref[t, :, lanes]
-    out = pltpu.make_async_copy(out_ref, out_hbm, sems.at[3])
+    out = pltpu.make_async_copy(out_ref, slots_hbm.at[:HEADS], sems.at[3])
     out.start()
     out.wait()
 
 
 def split(queries, keys, values):
     anywhere = pl.BlockSpec(memory_space=pl.ANY)
-    part = (HEADS, 3 * BLOCK, HEAD_DIM)
+    part = (3 * BLOCK, HEAD_DIM)
     return pl.pallas_call(
         split_kernel,
-        out_shape=(
-            jax.ShapeDtypeStruct(part, jnp.bfloat16),
-            jax.ShapeDtypeStruct((NZ,) + part[1:], jnp.bfloat16),
-        ),
+        out_shape=jax.ShapeDtypeStruct((NZ,) + part, jnp.bfloat16),
         in_specs=[anywhere] * 3,
-        out_specs=(anywhere,) * 2,
+        out_specs=anywhere,
         scratch_shapes=[
             pltpu.VMEM((3,) + queries.shape, jnp.bfloat16),
-            pltpu.VMEM(part, jnp.bfloat16),
+            pltpu.VMEM((HEADS,) + part, jnp.bfloat16),
             pltpu.SemaphoreType.DMA((4,)),
         ],
         compiler_params=pltpu.CompilerParams(vmem_limit_bytes=56 * MIB),
@@ -123,21 +113,24 @@
     lax.fori_loop(0, (count + (UNROLL - 1)) // UNROLL, mix, 0)
 
 
-def write_parcels(m_ref, l_ref, a_ref, stats_ref, keep_ref, send_ref):
-    core = lax.axis_index("c")
-    mine = pl.ds(pl.multiple_of(core * HALF, HALF), HALF)
-    other = pl.ds(pl.multiple_of((1 - core) * HALF, HALF), HALF)
+def write_parcels(m_ref, l_ref, a_ref, keep_ref, keep_stats_ref, send_ref, send_stats_ref):
+    plane = lax.axis_index("xh")
     lane = lax.broadcasted_iota(jnp.int32, (BLOCK, BLOCK), 1)
-    stats = jnp.zeros((BLOCK, BLOCK), jnp.float32)
-    for block in range(ROWS):
-        total = jnp.sum(l_ref[block], axis=1, keepdims=True)
-        stats = jnp.where(lane == block, m_ref[block], stats)
-        stats = jnp.where(lane == ROWS + block, total, stats)
-        keep_ref[block] = a_ref[block, mine, :]
-        send_ref[block] = a_ref[block, other, :]
-    stats_ref[...] = stats
-    keep_ref[ROWS] = stats_ref[mine, :]
-    send_ref[ROWS] = stats_ref[other, :]
+
+    def stats_of(first):
+        stats = jnp.zeros((BLOCK, BLOCK), jnp.float32)
+        for i in range(NZ):
+            total = jnp.sum(l_ref[first + i], axis=1, keepdims=True)
+            stats = jnp.where(lane == i, m_ref[first + i], stats)
+            stats = jnp.where(lane == NZ + i, total, stats)
+        return stats
+
+    own, other = plane * NZ, (1 - plane) * NZ
+    for i in range(NZ):
+        keep_ref[i] = a_ref[own + i]
+        send_ref[i] = a_ref[other + i].astype(jnp.bfloat16)
+    keep_stats_ref[...] = stats_of(own)
+    send_stats_ref[...] = stats_of(other).T[: 2 * NZ]
 
 
 def attend(tables, query, parts, state, last):
@@ -145,20 +138,26 @@
     slots = sum(part.shape[0] for part in parts)
     most = ROWS * slots
     whole = jax.ShapeDtypeStruct((ROWS, BLOCK, BLOCK), jnp.float32)
-    parcel = jax.ShapeDtypeStruct((ROWS + 1, HALF, HEAD_DIM), jnp.float32)
+    parcels = (
+        jax.ShapeDtypeStruct((NZ, BLOCK, HEAD_DIM), jnp.float32),
+        jax.ShapeDtypeStruct((BLOCK, BLOCK), jnp.float32),
+        jax.ShapeDtypeStruct((NZ, BLOCK, HEAD_DIM), jnp.bfloat16),
+        jax.ShapeDtypeStruct((2 * NZ, BLOCK), jnp.float32),
+    )
 
     def kernel(count_ref, block_ref, slot_ref, own_ref, other_ref, *refs):
         tables = (block_ref, slot_ref)
-        core = lax.axis_index("c")
+        plane = lax.axis_index("xh")
         part_refs, refs = refs[: len(parts)], refs[len(parts) :]
         if not first:
             (m_in, l_in, a_in), refs = refs[:3], refs[3:]
         if last:
-            keep_ref, send_ref, q_ref, kv_ref, s_ref, top_ref, m_ref, l_ref, a_ref, stats_ref = refs
+            parcel_refs, refs = refs[:4], refs[4:]
+            q_ref, kv_ref, s_ref, top_ref, m_ref, l_ref, a_ref = refs
         else:
             m_ref, l_ref, a_ref, q_ref, kv_ref, s_ref, top_ref = refs
-        q_ref[pl.ds(core * NZ, NZ)] = own_ref[...]
-        q_ref[pl.ds((1 - core) * NZ, NZ)] = other_ref[...]
+        q_ref[pl.ds(plane * NZ, NZ)] = own_ref[...]
+        q_ref[pl.ds((1 - plane) * NZ, NZ)] = other_ref[...]
         at = 0
         for part in part_refs:
             kv_ref[at : at + part.shape[0]] = part[...]
@@ -180,7 +179,7 @@
                 a_ref[block] = a_in[block] * fade
         mix_tiles(count, tables, kv_ref, s_ref, m_ref, l_ref, a_ref)
         if last:
-            write_parcels(m_ref, l_ref, a_ref, stats_ref, keep_ref, send_ref)
+            write_parcels(m_ref, l_ref, a_ref, *parcel_refs)
 
     scratch = [
         pltpu.VMEM((ROWS, BLOCK, HEAD_DIM), jnp.bfloat16),
@@ -190,12 +189,11 @@
     ]
     if last:
         scratch += [pltpu.VMEM((ROWS, BLOCK, BLOCK), jnp.float32)] * 3
-        scratch += [pltpu.VMEM((BLOCK, BLOCK), jnp.float32)]
     return pl.pallas_call(
         kernel,
-        out_shape=(parcel, parcel) if last else (whole, whole, whole),
+        out_shape=parcels if last else (whole, whole, whole),
         in_specs=in_smem(3) + in_vmem(2 + len(parts) + (0 if first else 3)),
-        out_specs=tuple(in_vmem(2 if last else 3)),
+        out_specs=tuple(in_vmem(4 if last else 3)),
         scratch_shapes=scratch,
         compiler_params=pltpu.CompilerParams(vmem_limit_bytes=28 * MIB),
         cost_estimate=pl.CostEstimate(
@@ -206,27 +204,29 @@
     )(*tables, *query, *parts, *(() if first else state))
 
 
-def merge_kernel(here_ref, there_ref, out_ref):
-    here, there = here_ref[ROWS], there_ref[ROWS]
-    for block in range(ROWS):
-        m0, m1 = here[:, block : block + 1], there[:, block : block + 1]
-        l0 = here[:, ROWS + block : ROWS + block + 1]
-        l1 = there[:, ROWS + block : ROWS + block + 1]
+def merge_kernel(here_ref, here_stats_ref, there_ref, there_stats_ref, out_ref, rows_ref):
+    rows_ref[: 2 * NZ, :] = there_stats_ref[...]
+    rows_ref[2 * NZ :, :] = jnp.zeros((BLOCK - 2 * NZ, BLOCK), jnp.float32)
+    here, there = here_stats_ref[...], rows_ref[...].T
+    for i in range(NZ):
+        m0, m1 = here[:, i : i + 1], there[:, i : i + 1]
+        l0, l1 = here[:, NZ + i : NZ + i + 1], there[:, NZ + i : NZ + i + 1]
         m = jnp.maximum(m0, m1)
         f0 = jnp.exp2((m0 - m) * EXP2_SCALE)
         f1 = jnp.exp2((m1 - m) * EXP2_SCALE)
-        mixed = here_ref[block] * f0 + there_ref[block] * f1
-        out_ref[block] = (mixed / (l0 * f0 + l1 * f1)).astype(jnp.bfloat16)
-
-
-def merge(here, there):
+        mixed = here_ref[i] * f0 + there_ref[i].astype(jnp.float32) * f1
+        out_ref[i] = (mixed / (l0 * f0 + l1 * f1)).astype(jnp.bfloat16)
+
+
+def merge(here, here_stats, there, there_stats):
     return pl.pallas_call(
         merge_kernel,
-        out_shape=jax.ShapeDtypeStruct((ROWS, HALF, HEAD_DIM), jnp.bfloat16),
-        in_specs=in_vmem(2),
+        out_shape=jax.ShapeDtypeStruct(here.shape, jnp.bfloat16),
+        in_specs=in_vmem(4),
         out_specs=in_vmem(1)[0],
+        scratch_shapes=[pltpu.VMEM((BLOCK, BLOCK), jnp.float32)],
         compiler_params=pltpu.CompilerParams(vmem_limit_bytes=4 * MIB),
-    )(here, there)
+    )(here, here_stats, there, there_stats)
 
 
 def project(a, b, w_own, w_other, added=None, staged=()):
@@ -248,14 +248,10 @@
         ]
         for copy in copies:
             copy.start()
-        core = lax.axis_index("c")
-        mine = pl.ds(pl.multiple_of(core * HALF, HALF), HALF)
-        other = pl.ds(pl.multiple_of((1 - core) * HALF, HALF), HALF)
-        for which, head_set in enumerate((core, 1 - core)):
+        for which, ref in enumerate((a_ref, b_ref)):
             for head in range(HEADS):
                 at = (which * HEADS + head) * HEAD_DIM
-                rows_ref[mine, at : at + HEAD_DIM] = a_ref[head_set * HEADS + head]
-                rows_ref[other, at : at + HEAD_DIM] = b_ref[head_set * HEADS + head]
+                rows_ref[:, at : at + HEAD_DIM] = ref[head]
         for at in range(0, width, TILE_N):
             lanes = slice(at, at + TILE_N)
             out = jnp.dot(rows_ref[:, :deep], w_ref[:, lanes], preferred_element_type=jnp.float32)
@@ -289,7 +285,7 @@
 
 
 def tiles_kernel(mask_ref, *refs):
-    y, core = lax.axis_index("y"), lax.axis_index("c")
+    y, plane = lax.axis_index("y"), lax.axis_index("xh")
     for group, columns in enumerate(GROUPS):
         count_ref, block_ref, slot_ref = refs[3 * group : 3 * group + 3]
 
@@ -297,7 +293,7 @@
             block_ref, slot_ref = refs
             row = block * NY + y
             for column, back in enumerate(columns):
-                first = core * (NZ * NY) + ((y - back + NY) & (NY - 1))
+                first = plane * (NZ * NY) + ((y - back + NY) & (NY - 1))
                 for i in range(NZ):
                     block_ref[at] = block
                     slot_ref[at] = column * NZ + i
@@ -335,19 +331,16 @@
     def w_columns(w, to_xl, to_c):
         return lax.dynamic_slice(w, (0, (to_xl * NC + to_c) * width), (w.shape[0], width))
 
-    sent, slots = split(queries, keys, values)
-    sent, w_out = lax.optimization_barrier((sent, w_out))
-    got = swap_planes(sent)
-    w_core = lax.ppermute(w_columns(w_out, xl, 1 - c), "c", shift(NC, 1))
-    slots = lax.dynamic_update_slice(slots, got, (0, 0, 0))
+    slots = split(queries, keys, values)
     slots, w_out = lax.optimization_barrier((slots, w_out))
-    w_here, w_next, w_last = (
+    w_here, w_core, w_next, w_last = (
         w_columns(w_out, xl, c),
+        w_columns(w_out, xl, 1 - c),
         w_columns(w_out, 1 - xl, c),
         w_columns(w_out, 1 - xl, 1 - c),
     )
-    w_here, w_next, w_last, frame_mask = lax.optimization_barrier(
-        (w_here, w_next, w_last, frame_mask)
+    w_here, w_core, w_next, w_last, frame_mask = lax.optimization_barrier(
+        (w_here, w_core, w_next, w_last, frame_mask)
     )
     places = [(x, core_) for x in range(XH * XL) for core_ in range(NC)]
     along_x = ("xh", "xl", "c")
@@ -366,7 +359,7 @@
     before_low = lax.ppermute(low, "y", shift(NY, 1))
     after_high = lax.ppermute(high, "y", shift(NY, -1))
     query = slots[:, :BLOCK]
-    query = (query, lax.ppermute(query, "c", shift(NC, 1)))
+    query = (query, lax.ppermute(query, "xh", shift(XH, 1)))
     before_high = lax.ppermute(high, "y", shift(NY, 1))
     after_low = lax.ppermute(low, "y", shift(NY, -1))
     state = attend(groups[0], query, [low, high], None, False)
@@ -376,18 +369,21 @@
     state = attend(
         groups[1], query, [before_low, before_high, after_low, after_high], state, False
     )
-    here, sent = attend(groups[2], query, [far_low, far_high], state, True)
-    there = lax.ppermute(sent, "c", shift(NC, 1))
-    there, w_next, w_last = lax.optimization_barrier((there, w_next, w_last))
-    rows = lax.all_to_all(merge(here, there), ("xh", "z"), 0, 0, tiled=True)
-    rows = rows.reshape(XH, NZ, HALF, HEAD_DIM)[:, :HEADS]
-    rows = rows.reshape(XH * HEADS, HALF, HEAD_DIM)
-    rows_xl = lax.ppermute(rows, "xl", shift(XL, 1))
-    rows_core = lax.ppermute(rows, "c", shift(NC, 1))
-    near, w_next, w_last = project(rows, rows_core, w_here, w_core, None, (w_next, w_last))
-    rows_xl, near = lax.optimization_barrier((rows_xl, near))
-    rows_both = lax.ppermute(rows_xl, "c", shift(NC, 1))
-    return project(rows_xl, rows_both, w_next, w_last, near)[0]
+    here, here_stats, sent, sent_stats = attend(
+        groups[2], query, [far_low, far_high], state, True
+    )
+    sent, w_core, w_next, w_last = lax.optimization_barrier((sent, w_core, w_next, w_last))
+    w_core = lax.ppermute(w_core, "c", shift(NC, 1))
+    there = lax.ppermute(sent, "xh", shift(XH, 1))
+    there_stats = lax.ppermute(sent_stats, "xh", shift(XH, 1))
+    heads = merge(here, here_stats, there, there_stats)
+    heads = lax.all_to_all(heads, "z", 0, 0, tiled=True)[:HEADS]
+    heads_xl = lax.ppermute(heads, "xl", shift(XL, 1))
+    heads_core = lax.ppermute(heads, "c", shift(NC, 1))
+    near, w_next, w_last = project(heads, heads_core, w_here, w_core, None, (w_next, w_last))
+    heads_xl, near = lax.optimization_barrier((heads_xl, near))
+    heads_both = lax.ppermute(heads_xl, "c", shift(NC, 1))
+    return project(heads_xl, heads_both, w_next, w_last, near)[0]
 
 
 def solution(mesh):

time: 104 us -> 124 us (1.19); the launches traced: 105 us -> 123 us
  waiting for transfers between devices: 23.6 us -> 39.8 us
  blocking collectives: 13.3 us -> 16.5 us
  local copies, waits for them, and re-layouts: 10 us -> 7.33 us
    ppermute x7, waiting for transfers between devices: 9.57 us -> 28.3 us  [the longest x1 18.4 us: local(): query = (query, lax.ppermute(query, 'xh', shift(XH, 1)))]
    ppermute x1, waiting for transfers between devices: 4.71 us -> 0.01 us  [local(): before_low = lax.ppermute(low, 'y', shift(NY, 1))]
    all_to_all x1, blocking collectives: 13.3 us -> 16.5 us  [local(): heads = lax.all_to_all(heads, 'z', 0, 0, tiled=True)[:HEADS]]
    dynamic_slice x2 -> x1, local copies, waits for them, and re-layouts: 7.13 us -> 5.28 us  [w_columns(): lax.dynamic_slice(w, (0, (to_xl * NC + to_c) * width), (w.shape[0], width))]
    all_to_all x1, waiting for transfers between devices: 8.79 us -> 10.3 us  [local(): slots = lax.all_to_all(slots, 'z', 0, 0, tiled=True)]
    ppermute x1, starting transfers between devices: 1.38 us -> 2.73 us  [local(): after_low = lax.ppermute(low, 'y', shift(NY, -1))]
  transfers between devices with their start and end apart: 16 -> 16, of which waited for: 8 -> 6; matrix products, arithmetic and copies ran while one was open for 10% -> 6% of each run, Pallas kernels for 18% -> 16%
where the time goes in v8:
time: 124 us; the launch traced here: 123 us
  waiting for transfers between devices  39.8 us (32%)
  starting transfers between devices  35.5 us (29%)
  Pallas kernels  23.5 us (19%)
  blocking collectives  16.5 us (13%)
  local copies, waits for them, and re-layouts  7.33 us (6%)
    ppermute x1, waiting for transfers between devices, local(): query = (query, lax.ppermute(query, 'xh', shift(XH, 1)))  18.4 us
    all_to_all x1, blocking collectives, local(): heads = lax.all_to_all(heads, 'z', 0, 0, tiled=True)[:HEADS]  16.5 us
    pallas_call x3, Pallas kernels, attend(): pl.pallas_call(kernel, out_shape=parcels if last else (whole, whole, whol...  13.2 us
    all_to_all x1, waiting for transfers between devices, local(): slots = lax.all_to_all(slots, 'z', 0, 0, tiled=True)  10.3 us
    all_to_all x1, starting transfers between devices, local(): slots = lax.all_to_all(slots, 'z', 0, 0, tiled=True)  9.03 us
    ppermute x1, waiting for transfers between devices, local(): there_stats = lax.ppermute(sent_stats, 'xh', shift(XH, 1))  6.56 us
    dynamic_slice x1, local copies, waits for them, and re-layouts, w_columns(): lax.dynamic_slice(w, (0, (to_xl * NC + to_c) * width), (w.shape[0], width))  5.28 us
    pallas_call x1, Pallas kernels, live_tiles(): pl.pallas_call(tiles_kernel, out_shape=tuple(out_shape), in_specs=in_smem...  4.3 us
  transfers between devices with their start and end apart: 16, of which 6 were waited for; matrix products, arithmetic and copies ran while one was open for 6% of the time, Pallas kernels for 16%

profile of v8, /device:TPU:1, one launch (start us, length us, event | category | flops | bytes accessed | tf_op | source)
XLA Modules:
  0.0 122.9 jit_solution(12246165805239779115)
XLA Ops:
  0.0 1.9 %shard_map.55 = bf16[8,384,128]{2,1,0:T(8,128)(2,1)} custom-call(bf16[128,640]{1,0:T(8,128)(2,1)} %q_hbm.1, bf16[128,640]{1,0:T(8,128)(2,1)} %k_hbm.1, bf16[128,640]{1,0:T(8,128)(2,1)} %v_hbm.1), custom_call_target="tpu_custom_call" | custom-call | tf_op jit(solution)/shard_map/pallas_call | solution.py:53
  1.9 9.0 %all-to-all-start = ((bf16[8,384,128]{2,1,0:T(8,128)(2,1)}), bf16[8,384,128]{2,1,0:T(8,128)(2,1)}, u32[]{:S(2)}, u32[]{:S(2)}) async-start(bf16[8,384,128]{2,1,0:T(8,128)(2,1)} %shard_map.55), calls=%async_computation | async-start | bytes 1572864 | tf_op jit(solution)/shard_map/all_to_all | solution.py:355
  10.9 5.3 %constant_dynamic-slice_fusion = (bf16[640,1280]{1,0:T(8,128)(2,1)}, bf16[640,1280]{1,0:T(8,128)(2,1)}, bf16[640,1280]{1,0:T(8,128)(2,1)}, bf16[640,1280]{1,0:T(8,128)(2,1)S(1)}) fusion(bf16[640,5120]{1,0:T(8,128)(2,1)} %param.9, s32[]{:T(128)S(6)} %select_n.15, s32[]{:T(128)S(6)} %select_n.14, s32[]{:T(128)S(6)} %select_n.13, s32[]{:T(128)S(6)} %select_n.12), kind=kLoop, calls=%fused_computation | loop fusion | bytes 13107216 | tf_op jit(solution)/shard_map/dynamic_slice | solution.py:332
  17.4 2.6 %collective-permute-start.8 = (bf16[640,1280]{1,0:T(8,128)(2,1)}, bf16[640,1280]{1,0:T(8,128)(2,1)}, u32[]{:S(2)}, u32[]{:S(2)}) collective-permute-start(bf16[640,1280]{1,0:T(8,128)(2,1)} %get-tuple-element.103), channel_id=1, source_target_pairs={{0,131},{1,130},{2,1},{3,0},{128,3},{129,2},{130,129},{131,128},{4... | collective-permute-start | bytes 4915208 | tf_op jit(solution)/shard_map/ppermute | solution.py:350
  20.0 4.3 %shard_map.56 = (s32[1]{0:T(128)}, s32[256]{0:T(256)S(1)}, s32[256]{0:T(256)S(1)}, s32[1]{0:T(128)}, s32[384]{0:T(512)S(1)}, /*index=5*/s32[384]{0:T(512)S(1)}, s32[1]{0:T(128)}, s32[256]{0:T(256)S(1)}, s32[256]{0:T(256)S(1)}) custom-call(s32[64,64]{1,0:T(8,128)S(1)} %copy-done), custom_call_target="tpu_custom_call" | custom-call | flops 1000000 | bytes 100000 | tf_op jit(solution)/shard_map/pallas_call | solution.py:315
  24.3 10.3 %all-to-all-done = bf16[8,384,128]{2,1,0:T(8,128)(2,1)} async-done(((bf16[8,384,128]{2,1,0:T(8,128)(2,1)}), bf16[8,384,128]{2,1,0:T(8,128)(2,1)}, u32[]{:S(2)}, u32[]{:S(2)}) %all-to-all-start) | async-done | bytes 786464 | tf_op jit(solution)/shard_map/all_to_all | solution.py:355
  36.7 2.8 %collective-permute-start = (bf16[8,128,128]{2,1,0:T(8,128)(2,1)S(1)}, bf16[8,128,128]{2,1,0:T(8,128)(2,1)S(1)}, u32[]{:S(2)}, u32[]{:S(2)}) collective-permute-start(bf16[8,128,128]{2,1,0:T(8,128)(2,1)S(1)} %slice.14.own_ref), channel_id=1, source_target_pairs={{0,128},{128,0},{1,129},{129,1},{2,130},{130,2},{3,131},{131,3},{4... | collective-permute-start | bytes 786440 | tf_op jit(solution)/shard_map/ppermute | solution.py:362
  39.5 1.3 %collective-permute-start.1 = (bf16[4,256,128]{2,1,0:T(8,128)(2,1)S(1)}, bf16[4,256,128]{2,1,0:T(8,128)(2,1)S(1)}, u32[]{:S(2)}, u32[]{:S(2)}) collective-permute-start(bf16[4,256,128]{2,1,0:T(8,128)(2,1)S(1)} %get-tuple-element.79.refs_0_), channel_id=1, source_target_pairs={{0,4},{4,8},{8,12},{12,0},{1,5},{5,9},{9,13},{13,1},{2,6},{6,10},{... | collective-permute-start | bytes 786440 | tf_op jit(solution)/shard_map/ppermute | solution.py:359
  40.8 1.4 %collective-permute-start.2 = (bf16[4,256,128]{2,1,0:T(8,128)(2,1)S(1)}, bf16[4,256,128]{2,1,0:T(8,128)(2,1)S(1)}, u32[]{:S(2)}, u32[]{:S(2)}) collective-permute-start(bf16[4,256,128]{2,1,0:T(8,128)(2,1)S(1)} %get-tuple-element.80.refs_1_), channel_id=1, source_target_pairs={{0,12},{4,0},{8,4},{12,8},{1,13},{5,1},{9,5},{13,9},{2,14},{6,2},{... | collective-permute-start | bytes 786440 | tf_op jit(solution)/shard_map/ppermute | solution.py:360
  42.2 18.4 %collective-permute-done.other_ref = bf16[8,128,128]{2,1,0:T(8,128)(2,1)S(1)} collective-permute-done((bf16[8,128,128]{2,1,0:T(8,128)(2,1)S(1)}, bf16[8,128,128]{2,1,0:T(8,128)(2,1)S(1)}, u32[]{:S(2)}, u32[]{:S(2)}) %collective-permute-start) | collective-permute-done | bytes 262176 | tf_op jit(solution)/shard_map/ppermute | solution.py:362
  60.6 2.7 %collective-permute-start.6 = (bf16[4,256,128]{2,1,0:T(8,128)(2,1)S(1)}, bf16[4,256,128]{2,1,0:T(8,128)(2,1)S(1)}, u32[]{:S(2)}, u32[]{:S(2)}) collective-permute-start(bf16[4,256,128]{2,1,0:T(8,128)(2,1)S(1)} %get-tuple-element.79.refs_0_), channel_id=1, source_target_pairs={{0,12},{4,0},{8,4},{12,8},{1,13},{5,1},{9,5},{13,9},{2,14},{6,2},{... | collective-permute-start | bytes 786440 | tf_op jit(solution)/shard_map/ppermute | solution.py:364
  63.3 4.2 %shard_map.57 = (f32[16,128,128]{2,1,0:T(8,128)S(1)}, f32[16,128,128]{2,1,0:T(8,128)S(1)}, f32[16,128,128]{2,1,0:T(8,128)S(1)}) custom-call(s32[1]{0:T(128)} %get-tuple-element.81.count_ref, s32[256]{0:T(256)S(1)} %get-tuple-element.82.block_ref, s32[256]{0:T(256)S(1)} %get-tuple-element.83.slot_ref, bf16[8,128,128]{2,1,0:T(8,128)(2,1)S(1)} %slice.14.own_ref, ...), custom_call_target="tpu_custom_call" | custom-call | flops 335544320 | bytes 6291456 | tf_op jit(solution)/shard_map/pallas_call | solution.py:192
  67.7 2.8 %collective-permute-start.4 = (bf16[4,256,128]{2,1,0:T(8,128)(2,1)S(1)}, bf16[4,256,128]{2,1,0:T(8,128)(2,1)S(1)}, u32[]{:S(2)}, u32[]{:S(2)}) collective-permute-start(bf16[4,256,128]{2,1,0:T(8,128)(2,1)S(1)} %collective-permute-done.2.refs_3_), channel_id=1, source_target_pairs={{0,12},{4,0},{8,4},{12,8},{1,13},{5,1},{9,5},{13,9},{2,14},{6,2},{... | collective-permute-start | bytes 786440 | tf_op jit(solution)/shard_map/ppermute | solution.py:368
  70.5 5.5 %shard_map.58 = (f32[16,128,128]{2,1,0:T(8,128)S(1)}, f32[16,128,128]{2,1,0:T(8,128)S(1)}, f32[16,128,128]{2,1,0:T(8,128)S(1)}) custom-call(s32[1]{0:T(128)} %get-tuple-element.89.count_ref, s32[384]{0:T(512)S(1)} %get-tuple-element.90.block_ref, s32[384]{0:T(512)S(1)} %get-tuple-element.91.slot_ref, bf16[8,128,128]{2,1,0:T(8,128)(2,1)S(1)} %slice.14.own_ref, ...), custom_call_target="tpu_custom_call" | custom-call | flops 671088640 | bytes 6291456 | tf_op jit(solution)/shard_map/pallas_call | solution.py:192
  77.1 3.5 %shard_map.59 = (f32[8,128,128]{2,1,0:T(8,128)S(1)}, f32[128,128]{1,0:T(8,128)S(1)}, bf16[8,128,128]{2,1,0:T(8,128)(2,1)S(1)}, f32[16,128]{1,0:T(8,128)S(1)}) custom-call(s32[1]{0:T(128)} %get-tuple-element.74.count_ref, s32[256]{0:T(256)S(1)} %get-tuple-element.75.block_ref, s32[256]{0:T(256)S(1)} %get-tuple-element.76.slot_ref, ...), custom_call_target="tpu_custom_call" | custom-call | flops 335544320 | bytes 6291456 | tf_op jit(solution)/shard_map/pallas_call | solution.py:192
  80.6 3.0 %collective-permute-start.13 = (bf16[640,1280]{1,0:T(8,128)(2,1)S(1)}, bf16[640,1280]{1,0:T(8,128)(2,1)S(1)}, u32[]{:S(2)}, u32[]{:S(2)}) collective-permute-start(bf16[640,1280]{1,0:T(8,128)(2,1)S(1)} %copy-done.1), channel_id=1, source_target_pairs={{0,1},{1,0},{2,3},{3,2},{4,5},{5,4},{6,7},{7,6},{8,9},{9,8},{10,11... | collective-permute-start | bytes 4915208 | tf_op jit(solution)/shard_map/ppermute | solution.py:376
  84.6 2.0 %collective-permute-start.10 = (f32[16,128]{1,0:T(8,128)S(1)}, f32[16,128]{1,0:T(8,128)S(1)}, u32[]{:S(2)}, u32[]{:S(2)}) collective-permute-start(f32[16,128]{1,0:T(8,128)S(1)} %get-tuple-element.105), channel_id=1, source_target_pairs={{0,128},{128,0},{1,129},{129,1},{2,130},{130,2},{3,131},{131,3},{4... | collective-permute-start | bytes 24584 | tf_op jit(solution)/shard_map/ppermute | solution.py:378
  86.6 6.6 %collective-permute-done.10.there_stats_ref = f32[16,128]{1,0:T(8,128)S(1)} collective-permute-done((f32[16,128]{1,0:T(8,128)S(1)}, f32[16,128]{1,0:T(8,128)S(1)}, u32[]{:S(2)}, u32[]{:S(2)}) %collective-permute-start.10) | collective-permute-done | bytes 8224 | tf_op jit(solution)/shard_map/ppermute | solution.py:378
  93.8 16.5 %all_to_all.10 = bf16[8,128,128]{2,1,0:T(8,128)(2,1)S(1)} all-to-all(bf16[8,128,128]{2,1,0:T(8,128)(2,1)S(1)} %shard_map.60), channel_id=1, replica_groups=mesh['xh'=2,'z'=8,'y'=4,'xl'=2,'c'=2] {'z'}, dimensions={0} | all-to-all | bytes 524288 | tf_op jit(solution)/shard_map/all_to_all | solution.py:380
  110.3 2.7 %collective-permute-start.12 = (bf16[5,128,128]{2,1,0:T(8,128)(2,1)S(1)}, bf16[5,128,128]{2,1,0:T(8,128)(2,1)S(1)}, u32[]{:S(2)}, u32[]{:S(2)}) collective-permute-start(bf16[5,128,128]{2,1,0:T(8,128)(2,1)S(1)} %slice.16.a_ref), channel_id=1, source_target_pairs={{0,1},{1,0},{2,3},{3,2},{4,5},{5,4},{6,7},{7,6},{8,9},{9,8},{10,11... | collective-permute-start | bytes 491528 | tf_op jit(solution)/shard_map/ppermute | solution.py:382
  113.1 2.1 %collective-permute-start.11 = (bf16[5,128,128]{2,1,0:T(8,128)(2,1)S(1)}, bf16[5,128,128]{2,1,0:T(8,128)(2,1)S(1)}, u32[]{:S(2)}, u32[]{:S(2)}) collective-permute-start(bf16[5,128,128]{2,1,0:T(8,128)(2,1)S(1)} %slice.16.a_ref), channel_id=1, source_target_pairs={{0,2},{2,0},{1,3},{3,1},{4,6},{6,4},{5,7},{7,5},{8,10},{10,8},{9,1... | collective-permute-start | bytes 491528 | tf_op jit(solution)/shard_map/ppermute | solution.py:381
  115.1 2.1 %shard_map.61 = (f32[128,1280]{1,0:T(8,128)S(1)}, bf16[640,1280]{1,0:T(8,128)(2,1)S(1)}, bf16[640,1280]{1,0:T(8,128)(2,1)S(1)}) custom-call(bf16[5,128,128]{2,1,0:T(8,128)(2,1)S(1)} %slice.16.a_ref, bf16[5,128,128]{2,1,0:T(8,128)(2,1)S(1)} %collective-permute-done.12.b_ref, bf16[640,1280]{1,0:T(8,128)(2,1)S(1)} %get-tuple-element.106.w_ref, ...), custom_call_target="tpu_custom_call" | custom-call | flops 419430400 | bytes 4194304 | tf_op jit(solution)/shard_map/pallas_call | solution.py:268
  117.2 2.4 %collective-permute-done.11.a_ref = bf16[5,128,128]{2,1,0:T(8,128)(2,1)S(1)} collective-permute-done((bf16[5,128,128]{2,1,0:T(8,128)(2,1)S(1)}, bf16[5,128,128]{2,1,0:T(8,128)(2,1)S(1)}, u32[]{:S(2)}, u32[]{:S(2)}) %collective-permute-start.11) | collective-permute-done | bytes 163872 | tf_op jit(solution)/shard_map/ppermute | solution.py:381
  121.3 1.4 %shard_map.62 = bf16[128,1280]{1,0:T(8,128)(2,1)} custom-call(bf16[5,128,128]{2,1,0:T(8,128)(2,1)S(1)} %collective-permute-done.11.a_ref, bf16[5,128,128]{2,1,0:T(8,128)(2,1)S(1)} %collective-permute-done.14.b_ref, bf16[640,1280]{1,0:T(8,128)(2,1)S(1)} %get-tuple-element.112.w_ref, bf16[640,1280]{1,0:T(8,128)(2,1)S(1)} %get-tuple-element.113.w2_ref, ...), custom_call_target="tpu_custom_call" | custom-call | flops 419430400 | bytes 4194304 | tf_op jit(solution)/shard_map/pallas_call | solution.py:268
  (25 shorter events, 7.8 us)
Async XLA Ops:
  1.9 32.7 %all-to-all-start = ((bf16[8,384,128]{2,1,0:T(8,128)(2,1)}), bf16[8,384,128]{2,1,0:T(8,128)(2,1)}, u32[]{:S(2)}, u32[]{:S(2)}) async-start(bf16[8,384,128]{2,1,0:T(8,128)(2,1)} %shard_map.55), calls=%async_computation | async-start | bytes 1572864 | tf_op jit(solution)/shard_map/all_to_all | solution.py:355
  10.9 9.1 %copy-start = (s32[64,64]{1,0:T(8,128)S(1)}, s32[64,64]{1,0:T(8,128)}, u32[]{:S(2)}) copy-start(s32[64,64]{1,0:T(8,128)} %mask_ref) | copy-start | bytes 49156
  16.2 64.4 %collective-permute-start.7 = (bf16[640,1280]{1,0:T(8,128)(2,1)}, bf16[640,1280]{1,0:T(8,128)(2,1)S(1)}, u32[]{:S(2)}, u32[]{:S(2)}) collective-permute-start(bf16[640,1280]{1,0:T(8,128)(2,1)} %get-tuple-element.102), channel_id=1, source_target_pairs={{0,2},{1,3},{2,128},{3,129},{128,130},{129,131},{130,0},{131,1},{4... | collective-permute-start | bytes 4915208 | tf_op jit(solution)/shard_map/ppermute | solution.py:347
  17.4 63.2 %collective-permute-start.8 = (bf16[640,1280]{1,0:T(8,128)(2,1)}, bf16[640,1280]{1,0:T(8,128)(2,1)}, u32[]{:S(2)}, u32[]{:S(2)}) collective-permute-start(bf16[640,1280]{1,0:T(8,128)(2,1)} %get-tuple-element.103), channel_id=1, source_target_pairs={{0,131},{1,130},{2,1},{3,0},{128,3},{129,2},{130,129},{131,128},{4... | collective-permute-start | bytes 4915208 | tf_op jit(solution)/shard_map/ppermute | solution.py:350
  36.7 23.9 %collective-permute-start = (bf16[8,128,128]{2,1,0:T(8,128)(2,1)S(1)}, bf16[8,128,128]{2,1,0:T(8,128)(2,1)S(1)}, u32[]{:S(2)}, u32[]{:S(2)}) collective-permute-start(bf16[8,128,128]{2,1,0:T(8,128)(2,1)S(1)} %slice.14.own_ref), channel_id=1, source_target_pairs={{0,128},{128,0},{1,129},{129,1},{2,130},{130,2},{3,131},{131,3},{4... | collective-permute-start | bytes 786440 | tf_op jit(solution)/shard_map/ppermute | solution.py:362
  39.5 23.8 %collective-permute-start.1 = (bf16[4,256,128]{2,1,0:T(8,128)(2,1)S(1)}, bf16[4,256,128]{2,1,0:T(8,128)(2,1)S(1)}, u32[]{:S(2)}, u32[]{:S(2)}) collective-permute-start(bf16[4,256,128]{2,1,0:T(8,128)(2,1)S(1)} %get-tuple-element.79.refs_0_), channel_id=1, source_target_pairs={{0,4},{4,8},{8,12},{12,0},{1,5},{5,9},{9,13},{13,1},{2,6},{6,10},{... | collective-permute-start | bytes 786440 | tf_op jit(solution)/shard_map/ppermute | solution.py:359
  40.8 26.8 %collective-permute-start.2 = (bf16[4,256,128]{2,1,0:T(8,128)(2,1)S(1)}, bf16[4,256,128]{2,1,0:T(8,128)(2,1)S(1)}, u32[]{:S(2)}, u32[]{:S(2)}) collective-permute-start(bf16[4,256,128]{2,1,0:T(8,128)(2,1)S(1)} %get-tuple-element.80.refs_1_), channel_id=1, source_target_pairs={{0,12},{4,0},{8,4},{12,8},{1,13},{5,1},{9,5},{13,9},{2,14},{6,2},{... | collective-permute-start | bytes 786440 | tf_op jit(solution)/shard_map/ppermute | solution.py:360
  60.6 7.1 %collective-permute-start.6 = (bf16[4,256,128]{2,1,0:T(8,128)(2,1)S(1)}, bf16[4,256,128]{2,1,0:T(8,128)(2,1)S(1)}, u32[]{:S(2)}, u32[]{:S(2)}) collective-permute-start(bf16[4,256,128]{2,1,0:T(8,128)(2,1)S(1)} %get-tuple-element.79.refs_0_), channel_id=1, source_target_pairs={{0,12},{4,0},{8,4},{12,8},{1,13},{5,1},{9,5},{13,9},{2,14},{6,2},{... | collective-permute-start | bytes 786440 | tf_op jit(solution)/shard_map/ppermute | solution.py:364
  63.3 7.1 %collective-permute-start.5 = (bf16[4,256,128]{2,1,0:T(8,128)(2,1)S(1)}, bf16[4,256,128]{2,1,0:T(8,128)(2,1)S(1)}, u32[]{:S(2)}, u32[]{:S(2)}) collective-permute-start(bf16[4,256,128]{2,1,0:T(8,128)(2,1)S(1)} %get-tuple-element.80.refs_1_), channel_id=1, source_target_pairs={{0,4},{4,8},{8,12},{12,0},{1,5},{5,9},{9,13},{13,1},{2,6},{6,10},{... | collective-permute-start | bytes 786440 | tf_op jit(solution)/shard_map/ppermute | solution.py:363
  67.6 9.5 %collective-permute-start.3 = (bf16[4,256,128]{2,1,0:T(8,128)(2,1)S(1)}, bf16[4,256,128]{2,1,0:T(8,128)(2,1)S(1)}, u32[]{:S(2)}, u32[]{:S(2)}) collective-permute-start(bf16[4,256,128]{2,1,0:T(8,128)(2,1)S(1)} %collective-permute-done.1.refs_0_), channel_id=1, source_target_pairs={{0,4},{4,8},{8,12},{12,0},{1,5},{5,9},{9,13},{13,1},{2,6},{6,10},{... | collective-permute-start | bytes 786440 | tf_op jit(solution)/shard_map/ppermute | solution.py:367
  67.7 9.4 %collective-permute-start.4 = (bf16[4,256,128]{2,1,0:T(8,128)(2,1)S(1)}, bf16[4,256,128]{2,1,0:T(8,128)(2,1)S(1)}, u32[]{:S(2)}, u32[]{:S(2)}) collective-permute-start(bf16[4,256,128]{2,1,0:T(8,128)(2,1)S(1)} %collective-permute-done.2.refs_3_), channel_id=1, source_target_pairs={{0,12},{4,0},{8,4},{12,8},{1,13},{5,1},{9,5},{13,9},{2,14},{6,2},{... | collective-permute-start | bytes 786440 | tf_op jit(solution)/shard_map/ppermute | solution.py:368
  77.1 3.5 %copy-start.1 = (bf16[640,1280]{1,0:T(8,128)(2,1)S(1)}, bf16[640,1280]{1,0:T(8,128)(2,1)}, u32[]{:S(2)}) copy-start(bf16[640,1280]{1,0:T(8,128)(2,1)} %get-tuple-element.107) | copy-start | bytes 4915204
  80.6 34.5 %collective-permute-start.13 = (bf16[640,1280]{1,0:T(8,128)(2,1)S(1)}, bf16[640,1280]{1,0:T(8,128)(2,1)S(1)}, u32[]{:S(2)}, u32[]{:S(2)}) collective-permute-start(bf16[640,1280]{1,0:T(8,128)(2,1)S(1)} %copy-done.1), channel_id=1, source_target_pairs={{0,1},{1,0},{2,3},{3,2},{4,5},{5,4},{6,7},{7,6},{8,9},{9,8},{10,11... | collective-permute-start | bytes 4915208 | tf_op jit(solution)/shard_map/ppermute | solution.py:376
  83.6 9.6 %collective-permute-start.9 = (bf16[8,128,128]{2,1,0:T(8,128)(2,1)S(1)}, bf16[8,128,128]{2,1,0:T(8,128)(2,1)S(1)}, u32[]{:S(2)}, u32[]{:S(2)}) collective-permute-start(bf16[8,128,128]{2,1,0:T(8,128)(2,1)S(1)} %get-tuple-element.104), channel_id=1, source_target_pairs={{0,128},{128,0},{1,129},{129,1},{2,130},{130,2},{3,131},{131,3},{4... | collective-permute-start | bytes 786440 | tf_op jit(solution)/shard_map/ppermute | solution.py:377
  84.6 8.6 %collective-permute-start.10 = (f32[16,128]{1,0:T(8,128)S(1)}, f32[16,128]{1,0:T(8,128)S(1)}, u32[]{:S(2)}, u32[]{:S(2)}) collective-permute-start(f32[16,128]{1,0:T(8,128)S(1)} %get-tuple-element.105), channel_id=1, source_target_pairs={{0,128},{128,0},{1,129},{129,1},{2,130},{130,2},{3,131},{131,3},{4... | collective-permute-start | bytes 24584 | tf_op jit(solution)/shard_map/ppermute | solution.py:378
  110.3 4.8 %collective-permute-start.12 = (bf16[5,128,128]{2,1,0:T(8,128)(2,1)S(1)}, bf16[5,128,128]{2,1,0:T(8,128)(2,1)S(1)}, u32[]{:S(2)}, u32[]{:S(2)}) collective-permute-start(bf16[5,128,128]{2,1,0:T(8,128)(2,1)S(1)} %slice.16.a_ref), channel_id=1, source_target_pairs={{0,1},{1,0},{2,3},{3,2},{4,5},{5,4},{6,7},{7,6},{8,9},{9,8},{10,11... | collective-permute-start | bytes 491528 | tf_op jit(solution)/shard_map/ppermute | solution.py:382
  113.1 6.5 %collective-permute-start.11 = (bf16[5,128,128]{2,1,0:T(8,128)(2,1)S(1)}, bf16[5,128,128]{2,1,0:T(8,128)(2,1)S(1)}, u32[]{:S(2)}, u32[]{:S(2)}) collective-permute-start(bf16[5,128,128]{2,1,0:T(8,128)(2,1)S(1)} %slice.16.a_ref), channel_id=1, source_target_pairs={{0,2},{2,0},{1,3},{3,1},{4,6},{6,4},{5,7},{7,5},{8,10},{10,8},{9,1... | collective-permute-start | bytes 491528 | tf_op jit(solution)/shard_map/ppermute | solution.py:381
  119.6 1.7 %collective-permute-start.14 = (bf16[5,128,128]{2,1,0:T(8,128)(2,1)S(1)}, bf16[5,128,128]{2,1,0:T(8,128)(2,1)S(1)}, u32[]{:S(2)}, u32[]{:S(2)}) collective-permute-start(bf16[5,128,128]{2,1,0:T(8,128)(2,1)S(1)} %collective-permute-done.11.a_ref), channel_id=1, source_target_pairs={{0,1},{1,0},{2,3},{3,2},{4,5},{5,4},{6,7},{7,6},{8,9},{9,8},{10,11... | collective-permute-start | bytes 491528 | tf_op jit(solution)/shard_map/ppermute | solution.py:385

commit v9 on v8

--- a/solution.py
+++ b/solution.py
@@ -113,37 +113,78 @@
     lax.fori_loop(0, (count + (UNROLL - 1)) // UNROLL, mix, 0)
 
 
-def write_parcels(m_ref, l_ref, a_ref, keep_ref, keep_stats_ref, send_ref, send_stats_ref):
-    plane = lax.axis_index("xh")
+def stats_of(m_ref, l_ref):
     lane = lax.broadcasted_iota(jnp.int32, (BLOCK, BLOCK), 1)
-
-    def stats_of(first):
-        stats = jnp.zeros((BLOCK, BLOCK), jnp.float32)
+    stats = jnp.zeros((BLOCK, BLOCK), jnp.float32)
+    for i in range(NZ):
+        total = jnp.sum(l_ref[i], axis=1, keepdims=True)
+        stats = jnp.where(lane == i, m_ref[i], stats)
+        stats = jnp.where(lane == NZ + i, total, stats)
+    return stats
+
+
+def hold_parts(parts, kv_ref):
+    at = 0
+    for part in parts:
+        kv_ref[at : at + part.shape[0]] = part[...]
+        at += part.shape[0]
+
+
+def attend_last(tables, query, parts, state, mine):
+    slots = sum(part.shape[0] for part in parts)
+
+    def kernel(count_ref, block_ref, slot_ref, q_ref, *refs):
+        part_refs, refs = refs[: len(parts)], refs[len(parts) :]
+        (m_in, l_in, a_in), refs = refs[:3], refs[3:]
+        sums_ref, stats_ref, kv_ref, s_ref, top_ref, m_ref, l_ref, a_ref = refs
+        tables = (block_ref, slot_ref)
+        plane = lax.axis_index("xh")
+        first = (plane if mine else 1 - plane) * NZ
+        hold_parts(part_refs, kv_ref)
+        count = count_ref[0]
+        top_ref[...] = jnp.full(top_ref.shape, LOW, jnp.float32)
+        score_tiles(count, tables, q_ref, kv_ref, s_ref, top_ref)
         for i in range(NZ):
-            total = jnp.sum(l_ref[first + i], axis=1, keepdims=True)
-            stats = jnp.where(lane == i, m_ref[first + i], stats)
-            stats = jnp.where(lane == NZ + i, total, stats)
-        return stats
-
-    own, other = plane * NZ, (1 - plane) * NZ
-    for i in range(NZ):
-        keep_ref[i] = a_ref[own + i]
-        send_ref[i] = a_ref[other + i].astype(jnp.bfloat16)
-    keep_stats_ref[...] = stats_of(own)
-    send_stats_ref[...] = stats_of(other).T[: 2 * NZ]
-
-
-def attend(tables, query, parts, state, last):
+            top = jnp.max(top_ref[i], axis=1, keepdims=True)
+            old = m_in[first + i]
+            new = jnp.maximum(old, top)
+            fade = jnp.exp2((old - new) * EXP2_SCALE)
+            m_ref[i] = new
+            l_ref[i] = l_in[first + i] * fade
+            a_ref[i] = a_in[first + i] * fade
+        mix_tiles(count, tables, kv_ref, s_ref, m_ref, l_ref, a_ref)
+        sums_ref[...] = a_ref[...].astype(sums_ref.dtype)
+        stats = stats_of(m_ref, l_ref)
+        stats_ref[...] = stats if mine else stats.T[: 2 * NZ]
+
+    half = pltpu.VMEM((NZ, BLOCK, BLOCK), jnp.float32)
+    return pl.pallas_call(
+        kernel,
+        out_shape=(
+            jax.ShapeDtypeStruct((NZ, BLOCK, HEAD_DIM), jnp.float32 if mine else jnp.bfloat16),
+            jax.ShapeDtypeStruct((BLOCK if mine else 2 * NZ, BLOCK), jnp.float32),
+        ),
+        in_specs=in_smem(3) + in_vmem(1 + len(parts) + 3),
+        out_specs=tuple(in_vmem(2)),
+        scratch_shapes=[
+            pltpu.VMEM((slots, 2 * BLOCK, HEAD_DIM), jnp.bfloat16),
+            pltpu.VMEM((NZ * slots, BLOCK, BLOCK), jnp.float32),
+            half,
+            half,
+            half,
+            half,
+        ],
+        compiler_params=pltpu.CompilerParams(vmem_limit_bytes=28 * MIB),
+        cost_estimate=pl.CostEstimate(
+            flops=20 * 2 * 128**3, bytes_accessed=3 * MIB, transcendentals=10 * 128 * 128
+        ),
+    )(*tables, query, *parts, *state)
+
+
+def attend(tables, query, parts, state):
     first = state is None
     slots = sum(part.shape[0] for part in parts)
-    most = ROWS * slots
     whole = jax.ShapeDtypeStruct((ROWS, BLOCK, BLOCK), jnp.float32)
-    parcels = (
-        jax.ShapeDtypeStruct((NZ, BLOCK, HEAD_DIM), jnp.float32),
-        jax.ShapeDtypeStruct((BLOCK, BLOCK), jnp.float32),
-        jax.ShapeDtypeStruct((NZ, BLOCK, HEAD_DIM), jnp.bfloat16),
-        jax.ShapeDtypeStruct((2 * NZ, BLOCK), jnp.float32),
-    )
 
     def kernel(count_ref, block_ref, slot_ref, own_ref, other_ref, *refs):
         tables = (block_ref, slot_ref)
@@ -151,17 +192,10 @@
         part_refs, refs = refs[: len(parts)], refs[len(parts) :]
         if not first:
             (m_in, l_in, a_in), refs = refs[:3], refs[3:]
-        if last:
-            parcel_refs, refs = refs[:4], refs[4:]
-            q_ref, kv_ref, s_ref, top_ref, m_ref, l_ref, a_ref = refs
-        else:
-            m_ref, l_ref, a_ref, q_ref, kv_ref, s_ref, top_ref = refs
+        m_ref, l_ref, a_ref, q_ref, kv_ref, s_ref, top_ref = refs
         q_ref[pl.ds(plane * NZ, NZ)] = own_ref[...]
         q_ref[pl.ds((1 - plane) * NZ, NZ)] = other_ref[...]
-        at = 0
-        for part in part_refs:
-            kv_ref[at : at + part.shape[0]] = part[...]
-            at += part.shape[0]
+        hold_parts(part_refs, kv_ref)
         count = count_ref[0]
         top_ref[...] = jnp.full(top_ref.shape, LOW, jnp.float32)
         score_tiles(count, tables, q_ref, kv_ref, s_ref, top_ref)
@@ -178,23 +212,18 @@
                 l_ref[block] = l_in[block] * fade
                 a_ref[block] = a_in[block] * fade
         mix_tiles(count, tables, kv_ref, s_ref, m_ref, l_ref, a_ref)
-        if last:
-            write_parcels(m_ref, l_ref, a_ref, *parcel_refs)
-
-    scratch = [
-        pltpu.VMEM((ROWS, BLOCK, HEAD_DIM), jnp.bfloat16),
-        pltpu.VMEM((slots, 2 * BLOCK, HEAD_DIM), jnp.bfloat16),
-        pltpu.VMEM((most, BLOCK, BLOCK), jnp.float32),
-        pltpu.VMEM((ROWS, BLOCK, BLOCK), jnp.float32),
-    ]
-    if last:
-        scratch += [pltpu.VMEM((ROWS, BLOCK, BLOCK), jnp.float32)] * 3
+
     return pl.pallas_call(
         kernel,
-        out_shape=parcels if last else (whole, whole, whole),
+        out_shape=(whole, whole, whole),
         in_specs=in_smem(3) + in_vmem(2 + len(parts) + (0 if first else 3)),
-        out_specs=tuple(in_vmem(4 if last else 3)),
-        scratch_shapes=scratch,
+        out_specs=tuple(in_vmem(3)),
+        scratch_shapes=[
+            pltpu.VMEM((ROWS, BLOCK, HEAD_DIM), jnp.bfloat16),
+            pltpu.VMEM((slots, 2 * BLOCK, HEAD_DIM), jnp.bfloat16),
+            pltpu.VMEM((ROWS * slots, BLOCK, BLOCK), jnp.float32),
+            pltpu.VMEM((ROWS, BLOCK, BLOCK), jnp.float32),
+        ],
         compiler_params=pltpu.CompilerParams(vmem_limit_bytes=28 * MIB),
         cost_estimate=pl.CostEstimate(
             flops=len(parts) * 40 * 2 * 128**3,
@@ -229,69 +258,80 @@
     )(here, here_stats, there, there_stats)
 
 
-def project(a, b, w_own, w_other, added=None, staged=()):
+def project(a, b, w_own, w_other, dtype):
     deep, width = w_own.shape
-    final = added is not None
-
-    def kernel(a_ref, b_ref, w_ref, w2_ref, *refs):
-        if final:
-            added_ref, refs = refs[0], refs[1:]
-        sources, out_ref, targets = (
-            refs[: len(staged)],
-            refs[len(staged)],
-            refs[len(staged) + 1 : 2 * len(staged) + 1],
-        )
-        rows_ref, sems = refs[2 * len(staged) + 1 :]
-        copies = [
-            pltpu.make_async_copy(source, target, sems.at[i])
-            for i, (source, target) in enumerate(zip(sources, targets))
-        ]
-        for copy in copies:
-            copy.start()
+    tiles = width // TILE_N
+
+    def kernel(a_ref, b_ref, w_hbm, w2_hbm, out_ref, rows_ref, w_ref, sems):
+        copies = []
+        for tile in range(tiles):
+            lanes = pl.ds(tile * TILE_N, TILE_N)
+            for which, source in enumerate((w_hbm, w2_hbm)):
+                copies.append(
+                    pltpu.make_async_copy(
+                        source.at[:, lanes], w_ref.at[which, tile], sems.at[which, tile]
+                    )
+                )
+                copies[-1].start()
         for which, ref in enumerate((a_ref, b_ref)):
             for head in range(HEADS):
                 at = (which * HEADS + head) * HEAD_DIM
                 rows_ref[:, at : at + HEAD_DIM] = ref[head]
-        for at in range(0, width, TILE_N):
-            lanes = slice(at, at + TILE_N)
-            out = jnp.dot(rows_ref[:, :deep], w_ref[:, lanes], preferred_element_type=jnp.float32)
+        for tile in range(tiles):
+            copies[2 * tile].wait()
+            copies[2 * tile + 1].wait()
+            out = jnp.dot(rows_ref[:, :deep], w_ref[0, tile], preferred_element_type=jnp.float32)
             out = out + jnp.dot(
-                rows_ref[:, deep:], w2_ref[:, lanes], preferred_element_type=jnp.float32
+                rows_ref[:, deep:], w_ref[1, tile], preferred_element_type=jnp.float32
             )
-            if final:
-                out = out + added_ref[:, lanes]
-            out_ref[:, lanes] = out.astype(out_ref.dtype)
-        for copy in copies:
-            copy.wait()
-
-    out = jax.ShapeDtypeStruct((BLOCK, width), jnp.bfloat16 if final else jnp.float32)
+            out_ref[:, tile * TILE_N : (tile + 1) * TILE_N] = out.astype(out_ref.dtype)
+
+    anywhere = pl.BlockSpec(memory_space=pl.ANY)
     return pl.pallas_call(
         kernel,
-        out_shape=(out,) + tuple(jax.ShapeDtypeStruct(x.shape, x.dtype) for x in staged),
-        in_specs=in_vmem(5 if final else 4) + [pl.BlockSpec(memory_space=pl.ANY)] * len(staged),
-        out_specs=tuple(in_vmem(1 + len(staged))),
+        out_shape=jax.ShapeDtypeStruct((BLOCK, width), dtype),
+        in_specs=in_vmem(2) + [anywhere] * 2,
+        out_specs=in_vmem(1)[0],
         scratch_shapes=[
             pltpu.VMEM((BLOCK, 2 * deep), jnp.bfloat16),
-            pltpu.SemaphoreType.DMA((max(len(staged), 1),)),
+            pltpu.VMEM((2, tiles, deep, TILE_N), jnp.bfloat16),
+            pltpu.SemaphoreType.DMA((2, tiles)),
         ],
-        compiler_params=pltpu.CompilerParams(vmem_limit_bytes=8 * MIB),
+        compiler_params=pltpu.CompilerParams(vmem_limit_bytes=12 * MIB),
         cost_estimate=pl.CostEstimate(
             flops=2 * BLOCK * 2 * deep * width, bytes_accessed=4 * MIB, transcendentals=0
         ),
-    )(a, b, w_own, w_other, *((added,) if final else ()), *staged)
-
-
-GROUPS = ((0,), (1, 3), (2,))
+    )(a, b, w_own, w_other)
+
+
+def add_kernel(near_ref, far_ref, out_ref):
+    out_ref[...] = (near_ref[...] + far_ref[...].astype(jnp.float32)).astype(out_ref.dtype)
+
+
+def add(near, far):
+    return pl.pallas_call(
+        add_kernel,
+        out_shape=jax.ShapeDtypeStruct(near.shape, jnp.bfloat16),
+        in_specs=in_vmem(2),
+        out_specs=in_vmem(1)[0],
+        compiler_params=pltpu.CompilerParams(vmem_limit_bytes=4 * MIB),
+    )(near, far)
+
+
+GROUPS = (((0,), None), ((1, 3), None), ((2,), 1), ((2,), 0))
 
 
 def tiles_kernel(mask_ref, *refs):
     y, plane = lax.axis_index("y"), lax.axis_index("xh")
-    for group, columns in enumerate(GROUPS):
+    for group, (columns, on) in enumerate(GROUPS):
         count_ref, block_ref, slot_ref = refs[3 * group : 3 * group + 3]
-
-        def one_query_block(block, at, columns=columns, refs=(block_ref, slot_ref)):
+        first_block = 0 if on is None else ((plane + on) & (XH - 1)) * NZ
+
+        def one_query_block(
+            block, at, columns=columns, refs=(block_ref, slot_ref), first_block=first_block
+        ):
             block_ref, slot_ref = refs
-            row = block * NY + y
+            row = (first_block + block) * NY + y
             for column, back in enumerate(columns):
                 first = plane * (NZ * NY) + ((y - back + NY) & (NY - 1))
                 for i in range(NZ):
@@ -300,7 +340,7 @@
                     at = at + jnp.where(mask_ref[row, first + i * NY] != 0, 1, 0)
             return at
 
-        total = lax.fori_loop(0, ROWS, one_query_block, jnp.int32(0))
+        total = lax.fori_loop(0, ROWS if on is None else NZ, one_query_block, jnp.int32(0))
         count_ref[0] = total
         for u in range(UNROLL):
             block_ref[total + u] = 0
@@ -309,8 +349,8 @@
 
 def live_tiles(frame_mask):
     out_shape = []
-    for columns in GROUPS:
-        most = ROWS * NZ * len(columns) + 128
+    for columns, on in GROUPS:
+        most = (ROWS if on is None else NZ) * NZ * len(columns) + 128
         out_shape += [jax.ShapeDtypeStruct((size,), jnp.int32) for size in (1, most, most)]
     flat = pl.pallas_call(
         tiles_kernel,
@@ -333,27 +373,13 @@
 
     slots = split(queries, keys, values)
     slots, w_out = lax.optimization_barrier((slots, w_out))
-    w_here, w_core, w_next, w_last = (
-        w_columns(w_out, xl, c),
-        w_columns(w_out, xl, 1 - c),
-        w_columns(w_out, 1 - xl, c),
-        w_columns(w_out, 1 - xl, 1 - c),
-    )
-    w_here, w_core, w_next, w_last, frame_mask = lax.optimization_barrier(
-        (w_here, w_core, w_next, w_last, frame_mask)
-    )
-    places = [(x, core_) for x in range(XH * XL) for core_ in range(NC)]
-    along_x = ("xh", "xl", "c")
-    w_next = lax.ppermute(
-        w_next, along_x, [(x * NC + k, (x + 1) % 4 * NC + k) for x, k in places]
-    )
-    w_last = lax.ppermute(
-        w_last, along_x, [(x * NC + k, (x + 3) % 4 * NC + 1 - k) for x, k in places]
-    )
+    w_own = [w_columns(w_out, to_xl, c) for to_xl in (1 - xl, xl)]
+    w_sent = [w_columns(w_out, to_xl, 1 - c) for to_xl in (1 - xl, xl)]
+    w_own, w_sent, frame_mask = lax.optimization_barrier((w_own, w_sent, frame_mask))
     groups = live_tiles(frame_mask)
 
     slots = lax.all_to_all(slots, "z", 0, 0, tiled=True)
-    slots, w_here, w_core, groups = lax.optimization_barrier((slots, w_here, w_core, groups))
+    slots, w_own, w_sent, groups = lax.optimization_barrier((slots, w_own, w_sent, groups))
     low, high = slots[: NZ // 2, BLOCK:], slots[NZ // 2 :, BLOCK:]
     slots, low, high = lax.optimization_barrier((slots, low, high))
     before_low = lax.ppermute(low, "y", shift(NY, 1))
@@ -362,28 +388,25 @@
     query = (query, lax.ppermute(query, "xh", shift(XH, 1)))
     before_high = lax.ppermute(high, "y", shift(NY, 1))
     after_low = lax.ppermute(low, "y", shift(NY, -1))
-    state = attend(groups[0], query, [low, high], None, False)
+    state = attend(groups[0], query, [low, high], None)
     before_low, after_high, state = lax.optimization_barrier((before_low, after_high, state))
     far_low = lax.ppermute(before_low, "y", shift(NY, 1))
     far_high = lax.ppermute(after_high, "y", shift(NY, -1))
-    state = attend(
-        groups[1], query, [before_low, before_high, after_low, after_high], state, False
-    )
-    here, here_stats, sent, sent_stats = attend(
-        groups[2], query, [far_low, far_high], state, True
-    )
-    sent, w_core, w_next, w_last = lax.optimization_barrier((sent, w_core, w_next, w_last))
-    w_core = lax.ppermute(w_core, "c", shift(NC, 1))
+    state = attend(groups[1], query, [before_low, before_high, after_low, after_high], state)
+    far_parts = [far_low, far_high]
+    sent, sent_stats = attend_last(groups[2], query[1], far_parts, state, False)
     there = lax.ppermute(sent, "xh", shift(XH, 1))
     there_stats = lax.ppermute(sent_stats, "xh", shift(XH, 1))
+    here, here_stats = attend_last(groups[3], query[0], far_parts, state, True)
+    here, w_sent = lax.optimization_barrier((here, w_sent))
+    w_here = [lax.ppermute(w, "c", shift(NC, 1)) for w in w_sent]
     heads = merge(here, here_stats, there, there_stats)
     heads = lax.all_to_all(heads, "z", 0, 0, tiled=True)[:HEADS]
-    heads_xl = lax.ppermute(heads, "xl", shift(XL, 1))
     heads_core = lax.ppermute(heads, "c", shift(NC, 1))
-    near, w_next, w_last = project(heads, heads_core, w_here, w_core, None, (w_next, w_last))
-    heads_xl, near = lax.optimization_barrier((heads_xl, near))
-    heads_both = lax.ppermute(heads_xl, "c", shift(NC, 1))
-    return project(heads_xl, heads_both, w_next, w_last, near)[0]
+    far = project(heads, heads_core, w_own[0], w_here[0], jnp.bfloat16)
+    far = lax.ppermute(far, "xl", shift(XL, 1))
+    near = project(heads, heads_core, w_own[1], w_here[1], jnp.float32)
+    return add(near, far)
 
 
 def solution(mesh):

time: 124 us -> 106 us (0.85)
  waiting for transfers between devices: 39.8 us -> 31.6 us
  starting transfers between devices: 35.5 us -> 28.2 us
  blocking collectives: 16.5 us -> 12.5 us
  Pallas kernels: 23.5 us -> 25.9 us
    ppermute x1, waiting for transfers between devices: 18.4 us -> 1.94 us  [local(): query = (query, lax.ppermute(query, 'xh', shift(XH, 1)))]
    ppermute x5 -> x3, starting transfers between devices: 9.54 us -> 2.86 us  [the longest x2 2.76 us: local(): w_here = [lax.ppermute(w, 'c', shift(NC, 1)) for w in w_sent]]
    all_to_all x1, blocking collectives: 16.5 us -> 12.5 us  [local(): heads = lax.all_to_all(heads, 'z', 0, 0, tiled=True)[:HEADS]]
    all_to_all x1, waiting for transfers between devices: 10.3 us -> 14.3 us  [local(): slots = lax.all_to_all(slots, 'z', 0, 0, tiled=True)]
    ppermute x5 -> x3, waiting for transfers between devices: 3.41 us -> 6.85 us  [the longest x1 6.84 us: local(): far = lax.ppermute(far, 'xl', shift(XL, 1))]
    pallas_call x5 -> x7, Pallas kernels: 16.7 us -> 18.9 us  [the longest x2 8.91 us: attend(): pl.pallas_call(kernel, out_shape=(whole, whole, whole), in_specs=in_smem(...]
    ppermute x1, starting transfers between devices: 0.08 us -> 1.78 us  [local(): far_low = lax.ppermute(before_low, 'y', shift(NY, 1))]
    ppermute x1, starting transfers between devices: 2.73 us -> 1.46 us  [local(): after_low = lax.ppermute(low, 'y', shift(NY, -1))]
  transfers between devices with their start and end apart: 16 -> 14, of which waited for: 6 -> 8; matrix products, arithmetic and copies ran while one was open for 6% -> 5% of each run, Pallas kernels for 16% -> 19%
where the time goes in v9:
time: 106 us; the launch traced here: 105 us
  waiting for transfers between devices  31.6 us (30%)
  starting transfers between devices  28.2 us (27%)
  Pallas kernels  25.9 us (24%)
  blocking collectives  12.5 us (12%)
  local copies, waits for them, and re-layouts  7.1 us (7%)
    all_to_all x1, waiting for transfers between devices, local(): slots = lax.all_to_all(slots, 'z', 0, 0, tiled=True)  14.3 us
    all_to_all x1, blocking collectives, local(): heads = lax.all_to_all(heads, 'z', 0, 0, tiled=True)[:HEADS]  12.5 us
    all_to_all x1, starting transfers between devices, local(): slots = lax.all_to_all(slots, 'z', 0, 0, tiled=True)  9.03 us
    pallas_call x2, Pallas kernels, attend(): pl.pallas_call(kernel, out_shape=(whole, whole, whole), in_specs=in_smem(...  8.91 us
    ppermute x1, waiting for transfers between devices, local(): far = lax.ppermute(far, 'xl', shift(XL, 1))  6.84 us
    ppermute x1, waiting for transfers between devices, local(): there_stats = lax.ppermute(sent_stats, 'xh', shift(XH, 1))  6.19 us
    pallas_call x2, Pallas kernels, attend_last(): pl.pallas_call(kernel, out_shape=(jax.ShapeDtypeStruct((NZ, BLOCK, HEAD_D...  5.16 us
    dynamic_slice x1, local copies, waits for them, and re-layouts, w_columns(): lax.dynamic_slice(w, (0, (to_xl * NC + to_c) * width), (w.shape[0], width))  5.03 us
  transfers between devices with their start and end apart: 14, of which 8 were waited for; matrix products, arithmetic and copies ran while one was open for 5% of the time, Pallas kernels for 19%

profile of v9, /device:TPU:1, one launch (start us, length us, event | category | flops | bytes accessed | tf_op | source)
XLA Modules:
  0.0 105.5 jit_solution(18002570771828839214)
XLA Ops:
  0.0 1.9 %shard_map.55 = bf16[8,384,128]{2,1,0:T(8,128)(2,1)} custom-call(bf16[128,640]{1,0:T(8,128)(2,1)} %q_hbm.1, bf16[128,640]{1,0:T(8,128)(2,1)} %k_hbm.1, bf16[128,640]{1,0:T(8,128)(2,1)} %v_hbm.1), custom_call_target="tpu_custom_call" | custom-call | tf_op jit(solution)/shard_map/pallas_call | solution.py:53
  1.9 9.0 %all-to-all-start = ((bf16[8,384,128]{2,1,0:T(8,128)(2,1)}), bf16[8,384,128]{2,1,0:T(8,128)(2,1)}, u32[]{:S(2)}, u32[]{:S(2)}) async-start(bf16[8,384,128]{2,1,0:T(8,128)(2,1)} %shard_map.55), calls=%async_computation | async-start | bytes 1572864 | tf_op jit(solution)/shard_map/all_to_all | solution.py:381
  11.0 5.0 %constant_dynamic-slice_fusion = (bf16[640,1280]{1,0:T(8,128)(2,1)}, bf16[640,1280]{1,0:T(8,128)(2,1)}, bf16[640,1280]{1,0:T(8,128)(2,1)S(1)}, bf16[640,1280]{1,0:T(8,128)(2,1)S(1)}) fusion(bf16[640,5120]{1,0:T(8,128)(2,1)} %param.9, s32[]{:T(128)S(6)} %select_n.15, s32[]{:T(128)S(6)} %select_n.14, s32[]{:T(128)S(6)} %select_n.13, s32[]{:T(128)S(6)} %select_n.12), kind=kLoop, calls=%fused_computation | loop fusion | bytes 13107216 | tf_op jit(solution)/shard_map/dynamic_slice | solution.py:372
  16.0 4.4 %shard_map.56 = (s32[1]{0:T(128)}, s32[256]{0:T(256)S(1)}, s32[256]{0:T(256)S(1)}, s32[1]{0:T(128)}, s32[384]{0:T(512)S(1)}, /*index=5*/s32[384]{0:T(512)S(1)}, ...) custom-call(s32[64,64]{1,0:T(8,128)S(1)} %copy-done), custom_call_target="tpu_custom_call" | custom-call | flops 1000000 | bytes 100000 | tf_op jit(solution)/shard_map/pallas_call | solution.py:355
  20.4 14.3 %all-to-all-done = bf16[8,384,128]{2,1,0:T(8,128)(2,1)} async-done(((bf16[8,384,128]{2,1,0:T(8,128)(2,1)}), bf16[8,384,128]{2,1,0:T(8,128)(2,1)}, u32[]{:S(2)}, u32[]{:S(2)}) %all-to-all-start) | async-done | bytes 786464 | tf_op jit(solution)/shard_map/all_to_all | solution.py:381
  36.7 2.8 %collective-permute-start.2 = (bf16[8,128,128]{2,1,0:T(8,128)(2,1)S(1)}, bf16[8,128,128]{2,1,0:T(8,128)(2,1)S(1)}, u32[]{:S(2)}, u32[]{:S(2)}) collective-permute-start(bf16[8,128,128]{2,1,0:T(8,128)(2,1)S(1)} %slice.14.own_ref.q_ref), channel_id=1, source_target_pairs={{0,128},{128,0},{1,129},{129,1},{2,130},{130,2},{3,131},{131,3},{4... | collective-permute-start | bytes 786440 | tf_op jit(solution)/shard_map/ppermute | solution.py:388
  39.5 1.3 %collective-permute-start = (bf16[4,256,128]{2,1,0:T(8,128)(2,1)S(1)}, bf16[4,256,128]{2,1,0:T(8,128)(2,1)S(1)}, u32[]{:S(2)}, u32[]{:S(2)}) collective-permute-start(bf16[4,256,128]{2,1,0:T(8,128)(2,1)S(1)} %get-tuple-element.86.refs_0_), channel_id=1, source_target_pairs={{0,4},{4,8},{8,12},{12,0},{1,5},{5,9},{9,13},{13,1},{2,6},{6,10},{... | collective-permute-start | bytes 786440 | tf_op jit(solution)/shard_map/ppermute | solution.py:385
  40.8 1.4 %collective-permute-start.1 = (bf16[4,256,128]{2,1,0:T(8,128)(2,1)S(1)}, bf16[4,256,128]{2,1,0:T(8,128)(2,1)S(1)}, u32[]{:S(2)}, u32[]{:S(2)}) collective-permute-start(bf16[4,256,128]{2,1,0:T(8,128)(2,1)S(1)} %get-tuple-element.87.refs_1_), channel_id=1, source_target_pairs={{0,12},{4,0},{8,4},{12,8},{1,13},{5,1},{9,5},{13,9},{2,14},{6,2},{... | collective-permute-start | bytes 786440 | tf_op jit(solution)/shard_map/ppermute | solution.py:386
  42.3 1.5 %collective-permute-start.6 = (bf16[4,256,128]{2,1,0:T(8,128)(2,1)S(1)}, bf16[4,256,128]{2,1,0:T(8,128)(2,1)S(1)}, u32[]{:S(2)}, u32[]{:S(2)}) collective-permute-start(bf16[4,256,128]{2,1,0:T(8,128)(2,1)S(1)} %get-tuple-element.86.refs_0_), channel_id=1, source_target_pairs={{0,12},{4,0},{8,4},{12,8},{1,13},{5,1},{9,5},{13,9},{2,14},{6,2},{... | collective-permute-start | bytes 786440 | tf_op jit(solution)/shard_map/ppermute | solution.py:390
  43.7 1.9 %collective-permute-done.2.other_ref.q_ref = bf16[8,128,128]{2,1,0:T(8,128)(2,1)S(1)} collective-permute-done((bf16[8,128,128]{2,1,0:T(8,128)(2,1)S(1)}, bf16[8,128,128]{2,1,0:T(8,128)(2,1)S(1)}, u32[]{:S(2)}, u32[]{:S(2)}) %collective-permute-start.2) | collective-permute-done | bytes 262176 | tf_op jit(solution)/shard_map/ppermute | solution.py:388
  45.7 3.4 %shard_map.57 = (f32[16,128,128]{2,1,0:T(8,128)S(1)}, f32[16,128,128]{2,1,0:T(8,128)S(1)}, f32[16,128,128]{2,1,0:T(8,128)S(1)}) custom-call(s32[1]{0:T(128)} %get-tuple-element.88.count_ref, s32[256]{0:T(256)S(1)} %get-tuple-element.89.block_ref, s32[256]{0:T(256)S(1)} %get-tuple-element.90.slot_ref, bf16[8,128,128]{2,1,0:T(8,128)(2,1)S(1)} %slice.14.own_ref.q_ref, ...), custom_call_target="tpu_custom_call" | custom-call | flops 335544320 | bytes 6291456 | tf_op jit(solution)/shard_map/pallas_call | solution.py:216
  49.1 1.8 %collective-permute-start.3 = (bf16[4,256,128]{2,1,0:T(8,128)(2,1)S(1)}, bf16[4,256,128]{2,1,0:T(8,128)(2,1)S(1)}, u32[]{:S(2)}, u32[]{:S(2)}) collective-permute-start(bf16[4,256,128]{2,1,0:T(8,128)(2,1)S(1)} %collective-permute-done.refs_0_), channel_id=1, source_target_pairs={{0,4},{4,8},{8,12},{12,0},{1,5},{5,9},{9,13},{13,1},{2,6},{6,10},{... | collective-permute-start | bytes 786440 | tf_op jit(solution)/shard_map/ppermute | solution.py:393
  50.9 1.5 %collective-permute-start.4 = (bf16[4,256,128]{2,1,0:T(8,128)(2,1)S(1)}, bf16[4,256,128]{2,1,0:T(8,128)(2,1)S(1)}, u32[]{:S(2)}, u32[]{:S(2)}) collective-permute-start(bf16[4,256,128]{2,1,0:T(8,128)(2,1)S(1)} %collective-permute-done.1.refs_3_), channel_id=1, source_target_pairs={{0,12},{4,0},{8,4},{12,8},{1,13},{5,1},{9,5},{13,9},{2,14},{6,2},{... | collective-permute-start | bytes 786440 | tf_op jit(solution)/shard_map/ppermute | solution.py:394
  53.5 5.5 %shard_map.58 = (f32[16,128,128]{2,1,0:T(8,128)S(1)}, f32[16,128,128]{2,1,0:T(8,128)S(1)}, f32[16,128,128]{2,1,0:T(8,128)S(1)}) custom-call(s32[1]{0:T(128)} %get-tuple-element.96.count_ref, s32[384]{0:T(512)S(1)} %get-tuple-element.97.block_ref, s32[384]{0:T(512)S(1)} %get-tuple-element.98.slot_ref, bf16[8,128,128]{2,1,0:T(8,128)(2,1)S(1)} %slice.14.own_ref.q_ref, ...), custom_call_target="tpu_custom_call" | custom-call | flops 671088640 | bytes 6291456 | tf_op jit(solution)/shard_map/pallas_call | solution.py:216
  59.3 3.0 %shard_map.59 = (f32[8,128,128]{2,1,0:T(8,128)S(1)}, f32[128,128]{1,0:T(8,128)S(1)}) custom-call(s32[1]{0:T(128)} %get-tuple-element.81.count_ref, s32[192]{0:T(256)S(1)} %get-tuple-element.82.block_ref, s32[192]{0:T(256)S(1)} %get-tuple-element.83.slot_ref, bf16[8,128,128]{2,1,0:T(8,128)(2,1)S(1)} %slice.14.own_ref.q_ref, ...), custom_call_target="tpu_custom_call" | custom-call | flops 83886080 | bytes 3145728 | tf_op jit(solution)/shard_map/pallas_call | solution.py:161
  62.3 2.7 %collective-permute-start.11 = (bf16[640,1280]{1,0:T(8,128)(2,1)S(1)}, bf16[640,1280]{1,0:T(8,128)(2,1)S(1)}, u32[]{:S(2)}, u32[]{:S(2)}) collective-permute-start(bf16[640,1280]{1,0:T(8,128)(2,1)S(1)} %copy-done.2), channel_id=1, source_target_pairs={{0,1},{1,0},{2,3},{3,2},{4,5},{5,4},{6,7},{7,6},{8,9},{9,8},{10,11... | collective-permute-start | bytes 4915208 | tf_op jit(solution)/shard_map/ppermute | solution.py:402
  65.1 2.1 %shard_map.60 = (bf16[8,128,128]{2,1,0:T(8,128)(2,1)S(1)}, f32[16,128]{1,0:T(8,128)S(1)}) custom-call(s32[1]{0:T(128)} %get-tuple-element.110.count_ref, s32[192]{0:T(256)S(1)} %get-tuple-element.111.block_ref, s32[192]{0:T(256)S(1)} %get-tuple-element.112.slot_ref, bf16[8,128,128]{2,1,0:T(8,128)(2,1)S(1)} %collective-permute-done.2.other_ref.q_ref, ...), custom_call_target="tpu_custom_call" | custom-call | flops 83886080 | bytes 3145728 | tf_op jit(solution)/shard_map/pallas_call | solution.py:161
  67.9 2.3 %collective-permute-start.8 = (f32[16,128]{1,0:T(8,128)S(1)}, f32[16,128]{1,0:T(8,128)S(1)}, u32[]{:S(2)}, u32[]{:S(2)}) collective-permute-start(f32[16,128]{1,0:T(8,128)S(1)} %get-tuple-element.114), channel_id=1, source_target_pairs={{0,128},{128,0},{1,129},{129,1},{2,130},{130,2},{3,131},{131,3},{4... | collective-permute-start | bytes 24584 | tf_op jit(solution)/shard_map/ppermute | solution.py:399
  70.2 6.2 %collective-permute-done.8.there_stats_ref = f32[16,128]{1,0:T(8,128)S(1)} collective-permute-done((f32[16,128]{1,0:T(8,128)S(1)}, f32[16,128]{1,0:T(8,128)S(1)}, u32[]{:S(2)}, u32[]{:S(2)}) %collective-permute-start.8) | collective-permute-done | bytes 8224 | tf_op jit(solution)/shard_map/ppermute | solution.py:399
  77.1 12.5 %all_to_all.10 = bf16[8,128,128]{2,1,0:T(8,128)(2,1)S(1)} all-to-all(bf16[8,128,128]{2,1,0:T(8,128)(2,1)S(1)} %shard_map.61), channel_id=1, replica_groups=mesh['xh'=2,'z'=8,'y'=4,'xl'=2,'c'=2] {'z'}, dimensions={0} | all-to-all | bytes 524288 | tf_op jit(solution)/shard_map/all_to_all | solution.py:404
  89.6 3.0 %collective-permute-start.9 = (bf16[5,128,128]{2,1,0:T(8,128)(2,1)S(1)}, bf16[5,128,128]{2,1,0:T(8,128)(2,1)S(1)}, u32[]{:S(2)}, u32[]{:S(2)}) collective-permute-start(bf16[5,128,128]{2,1,0:T(8,128)(2,1)S(1)} %slice.16.a_ref), channel_id=1, source_target_pairs={{0,1},{1,0},{2,3},{3,2},{4,5},{5,4},{6,7},{7,6},{8,9},{9,8},{10,11... | collective-permute-start | bytes 491528 | tf_op jit(solution)/shard_map/ppermute | solution.py:405
  93.6 2.0 %shard_map.63 = bf16[128,1280]{1,0:T(8,128)(2,1)S(1)} custom-call(bf16[5,128,128]{2,1,0:T(8,128)(2,1)S(1)} %slice.16.a_ref, bf16[5,128,128]{2,1,0:T(8,128)(2,1)S(1)} %collective-permute-done.9.b_ref, bf16[640,1280]{1,0:T(8,128)(2,1)S(1)} %get-tuple-element.117.w_hbm, bf16[640,1280]{1,0:T(8,128)(2,1)S(1)} %collective-permute-done.11.w2_hbm), custom_call_target="tpu_custom_call" | custom-call | flops 419430400 | bytes 4194304 | tf_op jit(solution)/shard_map/pallas_call | solution.py:290
  95.8 2.1 %shard_map.62.near_ref = f32[128,1280]{1,0:T(8,128)S(1)} custom-call(bf16[5,128,128]{2,1,0:T(8,128)(2,1)S(1)} %slice.16.a_ref, bf16[5,128,128]{2,1,0:T(8,128)(2,1)S(1)} %collective-permute-done.9.b_ref, bf16[640,1280]{1,0:T(8,128)(2,1)S(1)} %get-tuple-element.115.w_hbm, bf16[640,1280]{1,0:T(8,128)(2,1)S(1)} %collective-permute-done.10.w2_hbm), custom_call_target="tpu_custom_call" | custom-call | flops 419430400 | bytes 4194304 | tf_op jit(solution)/shard_map/pallas_call | solution.py:290
  97.8 6.8 %collective-permute-done.12.far_ref = bf16[128,1280]{1,0:T(8,128)(2,1)S(1)} collective-permute-done((bf16[128,1280]{1,0:T(8,128)(2,1)S(1)}, bf16[128,1280]{1,0:T(8,128)(2,1)S(1)}, u32[]{:S(2)}, u32[]{:S(2)}) %collective-permute-start.12) | collective-permute-done | bytes 327712 | tf_op jit(solution)/shard_map/ppermute | solution.py:407
  (25 shorter events, 6.8 us)
Async XLA Ops:
  1.9 32.7 %all-to-all-start = ((bf16[8,384,128]{2,1,0:T(8,128)(2,1)}), bf16[8,384,128]{2,1,0:T(8,128)(2,1)}, u32[]{:S(2)}, u32[]{:S(2)}) async-start(bf16[8,384,128]{2,1,0:T(8,128)(2,1)} %shard_map.55), calls=%async_computation | async-start | bytes 1572864 | tf_op jit(solution)/shard_map/all_to_all | solution.py:381
  11.0 5.0 %copy-start = (s32[64,64]{1,0:T(8,128)S(1)}, s32[64,64]{1,0:T(8,128)}, u32[]{:S(2)}) copy-start(s32[64,64]{1,0:T(8,128)} %mask_ref) | copy-start | bytes 49156
  36.7 9.0 %collective-permute-start.2 = (bf16[8,128,128]{2,1,0:T(8,128)(2,1)S(1)}, bf16[8,128,128]{2,1,0:T(8,128)(2,1)S(1)}, u32[]{:S(2)}, u32[]{:S(2)}) collective-permute-start(bf16[8,128,128]{2,1,0:T(8,128)(2,1)S(1)} %slice.14.own_ref.q_ref), channel_id=1, source_target_pairs={{0,128},{128,0},{1,129},{129,1},{2,130},{130,2},{3,131},{131,3},{4... | collective-permute-start | bytes 786440 | tf_op jit(solution)/shard_map/ppermute | solution.py:388
  39.5 9.5 %collective-permute-start = (bf16[4,256,128]{2,1,0:T(8,128)(2,1)S(1)}, bf16[4,256,128]{2,1,0:T(8,128)(2,1)S(1)}, u32[]{:S(2)}, u32[]{:S(2)}) collective-permute-start(bf16[4,256,128]{2,1,0:T(8,128)(2,1)S(1)} %get-tuple-element.86.refs_0_), channel_id=1, source_target_pairs={{0,4},{4,8},{8,12},{12,0},{1,5},{5,9},{9,13},{13,1},{2,6},{6,10},{... | collective-permute-start | bytes 786440 | tf_op jit(solution)/shard_map/ppermute | solution.py:385
  40.8 8.3 %collective-permute-start.1 = (bf16[4,256,128]{2,1,0:T(8,128)(2,1)S(1)}, bf16[4,256,128]{2,1,0:T(8,128)(2,1)S(1)}, u32[]{:S(2)}, u32[]{:S(2)}) collective-permute-start(bf16[4,256,128]{2,1,0:T(8,128)(2,1)S(1)} %get-tuple-element.87.refs_1_), channel_id=1, source_target_pairs={{0,12},{4,0},{8,4},{12,8},{1,13},{5,1},{9,5},{13,9},{2,14},{6,2},{... | collective-permute-start | bytes 786440 | tf_op jit(solution)/shard_map/ppermute | solution.py:386
  42.3 10.9 %collective-permute-start.6 = (bf16[4,256,128]{2,1,0:T(8,128)(2,1)S(1)}, bf16[4,256,128]{2,1,0:T(8,128)(2,1)S(1)}, u32[]{:S(2)}, u32[]{:S(2)}) collective-permute-start(bf16[4,256,128]{2,1,0:T(8,128)(2,1)S(1)} %get-tuple-element.86.refs_0_), channel_id=1, source_target_pairs={{0,12},{4,0},{8,4},{12,8},{1,13},{5,1},{9,5},{13,9},{2,14},{6,2},{... | collective-permute-start | bytes 786440 | tf_op jit(solution)/shard_map/ppermute | solution.py:390
  43.7 9.8 %collective-permute-start.5 = (bf16[4,256,128]{2,1,0:T(8,128)(2,1)S(1)}, bf16[4,256,128]{2,1,0:T(8,128)(2,1)S(1)}, u32[]{:S(2)}, u32[]{:S(2)}) collective-permute-start(bf16[4,256,128]{2,1,0:T(8,128)(2,1)S(1)} %get-tuple-element.87.refs_1_), channel_id=1, source_target_pairs={{0,4},{4,8},{8,12},{12,0},{1,5},{5,9},{9,13},{13,1},{2,6},{6,10},{... | collective-permute-start | bytes 786440 | tf_op jit(solution)/shard_map/ppermute | solution.py:389
  49.1 10.2 %collective-permute-start.3 = (bf16[4,256,128]{2,1,0:T(8,128)(2,1)S(1)}, bf16[4,256,128]{2,1,0:T(8,128)(2,1)S(1)}, u32[]{:S(2)}, u32[]{:S(2)}) collective-permute-start(bf16[4,256,128]{2,1,0:T(8,128)(2,1)S(1)} %collective-permute-done.refs_0_), channel_id=1, source_target_pairs={{0,4},{4,8},{8,12},{12,0},{1,5},{5,9},{9,13},{13,1},{2,6},{6,10},{... | collective-permute-start | bytes 786440 | tf_op jit(solution)/shard_map/ppermute | solution.py:393
  50.9 8.4 %collective-permute-start.4 = (bf16[4,256,128]{2,1,0:T(8,128)(2,1)S(1)}, bf16[4,256,128]{2,1,0:T(8,128)(2,1)S(1)}, u32[]{:S(2)}, u32[]{:S(2)}) collective-permute-start(bf16[4,256,128]{2,1,0:T(8,128)(2,1)S(1)} %collective-permute-done.1.refs_3_), channel_id=1, source_target_pairs={{0,12},{4,0},{8,4},{12,8},{1,13},{5,1},{9,5},{13,9},{2,14},{6,2},{... | collective-permute-start | bytes 786440 | tf_op jit(solution)/shard_map/ppermute | solution.py:394
  59.3 3.0 %copy-start.2 = (bf16[640,1280]{1,0:T(8,128)(2,1)S(1)}, bf16[640,1280]{1,0:T(8,128)(2,1)}, u32[]{:S(2)}) copy-start(bf16[640,1280]{1,0:T(8,128)(2,1)} %get-tuple-element.118) | copy-start | bytes 4915204
  59.3 5.7 %copy-start.1 = (bf16[640,1280]{1,0:T(8,128)(2,1)S(1)}, bf16[640,1280]{1,0:T(8,128)(2,1)}, u32[]{:S(2)}) copy-start(bf16[640,1280]{1,0:T(8,128)(2,1)} %get-tuple-element.116) | copy-start | bytes 4915204
  62.3 31.3 %collective-permute-start.11 = (bf16[640,1280]{1,0:T(8,128)(2,1)S(1)}, bf16[640,1280]{1,0:T(8,128)(2,1)S(1)}, u32[]{:S(2)}, u32[]{:S(2)}) collective-permute-start(bf16[640,1280]{1,0:T(8,128)(2,1)S(1)} %copy-done.2), channel_id=1, source_target_pairs={{0,1},{1,0},{2,3},{3,2},{4,5},{5,4},{6,7},{7,6},{8,9},{9,8},{10,11... | collective-permute-start | bytes 4915208 | tf_op jit(solution)/shard_map/ppermute | solution.py:402
  65.0 30.8 %collective-permute-start.10 = (bf16[640,1280]{1,0:T(8,128)(2,1)S(1)}, bf16[640,1280]{1,0:T(8,128)(2,1)S(1)}, u32[]{:S(2)}, u32[]{:S(2)}) collective-permute-start(bf16[640,1280]{1,0:T(8,128)(2,1)S(1)} %copy-done.1), channel_id=1, source_target_pairs={{0,1},{1,0},{2,3},{3,2},{4,5},{5,4},{6,7},{7,6},{8,9},{9,8},{10,11... | collective-permute-start | bytes 4915208 | tf_op jit(solution)/shard_map/ppermute | solution.py:402
  67.2 9.2 %collective-permute-start.7 = (bf16[8,128,128]{2,1,0:T(8,128)(2,1)S(1)}, bf16[8,128,128]{2,1,0:T(8,128)(2,1)S(1)}, u32[]{:S(2)}, u32[]{:S(2)}) collective-permute-start(bf16[8,128,128]{2,1,0:T(8,128)(2,1)S(1)} %get-tuple-element.113), channel_id=1, source_target_pairs={{0,128},{128,0},{1,129},{129,1},{2,130},{130,2},{3,131},{131,3},{4... | collective-permute-start | bytes 786440 | tf_op jit(solution)/shard_map/ppermute | solution.py:398
  67.9 8.5 %collective-permute-start.8 = (f32[16,128]{1,0:T(8,128)S(1)}, f32[16,128]{1,0:T(8,128)S(1)}, u32[]{:S(2)}, u32[]{:S(2)}) collective-permute-start(f32[16,128]{1,0:T(8,128)S(1)} %get-tuple-element.114), channel_id=1, source_target_pairs={{0,128},{128,0},{1,129},{129,1},{2,130},{130,2},{3,131},{131,3},{4... | collective-permute-start | bytes 24584 | tf_op jit(solution)/shard_map/ppermute | solution.py:399
  89.6 4.0 %collective-permute-start.9 = (bf16[5,128,128]{2,1,0:T(8,128)(2,1)S(1)}, bf16[5,128,128]{2,1,0:T(8,128)(2,1)S(1)}, u32[]{:S(2)}, u32[]{:S(2)}) collective-permute-start(bf16[5,128,128]{2,1,0:T(8,128)(2,1)S(1)} %slice.16.a_ref), channel_id=1, source_target_pairs={{0,1},{1,0},{2,3},{3,2},{4,5},{5,4},{6,7},{7,6},{8,9},{9,8},{10,11... | collective-permute-start | bytes 491528 | tf_op jit(solution)/shard_map/ppermute | solution.py:405
  95.7 9.0 %collective-permute-start.12 = (bf16[128,1280]{1,0:T(8,128)(2,1)S(1)}, bf16[128,1280]{1,0:T(8,128)(2,1)S(1)}, u32[]{:S(2)}, u32[]{:S(2)}) collective-permute-start(bf16[128,1280]{1,0:T(8,128)(2,1)S(1)} %shard_map.63), channel_id=1, source_target_pairs={{0,2},{2,0},{1,3},{3,1},{4,6},{6,4},{5,7},{7,5},{8,10},{10,8},{9,1... | collective-permute-start | bytes 983048 | tf_op jit(solution)/shard_map/ppermute | solution.py:407

commit v10 on v9

--- a/solution.py
+++ b/solution.py
@@ -395,12 +395,13 @@
     state = attend(groups[1], query, [before_low, before_high, after_low, after_high], state)
     far_parts = [far_low, far_high]
     sent, sent_stats = attend_last(groups[2], query[1], far_parts, state, False)
+    sent, sent_stats, state = lax.optimization_barrier((sent, sent_stats, state))
     there = lax.ppermute(sent, "xh", shift(XH, 1))
     there_stats = lax.ppermute(sent_stats, "xh", shift(XH, 1))
     here, here_stats = attend_last(groups[3], query[0], far_parts, state, True)
-    here, w_sent = lax.optimization_barrier((here, w_sent))
+    heads = merge(here, here_stats, there, there_stats)
+    heads, w_sent = lax.optimization_barrier((heads, w_sent))
     w_here = [lax.ppermute(w, "c", shift(NC, 1)) for w in w_sent]
-    heads = merge(here, here_stats, there, there_stats)
     heads = lax.all_to_all(heads, "z", 0, 0, tiled=True)[:HEADS]
     heads_core = lax.ppermute(heads, "c", shift(NC, 1))
     far = project(heads, heads_core, w_own[0], w_here[0], jnp.bfloat16)

time: 106 us -> 102 us (0.962)
  waiting for transfers between devices: 31.6 us -> 26.6 us
  blocking collectives: 12.5 us -> 14.7 us
    ppermute x1, waiting for transfers between devices: 6.19 us -> 1.39 us  [local(): there_stats = lax.ppermute(sent_stats, 'xh', shift(XH, 1))]
    ppermute x1, starting transfers between devices: 2.98 us -> 0.78 us  [local(): heads_core = lax.ppermute(heads, 'c', shift(NC, 1))]
    all_to_all x1, blocking collectives: 12.5 us -> 14.7 us  [local(): heads = lax.all_to_all(heads, 'z', 0, 0, tiled=True)[:HEADS]]
    ppermute x2, starting transfers between devices: 2.76 us -> 4.07 us  [local(): w_here = [lax.ppermute(w, 'c', shift(NC, 1)) for w in w_sent]]
  transfers between devices with their start and end apart: 14 -> 14, of which waited for: 8 -> 7; matrix products, arithmetic and copies ran while one was open for 5% -> 5% of each run, Pallas kernels for 19% -> 20%
where the time goes in v10:
time: 102 us
  starting transfers between devices  27.4 us (27%)
  waiting for transfers between devices  26.6 us (26%)
  Pallas kernels  25.7 us (25%)
  blocking collectives  14.7 us (14%)
  local copies, waits for them, and re-layouts  7.1 us (7%)
    all_to_all x1, blocking collectives, local(): heads = lax.all_to_all(heads, 'z', 0, 0, tiled=True)[:HEADS]  14.7 us
    all_to_all x1, waiting for transfers between devices, local(): slots = lax.all_to_all(slots, 'z', 0, 0, tiled=True)  14.3 us
    pallas_call x2, Pallas kernels, attend(): pl.pallas_call(kernel, out_shape=(whole, whole, whole), in_specs=in_smem(...  9.27 us
    all_to_all x1, starting transfers between devices, local(): slots = lax.all_to_all(slots, 'z', 0, 0, tiled=True)  9.03 us
    ppermute x1, waiting for transfers between devices, local(): far = lax.ppermute(far, 'xl', shift(XL, 1))  6.85 us
    dynamic_slice x1, local copies, waits for them, and re-layouts, w_columns(): lax.dynamic_slice(w, (0, (to_xl * NC + to_c) * width), (w.shape[0], width))  5.03 us
    pallas_call x2, Pallas kernels, attend_last(): pl.pallas_call(kernel, out_shape=(jax.ShapeDtypeStruct((NZ, BLOCK, HEAD_D...  4.65 us
    pallas_call x1, Pallas kernels, live_tiles(): pl.pallas_call(tiles_kernel, out_shape=tuple(out_shape), in_specs=in_smem...  4.35 us
  transfers between devices with their start and end apart: 14, of which 7 were waited for; matrix products, arithmetic and copies ran while one was open for 5% of the time, Pallas kernels for 20%

profile of v10, /device:TPU:1, one launch (start us, length us, event | category | flops | bytes accessed | tf_op | source)
XLA Modules:
  0.0 101.7 jit_solution(14180394630154700869)
XLA Ops:
  0.0 1.9 %shard_map.55 = bf16[8,384,128]{2,1,0:T(8,128)(2,1)} custom-call(bf16[128,640]{1,0:T(8,128)(2,1)} %q_hbm.1, bf16[128,640]{1,0:T(8,128)(2,1)} %k_hbm.1, bf16[128,640]{1,0:T(8,128)(2,1)} %v_hbm.1), custom_call_target="tpu_custom_call" | custom-call | tf_op jit(solution)/shard_map/pallas_call | solution.py:53
  1.9 9.0 %all-to-all-start = ((bf16[8,384,128]{2,1,0:T(8,128)(2,1)}), bf16[8,384,128]{2,1,0:T(8,128)(2,1)}, u32[]{:S(2)}, u32[]{:S(2)}) async-start(bf16[8,384,128]{2,1,0:T(8,128)(2,1)} %shard_map.55), calls=%async_computation | async-start | bytes 1572864 | tf_op jit(solution)/shard_map/all_to_all | solution.py:381
  11.0 5.0 %constant_dynamic-slice_fusion = (bf16[640,1280]{1,0:T(8,128)(2,1)}, bf16[640,1280]{1,0:T(8,128)(2,1)}, bf16[640,1280]{1,0:T(8,128)(2,1)S(1)}, bf16[640,1280]{1,0:T(8,128)(2,1)S(1)}) fusion(bf16[640,5120]{1,0:T(8,128)(2,1)} %param.9, s32[]{:T(128)S(6)} %select_n.15, s32[]{:T(128)S(6)} %select_n.14, s32[]{:T(128)S(6)} %select_n.13, s32[]{:T(128)S(6)} %select_n.12), kind=kLoop, calls=%fused_computation | loop fusion | bytes 13107216 | tf_op jit(solution)/shard_map/dynamic_slice | solution.py:372
  16.0 4.4 %shard_map.56 = (s32[1]{0:T(128)}, s32[256]{0:T(256)S(1)}, s32[256]{0:T(256)S(1)}, s32[1]{0:T(128)}, s32[384]{0:T(512)S(1)}, /*index=5*/s32[384]{0:T(512)S(1)}, ...) custom-call(s32[64,64]{1,0:T(8,128)S(1)} %copy-done), custom_call_target="tpu_custom_call" | custom-call | flops 1000000 | bytes 100000 | tf_op jit(solution)/shard_map/pallas_call | solution.py:355
  20.4 14.3 %all-to-all-done = bf16[8,384,128]{2,1,0:T(8,128)(2,1)} async-done(((bf16[8,384,128]{2,1,0:T(8,128)(2,1)}), bf16[8,384,128]{2,1,0:T(8,128)(2,1)}, u32[]{:S(2)}, u32[]{:S(2)}) %all-to-all-start) | async-done | bytes 786464 | tf_op jit(solution)/shard_map/all_to_all | solution.py:381
  36.7 2.8 %collective-permute-start.2 = (bf16[8,128,128]{2,1,0:T(8,128)(2,1)S(1)}, bf16[8,128,128]{2,1,0:T(8,128)(2,1)S(1)}, u32[]{:S(2)}, u32[]{:S(2)}) collective-permute-start(bf16[8,128,128]{2,1,0:T(8,128)(2,1)S(1)} %slice.14.own_ref.q_ref), channel_id=1, source_target_pairs={{0,128},{128,0},{1,129},{129,1},{2,130},{130,2},{3,131},{131,3},{4... | collective-permute-start | bytes 786440 | tf_op jit(solution)/shard_map/ppermute | solution.py:388
  39.5 1.3 %collective-permute-start = (bf16[4,256,128]{2,1,0:T(8,128)(2,1)S(1)}, bf16[4,256,128]{2,1,0:T(8,128)(2,1)S(1)}, u32[]{:S(2)}, u32[]{:S(2)}) collective-permute-start(bf16[4,256,128]{2,1,0:T(8,128)(2,1)S(1)} %get-tuple-element.91.refs_0_), channel_id=1, source_target_pairs={{0,4},{4,8},{8,12},{12,0},{1,5},{5,9},{9,13},{13,1},{2,6},{6,10},{... | collective-permute-start | bytes 786440 | tf_op jit(solution)/shard_map/ppermute | solution.py:385
  40.8 1.4 %collective-permute-start.1 = (bf16[4,256,128]{2,1,0:T(8,128)(2,1)S(1)}, bf16[4,256,128]{2,1,0:T(8,128)(2,1)S(1)}, u32[]{:S(2)}, u32[]{:S(2)}) collective-permute-start(bf16[4,256,128]{2,1,0:T(8,128)(2,1)S(1)} %get-tuple-element.92.refs_1_), channel_id=1, source_target_pairs={{0,12},{4,0},{8,4},{12,8},{1,13},{5,1},{9,5},{13,9},{2,14},{6,2},{... | collective-permute-start | bytes 786440 | tf_op jit(solution)/shard_map/ppermute | solution.py:386
  42.3 1.5 %collective-permute-start.6 = (bf16[4,256,128]{2,1,0:T(8,128)(2,1)S(1)}, bf16[4,256,128]{2,1,0:T(8,128)(2,1)S(1)}, u32[]{:S(2)}, u32[]{:S(2)}) collective-permute-start(bf16[4,256,128]{2,1,0:T(8,128)(2,1)S(1)} %get-tuple-element.91.refs_0_), channel_id=1, source_target_pairs={{0,12},{4,0},{8,4},{12,8},{1,13},{5,1},{9,5},{13,9},{2,14},{6,2},{... | collective-permute-start | bytes 786440 | tf_op jit(solution)/shard_map/ppermute | solution.py:390
  43.7 1.9 %collective-permute-done.2.other_ref.q_ref = bf16[8,128,128]{2,1,0:T(8,128)(2,1)S(1)} collective-permute-done((bf16[8,128,128]{2,1,0:T(8,128)(2,1)S(1)}, bf16[8,128,128]{2,1,0:T(8,128)(2,1)S(1)}, u32[]{:S(2)}, u32[]{:S(2)}) %collective-permute-start.2) | collective-permute-done | bytes 262176 | tf_op jit(solution)/shard_map/ppermute | solution.py:388
  45.7 3.4 %shard_map.57 = (f32[16,128,128]{2,1,0:T(8,128)S(1)}, f32[16,128,128]{2,1,0:T(8,128)S(1)}, f32[16,128,128]{2,1,0:T(8,128)S(1)}) custom-call(s32[1]{0:T(128)} %get-tuple-element.93.count_ref, s32[256]{0:T(256)S(1)} %get-tuple-element.94.block_ref, s32[256]{0:T(256)S(1)} %get-tuple-element.95.slot_ref, bf16[8,128,128]{2,1,0:T(8,128)(2,1)S(1)} %slice.14.own_ref.q_ref, ...), custom_call_target="tpu_custom_call" | custom-call | flops 335544320 | bytes 6291456 | tf_op jit(solution)/shard_map/pallas_call | solution.py:216
  49.1 1.8 %collective-permute-start.3 = (bf16[4,256,128]{2,1,0:T(8,128)(2,1)S(1)}, bf16[4,256,128]{2,1,0:T(8,128)(2,1)S(1)}, u32[]{:S(2)}, u32[]{:S(2)}) collective-permute-start(bf16[4,256,128]{2,1,0:T(8,128)(2,1)S(1)} %collective-permute-done.refs_0_), channel_id=1, source_target_pairs={{0,4},{4,8},{8,12},{12,0},{1,5},{5,9},{9,13},{13,1},{2,6},{6,10},{... | collective-permute-start | bytes 786440 | tf_op jit(solution)/shard_map/ppermute | solution.py:393
  50.9 1.5 %collective-permute-start.4 = (bf16[4,256,128]{2,1,0:T(8,128)(2,1)S(1)}, bf16[4,256,128]{2,1,0:T(8,128)(2,1)S(1)}, u32[]{:S(2)}, u32[]{:S(2)}) collective-permute-start(bf16[4,256,128]{2,1,0:T(8,128)(2,1)S(1)} %collective-permute-done.1.refs_3_), channel_id=1, source_target_pairs={{0,12},{4,0},{8,4},{12,8},{1,13},{5,1},{9,5},{13,9},{2,14},{6,2},{... | collective-permute-start | bytes 786440 | tf_op jit(solution)/shard_map/ppermute | solution.py:394
  53.5 5.9 %shard_map.58 = (f32[16,128,128]{2,1,0:T(8,128)S(1)}, f32[16,128,128]{2,1,0:T(8,128)S(1)}, f32[16,128,128]{2,1,0:T(8,128)S(1)}) custom-call(s32[1]{0:T(128)} %get-tuple-element.104.count_ref, s32[384]{0:T(512)S(1)} %get-tuple-element.105.block_ref, s32[384]{0:T(512)S(1)} %get-tuple-element.106.slot_ref, bf16[8,128,128]{2,1,0:T(8,128)(2,1)S(1)} %slice.14.own_ref.q_ref, ...), custom_call_target="tpu_custom_call" | custom-call | flops 671088640 | bytes 6291456 | tf_op jit(solution)/shard_map/pallas_call | solution.py:216
  59.4 2.2 %shard_map.59 = (bf16[8,128,128]{2,1,0:T(8,128)(2,1)S(1)}, f32[16,128]{1,0:T(8,128)S(1)}) custom-call(s32[1]{0:T(128)} %get-tuple-element.101.count_ref, s32[192]{0:T(256)S(1)} %get-tuple-element.102.block_ref, s32[192]{0:T(256)S(1)} %get-tuple-element.103.slot_ref, bf16[8,128,128]{2,1,0:T(8,128)(2,1)S(1)} %collective-permute-done.2.other_ref.q_ref, ...), custom_call_target="tpu_custom_call" | custom-call | flops 83886080 | bytes 3145728 | tf_op jit(solution)/shard_map/pallas_call | solution.py:161
  61.6 1.1 %collective-permute-start.7 = (bf16[8,128,128]{2,1,0:T(8,128)(2,1)S(1)}, bf16[8,128,128]{2,1,0:T(8,128)(2,1)S(1)}, u32[]{:S(2)}, u32[]{:S(2)}) collective-permute-start(bf16[8,128,128]{2,1,0:T(8,128)(2,1)S(1)} %get-tuple-element.120), channel_id=1, source_target_pairs={{0,128},{128,0},{1,129},{129,1},{2,130},{130,2},{3,131},{131,3},{4... | collective-permute-start | bytes 786440 | tf_op jit(solution)/shard_map/ppermute | solution.py:399
  62.8 1.9 %collective-permute-start.8 = (f32[16,128]{1,0:T(8,128)S(1)}, f32[16,128]{1,0:T(8,128)S(1)}, u32[]{:S(2)}, u32[]{:S(2)}) collective-permute-start(f32[16,128]{1,0:T(8,128)S(1)} %get-tuple-element.121), channel_id=1, source_target_pairs={{0,128},{128,0},{1,129},{129,1},{2,130},{130,2},{3,131},{131,3},{4... | collective-permute-start | bytes 24584 | tf_op jit(solution)/shard_map/ppermute | solution.py:400
  64.7 2.5 %shard_map.60 = (f32[8,128,128]{2,1,0:T(8,128)S(1)}, f32[128,128]{1,0:T(8,128)S(1)}) custom-call(s32[1]{0:T(128)} %get-tuple-element.86.count_ref, s32[192]{0:T(256)S(1)} %get-tuple-element.87.block_ref, s32[192]{0:T(256)S(1)} %get-tuple-element.88.slot_ref, bf16[8,128,128]{2,1,0:T(8,128)(2,1)S(1)} %slice.14.own_ref.q_ref, ...), custom_call_target="tpu_custom_call" | custom-call | flops 83886080 | bytes 3145728 | tf_op jit(solution)/shard_map/pallas_call | solution.py:161
  67.1 1.4 %collective-permute-done.8.there_stats_ref = f32[16,128]{1,0:T(8,128)S(1)} collective-permute-done((f32[16,128]{1,0:T(8,128)S(1)}, f32[16,128]{1,0:T(8,128)S(1)}, u32[]{:S(2)}, u32[]{:S(2)}) %collective-permute-start.8) | collective-permute-done | bytes 8224 | tf_op jit(solution)/shard_map/ppermute | solution.py:400
  69.2 4.0 %collective-permute-start.11 = (bf16[640,1280]{1,0:T(8,128)(2,1)S(1)}, bf16[640,1280]{1,0:T(8,128)(2,1)S(1)}, u32[]{:S(2)}, u32[]{:S(2)}) collective-permute-start(bf16[640,1280]{1,0:T(8,128)(2,1)S(1)} %copy-done.2), channel_id=1, source_target_pairs={{0,1},{1,0},{2,3},{3,2},{4,5},{5,4},{6,7},{7,6},{8,9},{9,8},{10,11... | collective-permute-start | bytes 4915208 | tf_op jit(solution)/shard_map/ppermute | solution.py:404
  73.3 14.7 %all_to_all.10 = bf16[8,128,128]{2,1,0:T(8,128)(2,1)S(1)} all-to-all(bf16[8,128,128]{2,1,0:T(8,128)(2,1)S(1)} %shard_map.61), channel_id=1, replica_groups=mesh['xh'=2,'z'=8,'y'=4,'xl'=2,'c'=2] {'z'}, dimensions={0} | all-to-all | bytes 524288 | tf_op jit(solution)/shard_map/all_to_all | solution.py:405
  89.8 2.0 %shard_map.63 = bf16[128,1280]{1,0:T(8,128)(2,1)S(1)} custom-call(bf16[5,128,128]{2,1,0:T(8,128)(2,1)S(1)} %slice.16.a_ref, bf16[5,128,128]{2,1,0:T(8,128)(2,1)S(1)} %collective-permute-done.9.b_ref, bf16[640,1280]{1,0:T(8,128)(2,1)S(1)} %get-tuple-element.127.w_hbm, bf16[640,1280]{1,0:T(8,128)(2,1)S(1)} %collective-permute-done.11.w2_hbm), custom_call_target="tpu_custom_call" | custom-call | flops 419430400 | bytes 4194304 | tf_op jit(solution)/shard_map/pallas_call | solution.py:290
  92.0 2.0 %shard_map.62.near_ref = f32[128,1280]{1,0:T(8,128)S(1)} custom-call(bf16[5,128,128]{2,1,0:T(8,128)(2,1)S(1)} %slice.16.a_ref, bf16[5,128,128]{2,1,0:T(8,128)(2,1)S(1)} %collective-permute-done.9.b_ref, bf16[640,1280]{1,0:T(8,128)(2,1)S(1)} %get-tuple-element.125.w_hbm, bf16[640,1280]{1,0:T(8,128)(2,1)S(1)} %collective-permute-done.10.w2_hbm), custom_call_target="tpu_custom_call" | custom-call | flops 419430400 | bytes 4194304 | tf_op jit(solution)/shard_map/pallas_call | solution.py:290
  94.0 6.8 %collective-permute-done.12.far_ref = bf16[128,1280]{1,0:T(8,128)(2,1)S(1)} collective-permute-done((bf16[128,1280]{1,0:T(8,128)(2,1)S(1)}, bf16[128,1280]{1,0:T(8,128)(2,1)S(1)}, u32[]{:S(2)}, u32[]{:S(2)}) %collective-permute-start.12) | collective-permute-done | bytes 327712 | tf_op jit(solution)/shard_map/ppermute | solution.py:408
  (25 shorter events, 6.7 us)
Async XLA Ops:
  1.9 32.7 %all-to-all-start = ((bf16[8,384,128]{2,1,0:T(8,128)(2,1)}), bf16[8,384,128]{2,1,0:T(8,128)(2,1)}, u32[]{:S(2)}, u32[]{:S(2)}) async-start(bf16[8,384,128]{2,1,0:T(8,128)(2,1)} %shard_map.55), calls=%async_computation | async-start | bytes 1572864 | tf_op jit(solution)/shard_map/all_to_all | solution.py:381
  11.0 5.0 %copy-start = (s32[64,64]{1,0:T(8,128)S(1)}, s32[64,64]{1,0:T(8,128)}, u32[]{:S(2)}) copy-start(s32[64,64]{1,0:T(8,128)} %mask_ref) | copy-start | bytes 49156
  36.7 9.0 %collective-permute-start.2 = (bf16[8,128,128]{2,1,0:T(8,128)(2,1)S(1)}, bf16[8,128,128]{2,1,0:T(8,128)(2,1)S(1)}, u32[]{:S(2)}, u32[]{:S(2)}) collective-permute-start(bf16[8,128,128]{2,1,0:T(8,128)(2,1)S(1)} %slice.14.own_ref.q_ref), channel_id=1, source_target_pairs={{0,128},{128,0},{1,129},{129,1},{2,130},{130,2},{3,131},{131,3},{4... | collective-permute-start | bytes 786440 | tf_op jit(solution)/shard_map/ppermute | solution.py:388
  39.5 9.5 %collective-permute-start = (bf16[4,256,128]{2,1,0:T(8,128)(2,1)S(1)}, bf16[4,256,128]{2,1,0:T(8,128)(2,1)S(1)}, u32[]{:S(2)}, u32[]{:S(2)}) collective-permute-start(bf16[4,256,128]{2,1,0:T(8,128)(2,1)S(1)} %get-tuple-element.91.refs_0_), channel_id=1, source_target_pairs={{0,4},{4,8},{8,12},{12,0},{1,5},{5,9},{9,13},{13,1},{2,6},{6,10},{... | collective-permute-start | bytes 786440 | tf_op jit(solution)/shard_map/ppermute | solution.py:385
  40.8 8.3 %collective-permute-start.1 = (bf16[4,256,128]{2,1,0:T(8,128)(2,1)S(1)}, bf16[4,256,128]{2,1,0:T(8,128)(2,1)S(1)}, u32[]{:S(2)}, u32[]{:S(2)}) collective-permute-start(bf16[4,256,128]{2,1,0:T(8,128)(2,1)S(1)} %get-tuple-element.92.refs_1_), channel_id=1, source_target_pairs={{0,12},{4,0},{8,4},{12,8},{1,13},{5,1},{9,5},{13,9},{2,14},{6,2},{... | collective-permute-start | bytes 786440 | tf_op jit(solution)/shard_map/ppermute | solution.py:386
  42.3 10.9 %collective-permute-start.6 = (bf16[4,256,128]{2,1,0:T(8,128)(2,1)S(1)}, bf16[4,256,128]{2,1,0:T(8,128)(2,1)S(1)}, u32[]{:S(2)}, u32[]{:S(2)}) collective-permute-start(bf16[4,256,128]{2,1,0:T(8,128)(2,1)S(1)} %get-tuple-element.91.refs_0_), channel_id=1, source_target_pairs={{0,12},{4,0},{8,4},{12,8},{1,13},{5,1},{9,5},{13,9},{2,14},{6,2},{... | collective-permute-start | bytes 786440 | tf_op jit(solution)/shard_map/ppermute | solution.py:390
  43.7 9.8 %collective-permute-start.5 = (bf16[4,256,128]{2,1,0:T(8,128)(2,1)S(1)}, bf16[4,256,128]{2,1,0:T(8,128)(2,1)S(1)}, u32[]{:S(2)}, u32[]{:S(2)}) collective-permute-start(bf16[4,256,128]{2,1,0:T(8,128)(2,1)S(1)} %get-tuple-element.92.refs_1_), channel_id=1, source_target_pairs={{0,4},{4,8},{8,12},{12,0},{1,5},{5,9},{9,13},{13,1},{2,6},{6,10},{... | collective-permute-start | bytes 786440 | tf_op jit(solution)/shard_map/ppermute | solution.py:389
  49.1 10.3 %collective-permute-start.3 = (bf16[4,256,128]{2,1,0:T(8,128)(2,1)S(1)}, bf16[4,256,128]{2,1,0:T(8,128)(2,1)S(1)}, u32[]{:S(2)}, u32[]{:S(2)}) collective-permute-start(bf16[4,256,128]{2,1,0:T(8,128)(2,1)S(1)} %collective-permute-done.refs_0_), channel_id=1, source_target_pairs={{0,4},{4,8},{8,12},{12,0},{1,5},{5,9},{9,13},{13,1},{2,6},{6,10},{... | collective-permute-start | bytes 786440 | tf_op jit(solution)/shard_map/ppermute | solution.py:393
  50.9 8.6 %collective-permute-start.4 = (bf16[4,256,128]{2,1,0:T(8,128)(2,1)S(1)}, bf16[4,256,128]{2,1,0:T(8,128)(2,1)S(1)}, u32[]{:S(2)}, u32[]{:S(2)}) collective-permute-start(bf16[4,256,128]{2,1,0:T(8,128)(2,1)S(1)} %collective-permute-done.1.refs_3_), channel_id=1, source_target_pairs={{0,12},{4,0},{8,4},{12,8},{1,13},{5,1},{9,5},{13,9},{2,14},{6,2},{... | collective-permute-start | bytes 786440 | tf_op jit(solution)/shard_map/ppermute | solution.py:394
  61.6 7.6 %copy-start.2 = (bf16[640,1280]{1,0:T(8,128)(2,1)S(1)}, bf16[640,1280]{1,0:T(8,128)(2,1)}, u32[]{:S(2)}) copy-start(bf16[640,1280]{1,0:T(8,128)(2,1)} %get-tuple-element.128) | copy-start | bytes 4915204
  61.6 11.5 %copy-start.1 = (bf16[640,1280]{1,0:T(8,128)(2,1)S(1)}, bf16[640,1280]{1,0:T(8,128)(2,1)}, u32[]{:S(2)}) copy-start(bf16[640,1280]{1,0:T(8,128)(2,1)} %get-tuple-element.126) | copy-start | bytes 4915204
  61.6 6.9 %collective-permute-start.7 = (bf16[8,128,128]{2,1,0:T(8,128)(2,1)S(1)}, bf16[8,128,128]{2,1,0:T(8,128)(2,1)S(1)}, u32[]{:S(2)}, u32[]{:S(2)}) collective-permute-start(bf16[8,128,128]{2,1,0:T(8,128)(2,1)S(1)} %get-tuple-element.120), channel_id=1, source_target_pairs={{0,128},{128,0},{1,129},{129,1},{2,130},{130,2},{3,131},{131,3},{4... | collective-permute-start | bytes 786440 | tf_op jit(solution)/shard_map/ppermute | solution.py:399
  62.8 5.8 %collective-permute-start.8 = (f32[16,128]{1,0:T(8,128)S(1)}, f32[16,128]{1,0:T(8,128)S(1)}, u32[]{:S(2)}, u32[]{:S(2)}) collective-permute-start(f32[16,128]{1,0:T(8,128)S(1)} %get-tuple-element.121), channel_id=1, source_target_pairs={{0,128},{128,0},{1,129},{129,1},{2,130},{130,2},{3,131},{131,3},{4... | collective-permute-start | bytes 24584 | tf_op jit(solution)/shard_map/ppermute | solution.py:400
  69.2 20.6 %collective-permute-start.11 = (bf16[640,1280]{1,0:T(8,128)(2,1)S(1)}, bf16[640,1280]{1,0:T(8,128)(2,1)S(1)}, u32[]{:S(2)}, u32[]{:S(2)}) collective-permute-start(bf16[640,1280]{1,0:T(8,128)(2,1)S(1)} %copy-done.2), channel_id=1, source_target_pairs={{0,1},{1,0},{2,3},{3,2},{4,5},{5,4},{6,7},{7,6},{8,9},{9,8},{10,11... | collective-permute-start | bytes 4915208 | tf_op jit(solution)/shard_map/ppermute | solution.py:404
  73.2 18.8 %collective-permute-start.10 = (bf16[640,1280]{1,0:T(8,128)(2,1)S(1)}, bf16[640,1280]{1,0:T(8,128)(2,1)S(1)}, u32[]{:S(2)}, u32[]{:S(2)}) collective-permute-start(bf16[640,1280]{1,0:T(8,128)(2,1)S(1)} %copy-done.1), channel_id=1, source_target_pairs={{0,1},{1,0},{2,3},{3,2},{4,5},{5,4},{6,7},{7,6},{8,9},{9,8},{10,11... | collective-permute-start | bytes 4915208 | tf_op jit(solution)/shard_map/ppermute | solution.py:404
  88.0 1.8 %collective-permute-start.9 = (bf16[5,128,128]{2,1,0:T(8,128)(2,1)S(1)}, bf16[5,128,128]{2,1,0:T(8,128)(2,1)S(1)}, u32[]{:S(2)}, u32[]{:S(2)}) collective-permute-start(bf16[5,128,128]{2,1,0:T(8,128)(2,1)S(1)} %slice.16.a_ref), channel_id=1, source_target_pairs={{0,1},{1,0},{2,3},{3,2},{4,5},{5,4},{6,7},{7,6},{8,9},{9,8},{10,11... | collective-permute-start | bytes 491528 | tf_op jit(solution)/shard_map/ppermute | solution.py:406
  91.9 9.0 %collective-permute-start.12 = (bf16[128,1280]{1,0:T(8,128)(2,1)S(1)}, bf16[128,1280]{1,0:T(8,128)(2,1)S(1)}, u32[]{:S(2)}, u32[]{:S(2)}) collective-permute-start(bf16[128,1280]{1,0:T(8,128)(2,1)S(1)} %shard_map.63), channel_id=1, source_target_pairs={{0,2},{2,0},{1,3},{3,1},{4,6},{6,4},{5,7},{7,5},{8,10},{10,8},{9,1... | collective-permute-start | bytes 983048 | tf_op jit(solution)/shard_map/ppermute | solution.py:408

commit v11 on v10

--- a/solution.py
+++ b/solution.py
@@ -258,14 +258,14 @@
     )(here, here_stats, there, there_stats)
 
 
-def project(a, b, w_own, w_other, dtype):
-    deep, width = w_own.shape
+def project(a, b, w_own, w_other, first, width, dtype):
+    deep = w_own.shape[0]
     tiles = width // TILE_N
 
     def kernel(a_ref, b_ref, w_hbm, w2_hbm, out_ref, rows_ref, w_ref, sems):
         copies = []
         for tile in range(tiles):
-            lanes = pl.ds(tile * TILE_N, TILE_N)
+            lanes = pl.ds(first + tile * TILE_N, TILE_N)
             for which, source in enumerate((w_hbm, w2_hbm)):
                 copies.append(
                     pltpu.make_async_copy(
@@ -304,18 +304,24 @@
     )(a, b, w_own, w_other)
 
 
-def add_kernel(near_ref, far_ref, out_ref):
-    out_ref[...] = (near_ref[...] + far_ref[...].astype(jnp.float32)).astype(out_ref.dtype)
+def add_kernel(near_ref, *refs):
+    out_ref = refs[-1]
+    at = 0
+    for far_ref in refs[:-1]:
+        lanes = slice(at, at + far_ref.shape[1])
+        out = near_ref[:, lanes] + far_ref[...].astype(jnp.float32)
+        out_ref[:, lanes] = out.astype(out_ref.dtype)
+        at += far_ref.shape[1]
 
 
 def add(near, far):
     return pl.pallas_call(
         add_kernel,
         out_shape=jax.ShapeDtypeStruct(near.shape, jnp.bfloat16),
-        in_specs=in_vmem(2),
+        in_specs=in_vmem(1 + len(far)),
         out_specs=in_vmem(1)[0],
         compiler_params=pltpu.CompilerParams(vmem_limit_bytes=4 * MIB),
-    )(near, far)
+    )(near, *far)
 
 
 GROUPS = (((0,), None), ((1, 3), None), ((2,), 1), ((2,), 0))
@@ -376,10 +382,11 @@
     w_own = [w_columns(w_out, to_xl, c) for to_xl in (1 - xl, xl)]
     w_sent = [w_columns(w_out, to_xl, 1 - c) for to_xl in (1 - xl, xl)]
     w_own, w_sent, frame_mask = lax.optimization_barrier((w_own, w_sent, frame_mask))
+    w_here = [lax.ppermute(w, "c", shift(NC, 1)) for w in w_sent]
     groups = live_tiles(frame_mask)
 
     slots = lax.all_to_all(slots, "z", 0, 0, tiled=True)
-    slots, w_own, w_sent, groups = lax.optimization_barrier((slots, w_own, w_sent, groups))
+    slots, w_own, groups = lax.optimization_barrier((slots, w_own, groups))
     low, high = slots[: NZ // 2, BLOCK:], slots[NZ // 2 :, BLOCK:]
     slots, low, high = lax.optimization_barrier((slots, low, high))
     before_low = lax.ppermute(low, "y", shift(NY, 1))
@@ -399,14 +406,20 @@
     there = lax.ppermute(sent, "xh", shift(XH, 1))
     there_stats = lax.ppermute(sent_stats, "xh", shift(XH, 1))
     here, here_stats = attend_last(groups[3], query[0], far_parts, state, True)
+    there, w_here = lax.optimization_barrier((there, w_here))
     heads = merge(here, here_stats, there, there_stats)
-    heads, w_sent = lax.optimization_barrier((heads, w_sent))
-    w_here = [lax.ppermute(w, "c", shift(NC, 1)) for w in w_sent]
     heads = lax.all_to_all(heads, "z", 0, 0, tiled=True)[:HEADS]
     heads_core = lax.ppermute(heads, "c", shift(NC, 1))
-    far = project(heads, heads_core, w_own[0], w_here[0], jnp.bfloat16)
-    far = lax.ppermute(far, "xl", shift(XL, 1))
-    near = project(heads, heads_core, w_own[1], w_here[1], jnp.float32)
+    early = width // TILE_N // 2 * TILE_N
+    far = [
+        lax.ppermute(
+            project(heads, heads_core, w_own[0], w_here[0], first, columns, jnp.bfloat16),
+            "xl",
+            shift(XL, 1),
+        )
+        for first, columns in ((0, early), (early, width - early))
+    ]
+    near = project(heads, heads_core, w_own[1], w_here[1], 0, width, jnp.float32)
     return add(near, far)
 
 

time: 102 us -> 103 us (level)
  starting transfers between devices: 27.4 us -> 34.2 us
  blocking collectives: 14.7 us -> 11.7 us
  waiting for transfers between devices: 26.6 us -> 23.6 us
    ppermute x1, starting transfers between devices: 0.78 us -> 7.17 us  [local(): heads_core = lax.ppermute(heads, 'c', shift(NC, 1))]
    ppermute x1 -> x2, waiting for transfers between devices: 6.85 us -> 3.71 us  [local(): lax.ppermute(project(heads, heads_core, w_own[0], w_here[0], first, colum...]
    ppermute x2, starting transfers between devices: 4.07 us -> 0.96 us  [local(): w_here = [lax.ppermute(w, 'c', shift(NC, 1)) for w in w_sent]]
    all_to_all x1, blocking collectives: 14.7 us -> 11.7 us  [local(): heads = lax.all_to_all(heads, 'z', 0, 0, tiled=True)[:HEADS]]
    ppermute x1, starting transfers between devices: 1.14 us -> 3.29 us  [local(): there = lax.ppermute(sent, 'xh', shift(XH, 1))]
    ppermute x1, starting transfers between devices: 1.91 us -> 0.1 us  [local(): there_stats = lax.ppermute(sent_stats, 'xh', shift(XH, 1))]
    ppermute x1 -> x2, starting transfers between devices: 0.11 us -> 1.64 us  [local(): lax.ppermute(project(heads, heads_core, w_own[0], w_here[0], first, colum...]
    ppermute x1, waiting for transfers between devices: 1.94 us -> 3.4 us  [local(): query = (query, lax.ppermute(query, 'xh', shift(XH, 1)))]
  transfers between devices with their start and end apart: 14 -> 15, of which waited for: 7 -> 8; matrix products, arithmetic and copies ran while one was open for 5% -> 7% of each run, Pallas kernels for 20% -> 21%
where the time goes in v11:
time: 103 us
  starting transfers between devices  34.2 us (33%)
  Pallas kernels  25.7 us (25%)
  waiting for transfers between devices  23.6 us (23%)
  blocking collectives  11.7 us (11%)
  local copies, waits for them, and re-layouts  7.32 us (7%)
    all_to_all x1, waiting for transfers between devices, local(): slots = lax.all_to_all(slots, 'z', 0, 0, tiled=True)  13.1 us
    all_to_all x1, blocking collectives, local(): heads = lax.all_to_all(heads, 'z', 0, 0, tiled=True)[:HEADS]  11.7 us
    all_to_all x1, starting transfers between devices, local(): slots = lax.all_to_all(slots, 'z', 0, 0, tiled=True)  9.03 us
    pallas_call x2, Pallas kernels, attend(): pl.pallas_call(kernel, out_shape=(whole, whole, whole), in_specs=in_smem(...  8.02 us
    ppermute x1, starting transfers between devices, local(): heads_core = lax.ppermute(heads, 'c', shift(NC, 1))  7.17 us
    dynamic_slice x1, local copies, waits for them, and re-layouts, w_columns(): lax.dynamic_slice(w, (0, (to_xl * NC + to_c) * width), (w.shape[0], width))  5.26 us
    pallas_call x2, Pallas kernels, attend_last(): pl.pallas_call(kernel, out_shape=(jax.ShapeDtypeStruct((NZ, BLOCK, HEAD_D...  5.1 us
    pallas_call x3, Pallas kernels, project(): pl.pallas_call(kernel, out_shape=jax.ShapeDtypeStruct((BLOCK, width), dty...  4.86 us
  transfers between devices with their start and end apart: 15, of which 8 were waited for; matrix products, arithmetic and copies ran while one was open for 7% of the time, Pallas kernels for 21%

profile of v11, /device:TPU:1, one launch (start us, length us, event | category | flops | bytes accessed | tf_op | source)
XLA Modules:
  0.0 102.6 jit_solution(9313612922944402918)
XLA Ops:
  0.0 1.9 %shard_map.55 = bf16[8,384,128]{2,1,0:T(8,128)(2,1)} custom-call(bf16[128,640]{1,0:T(8,128)(2,1)} %q_hbm.1, bf16[128,640]{1,0:T(8,128)(2,1)} %k_hbm.1, bf16[128,640]{1,0:T(8,128)(2,1)} %v_hbm.1), custom_call_target="tpu_custom_call" | custom-call | tf_op jit(solution)/shard_map/pallas_call | solution.py:53
  1.9 9.0 %all-to-all-start = ((bf16[8,384,128]{2,1,0:T(8,128)(2,1)}), bf16[8,384,128]{2,1,0:T(8,128)(2,1)}, u32[]{:S(2)}, u32[]{:S(2)}) async-start(bf16[8,384,128]{2,1,0:T(8,128)(2,1)} %shard_map.55), calls=%async_computation | async-start | bytes 1572864 | tf_op jit(solution)/shard_map/all_to_all | solution.py:388
  11.0 5.3 %constant_dynamic-slice_fusion = (bf16[640,1280]{1,0:T(8,128)(2,1)}, bf16[640,1280]{1,0:T(8,128)(2,1)}, bf16[640,1280]{1,0:T(8,128)(2,1)}, bf16[640,1280]{1,0:T(8,128)(2,1)S(1)}) fusion(bf16[640,5120]{1,0:T(8,128)(2,1)} %param.9, s32[]{:T(128)S(6)} %select_n.15, s32[]{:T(128)S(6)} %select_n.14, s32[]{:T(128)S(6)} %select_n.13, s32[]{:T(128)S(6)} %select_n.12), kind=kLoop, calls=%fused_computation | loop fusion | bytes 13107216 | tf_op jit(solution)/shard_map/dynamic_slice | solution.py:378
  17.2 4.4 %shard_map.56 = (s32[1]{0:T(128)}, s32[256]{0:T(256)S(1)}, s32[256]{0:T(256)S(1)}, s32[1]{0:T(128)}, s32[384]{0:T(512)S(1)}, /*index=5*/s32[384]{0:T(512)S(1)}, ...) custom-call(s32[64,64]{1,0:T(8,128)S(1)} %copy-done.1), custom_call_target="tpu_custom_call" | custom-call | flops 1000000 | bytes 100000 | tf_op jit(solution)/shard_map/pallas_call | solution.py:361
  21.5 13.1 %all-to-all-done = bf16[8,384,128]{2,1,0:T(8,128)(2,1)} async-done(((bf16[8,384,128]{2,1,0:T(8,128)(2,1)}), bf16[8,384,128]{2,1,0:T(8,128)(2,1)}, u32[]{:S(2)}, u32[]{:S(2)}) %all-to-all-start) | async-done | bytes 786464 | tf_op jit(solution)/shard_map/all_to_all | solution.py:388
  34.6 1.1 %fusion = (bf16[4,256,128]{2,1,0:T(8,128)(2,1)S(1)}, bf16[4,256,128]{2,1,0:T(8,128)(2,1)S(1)}) fusion(bf16[8,384,128]{2,1,0:T(8,128)(2,1)} %all-to-all-done), kind=kLoop, calls=%fused_computation.4 | loop fusion | bytes 1048576 | tf_op jit(solution)/shard_map/slice | solution.py:390
  36.7 2.8 %collective-permute-start.2 = (bf16[8,128,128]{2,1,0:T(8,128)(2,1)S(1)}, bf16[8,128,128]{2,1,0:T(8,128)(2,1)S(1)}, u32[]{:S(2)}, u32[]{:S(2)}) collective-permute-start(bf16[8,128,128]{2,1,0:T(8,128)(2,1)S(1)} %slice.14.own_ref.q_ref), channel_id=1, source_target_pairs={{0,128},{128,0},{1,129},{129,1},{2,130},{130,2},{3,131},{131,3},{4... | collective-permute-start | bytes 786440 | tf_op jit(solution)/shard_map/ppermute | solution.py:395
  39.5 1.3 %collective-permute-start = (bf16[4,256,128]{2,1,0:T(8,128)(2,1)S(1)}, bf16[4,256,128]{2,1,0:T(8,128)(2,1)S(1)}, u32[]{:S(2)}, u32[]{:S(2)}) collective-permute-start(bf16[4,256,128]{2,1,0:T(8,128)(2,1)S(1)} %get-tuple-element.87.refs_0_), channel_id=1, source_target_pairs={{0,4},{4,8},{8,12},{12,0},{1,5},{5,9},{9,13},{13,1},{2,6},{6,10},{... | collective-permute-start | bytes 786440 | tf_op jit(solution)/shard_map/ppermute | solution.py:392
  40.8 1.4 %collective-permute-start.1 = (bf16[4,256,128]{2,1,0:T(8,128)(2,1)S(1)}, bf16[4,256,128]{2,1,0:T(8,128)(2,1)S(1)}, u32[]{:S(2)}, u32[]{:S(2)}) collective-permute-start(bf16[4,256,128]{2,1,0:T(8,128)(2,1)S(1)} %get-tuple-element.88.refs_1_), channel_id=1, source_target_pairs={{0,12},{4,0},{8,4},{12,8},{1,13},{5,1},{9,5},{13,9},{2,14},{6,2},{... | collective-permute-start | bytes 786440 | tf_op jit(solution)/shard_map/ppermute | solution.py:393
  42.2 3.4 %collective-permute-done.2.other_ref.q_ref = bf16[8,128,128]{2,1,0:T(8,128)(2,1)S(1)} collective-permute-done((bf16[8,128,128]{2,1,0:T(8,128)(2,1)S(1)}, bf16[8,128,128]{2,1,0:T(8,128)(2,1)S(1)}, u32[]{:S(2)}, u32[]{:S(2)}) %collective-permute-start.2) | collective-permute-done | bytes 262176 | tf_op jit(solution)/shard_map/ppermute | solution.py:395
  45.7 2.7 %collective-permute-start.6 = (bf16[4,256,128]{2,1,0:T(8,128)(2,1)S(1)}, bf16[4,256,128]{2,1,0:T(8,128)(2,1)S(1)}, u32[]{:S(2)}, u32[]{:S(2)}) collective-permute-start(bf16[4,256,128]{2,1,0:T(8,128)(2,1)S(1)} %get-tuple-element.87.refs_0_), channel_id=1, source_target_pairs={{0,12},{4,0},{8,4},{12,8},{1,13},{5,1},{9,5},{13,9},{2,14},{6,2},{... | collective-permute-start | bytes 786440 | tf_op jit(solution)/shard_map/ppermute | solution.py:397
  48.4 3.4 %shard_map.57 = (f32[16,128,128]{2,1,0:T(8,128)S(1)}, f32[16,128,128]{2,1,0:T(8,128)S(1)}, f32[16,128,128]{2,1,0:T(8,128)S(1)}) custom-call(s32[1]{0:T(128)} %get-tuple-element.89.count_ref, s32[256]{0:T(256)S(1)} %get-tuple-element.90.block_ref, s32[256]{0:T(256)S(1)} %get-tuple-element.91.slot_ref, bf16[8,128,128]{2,1,0:T(8,128)(2,1)S(1)} %slice.14.own_ref.q_ref, ...), custom_call_target="tpu_custom_call" | custom-call | flops 335544320 | bytes 6291456 | tf_op jit(solution)/shard_map/pallas_call | solution.py:216
  51.8 1.3 %collective-permute-start.3 = (bf16[4,256,128]{2,1,0:T(8,128)(2,1)S(1)}, bf16[4,256,128]{2,1,0:T(8,128)(2,1)S(1)}, u32[]{:S(2)}, u32[]{:S(2)}) collective-permute-start(bf16[4,256,128]{2,1,0:T(8,128)(2,1)S(1)} %collective-permute-done.refs_0_), channel_id=1, source_target_pairs={{0,4},{4,8},{8,12},{12,0},{1,5},{5,9},{9,13},{13,1},{2,6},{6,10},{... | collective-permute-start | bytes 786440 | tf_op jit(solution)/shard_map/ppermute | solution.py:400
  53.7 2.4 %collective-permute-start.4 = (bf16[4,256,128]{2,1,0:T(8,128)(2,1)S(1)}, bf16[4,256,128]{2,1,0:T(8,128)(2,1)S(1)}, u32[]{:S(2)}, u32[]{:S(2)}) collective-permute-start(bf16[4,256,128]{2,1,0:T(8,128)(2,1)S(1)} %collective-permute-done.1.refs_3_), channel_id=1, source_target_pairs={{0,12},{4,0},{8,4},{12,8},{1,13},{5,1},{9,5},{13,9},{2,14},{6,2},{... | collective-permute-start | bytes 786440 | tf_op jit(solution)/shard_map/ppermute | solution.py:401
  56.1 4.6 %shard_map.58 = (f32[16,128,128]{2,1,0:T(8,128)S(1)}, f32[16,128,128]{2,1,0:T(8,128)S(1)}, f32[16,128,128]{2,1,0:T(8,128)S(1)}) custom-call(s32[1]{0:T(128)} %get-tuple-element.100.count_ref, s32[384]{0:T(512)S(1)} %get-tuple-element.101.block_ref, s32[384]{0:T(512)S(1)} %get-tuple-element.102.slot_ref, bf16[8,128,128]{2,1,0:T(8,128)(2,1)S(1)} %slice.14.own_ref.q_ref, ...), custom_call_target="tpu_custom_call" | custom-call | flops 671088640 | bytes 6291456 | tf_op jit(solution)/shard_map/pallas_call | solution.py:216
  61.5 2.2 %shard_map.59 = (bf16[8,128,128]{2,1,0:T(8,128)(2,1)S(1)}, f32[16,128]{1,0:T(8,128)S(1)}) custom-call(s32[1]{0:T(128)} %get-tuple-element.97.count_ref, s32[192]{0:T(256)S(1)} %get-tuple-element.98.block_ref, s32[192]{0:T(256)S(1)} %get-tuple-element.99.slot_ref, bf16[8,128,128]{2,1,0:T(8,128)(2,1)S(1)} %collective-permute-done.2.other_ref.q_ref, ...), custom_call_target="tpu_custom_call" | custom-call | flops 83886080 | bytes 3145728 | tf_op jit(solution)/shard_map/pallas_call | solution.py:161
  63.7 3.3 %collective-permute-start.7 = (bf16[8,128,128]{2,1,0:T(8,128)(2,1)S(1)}, bf16[8,128,128]{2,1,0:T(8,128)(2,1)S(1)}, u32[]{:S(2)}, u32[]{:S(2)}) collective-permute-start(bf16[8,128,128]{2,1,0:T(8,128)(2,1)S(1)} %get-tuple-element.116), channel_id=1, source_target_pairs={{0,128},{128,0},{1,129},{129,1},{2,130},{130,2},{3,131},{131,3},{4... | collective-permute-start | bytes 786440 | tf_op jit(solution)/shard_map/ppermute | solution.py:406
  67.1 2.9 %shard_map.60 = (f32[8,128,128]{2,1,0:T(8,128)S(1)}, f32[128,128]{1,0:T(8,128)S(1)}) custom-call(s32[1]{0:T(128)} %get-tuple-element.82.count_ref, s32[192]{0:T(256)S(1)} %get-tuple-element.83.block_ref, s32[192]{0:T(256)S(1)} %get-tuple-element.84.slot_ref, bf16[8,128,128]{2,1,0:T(8,128)(2,1)S(1)} %slice.14.own_ref.q_ref, ...), custom_call_target="tpu_custom_call" | custom-call | flops 83886080 | bytes 3145728 | tf_op jit(solution)/shard_map/pallas_call | solution.py:161
  71.6 11.7 %all_to_all.10 = bf16[8,128,128]{2,1,0:T(8,128)(2,1)S(1)} all-to-all(bf16[8,128,128]{2,1,0:T(8,128)(2,1)S(1)} %shard_map.61), channel_id=1, replica_groups=mesh['xh'=2,'z'=8,'y'=4,'xl'=2,'c'=2] {'z'}, dimensions={0} | all-to-all | bytes 524288 | tf_op jit(solution)/shard_map/all_to_all | solution.py:411
  83.4 7.2 %collective-permute-start.11 = (bf16[5,128,128]{2,1,0:T(8,128)(2,1)S(1)}, bf16[5,128,128]{2,1,0:T(8,128)(2,1)S(1)}, u32[]{:S(2)}, u32[]{:S(2)}) collective-permute-start(bf16[5,128,128]{2,1,0:T(8,128)(2,1)S(1)} %slice.16.a_ref), channel_id=1, source_target_pairs={{0,1},{1,0},{2,3},{3,2},{4,5},{5,4},{6,7},{7,6},{8,9},{9,8},{10,11... | collective-permute-start | bytes 491528 | tf_op jit(solution)/shard_map/ppermute | solution.py:412
  91.6 1.2 %shard_map.64 = bf16[128,768]{1,0:T(8,128)(2,1)S(1)} custom-call(bf16[5,128,128]{2,1,0:T(8,128)(2,1)S(1)} %slice.16.a_ref, bf16[5,128,128]{2,1,0:T(8,128)(2,1)S(1)} %collective-permute-done.11.b_ref, bf16[640,1280]{1,0:T(8,128)(2,1)S(1)} %get-tuple-element.123.w_hbm, bf16[640,1280]{1,0:T(8,128)(2,1)S(1)} %collective-permute-done.8.w2_hbm), custom_call_target="tpu_custom_call" | custom-call | flops 251658240 | bytes 4194304 | tf_op jit(solution)/shard_map/pallas_call | solution.py:290
  94.1 1.3 %collective-permute-start.12 = (bf16[128,512]{1,0:T(8,128)(2,1)S(1)}, bf16[128,512]{1,0:T(8,128)(2,1)S(1)}, u32[]{:S(2)}, u32[]{:S(2)}) collective-permute-start(bf16[128,512]{1,0:T(8,128)(2,1)S(1)} %shard_map.63), channel_id=1, source_target_pairs={{0,2},{2,0},{1,3},{3,1},{4,6},{6,4},{5,7},{7,5},{8,10},{10,8},{9,1... | collective-permute-start | bytes 393224 | tf_op jit(solution)/shard_map/ppermute | solution.py:415
  95.3 2.8 %shard_map.62.near_ref = f32[128,1280]{1,0:T(8,128)S(1)} custom-call(bf16[5,128,128]{2,1,0:T(8,128)(2,1)S(1)} %slice.16.a_ref, bf16[5,128,128]{2,1,0:T(8,128)(2,1)S(1)} %collective-permute-done.11.b_ref, bf16[640,1280]{1,0:T(8,128)(2,1)S(1)} %copy-done, bf16[640,1280]{1,0:T(8,128)(2,1)} %collective-permute-done.9.w2_hbm), custom_call_target="tpu_custom_call" | custom-call | flops 419430400 | bytes 4194304 | tf_op jit(solution)/shard_map/pallas_call | solution.py:290
  98.1 3.7 %collective-permute-done.12.refs_0_ = bf16[128,512]{1,0:T(8,128)(2,1)S(1)} collective-permute-done((bf16[128,512]{1,0:T(8,128)(2,1)S(1)}, bf16[128,512]{1,0:T(8,128)(2,1)S(1)}, u32[]{:S(2)}, u32[]{:S(2)}) %collective-permute-start.12) | collective-permute-done | bytes 131104 | tf_op jit(solution)/shard_map/ppermute | solution.py:415
  (26 shorter events, 8.1 us)
Async XLA Ops:
  1.9 32.7 %all-to-all-start = ((bf16[8,384,128]{2,1,0:T(8,128)(2,1)}), bf16[8,384,128]{2,1,0:T(8,128)(2,1)}, u32[]{:S(2)}, u32[]{:S(2)}) async-start(bf16[8,384,128]{2,1,0:T(8,128)(2,1)} %shard_map.55), calls=%async_computation | async-start | bytes 1572864 | tf_op jit(solution)/shard_map/all_to_all | solution.py:388
  11.0 6.2 %copy-start.1 = (s32[64,64]{1,0:T(8,128)S(1)}, s32[64,64]{1,0:T(8,128)}, u32[]{:S(2)}) copy-start(s32[64,64]{1,0:T(8,128)} %mask_ref) | copy-start | bytes 49156
  16.2 53.8 %collective-permute-start.8 = (bf16[640,1280]{1,0:T(8,128)(2,1)}, bf16[640,1280]{1,0:T(8,128)(2,1)S(1)}, u32[]{:S(2)}, u32[]{:S(2)}) collective-permute-start(bf16[640,1280]{1,0:T(8,128)(2,1)} %get-tuple-element.117), channel_id=1, source_target_pairs={{0,1},{1,0},{2,3},{3,2},{4,5},{5,4},{6,7},{7,6},{8,9},{9,8},{10,11... | collective-permute-start | bytes 4915208 | tf_op jit(solution)/shard_map/ppermute | solution.py:385
  17.2 52.8 %collective-permute-start.9 = (bf16[640,1280]{1,0:T(8,128)(2,1)}, bf16[640,1280]{1,0:T(8,128)(2,1)}, u32[]{:S(2)}, u32[]{:S(2)}) collective-permute-start(bf16[640,1280]{1,0:T(8,128)(2,1)} %get-tuple-element.118), channel_id=1, source_target_pairs={{0,1},{1,0},{2,3},{3,2},{4,5},{5,4},{6,7},{7,6},{8,9},{9,8},{10,11... | collective-permute-start | bytes 4915208 | tf_op jit(solution)/shard_map/ppermute | solution.py:385
  36.7 9.0 %collective-permute-start.2 = (bf16[8,128,128]{2,1,0:T(8,128)(2,1)S(1)}, bf16[8,128,128]{2,1,0:T(8,128)(2,1)S(1)}, u32[]{:S(2)}, u32[]{:S(2)}) collective-permute-start(bf16[8,128,128]{2,1,0:T(8,128)(2,1)S(1)} %slice.14.own_ref.q_ref), channel_id=1, source_target_pairs={{0,128},{128,0},{1,129},{129,1},{2,130},{130,2},{3,131},{131,3},{4... | collective-permute-start | bytes 786440 | tf_op jit(solution)/shard_map/ppermute | solution.py:395
  39.5 8.9 %collective-permute-start = (bf16[4,256,128]{2,1,0:T(8,128)(2,1)S(1)}, bf16[4,256,128]{2,1,0:T(8,128)(2,1)S(1)}, u32[]{:S(2)}, u32[]{:S(2)}) collective-permute-start(bf16[4,256,128]{2,1,0:T(8,128)(2,1)S(1)} %get-tuple-element.87.refs_0_), channel_id=1, source_target_pairs={{0,4},{4,8},{8,12},{12,0},{1,5},{5,9},{9,13},{13,1},{2,6},{6,10},{... | collective-permute-start | bytes 786440 | tf_op jit(solution)/shard_map/ppermute | solution.py:392
  40.8 11.0 %collective-permute-start.1 = (bf16[4,256,128]{2,1,0:T(8,128)(2,1)S(1)}, bf16[4,256,128]{2,1,0:T(8,128)(2,1)S(1)}, u32[]{:S(2)}, u32[]{:S(2)}) collective-permute-start(bf16[4,256,128]{2,1,0:T(8,128)(2,1)S(1)} %get-tuple-element.88.refs_1_), channel_id=1, source_target_pairs={{0,12},{4,0},{8,4},{12,8},{1,13},{5,1},{9,5},{13,9},{2,14},{6,2},{... | collective-permute-start | bytes 786440 | tf_op jit(solution)/shard_map/ppermute | solution.py:393
  45.7 8.0 %collective-permute-start.6 = (bf16[4,256,128]{2,1,0:T(8,128)(2,1)S(1)}, bf16[4,256,128]{2,1,0:T(8,128)(2,1)S(1)}, u32[]{:S(2)}, u32[]{:S(2)}) collective-permute-start(bf16[4,256,128]{2,1,0:T(8,128)(2,1)S(1)} %get-tuple-element.87.refs_0_), channel_id=1, source_target_pairs={{0,12},{4,0},{8,4},{12,8},{1,13},{5,1},{9,5},{13,9},{2,14},{6,2},{... | collective-permute-start | bytes 786440 | tf_op jit(solution)/shard_map/ppermute | solution.py:397
  48.4 7.7 %collective-permute-start.5 = (bf16[4,256,128]{2,1,0:T(8,128)(2,1)S(1)}, bf16[4,256,128]{2,1,0:T(8,128)(2,1)S(1)}, u32[]{:S(2)}, u32[]{:S(2)}) collective-permute-start(bf16[4,256,128]{2,1,0:T(8,128)(2,1)S(1)} %get-tuple-element.88.refs_1_), channel_id=1, source_target_pairs={{0,4},{4,8},{8,12},{12,0},{1,5},{5,9},{9,13},{13,1},{2,6},{6,10},{... | collective-permute-start | bytes 786440 | tf_op jit(solution)/shard_map/ppermute | solution.py:396
  51.8 9.7 %collective-permute-start.3 = (bf16[4,256,128]{2,1,0:T(8,128)(2,1)S(1)}, bf16[4,256,128]{2,1,0:T(8,128)(2,1)S(1)}, u32[]{:S(2)}, u32[]{:S(2)}) collective-permute-start(bf16[4,256,128]{2,1,0:T(8,128)(2,1)S(1)} %collective-permute-done.refs_0_), channel_id=1, source_target_pairs={{0,4},{4,8},{8,12},{12,0},{1,5},{5,9},{9,13},{13,1},{2,6},{6,10},{... | collective-permute-start | bytes 786440 | tf_op jit(solution)/shard_map/ppermute | solution.py:400
  53.7 7.8 %collective-permute-start.4 = (bf16[4,256,128]{2,1,0:T(8,128)(2,1)S(1)}, bf16[4,256,128]{2,1,0:T(8,128)(2,1)S(1)}, u32[]{:S(2)}, u32[]{:S(2)}) collective-permute-start(bf16[4,256,128]{2,1,0:T(8,128)(2,1)S(1)} %collective-permute-done.1.refs_3_), channel_id=1, source_target_pairs={{0,12},{4,0},{8,4},{12,8},{1,13},{5,1},{9,5},{13,9},{2,14},{6,2},{... | collective-permute-start | bytes 786440 | tf_op jit(solution)/shard_map/ppermute | solution.py:401
  63.7 7.1 %collective-permute-start.7 = (bf16[8,128,128]{2,1,0:T(8,128)(2,1)S(1)}, bf16[8,128,128]{2,1,0:T(8,128)(2,1)S(1)}, u32[]{:S(2)}, u32[]{:S(2)}) collective-permute-start(bf16[8,128,128]{2,1,0:T(8,128)(2,1)S(1)} %get-tuple-element.116), channel_id=1, source_target_pairs={{0,128},{128,0},{1,129},{129,1},{2,130},{130,2},{3,131},{131,3},{4... | collective-permute-start | bytes 786440 | tf_op jit(solution)/shard_map/ppermute | solution.py:406
  67.0 4.0 %collective-permute-start.10 = (f32[16,128]{1,0:T(8,128)S(1)}, f32[16,128]{1,0:T(8,128)S(1)}, u32[]{:S(2)}, u32[]{:S(2)}) collective-permute-start(f32[16,128]{1,0:T(8,128)S(1)} %get-tuple-element.120), channel_id=1, source_target_pairs={{0,128},{128,0},{1,129},{129,1},{2,130},{130,2},{3,131},{131,3},{4... | collective-permute-start | bytes 24584 | tf_op jit(solution)/shard_map/ppermute | solution.py:407
  83.4 8.2 %collective-permute-start.11 = (bf16[5,128,128]{2,1,0:T(8,128)(2,1)S(1)}, bf16[5,128,128]{2,1,0:T(8,128)(2,1)S(1)}, u32[]{:S(2)}, u32[]{:S(2)}) collective-permute-start(bf16[5,128,128]{2,1,0:T(8,128)(2,1)S(1)} %slice.16.a_ref), channel_id=1, source_target_pairs={{0,1},{1,0},{2,3},{3,2},{4,5},{5,4},{6,7},{7,6},{8,9},{9,8},{10,11... | collective-permute-start | bytes 491528 | tf_op jit(solution)/shard_map/ppermute | solution.py:412
  92.8 2.6 %copy-start = (bf16[640,1280]{1,0:T(8,128)(2,1)S(1)}, bf16[640,1280]{1,0:T(8,128)(2,1)}, u32[]{:S(2)}) copy-start(bf16[640,1280]{1,0:T(8,128)(2,1)} %get-tuple-element.121.w_hbm) | copy-start | bytes 4915204
  92.8 9.0 %collective-permute-start.13 = (bf16[128,768]{1,0:T(8,128)(2,1)S(1)}, bf16[128,768]{1,0:T(8,128)(2,1)S(1)}, u32[]{:S(2)}, u32[]{:S(2)}) collective-permute-start(bf16[128,768]{1,0:T(8,128)(2,1)S(1)} %shard_map.64), channel_id=1, source_target_pairs={{0,2},{2,0},{1,3},{3,1},{4,6},{6,4},{5,7},{7,5},{8,10},{10,8},{9,1... | collective-permute-start | bytes 589832 | tf_op jit(solution)/shard_map/ppermute | solution.py:415
  94.1 7.7 %collective-permute-start.12 = (bf16[128,512]{1,0:T(8,128)(2,1)S(1)}, bf16[128,512]{1,0:T(8,128)(2,1)S(1)}, u32[]{:S(2)}, u32[]{:S(2)}) collective-permute-start(bf16[128,512]{1,0:T(8,128)(2,1)S(1)} %shard_map.63), channel_id=1, source_target_pairs={{0,2},{2,0},{1,3},{3,1},{4,6},{6,4},{5,7},{7,5},{8,10},{10,8},{9,1... | collective-permute-start | bytes 393224 | tf_op jit(solution)/shard_map/ppermute | solution.py:415

commit v12 on v11

--- a/solution.py
+++ b/solution.py
@@ -393,8 +393,9 @@
     after_high = lax.ppermute(high, "y", shift(NY, -1))
     query = slots[:, :BLOCK]
     query = (query, lax.ppermute(query, "xh", shift(XH, 1)))
-    before_high = lax.ppermute(high, "y", shift(NY, 1))
-    after_low = lax.ppermute(low, "y", shift(NY, -1))
+    late_low, late_high, w_here = lax.optimization_barrier((low, high, w_here))
+    before_high = lax.ppermute(late_high, "y", shift(NY, 1))
+    after_low = lax.ppermute(late_low, "y", shift(NY, -1))
     state = attend(groups[0], query, [low, high], None)
     before_low, after_high, state = lax.optimization_barrier((before_low, after_high, state))
     far_low = lax.ppermute(before_low, "y", shift(NY, 1))
@@ -406,7 +407,6 @@
     there = lax.ppermute(sent, "xh", shift(XH, 1))
     there_stats = lax.ppermute(sent_stats, "xh", shift(XH, 1))
     here, here_stats = attend_last(groups[3], query[0], far_parts, state, True)
-    there, w_here = lax.optimization_barrier((there, w_here))
     heads = merge(here, here_stats, there, there_stats)
     heads = lax.all_to_all(heads, "z", 0, 0, tiled=True)[:HEADS]
     heads_core = lax.ppermute(heads, "c", shift(NC, 1))

time: 103 us -> 98.4 us (0.955)
  starting transfers between devices: 34.2 us -> 30.2 us
  waiting for transfers between devices: 23.6 us -> 21.7 us
  Pallas kernels: 25.7 us -> 26.9 us
    ppermute x1, starting transfers between devices: 7.17 us -> 4.41 us  [local(): heads_core = lax.ppermute(heads, 'c', shift(NC, 1))]
    ppermute x1, waiting for transfers between devices: 3.4 us -> 0.72 us  [local(): query = (query, lax.ppermute(query, 'xh', shift(XH, 1)))]
    ppermute x1, starting transfers between devices: 3.29 us -> 0.67 us  [local(): there = lax.ppermute(sent, 'xh', shift(XH, 1))]
    ppermute x1, starting transfers between devices: 0.1 us -> 2.36 us  [local(): there_stats = lax.ppermute(sent_stats, 'xh', shift(XH, 1))]
  transfers between devices with their start and end apart: 15 -> 15, of which waited for: 8 -> 8; matrix products, arithmetic and copies ran while one was open for 7% -> 7% of each run, Pallas kernels for 21% -> 20%
where the time goes in v12:
time: 98.4 us; the launch traced here: 98.2 us
  starting transfers between devices  30.2 us (31%)
  Pallas kernels  26.9 us (27%)
  waiting for transfers between devices  21.7 us (22%)
  blocking collectives  11.9 us (12%)
  local copies, waits for them, and re-layouts  7.3 us (7%)
    all_to_all x1, waiting for transfers between devices, local(): slots = lax.all_to_all(slots, 'z', 0, 0, tiled=True)  13.1 us
    all_to_all x1, blocking collectives, local(): heads = lax.all_to_all(heads, 'z', 0, 0, tiled=True)[:HEADS]  11.9 us
    all_to_all x1, starting transfers between devices, local(): slots = lax.all_to_all(slots, 'z', 0, 0, tiled=True)  9.03 us
    pallas_call x2, Pallas kernels, attend(): pl.pallas_call(kernel, out_shape=(whole, whole, whole), in_specs=in_smem(...  8.44 us
    pallas_call x2, Pallas kernels, attend_last(): pl.pallas_call(kernel, out_shape=(jax.ShapeDtypeStruct((NZ, BLOCK, HEAD_D...  5.92 us
    dynamic_slice x1, local copies, waits for them, and re-layouts, w_columns(): lax.dynamic_slice(w, (0, (to_xl * NC + to_c) * width), (w.shape[0], width))  5.24 us
    pallas_call x3, Pallas kernels, project(): pl.pallas_call(kernel, out_shape=jax.ShapeDtypeStruct((BLOCK, width), dty...  4.86 us
    ppermute x1, starting transfers between devices, local(): heads_core = lax.ppermute(heads, 'c', shift(NC, 1))  4.41 us
  transfers between devices with their start and end apart: 15, of which 8 were waited for; matrix products, arithmetic and copies ran while one was open for 7% of the time, Pallas kernels for 20%

profile of v12, /device:TPU:1, one launch (start us, length us, event | category | flops | bytes accessed | tf_op | source)
XLA Modules:
  0.0 98.2 jit_solution(13956143522068232455)
XLA Ops:
  0.0 1.9 %shard_map.55 = bf16[8,384,128]{2,1,0:T(8,128)(2,1)} custom-call(bf16[128,640]{1,0:T(8,128)(2,1)} %q_hbm.1, bf16[128,640]{1,0:T(8,128)(2,1)} %k_hbm.1, bf16[128,640]{1,0:T(8,128)(2,1)} %v_hbm.1), custom_call_target="tpu_custom_call" | custom-call | tf_op jit(solution)/shard_map/pallas_call | solution.py:53
  1.9 9.0 %all-to-all-start = ((bf16[8,384,128]{2,1,0:T(8,128)(2,1)}), bf16[8,384,128]{2,1,0:T(8,128)(2,1)}, u32[]{:S(2)}, u32[]{:S(2)}) async-start(bf16[8,384,128]{2,1,0:T(8,128)(2,1)} %shard_map.55), calls=%async_computation | async-start | bytes 1572864 | tf_op jit(solution)/shard_map/all_to_all | solution.py:388
  11.0 5.2 %constant_dynamic-slice_fusion = (bf16[640,1280]{1,0:T(8,128)(2,1)}, bf16[640,1280]{1,0:T(8,128)(2,1)}, bf16[640,1280]{1,0:T(8,128)(2,1)}, bf16[640,1280]{1,0:T(8,128)(2,1)S(1)}) fusion(bf16[640,5120]{1,0:T(8,128)(2,1)} %param.9, s32[]{:T(128)S(6)} %select_n.15, s32[]{:T(128)S(6)} %select_n.14, s32[]{:T(128)S(6)} %select_n.13, s32[]{:T(128)S(6)} %select_n.12), kind=kLoop, calls=%fused_computation | loop fusion | bytes 13107216 | tf_op jit(solution)/shard_map/dynamic_slice | solution.py:378
  17.2 4.4 %shard_map.56 = (s32[1]{0:T(128)}, s32[256]{0:T(256)S(1)}, s32[256]{0:T(256)S(1)}, s32[1]{0:T(128)}, s32[384]{0:T(512)S(1)}, /*index=5*/s32[384]{0:T(512)S(1)}, ...) custom-call(s32[64,64]{1,0:T(8,128)S(1)} %copy-done.1), custom_call_target="tpu_custom_call" | custom-call | flops 1000000 | bytes 100000 | tf_op jit(solution)/shard_map/pallas_call | solution.py:361
  21.5 13.1 %all-to-all-done = bf16[8,384,128]{2,1,0:T(8,128)(2,1)} async-done(((bf16[8,384,128]{2,1,0:T(8,128)(2,1)}), bf16[8,384,128]{2,1,0:T(8,128)(2,1)}, u32[]{:S(2)}, u32[]{:S(2)}) %all-to-all-start) | async-done | bytes 786464 | tf_op jit(solution)/shard_map/all_to_all | solution.py:388
  34.6 1.1 %fusion = (bf16[4,256,128]{2,1,0:T(8,128)(2,1)S(1)}, bf16[4,256,128]{2,1,0:T(8,128)(2,1)S(1)}) fusion(bf16[8,384,128]{2,1,0:T(8,128)(2,1)} %all-to-all-done), kind=kLoop, calls=%fused_computation.4 | loop fusion | bytes 1048576 | tf_op jit(solution)/shard_map/slice | solution.py:390
  36.7 2.8 %collective-permute-start.2 = (bf16[8,128,128]{2,1,0:T(8,128)(2,1)S(1)}, bf16[8,128,128]{2,1,0:T(8,128)(2,1)S(1)}, u32[]{:S(2)}, u32[]{:S(2)}) collective-permute-start(bf16[8,128,128]{2,1,0:T(8,128)(2,1)S(1)} %slice.14.own_ref.q_ref), channel_id=1, source_target_pairs={{0,128},{128,0},{1,129},{129,1},{2,130},{130,2},{3,131},{131,3},{4... | collective-permute-start | bytes 786440 | tf_op jit(solution)/shard_map/ppermute | solution.py:395
  39.5 1.3 %collective-permute-start = (bf16[4,256,128]{2,1,0:T(8,128)(2,1)S(1)}, bf16[4,256,128]{2,1,0:T(8,128)(2,1)S(1)}, u32[]{:S(2)}, u32[]{:S(2)}) collective-permute-start(bf16[4,256,128]{2,1,0:T(8,128)(2,1)S(1)} %get-tuple-element.107.refs_0_), channel_id=1, source_target_pairs={{0,4},{4,8},{8,12},{12,0},{1,5},{5,9},{9,13},{13,1},{2,6},{6,10},{... | collective-permute-start | bytes 786440 | tf_op jit(solution)/shard_map/ppermute | solution.py:392
  40.8 1.4 %collective-permute-start.1 = (bf16[4,256,128]{2,1,0:T(8,128)(2,1)S(1)}, bf16[4,256,128]{2,1,0:T(8,128)(2,1)S(1)}, u32[]{:S(2)}, u32[]{:S(2)}) collective-permute-start(bf16[4,256,128]{2,1,0:T(8,128)(2,1)S(1)} %get-tuple-element.106.refs_1_), channel_id=1, source_target_pairs={{0,12},{4,0},{8,4},{12,8},{1,13},{5,1},{9,5},{13,9},{2,14},{6,2},{... | collective-permute-start | bytes 786440 | tf_op jit(solution)/shard_map/ppermute | solution.py:393
  42.3 2.7 %collective-permute-start.8 = (bf16[4,256,128]{2,1,0:T(8,128)(2,1)S(1)}, bf16[4,256,128]{2,1,0:T(8,128)(2,1)S(1)}, u32[]{:S(2)}, u32[]{:S(2)}) collective-permute-start(bf16[4,256,128]{2,1,0:T(8,128)(2,1)S(1)} %get-tuple-element.107.refs_0_), channel_id=1, source_target_pairs={{0,12},{4,0},{8,4},{12,8},{1,13},{5,1},{9,5},{13,9},{2,14},{6,2},{... | collective-permute-start | bytes 786440 | tf_op jit(solution)/shard_map/ppermute | solution.py:398
  45.7 3.4 %shard_map.57 = (f32[16,128,128]{2,1,0:T(8,128)S(1)}, f32[16,128,128]{2,1,0:T(8,128)S(1)}, f32[16,128,128]{2,1,0:T(8,128)S(1)}) custom-call(s32[1]{0:T(128)} %get-tuple-element.90.count_ref, s32[256]{0:T(256)S(1)} %get-tuple-element.91.block_ref, s32[256]{0:T(256)S(1)} %get-tuple-element.92.slot_ref, bf16[8,128,128]{2,1,0:T(8,128)(2,1)S(1)} %slice.14.own_ref.q_ref, ...), custom_call_target="tpu_custom_call" | custom-call | flops 335544320 | bytes 6291456 | tf_op jit(solution)/shard_map/pallas_call | solution.py:216
  49.1 1.4 %collective-permute-start.3 = (bf16[4,256,128]{2,1,0:T(8,128)(2,1)S(1)}, bf16[4,256,128]{2,1,0:T(8,128)(2,1)S(1)}, u32[]{:S(2)}, u32[]{:S(2)}) collective-permute-start(bf16[4,256,128]{2,1,0:T(8,128)(2,1)S(1)} %collective-permute-done.refs_0_), channel_id=1, source_target_pairs={{0,4},{4,8},{8,12},{12,0},{1,5},{5,9},{9,13},{13,1},{2,6},{6,10},{... | collective-permute-start | bytes 786440 | tf_op jit(solution)/shard_map/ppermute | solution.py:401
  50.4 1.5 %collective-permute-start.4 = (bf16[4,256,128]{2,1,0:T(8,128)(2,1)S(1)}, bf16[4,256,128]{2,1,0:T(8,128)(2,1)S(1)}, u32[]{:S(2)}, u32[]{:S(2)}) collective-permute-start(bf16[4,256,128]{2,1,0:T(8,128)(2,1)S(1)} %collective-permute-done.1.refs_3_), channel_id=1, source_target_pairs={{0,12},{4,0},{8,4},{12,8},{1,13},{5,1},{9,5},{13,9},{2,14},{6,2},{... | collective-permute-start | bytes 786440 | tf_op jit(solution)/shard_map/ppermute | solution.py:402
  52.0 1.5 %collective-permute-done.7.refs_1_ = bf16[4,256,128]{2,1,0:T(8,128)(2,1)S(1)} collective-permute-done((bf16[4,256,128]{2,1,0:T(8,128)(2,1)S(1)}, bf16[4,256,128]{2,1,0:T(8,128)(2,1)S(1)}, u32[]{:S(2)}, u32[]{:S(2)}) %collective-permute-start.7) | collective-permute-done | bytes 262176 | tf_op jit(solution)/shard_map/ppermute | solution.py:397
  53.5 5.0 %shard_map.58 = (f32[16,128,128]{2,1,0:T(8,128)S(1)}, f32[16,128,128]{2,1,0:T(8,128)S(1)}, f32[16,128,128]{2,1,0:T(8,128)S(1)}) custom-call(s32[1]{0:T(128)} %get-tuple-element.101.count_ref, s32[384]{0:T(512)S(1)} %get-tuple-element.102.block_ref, s32[384]{0:T(512)S(1)} %get-tuple-element.103.slot_ref, bf16[8,128,128]{2,1,0:T(8,128)(2,1)S(1)} %slice.14.own_ref.q_ref, ...), custom_call_target="tpu_custom_call" | custom-call | flops 671088640 | bytes 6291456 | tf_op jit(solution)/shard_map/pallas_call | solution.py:216
  59.2 2.6 %shard_map.59 = (bf16[8,128,128]{2,1,0:T(8,128)(2,1)S(1)}, f32[16,128]{1,0:T(8,128)S(1)}) custom-call(s32[1]{0:T(128)} %get-tuple-element.98.count_ref, s32[192]{0:T(256)S(1)} %get-tuple-element.99.block_ref, s32[192]{0:T(256)S(1)} %get-tuple-element.100.slot_ref, bf16[8,128,128]{2,1,0:T(8,128)(2,1)S(1)} %collective-permute-done.2.other_ref.q_ref, ...), custom_call_target="tpu_custom_call" | custom-call | flops 83886080 | bytes 3145728 | tf_op jit(solution)/shard_map/pallas_call | solution.py:161
  62.5 2.4 %collective-permute-start.10 = (f32[16,128]{1,0:T(8,128)S(1)}, f32[16,128]{1,0:T(8,128)S(1)}, u32[]{:S(2)}, u32[]{:S(2)}) collective-permute-start(f32[16,128]{1,0:T(8,128)S(1)} %get-tuple-element.122), channel_id=1, source_target_pairs={{0,128},{128,0},{1,129},{129,1},{2,130},{130,2},{3,131},{131,3},{4... | collective-permute-start | bytes 24584 | tf_op jit(solution)/shard_map/ppermute | solution.py:408
  64.8 3.3 %shard_map.60 = (f32[8,128,128]{2,1,0:T(8,128)S(1)}, f32[128,128]{1,0:T(8,128)S(1)}) custom-call(s32[1]{0:T(128)} %get-tuple-element.83.count_ref, s32[192]{0:T(256)S(1)} %get-tuple-element.84.block_ref, s32[192]{0:T(256)S(1)} %get-tuple-element.85.slot_ref, bf16[8,128,128]{2,1,0:T(8,128)(2,1)S(1)} %slice.14.own_ref.q_ref, ...), custom_call_target="tpu_custom_call" | custom-call | flops 83886080 | bytes 3145728 | tf_op jit(solution)/shard_map/pallas_call | solution.py:161
  69.8 11.9 %all_to_all.10 = bf16[8,128,128]{2,1,0:T(8,128)(2,1)S(1)} all-to-all(bf16[8,128,128]{2,1,0:T(8,128)(2,1)S(1)} %shard_map.61), channel_id=1, replica_groups=mesh['xh'=2,'z'=8,'y'=4,'xl'=2,'c'=2] {'z'}, dimensions={0} | all-to-all | bytes 524288 | tf_op jit(solution)/shard_map/all_to_all | solution.py:411
  81.7 4.4 %collective-permute-start.11 = (bf16[5,128,128]{2,1,0:T(8,128)(2,1)S(1)}, bf16[5,128,128]{2,1,0:T(8,128)(2,1)S(1)}, u32[]{:S(2)}, u32[]{:S(2)}) collective-permute-start(bf16[5,128,128]{2,1,0:T(8,128)(2,1)S(1)} %slice.16.a_ref), channel_id=1, source_target_pairs={{0,1},{1,0},{2,3},{3,2},{4,5},{5,4},{6,7},{7,6},{8,9},{9,8},{10,11... | collective-permute-start | bytes 491528 | tf_op jit(solution)/shard_map/ppermute | solution.py:412
  87.1 1.2 %shard_map.64 = bf16[128,768]{1,0:T(8,128)(2,1)S(1)} custom-call(bf16[5,128,128]{2,1,0:T(8,128)(2,1)S(1)} %slice.16.a_ref, bf16[5,128,128]{2,1,0:T(8,128)(2,1)S(1)} %collective-permute-done.11.b_ref, bf16[640,1280]{1,0:T(8,128)(2,1)S(1)} %get-tuple-element.125.w_hbm, bf16[640,1280]{1,0:T(8,128)(2,1)S(1)} %collective-permute-done.5.w2_hbm), custom_call_target="tpu_custom_call" | custom-call | flops 251658240 | bytes 4194304 | tf_op jit(solution)/shard_map/pallas_call | solution.py:290
  89.7 1.2 %collective-permute-start.12 = (bf16[128,512]{1,0:T(8,128)(2,1)S(1)}, bf16[128,512]{1,0:T(8,128)(2,1)S(1)}, u32[]{:S(2)}, u32[]{:S(2)}) collective-permute-start(bf16[128,512]{1,0:T(8,128)(2,1)S(1)} %shard_map.63), channel_id=1, source_target_pairs={{0,2},{2,0},{1,3},{3,1},{4,6},{6,4},{5,7},{7,5},{8,10},{10,8},{9,1... | collective-permute-start | bytes 393224 | tf_op jit(solution)/shard_map/ppermute | solution.py:415
  90.9 2.8 %shard_map.62.near_ref = f32[128,1280]{1,0:T(8,128)S(1)} custom-call(bf16[5,128,128]{2,1,0:T(8,128)(2,1)S(1)} %slice.16.a_ref, bf16[5,128,128]{2,1,0:T(8,128)(2,1)S(1)} %collective-permute-done.11.b_ref, bf16[640,1280]{1,0:T(8,128)(2,1)S(1)} %copy-done, bf16[640,1280]{1,0:T(8,128)(2,1)} %collective-permute-done.6.w2_hbm), custom_call_target="tpu_custom_call" | custom-call | flops 419430400 | bytes 4194304 | tf_op jit(solution)/shard_map/pallas_call | solution.py:290
  93.7 3.7 %collective-permute-done.12.refs_0_ = bf16[128,512]{1,0:T(8,128)(2,1)S(1)} collective-permute-done((bf16[128,512]{1,0:T(8,128)(2,1)S(1)}, bf16[128,512]{1,0:T(8,128)(2,1)S(1)}, u32[]{:S(2)}, u32[]{:S(2)}) %collective-permute-start.12) | collective-permute-done | bytes 131104 | tf_op jit(solution)/shard_map/ppermute | solution.py:415
  (26 shorter events, 8.8 us)
Async XLA Ops:
  1.9 32.7 %all-to-all-start = ((bf16[8,384,128]{2,1,0:T(8,128)(2,1)}), bf16[8,384,128]{2,1,0:T(8,128)(2,1)}, u32[]{:S(2)}, u32[]{:S(2)}) async-start(bf16[8,384,128]{2,1,0:T(8,128)(2,1)} %shard_map.55), calls=%async_computation | async-start | bytes 1572864 | tf_op jit(solution)/shard_map/all_to_all | solution.py:388
  11.0 6.2 %copy-start.1 = (s32[64,64]{1,0:T(8,128)S(1)}, s32[64,64]{1,0:T(8,128)}, u32[]{:S(2)}) copy-start(s32[64,64]{1,0:T(8,128)} %mask_ref) | copy-start | bytes 49156
  16.2 26.1 %collective-permute-start.5 = (bf16[640,1280]{1,0:T(8,128)(2,1)}, bf16[640,1280]{1,0:T(8,128)(2,1)S(1)}, u32[]{:S(2)}, u32[]{:S(2)}) collective-permute-start(bf16[640,1280]{1,0:T(8,128)(2,1)} %get-tuple-element.104), channel_id=1, source_target_pairs={{0,1},{1,0},{2,3},{3,2},{4,5},{5,4},{6,7},{7,6},{8,9},{9,8},{10,11... | collective-permute-start | bytes 4915208 | tf_op jit(solution)/shard_map/ppermute | solution.py:385
  17.2 25.1 %collective-permute-start.6 = (bf16[640,1280]{1,0:T(8,128)(2,1)}, bf16[640,1280]{1,0:T(8,128)(2,1)}, u32[]{:S(2)}, u32[]{:S(2)}) collective-permute-start(bf16[640,1280]{1,0:T(8,128)(2,1)} %get-tuple-element.105), channel_id=1, source_target_pairs={{0,1},{1,0},{2,3},{3,2},{4,5},{5,4},{6,7},{7,6},{8,9},{9,8},{10,11... | collective-permute-start | bytes 4915208 | tf_op jit(solution)/shard_map/ppermute | solution.py:385
  36.7 9.0 %collective-permute-start.2 = (bf16[8,128,128]{2,1,0:T(8,128)(2,1)S(1)}, bf16[8,128,128]{2,1,0:T(8,128)(2,1)S(1)}, u32[]{:S(2)}, u32[]{:S(2)}) collective-permute-start(bf16[8,128,128]{2,1,0:T(8,128)(2,1)S(1)} %slice.14.own_ref.q_ref), channel_id=1, source_target_pairs={{0,128},{128,0},{1,129},{129,1},{2,130},{130,2},{3,131},{131,3},{4... | collective-permute-start | bytes 786440 | tf_op jit(solution)/shard_map/ppermute | solution.py:395
  39.5 9.5 %collective-permute-start = (bf16[4,256,128]{2,1,0:T(8,128)(2,1)S(1)}, bf16[4,256,128]{2,1,0:T(8,128)(2,1)S(1)}, u32[]{:S(2)}, u32[]{:S(2)}) collective-permute-start(bf16[4,256,128]{2,1,0:T(8,128)(2,1)S(1)} %get-tuple-element.107.refs_0_), channel_id=1, source_target_pairs={{0,4},{4,8},{8,12},{12,0},{1,5},{5,9},{9,13},{13,1},{2,6},{6,10},{... | collective-permute-start | bytes 786440 | tf_op jit(solution)/shard_map/ppermute | solution.py:392
  40.8 8.3 %collective-permute-start.1 = (bf16[4,256,128]{2,1,0:T(8,128)(2,1)S(1)}, bf16[4,256,128]{2,1,0:T(8,128)(2,1)S(1)}, u32[]{:S(2)}, u32[]{:S(2)}) collective-permute-start(bf16[4,256,128]{2,1,0:T(8,128)(2,1)S(1)} %get-tuple-element.106.refs_1_), channel_id=1, source_target_pairs={{0,12},{4,0},{8,4},{12,8},{1,13},{5,1},{9,5},{13,9},{2,14},{6,2},{... | collective-permute-start | bytes 786440 | tf_op jit(solution)/shard_map/ppermute | solution.py:393
  42.3 11.3 %collective-permute-start.7 = (bf16[4,256,128]{2,1,0:T(8,128)(2,1)S(1)}, bf16[4,256,128]{2,1,0:T(8,128)(2,1)S(1)}, u32[]{:S(2)}, u32[]{:S(2)}) collective-permute-start(bf16[4,256,128]{2,1,0:T(8,128)(2,1)S(1)} %get-tuple-element.106.refs_1_), channel_id=1, source_target_pairs={{0,4},{4,8},{8,12},{12,0},{1,5},{5,9},{9,13},{13,1},{2,6},{6,10},{... | collective-permute-start | bytes 786440 | tf_op jit(solution)/shard_map/ppermute | solution.py:397
  42.3 11.3 %collective-permute-start.8 = (bf16[4,256,128]{2,1,0:T(8,128)(2,1)S(1)}, bf16[4,256,128]{2,1,0:T(8,128)(2,1)S(1)}, u32[]{:S(2)}, u32[]{:S(2)}) collective-permute-start(bf16[4,256,128]{2,1,0:T(8,128)(2,1)S(1)} %get-tuple-element.107.refs_0_), channel_id=1, source_target_pairs={{0,12},{4,0},{8,4},{12,8},{1,13},{5,1},{9,5},{13,9},{2,14},{6,2},{... | collective-permute-start | bytes 786440 | tf_op jit(solution)/shard_map/ppermute | solution.py:398
  49.1 10.1 %collective-permute-start.3 = (bf16[4,256,128]{2,1,0:T(8,128)(2,1)S(1)}, bf16[4,256,128]{2,1,0:T(8,128)(2,1)S(1)}, u32[]{:S(2)}, u32[]{:S(2)}) collective-permute-start(bf16[4,256,128]{2,1,0:T(8,128)(2,1)S(1)} %collective-permute-done.refs_0_), channel_id=1, source_target_pairs={{0,4},{4,8},{8,12},{12,0},{1,5},{5,9},{9,13},{13,1},{2,6},{6,10},{... | collective-permute-start | bytes 786440 | tf_op jit(solution)/shard_map/ppermute | solution.py:401
  50.4 8.8 %collective-permute-start.4 = (bf16[4,256,128]{2,1,0:T(8,128)(2,1)S(1)}, bf16[4,256,128]{2,1,0:T(8,128)(2,1)S(1)}, u32[]{:S(2)}, u32[]{:S(2)}) collective-permute-start(bf16[4,256,128]{2,1,0:T(8,128)(2,1)S(1)} %collective-permute-done.1.refs_3_), channel_id=1, source_target_pairs={{0,12},{4,0},{8,4},{12,8},{1,13},{5,1},{9,5},{13,9},{2,14},{6,2},{... | collective-permute-start | bytes 786440 | tf_op jit(solution)/shard_map/ppermute | solution.py:402
  61.8 7.4 %collective-permute-start.9 = (bf16[8,128,128]{2,1,0:T(8,128)(2,1)S(1)}, bf16[8,128,128]{2,1,0:T(8,128)(2,1)S(1)}, u32[]{:S(2)}, u32[]{:S(2)}) collective-permute-start(bf16[8,128,128]{2,1,0:T(8,128)(2,1)S(1)} %get-tuple-element.121), channel_id=1, source_target_pairs={{0,128},{128,0},{1,129},{129,1},{2,130},{130,2},{3,131},{131,3},{4... | collective-permute-start | bytes 786440 | tf_op jit(solution)/shard_map/ppermute | solution.py:407
  62.5 6.7 %collective-permute-start.10 = (f32[16,128]{1,0:T(8,128)S(1)}, f32[16,128]{1,0:T(8,128)S(1)}, u32[]{:S(2)}, u32[]{:S(2)}) collective-permute-start(f32[16,128]{1,0:T(8,128)S(1)} %get-tuple-element.122), channel_id=1, source_target_pairs={{0,128},{128,0},{1,129},{129,1},{2,130},{130,2},{3,131},{131,3},{4... | collective-permute-start | bytes 24584 | tf_op jit(solution)/shard_map/ppermute | solution.py:408
  81.7 5.4 %collective-permute-start.11 = (bf16[5,128,128]{2,1,0:T(8,128)(2,1)S(1)}, bf16[5,128,128]{2,1,0:T(8,128)(2,1)S(1)}, u32[]{:S(2)}, u32[]{:S(2)}) collective-permute-start(bf16[5,128,128]{2,1,0:T(8,128)(2,1)S(1)} %slice.16.a_ref), channel_id=1, source_target_pairs={{0,1},{1,0},{2,3},{3,2},{4,5},{5,4},{6,7},{7,6},{8,9},{9,8},{10,11... | collective-permute-start | bytes 491528 | tf_op jit(solution)/shard_map/ppermute | solution.py:412
  88.3 2.6 %copy-start = (bf16[640,1280]{1,0:T(8,128)(2,1)S(1)}, bf16[640,1280]{1,0:T(8,128)(2,1)}, u32[]{:S(2)}) copy-start(bf16[640,1280]{1,0:T(8,128)(2,1)} %get-tuple-element.123.w_hbm) | copy-start | bytes 4915204
  88.4 9.0 %collective-permute-start.13 = (bf16[128,768]{1,0:T(8,128)(2,1)S(1)}, bf16[128,768]{1,0:T(8,128)(2,1)S(1)}, u32[]{:S(2)}, u32[]{:S(2)}) collective-permute-start(bf16[128,768]{1,0:T(8,128)(2,1)S(1)} %shard_map.64), channel_id=1, source_target_pairs={{0,2},{2,0},{1,3},{3,1},{4,6},{6,4},{5,7},{7,5},{8,10},{10,8},{9,1... | collective-permute-start | bytes 589832 | tf_op jit(solution)/shard_map/ppermute | solution.py:415
  89.7 7.7 %collective-permute-start.12 = (bf16[128,512]{1,0:T(8,128)(2,1)S(1)}, bf16[128,512]{1,0:T(8,128)(2,1)S(1)}, u32[]{:S(2)}, u32[]{:S(2)}) collective-permute-start(bf16[128,512]{1,0:T(8,128)(2,1)S(1)} %shard_map.63), channel_id=1, source_target_pairs={{0,2},{2,0},{1,3},{3,1},{4,6},{6,4},{5,7},{7,5},{8,10},{10,8},{9,1... | collective-permute-start | bytes 393224 | tf_op jit(solution)/shard_map/ppermute | solution.py:415

commit v13 on v12

--- a/solution.py
+++ b/solution.py
@@ -11,7 +11,7 @@
 HEADS = 5
 XH, NZ, NY, XL, NC = 2, 8, 4, 2, 2
 ROWS = XH * NZ
-UNROLL = 4
+UNROLL = 8
 TILE_N = 256
 LOW = -1e30
 EXP2_SCALE = HEAD_DIM ** (-0.5) * 1.4426950408889634

time: 98.4 us -> 97.7 us (level)
  Pallas kernels: 26.9 us -> 25.8 us
  waiting for transfers between devices: 21.7 us -> 22.7 us
  transfers between devices with their start and end apart: 15 -> 15, of which waited for: 8 -> 7; matrix products, arithmetic and copies ran while one was open for 7% -> 7% of each run, Pallas kernels for 20% -> 19%
where the time goes in v13:
time: 97.7 us
  starting transfers between devices  29.8 us (31%)
  Pallas kernels  25.8 us (26%)
  waiting for transfers between devices  22.7 us (23%)
  blocking collectives  11.8 us (12%)
  local copies, waits for them, and re-layouts  7.3 us (7%)
    all_to_all x1, waiting for transfers between devices, local(): slots = lax.all_to_all(slots, 'z', 0, 0, tiled=True)  13.1 us
    all_to_all x1, blocking collectives, local(): heads = lax.all_to_all(heads, 'z', 0, 0, tiled=True)[:HEADS]  11.8 us
    all_to_all x1, starting transfers between devices, local(): slots = lax.all_to_all(slots, 'z', 0, 0, tiled=True)  9.03 us
    pallas_call x2, Pallas kernels, attend(): pl.pallas_call(kernel, out_shape=(whole, whole, whole), in_specs=in_smem(...  7.95 us
    pallas_call x2, Pallas kernels, attend_last(): pl.pallas_call(kernel, out_shape=(jax.ShapeDtypeStruct((NZ, BLOCK, HEAD_D...  5.32 us
    dynamic_slice x1, local copies, waits for them, and re-layouts, w_columns(): lax.dynamic_slice(w, (0, (to_xl * NC + to_c) * width), (w.shape[0], width))  5.24 us
    pallas_call x3, Pallas kernels, project(): pl.pallas_call(kernel, out_shape=jax.ShapeDtypeStruct((BLOCK, width), dty...  4.85 us
    pallas_call x1, Pallas kernels, live_tiles(): pl.pallas_call(tiles_kernel, out_shape=tuple(out_shape), in_specs=in_smem...  4.37 us
  transfers between devices with their start and end apart: 15, of which 7 were waited for; matrix products, arithmetic and copies ran while one was open for 7% of the time, Pallas kernels for 19%

profile of v13, /device:TPU:1, one launch (start us, length us, event | category | flops | bytes accessed | tf_op | source)
XLA Modules:
  0.0 97.7 jit_solution(12104113621426017462)
XLA Ops:
  0.0 1.9 %shard_map.55 = bf16[8,384,128]{2,1,0:T(8,128)(2,1)} custom-call(bf16[128,640]{1,0:T(8,128)(2,1)} %q_hbm.1, bf16[128,640]{1,0:T(8,128)(2,1)} %k_hbm.1, bf16[128,640]{1,0:T(8,128)(2,1)} %v_hbm.1), custom_call_target="tpu_custom_call" | custom-call | tf_op jit(solution)/shard_map/pallas_call | solution.py:53
  1.9 9.0 %all-to-all-start = ((bf16[8,384,128]{2,1,0:T(8,128)(2,1)}), bf16[8,384,128]{2,1,0:T(8,128)(2,1)}, u32[]{:S(2)}, u32[]{:S(2)}) async-start(bf16[8,384,128]{2,1,0:T(8,128)(2,1)} %shard_map.55), calls=%async_computation | async-start | bytes 1572864 | tf_op jit(solution)/shard_map/all_to_all | solution.py:388
  11.0 5.2 %constant_dynamic-slice_fusion = (bf16[640,1280]{1,0:T(8,128)(2,1)}, bf16[640,1280]{1,0:T(8,128)(2,1)}, bf16[640,1280]{1,0:T(8,128)(2,1)}, bf16[640,1280]{1,0:T(8,128)(2,1)S(1)}) fusion(bf16[640,5120]{1,0:T(8,128)(2,1)} %param.9, s32[]{:T(128)S(6)} %select_n.15, s32[]{:T(128)S(6)} %select_n.14, s32[]{:T(128)S(6)} %select_n.13, s32[]{:T(128)S(6)} %select_n.12), kind=kLoop, calls=%fused_computation | loop fusion | bytes 13107216 | tf_op jit(solution)/shard_map/dynamic_slice | solution.py:378
  17.2 4.4 %shard_map.56 = (s32[1]{0:T(128)}, s32[256]{0:T(256)S(1)}, s32[256]{0:T(256)S(1)}, s32[1]{0:T(128)}, s32[384]{0:T(512)S(1)}, /*index=5*/s32[384]{0:T(512)S(1)}, ...) custom-call(s32[64,64]{1,0:T(8,128)S(1)} %copy-done.1), custom_call_target="tpu_custom_call" | custom-call | flops 1000000 | bytes 100000 | tf_op jit(solution)/shard_map/pallas_call | solution.py:361
  21.5 13.1 %all-to-all-done = bf16[8,384,128]{2,1,0:T(8,128)(2,1)} async-done(((bf16[8,384,128]{2,1,0:T(8,128)(2,1)}), bf16[8,384,128]{2,1,0:T(8,128)(2,1)}, u32[]{:S(2)}, u32[]{:S(2)}) %all-to-all-start) | async-done | bytes 786464 | tf_op jit(solution)/shard_map/all_to_all | solution.py:388
  36.7 2.8 %collective-permute-start.2 = (bf16[8,128,128]{2,1,0:T(8,128)(2,1)S(1)}, bf16[8,128,128]{2,1,0:T(8,128)(2,1)S(1)}, u32[]{:S(2)}, u32[]{:S(2)}) collective-permute-start(bf16[8,128,128]{2,1,0:T(8,128)(2,1)S(1)} %slice.14.own_ref.q_ref), channel_id=1, source_target_pairs={{0,128},{128,0},{1,129},{129,1},{2,130},{130,2},{3,131},{131,3},{4... | collective-permute-start | bytes 786440 | tf_op jit(solution)/shard_map/ppermute | solution.py:395
  39.5 1.3 %collective-permute-start = (bf16[4,256,128]{2,1,0:T(8,128)(2,1)S(1)}, bf16[4,256,128]{2,1,0:T(8,128)(2,1)S(1)}, u32[]{:S(2)}, u32[]{:S(2)}) collective-permute-start(bf16[4,256,128]{2,1,0:T(8,128)(2,1)S(1)} %get-tuple-element.107.refs_0_), channel_id=1, source_target_pairs={{0,4},{4,8},{8,12},{12,0},{1,5},{5,9},{9,13},{13,1},{2,6},{6,10},{... | collective-permute-start | bytes 786440 | tf_op jit(solution)/shard_map/ppermute | solution.py:392
  40.8 1.4 %collective-permute-start.1 = (bf16[4,256,128]{2,1,0:T(8,128)(2,1)S(1)}, bf16[4,256,128]{2,1,0:T(8,128)(2,1)S(1)}, u32[]{:S(2)}, u32[]{:S(2)}) collective-permute-start(bf16[4,256,128]{2,1,0:T(8,128)(2,1)S(1)} %get-tuple-element.106.refs_1_), channel_id=1, source_target_pairs={{0,12},{4,0},{8,4},{12,8},{1,13},{5,1},{9,5},{13,9},{2,14},{6,2},{... | collective-permute-start | bytes 786440 | tf_op jit(solution)/shard_map/ppermute | solution.py:393
  42.3 2.7 %collective-permute-start.8 = (bf16[4,256,128]{2,1,0:T(8,128)(2,1)S(1)}, bf16[4,256,128]{2,1,0:T(8,128)(2,1)S(1)}, u32[]{:S(2)}, u32[]{:S(2)}) collective-permute-start(bf16[4,256,128]{2,1,0:T(8,128)(2,1)S(1)} %get-tuple-element.107.refs_0_), channel_id=1, source_target_pairs={{0,12},{4,0},{8,4},{12,8},{1,13},{5,1},{9,5},{13,9},{2,14},{6,2},{... | collective-permute-start | bytes 786440 | tf_op jit(solution)/shard_map/ppermute | solution.py:398
  45.7 3.4 %shard_map.57 = (f32[16,128,128]{2,1,0:T(8,128)S(1)}, f32[16,128,128]{2,1,0:T(8,128)S(1)}, f32[16,128,128]{2,1,0:T(8,128)S(1)}) custom-call(s32[1]{0:T(128)} %get-tuple-element.90.count_ref, s32[256]{0:T(256)S(1)} %get-tuple-element.91.block_ref, s32[256]{0:T(256)S(1)} %get-tuple-element.92.slot_ref, bf16[8,128,128]{2,1,0:T(8,128)(2,1)S(1)} %slice.14.own_ref.q_ref, ...), custom_call_target="tpu_custom_call" | custom-call | flops 335544320 | bytes 6291456 | tf_op jit(solution)/shard_map/pallas_call | solution.py:216
  49.9 1.9 %collective-permute-start.4 = (bf16[4,256,128]{2,1,0:T(8,128)(2,1)S(1)}, bf16[4,256,128]{2,1,0:T(8,128)(2,1)S(1)}, u32[]{:S(2)}, u32[]{:S(2)}) collective-permute-start(bf16[4,256,128]{2,1,0:T(8,128)(2,1)S(1)} %collective-permute-done.1.refs_3_), channel_id=1, source_target_pairs={{0,12},{4,0},{8,4},{12,8},{1,13},{5,1},{9,5},{13,9},{2,14},{6,2},{... | collective-permute-start | bytes 786440 | tf_op jit(solution)/shard_map/ppermute | solution.py:402
  51.9 1.7 %collective-permute-done.7.refs_1_ = bf16[4,256,128]{2,1,0:T(8,128)(2,1)S(1)} collective-permute-done((bf16[4,256,128]{2,1,0:T(8,128)(2,1)S(1)}, bf16[4,256,128]{2,1,0:T(8,128)(2,1)S(1)}, u32[]{:S(2)}, u32[]{:S(2)}) %collective-permute-start.7) | collective-permute-done | bytes 262176 | tf_op jit(solution)/shard_map/ppermute | solution.py:397
  53.5 4.5 %shard_map.58 = (f32[16,128,128]{2,1,0:T(8,128)S(1)}, f32[16,128,128]{2,1,0:T(8,128)S(1)}, f32[16,128,128]{2,1,0:T(8,128)S(1)}) custom-call(s32[1]{0:T(128)} %get-tuple-element.101.count_ref, s32[384]{0:T(512)S(1)} %get-tuple-element.102.block_ref, s32[384]{0:T(512)S(1)} %get-tuple-element.103.slot_ref, bf16[8,128,128]{2,1,0:T(8,128)(2,1)S(1)} %slice.14.own_ref.q_ref, ...), custom_call_target="tpu_custom_call" | custom-call | flops 671088640 | bytes 6291456 | tf_op jit(solution)/shard_map/pallas_call | solution.py:216
  58.1 1.1 %collective-permute-done.3.refs_0_ = bf16[4,256,128]{2,1,0:T(8,128)(2,1)S(1)} collective-permute-done((bf16[4,256,128]{2,1,0:T(8,128)(2,1)S(1)}, bf16[4,256,128]{2,1,0:T(8,128)(2,1)S(1)}, u32[]{:S(2)}, u32[]{:S(2)}) %collective-permute-start.3) | collective-permute-done | bytes 262176 | tf_op jit(solution)/shard_map/ppermute | solution.py:401
  59.2 2.3 %shard_map.59 = (bf16[8,128,128]{2,1,0:T(8,128)(2,1)S(1)}, f32[16,128]{1,0:T(8,128)S(1)}) custom-call(s32[1]{0:T(128)} %get-tuple-element.98.count_ref, s32[192]{0:T(256)S(1)} %get-tuple-element.99.block_ref, s32[192]{0:T(256)S(1)} %get-tuple-element.100.slot_ref, bf16[8,128,128]{2,1,0:T(8,128)(2,1)S(1)} %collective-permute-done.2.other_ref.q_ref, ...), custom_call_target="tpu_custom_call" | custom-call | flops 83886080 | bytes 3145728 | tf_op jit(solution)/shard_map/pallas_call | solution.py:161
  61.8 2.7 %collective-permute-start.10 = (f32[16,128]{1,0:T(8,128)S(1)}, f32[16,128]{1,0:T(8,128)S(1)}, u32[]{:S(2)}, u32[]{:S(2)}) collective-permute-start(f32[16,128]{1,0:T(8,128)S(1)} %get-tuple-element.122), channel_id=1, source_target_pairs={{0,128},{128,0},{1,129},{129,1},{2,130},{130,2},{3,131},{131,3},{4... | collective-permute-start | bytes 24584 | tf_op jit(solution)/shard_map/ppermute | solution.py:408
  64.5 3.0 %shard_map.60 = (f32[8,128,128]{2,1,0:T(8,128)S(1)}, f32[128,128]{1,0:T(8,128)S(1)}) custom-call(s32[1]{0:T(128)} %get-tuple-element.83.count_ref, s32[192]{0:T(256)S(1)} %get-tuple-element.84.block_ref, s32[192]{0:T(256)S(1)} %get-tuple-element.85.slot_ref, bf16[8,128,128]{2,1,0:T(8,128)(2,1)S(1)} %slice.14.own_ref.q_ref, ...), custom_call_target="tpu_custom_call" | custom-call | flops 83886080 | bytes 3145728 | tf_op jit(solution)/shard_map/pallas_call | solution.py:161
  67.5 1.4 %collective-permute-done.10.there_stats_ref = f32[16,128]{1,0:T(8,128)S(1)} collective-permute-done((f32[16,128]{1,0:T(8,128)S(1)}, f32[16,128]{1,0:T(8,128)S(1)}, u32[]{:S(2)}, u32[]{:S(2)}) %collective-permute-start.10) | collective-permute-done | bytes 8224 | tf_op jit(solution)/shard_map/ppermute | solution.py:408
  69.6 11.8 %all_to_all.10 = bf16[8,128,128]{2,1,0:T(8,128)(2,1)S(1)} all-to-all(bf16[8,128,128]{2,1,0:T(8,128)(2,1)S(1)} %shard_map.61), channel_id=1, replica_groups=mesh['xh'=2,'z'=8,'y'=4,'xl'=2,'c'=2] {'z'}, dimensions={0} | all-to-all | bytes 524288 | tf_op jit(solution)/shard_map/all_to_all | solution.py:411
  81.4 4.2 %collective-permute-start.11 = (bf16[5,128,128]{2,1,0:T(8,128)(2,1)S(1)}, bf16[5,128,128]{2,1,0:T(8,128)(2,1)S(1)}, u32[]{:S(2)}, u32[]{:S(2)}) collective-permute-start(bf16[5,128,128]{2,1,0:T(8,128)(2,1)S(1)} %slice.16.a_ref), channel_id=1, source_target_pairs={{0,1},{1,0},{2,3},{3,2},{4,5},{5,4},{6,7},{7,6},{8,9},{9,8},{10,11... | collective-permute-start | bytes 491528 | tf_op jit(solution)/shard_map/ppermute | solution.py:412
  86.6 1.2 %shard_map.64 = bf16[128,768]{1,0:T(8,128)(2,1)S(1)} custom-call(bf16[5,128,128]{2,1,0:T(8,128)(2,1)S(1)} %slice.16.a_ref, bf16[5,128,128]{2,1,0:T(8,128)(2,1)S(1)} %collective-permute-done.11.b_ref, bf16[640,1280]{1,0:T(8,128)(2,1)S(1)} %get-tuple-element.125.w_hbm, bf16[640,1280]{1,0:T(8,128)(2,1)S(1)} %collective-permute-done.5.w2_hbm), custom_call_target="tpu_custom_call" | custom-call | flops 251658240 | bytes 4194304 | tf_op jit(solution)/shard_map/pallas_call | solution.py:290
  89.2 1.2 %collective-permute-start.12 = (bf16[128,512]{1,0:T(8,128)(2,1)S(1)}, bf16[128,512]{1,0:T(8,128)(2,1)S(1)}, u32[]{:S(2)}, u32[]{:S(2)}) collective-permute-start(bf16[128,512]{1,0:T(8,128)(2,1)S(1)} %shard_map.63), channel_id=1, source_target_pairs={{0,2},{2,0},{1,3},{3,1},{4,6},{6,4},{5,7},{7,5},{8,10},{10,8},{9,1... | collective-permute-start | bytes 393224 | tf_op jit(solution)/shard_map/ppermute | solution.py:415
  90.4 2.8 %shard_map.62.near_ref = f32[128,1280]{1,0:T(8,128)S(1)} custom-call(bf16[5,128,128]{2,1,0:T(8,128)(2,1)S(1)} %slice.16.a_ref, bf16[5,128,128]{2,1,0:T(8,128)(2,1)S(1)} %collective-permute-done.11.b_ref, bf16[640,1280]{1,0:T(8,128)(2,1)S(1)} %copy-done, bf16[640,1280]{1,0:T(8,128)(2,1)} %collective-permute-done.6.w2_hbm), custom_call_target="tpu_custom_call" | custom-call | flops 419430400 | bytes 4194304 | tf_op jit(solution)/shard_map/pallas_call | solution.py:290
  93.2 3.7 %collective-permute-done.12.refs_0_ = bf16[128,512]{1,0:T(8,128)(2,1)S(1)} collective-permute-done((bf16[128,512]{1,0:T(8,128)(2,1)S(1)}, bf16[128,512]{1,0:T(8,128)(2,1)S(1)}, u32[]{:S(2)}, u32[]{:S(2)}) %collective-permute-start.12) | collective-permute-done | bytes 131104 | tf_op jit(solution)/shard_map/ppermute | solution.py:415
  (26 shorter events, 8.7 us)
Async XLA Ops:
  1.9 32.7 %all-to-all-start = ((bf16[8,384,128]{2,1,0:T(8,128)(2,1)}), bf16[8,384,128]{2,1,0:T(8,128)(2,1)}, u32[]{:S(2)}, u32[]{:S(2)}) async-start(bf16[8,384,128]{2,1,0:T(8,128)(2,1)} %shard_map.55), calls=%async_computation | async-start | bytes 1572864 | tf_op jit(solution)/shard_map/all_to_all | solution.py:388
  11.0 6.2 %copy-start.1 = (s32[64,64]{1,0:T(8,128)S(1)}, s32[64,64]{1,0:T(8,128)}, u32[]{:S(2)}) copy-start(s32[64,64]{1,0:T(8,128)} %mask_ref) | copy-start | bytes 49156
  16.2 26.1 %collective-permute-start.5 = (bf16[640,1280]{1,0:T(8,128)(2,1)}, bf16[640,1280]{1,0:T(8,128)(2,1)S(1)}, u32[]{:S(2)}, u32[]{:S(2)}) collective-permute-start(bf16[640,1280]{1,0:T(8,128)(2,1)} %get-tuple-element.104), channel_id=1, source_target_pairs={{0,1},{1,0},{2,3},{3,2},{4,5},{5,4},{6,7},{7,6},{8,9},{9,8},{10,11... | collective-permute-start | bytes 4915208 | tf_op jit(solution)/shard_map/ppermute | solution.py:385
  17.2 25.1 %collective-permute-start.6 = (bf16[640,1280]{1,0:T(8,128)(2,1)}, bf16[640,1280]{1,0:T(8,128)(2,1)}, u32[]{:S(2)}, u32[]{:S(2)}) collective-permute-start(bf16[640,1280]{1,0:T(8,128)(2,1)} %get-tuple-element.105), channel_id=1, source_target_pairs={{0,1},{1,0},{2,3},{3,2},{4,5},{5,4},{6,7},{7,6},{8,9},{9,8},{10,11... | collective-permute-start | bytes 4915208 | tf_op jit(solution)/shard_map/ppermute | solution.py:385
  36.7 9.0 %collective-permute-start.2 = (bf16[8,128,128]{2,1,0:T(8,128)(2,1)S(1)}, bf16[8,128,128]{2,1,0:T(8,128)(2,1)S(1)}, u32[]{:S(2)}, u32[]{:S(2)}) collective-permute-start(bf16[8,128,128]{2,1,0:T(8,128)(2,1)S(1)} %slice.14.own_ref.q_ref), channel_id=1, source_target_pairs={{0,128},{128,0},{1,129},{129,1},{2,130},{130,2},{3,131},{131,3},{4... | collective-permute-start | bytes 786440 | tf_op jit(solution)/shard_map/ppermute | solution.py:395
  39.5 9.6 %collective-permute-start = (bf16[4,256,128]{2,1,0:T(8,128)(2,1)S(1)}, bf16[4,256,128]{2,1,0:T(8,128)(2,1)S(1)}, u32[]{:S(2)}, u32[]{:S(2)}) collective-permute-start(bf16[4,256,128]{2,1,0:T(8,128)(2,1)S(1)} %get-tuple-element.107.refs_0_), channel_id=1, source_target_pairs={{0,4},{4,8},{8,12},{12,0},{1,5},{5,9},{9,13},{13,1},{2,6},{6,10},{... | collective-permute-start | bytes 786440 | tf_op jit(solution)/shard_map/ppermute | solution.py:392
  40.8 8.3 %collective-permute-start.1 = (bf16[4,256,128]{2,1,0:T(8,128)(2,1)S(1)}, bf16[4,256,128]{2,1,0:T(8,128)(2,1)S(1)}, u32[]{:S(2)}, u32[]{:S(2)}) collective-permute-start(bf16[4,256,128]{2,1,0:T(8,128)(2,1)S(1)} %get-tuple-element.106.refs_1_), channel_id=1, source_target_pairs={{0,12},{4,0},{8,4},{12,8},{1,13},{5,1},{9,5},{13,9},{2,14},{6,2},{... | collective-permute-start | bytes 786440 | tf_op jit(solution)/shard_map/ppermute | solution.py:393
  42.3 11.3 %collective-permute-start.7 = (bf16[4,256,128]{2,1,0:T(8,128)(2,1)S(1)}, bf16[4,256,128]{2,1,0:T(8,128)(2,1)S(1)}, u32[]{:S(2)}, u32[]{:S(2)}) collective-permute-start(bf16[4,256,128]{2,1,0:T(8,128)(2,1)S(1)} %get-tuple-element.106.refs_1_), channel_id=1, source_target_pairs={{0,4},{4,8},{8,12},{12,0},{1,5},{5,9},{9,13},{13,1},{2,6},{6,10},{... | collective-permute-start | bytes 786440 | tf_op jit(solution)/shard_map/ppermute | solution.py:397
  42.3 11.3 %collective-permute-start.8 = (bf16[4,256,128]{2,1,0:T(8,128)(2,1)S(1)}, bf16[4,256,128]{2,1,0:T(8,128)(2,1)S(1)}, u32[]{:S(2)}, u32[]{:S(2)}) collective-permute-start(bf16[4,256,128]{2,1,0:T(8,128)(2,1)S(1)} %get-tuple-element.107.refs_0_), channel_id=1, source_target_pairs={{0,12},{4,0},{8,4},{12,8},{1,13},{5,1},{9,5},{13,9},{2,14},{6,2},{... | collective-permute-start | bytes 786440 | tf_op jit(solution)/shard_map/ppermute | solution.py:398
  49.1 10.0 %collective-permute-start.3 = (bf16[4,256,128]{2,1,0:T(8,128)(2,1)S(1)}, bf16[4,256,128]{2,1,0:T(8,128)(2,1)S(1)}, u32[]{:S(2)}, u32[]{:S(2)}) collective-permute-start(bf16[4,256,128]{2,1,0:T(8,128)(2,1)S(1)} %collective-permute-done.refs_0_), channel_id=1, source_target_pairs={{0,4},{4,8},{8,12},{12,0},{1,5},{5,9},{9,13},{13,1},{2,6},{6,10},{... | collective-permute-start | bytes 786440 | tf_op jit(solution)/shard_map/ppermute | solution.py:401
  49.9 9.2 %collective-permute-start.4 = (bf16[4,256,128]{2,1,0:T(8,128)(2,1)S(1)}, bf16[4,256,128]{2,1,0:T(8,128)(2,1)S(1)}, u32[]{:S(2)}, u32[]{:S(2)}) collective-permute-start(bf16[4,256,128]{2,1,0:T(8,128)(2,1)S(1)} %collective-permute-done.1.refs_3_), channel_id=1, source_target_pairs={{0,12},{4,0},{8,4},{12,8},{1,13},{5,1},{9,5},{13,9},{2,14},{6,2},{... | collective-permute-start | bytes 786440 | tf_op jit(solution)/shard_map/ppermute | solution.py:402
  61.5 7.4 %collective-permute-start.9 = (bf16[8,128,128]{2,1,0:T(8,128)(2,1)S(1)}, bf16[8,128,128]{2,1,0:T(8,128)(2,1)S(1)}, u32[]{:S(2)}, u32[]{:S(2)}) collective-permute-start(bf16[8,128,128]{2,1,0:T(8,128)(2,1)S(1)} %get-tuple-element.121), channel_id=1, source_target_pairs={{0,128},{128,0},{1,129},{129,1},{2,130},{130,2},{3,131},{131,3},{4... | collective-permute-start | bytes 786440 | tf_op jit(solution)/shard_map/ppermute | solution.py:407
  61.8 7.1 %collective-permute-start.10 = (f32[16,128]{1,0:T(8,128)S(1)}, f32[16,128]{1,0:T(8,128)S(1)}, u32[]{:S(2)}, u32[]{:S(2)}) collective-permute-start(f32[16,128]{1,0:T(8,128)S(1)} %get-tuple-element.122), channel_id=1, source_target_pairs={{0,128},{128,0},{1,129},{129,1},{2,130},{130,2},{3,131},{131,3},{4... | collective-permute-start | bytes 24584 | tf_op jit(solution)/shard_map/ppermute | solution.py:408
  81.4 5.2 %collective-permute-start.11 = (bf16[5,128,128]{2,1,0:T(8,128)(2,1)S(1)}, bf16[5,128,128]{2,1,0:T(8,128)(2,1)S(1)}, u32[]{:S(2)}, u32[]{:S(2)}) collective-permute-start(bf16[5,128,128]{2,1,0:T(8,128)(2,1)S(1)} %slice.16.a_ref), channel_id=1, source_target_pairs={{0,1},{1,0},{2,3},{3,2},{4,5},{5,4},{6,7},{7,6},{8,9},{9,8},{10,11... | collective-permute-start | bytes 491528 | tf_op jit(solution)/shard_map/ppermute | solution.py:412
  87.9 2.5 %copy-start = (bf16[640,1280]{1,0:T(8,128)(2,1)S(1)}, bf16[640,1280]{1,0:T(8,128)(2,1)}, u32[]{:S(2)}) copy-start(bf16[640,1280]{1,0:T(8,128)(2,1)} %get-tuple-element.123.w_hbm) | copy-start | bytes 4915204
  87.9 9.0 %collective-permute-start.13 = (bf16[128,768]{1,0:T(8,128)(2,1)S(1)}, bf16[128,768]{1,0:T(8,128)(2,1)S(1)}, u32[]{:S(2)}, u32[]{:S(2)}) collective-permute-start(bf16[128,768]{1,0:T(8,128)(2,1)S(1)} %shard_map.64), channel_id=1, source_target_pairs={{0,2},{2,0},{1,3},{3,1},{4,6},{6,4},{5,7},{7,5},{8,10},{10,8},{9,1... | collective-permute-start | bytes 589832 | tf_op jit(solution)/shard_map/ppermute | solution.py:415
  89.2 7.7 %collective-permute-start.12 = (bf16[128,512]{1,0:T(8,128)(2,1)S(1)}, bf16[128,512]{1,0:T(8,128)(2,1)S(1)}, u32[]{:S(2)}, u32[]{:S(2)}) collective-permute-start(bf16[128,512]{1,0:T(8,128)(2,1)S(1)} %shard_map.63), channel_id=1, source_target_pairs={{0,2},{2,0},{1,3},{3,1},{4,6},{6,4},{5,7},{7,5},{8,10},{10,8},{9,1... | collective-permute-start | bytes 393224 | tf_op jit(solution)/shard_map/ppermute | solution.py:415

commit v14 on v13

--- a/solution.py
+++ b/solution.py
@@ -64,13 +64,13 @@
     )(queries, keys, values)
 
 
-def score_tiles(count, tables, q_ref, kv_ref, s_ref, top_ref):
+def score_tiles(unroll, count, tables, q_ref, kv_ref, s_ref, top_ref):
     block_ref, slot_ref = tables
 
     def score(step, carry):
         tiles = []
-        for u in range(UNROLL):
-            e = step * UNROLL + u
+        for u in range(unroll):
+            e = step * unroll + u
             s = lax.dot_general(
                 q_ref[block_ref[e]],
                 kv_ref[slot_ref[e], :BLOCK, :],
@@ -80,21 +80,21 @@
             s = jnp.where(e < count, s, LOW)
             s_ref[e] = s
             tiles.append(s)
-        for u in range(UNROLL):
-            block = block_ref[step * UNROLL + u]
+        for u in range(unroll):
+            block = block_ref[step * unroll + u]
             top_ref[block] = jnp.maximum(top_ref[block], tiles[u])
         return carry
 
-    lax.fori_loop(0, (count + (UNROLL - 1)) // UNROLL, score, 0)
-
-
-def mix_tiles(count, tables, kv_ref, s_ref, m_ref, l_ref, a_ref):
+    lax.fori_loop(0, (count + (unroll - 1)) // unroll, score, 0)
+
+
+def mix_tiles(unroll, count, tables, kv_ref, s_ref, m_ref, l_ref, a_ref):
     block_ref, slot_ref = tables
 
     def mix(step, carry):
         weights, products = [], []
-        for u in range(UNROLL):
-            e = step * UNROLL + u
+        for u in range(unroll):
+            e = step * unroll + u
             weight = jnp.exp2((s_ref[e] - m_ref[block_ref[e]]) * EXP2_SCALE)
             weights.append(weight)
             products.append(
@@ -104,13 +104,13 @@
                     preferred_element_type=jnp.float32,
                 )
             )
-        for u in range(UNROLL):
-            block = block_ref[step * UNROLL + u]
+        for u in range(unroll):
+            block = block_ref[step * unroll + u]
             l_ref[block] = l_ref[block] + weights[u]
             a_ref[block] = a_ref[block] + products[u]
         return carry
 
-    lax.fori_loop(0, (count + (UNROLL - 1)) // UNROLL, mix, 0)
+    lax.fori_loop(0, (count + (unroll - 1)) // unroll, mix, 0)
 
 
 def stats_of(m_ref, l_ref):
@@ -132,6 +132,7 @@
 
 def attend_last(tables, query, parts, state, mine):
     slots = sum(part.shape[0] for part in parts)
+    unroll = UNROLL if mine else UNROLL // 2
 
     def kernel(count_ref, block_ref, slot_ref, q_ref, *refs):
         part_refs, refs = refs[: len(parts)], refs[len(parts) :]
@@ -143,7 +144,7 @@
         hold_parts(part_refs, kv_ref)
         count = count_ref[0]
         top_ref[...] = jnp.full(top_ref.shape, LOW, jnp.float32)
-        score_tiles(count, tables, q_ref, kv_ref, s_ref, top_ref)
+        score_tiles(unroll, count, tables, q_ref, kv_ref, s_ref, top_ref)
         for i in range(NZ):
             top = jnp.max(top_ref[i], axis=1, keepdims=True)
             old = m_in[first + i]
@@ -152,7 +153,7 @@
             m_ref[i] = new
             l_ref[i] = l_in[first + i] * fade
             a_ref[i] = a_in[first + i] * fade
-        mix_tiles(count, tables, kv_ref, s_ref, m_ref, l_ref, a_ref)
+        mix_tiles(unroll, count, tables, kv_ref, s_ref, m_ref, l_ref, a_ref)
         sums_ref[...] = a_ref[...].astype(sums_ref.dtype)
         stats = stats_of(m_ref, l_ref)
         stats_ref[...] = stats if mine else stats.T[: 2 * NZ]
@@ -198,7 +199,7 @@
         hold_parts(part_refs, kv_ref)
         count = count_ref[0]
         top_ref[...] = jnp.full(top_ref.shape, LOW, jnp.float32)
-        score_tiles(count, tables, q_ref, kv_ref, s_ref, top_ref)
+        score_tiles(UNROLL, count, tables, q_ref, kv_ref, s_ref, top_ref)
         for block in range(ROWS):
             top = jnp.max(top_ref[block], axis=1, keepdims=True)
             if first:
@@ -211,7 +212,7 @@
                 m_ref[block] = new
                 l_ref[block] = l_in[block] * fade
                 a_ref[block] = a_in[block] * fade
-        mix_tiles(count, tables, kv_ref, s_ref, m_ref, l_ref, a_ref)
+        mix_tiles(UNROLL, count, tables, kv_ref, s_ref, m_ref, l_ref, a_ref)
 
     return pl.pallas_call(
         kernel,
@@ -391,15 +392,14 @@
     slots, low, high = lax.optimization_barrier((slots, low, high))
     before_low = lax.ppermute(low, "y", shift(NY, 1))
     after_high = lax.ppermute(high, "y", shift(NY, -1))
+    slots, late_low, late_high, w_here = lax.optimization_barrier((slots, low, high, w_here))
     query = slots[:, :BLOCK]
     query = (query, lax.ppermute(query, "xh", shift(XH, 1)))
-    late_low, late_high, w_here = lax.optimization_barrier((low, high, w_here))
     before_high = lax.ppermute(late_high, "y", shift(NY, 1))
     after_low = lax.ppermute(late_low, "y", shift(NY, -1))
-    state = attend(groups[0], query, [low, high], None)
-    before_low, after_high, state = lax.optimization_barrier((before_low, after_high, state))
     far_low = lax.ppermute(before_low, "y", shift(NY, 1))
     far_high = lax.ppermute(after_high, "y", shift(NY, -1))
+    state = attend(groups[0], query, [low, high], None)
     state = attend(groups[1], query, [before_low, before_high, after_low, after_high], state)
     far_parts = [far_low, far_high]
     sent, sent_stats = attend_last(groups[2], query[1], far_parts, state, False)

time: 97.7 us -> 95.1 us (0.973)
  waiting for transfers between devices: 22.7 us -> 19.1 us
    ppermute x1, starting transfers between devices: 2.73 us -> 0.58 us  [local(): there_stats = lax.ppermute(sent_stats, 'xh', shift(XH, 1))]
    ppermute x1, starting transfers between devices: 0.29 us -> 2.44 us  [local(): there = lax.ppermute(sent, 'xh', shift(XH, 1))]
    ppermute x1, waiting for transfers between devices: 1.67 us -> 0.01 us  [local(): before_high = lax.ppermute(late_high, 'y', shift(NY, 1))]
    ppermute x1, waiting for transfers between devices: 1.08 us -> 0.01 us  [local(): far_low = lax.ppermute(before_low, 'y', shift(NY, 1))]
  transfers between devices with their start and end apart: 15 -> 15, of which waited for: 7 -> 5; matrix products, arithmetic and copies ran while one was open for 7% -> 8% of each run, Pallas kernels for 19% -> 20%
where the time goes in v14:
time: 95.1 us; the launch traced here: 94.5 us
  starting transfers between devices  30.5 us (32%)
  Pallas kernels  25.7 us (27%)
  waiting for transfers between devices  19.1 us (20%)
  blocking collectives  11.9 us (13%)
  local copies, waits for them, and re-layouts  7.3 us (8%)
    all_to_all x1, waiting for transfers between devices, local(): slots = lax.all_to_all(slots, 'z', 0, 0, tiled=True)  13.1 us
    all_to_all x1, blocking collectives, local(): heads = lax.all_to_all(heads, 'z', 0, 0, tiled=True)[:HEADS]  11.9 us
    all_to_all x1, starting transfers between devices, local(): slots = lax.all_to_all(slots, 'z', 0, 0, tiled=True)  9.03 us
    pallas_call x2, Pallas kernels, attend(): pl.pallas_call(kernel, out_shape=(whole, whole, whole), in_specs=in_smem(...  7.95 us
    dynamic_slice x1, local copies, waits for them, and re-layouts, w_columns(): lax.dynamic_slice(w, (0, (to_xl * NC + to_c) * width), (w.shape[0], width))  5.24 us
    pallas_call x2, Pallas kernels, attend_last(): pl.pallas_call(kernel, out_shape=(jax.ShapeDtypeStruct((NZ, BLOCK, HEAD_D...  5.17 us
    pallas_call x3, Pallas kernels, project(): pl.pallas_call(kernel, out_shape=jax.ShapeDtypeStruct((BLOCK, width), dty...  4.85 us
    ppermute x1, starting transfers between devices, local(): heads_core = lax.ppermute(heads, 'c', shift(NC, 1))  4.72 us
  transfers between devices with their start and end apart: 15, of which 5 were waited for; matrix products, arithmetic and copies ran while one was open for 8% of the time, Pallas kernels for 20%

profile of v14, /device:TPU:1, one launch (start us, length us, event | category | flops | bytes accessed | tf_op | source)
XLA Modules:
  0.0 94.5 jit_solution(12776737712247446592)
XLA Ops:
  0.0 1.9 %shard_map.55 = bf16[8,384,128]{2,1,0:T(8,128)(2,1)} custom-call(bf16[128,640]{1,0:T(8,128)(2,1)} %q_hbm.1, bf16[128,640]{1,0:T(8,128)(2,1)} %k_hbm.1, bf16[128,640]{1,0:T(8,128)(2,1)} %v_hbm.1), custom_call_target="tpu_custom_call" | custom-call | tf_op jit(solution)/shard_map/pallas_call | solution.py:53
  1.9 9.0 %all-to-all-start = ((bf16[8,384,128]{2,1,0:T(8,128)(2,1)}), bf16[8,384,128]{2,1,0:T(8,128)(2,1)}, u32[]{:S(2)}, u32[]{:S(2)}) async-start(bf16[8,384,128]{2,1,0:T(8,128)(2,1)} %shard_map.55), calls=%async_computation | async-start | bytes 1572864 | tf_op jit(solution)/shard_map/all_to_all | solution.py:389
  11.0 5.2 %constant_dynamic-slice_fusion = (bf16[640,1280]{1,0:T(8,128)(2,1)}, bf16[640,1280]{1,0:T(8,128)(2,1)}, bf16[640,1280]{1,0:T(8,128)(2,1)}, bf16[640,1280]{1,0:T(8,128)(2,1)S(1)}) fusion(bf16[640,5120]{1,0:T(8,128)(2,1)} %param.9, s32[]{:T(128)S(6)} %select_n.15, s32[]{:T(128)S(6)} %select_n.14, s32[]{:T(128)S(6)} %select_n.13, s32[]{:T(128)S(6)} %select_n.12), kind=kLoop, calls=%fused_computation | loop fusion | bytes 13107216 | tf_op jit(solution)/shard_map/dynamic_slice | solution.py:379
  17.2 4.4 %shard_map.56 = (s32[1]{0:T(128)}, s32[256]{0:T(256)S(1)}, s32[256]{0:T(256)S(1)}, s32[1]{0:T(128)}, s32[384]{0:T(512)S(1)}, /*index=5*/s32[384]{0:T(512)S(1)}, ...) custom-call(s32[64,64]{1,0:T(8,128)S(1)} %copy-done.1), custom_call_target="tpu_custom_call" | custom-call | flops 1000000 | bytes 100000 | tf_op jit(solution)/shard_map/pallas_call | solution.py:362
  21.5 13.1 %all-to-all-done = bf16[8,384,128]{2,1,0:T(8,128)(2,1)} async-done(((bf16[8,384,128]{2,1,0:T(8,128)(2,1)}), bf16[8,384,128]{2,1,0:T(8,128)(2,1)}, u32[]{:S(2)}, u32[]{:S(2)}) %all-to-all-start) | async-done | bytes 786464 | tf_op jit(solution)/shard_map/all_to_all | solution.py:389
  34.6 1.1 %fusion = (bf16[4,256,128]{2,1,0:T(8,128)(2,1)S(1)}, bf16[4,256,128]{2,1,0:T(8,128)(2,1)S(1)}) fusion(bf16[8,384,128]{2,1,0:T(8,128)(2,1)} %all-to-all-done), kind=kLoop, calls=%fused_computation.4 | loop fusion | bytes 1048576 | tf_op jit(solution)/shard_map/slice | solution.py:391
  35.7 1.4 %collective-permute-start.2 = (bf16[4,256,128]{2,1,0:T(8,128)(2,1)S(1)}, bf16[4,256,128]{2,1,0:T(8,128)(2,1)S(1)}, u32[]{:S(2)}, u32[]{:S(2)}) collective-permute-start(bf16[4,256,128]{2,1,0:T(8,128)(2,1)S(1)} %get-tuple-element.96.refs_0_), channel_id=1, source_target_pairs={{0,4},{4,8},{8,12},{12,0},{1,5},{5,9},{9,13},{13,1},{2,6},{6,10},{... | collective-permute-start | bytes 786440 | tf_op jit(solution)/shard_map/ppermute | solution.py:393
  37.1 1.5 %collective-permute-start.4 = (bf16[4,256,128]{2,1,0:T(8,128)(2,1)S(1)}, bf16[4,256,128]{2,1,0:T(8,128)(2,1)S(1)}, u32[]{:S(2)}, u32[]{:S(2)}) collective-permute-start(bf16[4,256,128]{2,1,0:T(8,128)(2,1)S(1)} %get-tuple-element.95.refs_1_), channel_id=1, source_target_pairs={{0,12},{4,0},{8,4},{12,8},{1,13},{5,1},{9,5},{13,9},{2,14},{6,2},{... | collective-permute-start | bytes 786440 | tf_op jit(solution)/shard_map/ppermute | solution.py:394
  38.6 1.0 %slice.14.own_ref.q_ref = bf16[8,128,128]{2,1,0:T(8,128)(2,1)S(1)} slice(bf16[8,384,128]{2,1,0:T(8,128)(2,1)} %all-to-all-done), slice={[0:8], [0:128], [0:128]} | slice | bytes 524288 | tf_op jit(solution)/shard_map/slice | solution.py:396
  39.6 2.8 %collective-permute-start.6 = (bf16[8,128,128]{2,1,0:T(8,128)(2,1)S(1)}, bf16[8,128,128]{2,1,0:T(8,128)(2,1)S(1)}, u32[]{:S(2)}, u32[]{:S(2)}) collective-permute-start(bf16[8,128,128]{2,1,0:T(8,128)(2,1)S(1)} %slice.14.own_ref.q_ref), channel_id=1, source_target_pairs={{0,128},{128,0},{1,129},{129,1},{2,130},{130,2},{3,131},{131,3},{4... | collective-permute-start | bytes 786440 | tf_op jit(solution)/shard_map/ppermute | solution.py:397
  42.4 2.7 %collective-permute-start.8 = (bf16[4,256,128]{2,1,0:T(8,128)(2,1)S(1)}, bf16[4,256,128]{2,1,0:T(8,128)(2,1)S(1)}, u32[]{:S(2)}, u32[]{:S(2)}) collective-permute-start(bf16[4,256,128]{2,1,0:T(8,128)(2,1)S(1)} %get-tuple-element.96.refs_0_), channel_id=1, source_target_pairs={{0,12},{4,0},{8,4},{12,8},{1,13},{5,1},{9,5},{13,9},{2,14},{6,2},{... | collective-permute-start | bytes 786440 | tf_op jit(solution)/shard_map/ppermute | solution.py:399
  45.1 2.7 %collective-permute-start.5 = (bf16[4,256,128]{2,1,0:T(8,128)(2,1)S(1)}, bf16[4,256,128]{2,1,0:T(8,128)(2,1)S(1)}, u32[]{:S(2)}, u32[]{:S(2)}) collective-permute-start(bf16[4,256,128]{2,1,0:T(8,128)(2,1)S(1)} %collective-permute-done.4.refs_3_), channel_id=1, source_target_pairs={{0,12},{4,0},{8,4},{12,8},{1,13},{5,1},{9,5},{13,9},{2,14},{6,2},{... | collective-permute-start | bytes 786440 | tf_op jit(solution)/shard_map/ppermute | solution.py:401
  48.1 3.4 %shard_map.57 = (f32[16,128,128]{2,1,0:T(8,128)S(1)}, f32[16,128,128]{2,1,0:T(8,128)S(1)}, f32[16,128,128]{2,1,0:T(8,128)S(1)}) custom-call(s32[1]{0:T(128)} %get-tuple-element.97.count_ref, s32[256]{0:T(256)S(1)} %get-tuple-element.98.block_ref, s32[256]{0:T(256)S(1)} %get-tuple-element.99.slot_ref, bf16[8,128,128]{2,1,0:T(8,128)(2,1)S(1)} %slice.14.own_ref.q_ref, ...), custom_call_target="tpu_custom_call" | custom-call | flops 335544320 | bytes 6291456 | tf_op jit(solution)/shard_map/pallas_call | solution.py:217
  51.5 4.5 %shard_map.58 = (f32[16,128,128]{2,1,0:T(8,128)S(1)}, f32[16,128,128]{2,1,0:T(8,128)S(1)}, f32[16,128,128]{2,1,0:T(8,128)S(1)}) custom-call(s32[1]{0:T(128)} %get-tuple-element.92.count_ref, s32[384]{0:T(512)S(1)} %get-tuple-element.93.block_ref, s32[384]{0:T(512)S(1)} %get-tuple-element.94.slot_ref, bf16[8,128,128]{2,1,0:T(8,128)(2,1)S(1)} %slice.14.own_ref.q_ref, ...), custom_call_target="tpu_custom_call" | custom-call | flops 671088640 | bytes 6291456 | tf_op jit(solution)/shard_map/pallas_call | solution.py:217
  56.1 2.2 %shard_map.59 = (bf16[8,128,128]{2,1,0:T(8,128)(2,1)S(1)}, f32[16,128]{1,0:T(8,128)S(1)}) custom-call(s32[1]{0:T(128)} %get-tuple-element.89.count_ref, s32[192]{0:T(256)S(1)} %get-tuple-element.90.block_ref, s32[192]{0:T(256)S(1)} %get-tuple-element.91.slot_ref, bf16[8,128,128]{2,1,0:T(8,128)(2,1)S(1)} %collective-permute-done.6.other_ref.q_ref, ...), custom_call_target="tpu_custom_call" | custom-call | flops 83886080 | bytes 3145728 | tf_op jit(solution)/shard_map/pallas_call | solution.py:162
  58.3 2.4 %collective-permute-start.9 = (bf16[8,128,128]{2,1,0:T(8,128)(2,1)S(1)}, bf16[8,128,128]{2,1,0:T(8,128)(2,1)S(1)}, u32[]{:S(2)}, u32[]{:S(2)}) collective-permute-start(bf16[8,128,128]{2,1,0:T(8,128)(2,1)S(1)} %get-tuple-element.113), channel_id=1, source_target_pairs={{0,128},{128,0},{1,129},{129,1},{2,130},{130,2},{3,131},{131,3},{4... | collective-permute-start | bytes 786440 | tf_op jit(solution)/shard_map/ppermute | solution.py:407
  61.3 3.0 %shard_map.60 = (f32[8,128,128]{2,1,0:T(8,128)S(1)}, f32[128,128]{1,0:T(8,128)S(1)}) custom-call(s32[1]{0:T(128)} %get-tuple-element.79.count_ref, s32[192]{0:T(256)S(1)} %get-tuple-element.80.block_ref, s32[192]{0:T(256)S(1)} %get-tuple-element.81.slot_ref, bf16[8,128,128]{2,1,0:T(8,128)(2,1)S(1)} %slice.14.own_ref.q_ref, ...), custom_call_target="tpu_custom_call" | custom-call | flops 83886080 | bytes 3145728 | tf_op jit(solution)/shard_map/pallas_call | solution.py:162
  65.9 11.9 %all_to_all.10 = bf16[8,128,128]{2,1,0:T(8,128)(2,1)S(1)} all-to-all(bf16[8,128,128]{2,1,0:T(8,128)(2,1)S(1)} %shard_map.61), channel_id=1, replica_groups=mesh['xh'=2,'z'=8,'y'=4,'xl'=2,'c'=2] {'z'}, dimensions={0} | all-to-all | bytes 524288 | tf_op jit(solution)/shard_map/all_to_all | solution.py:411
  77.8 4.7 %collective-permute-start.11 = (bf16[5,128,128]{2,1,0:T(8,128)(2,1)S(1)}, bf16[5,128,128]{2,1,0:T(8,128)(2,1)S(1)}, u32[]{:S(2)}, u32[]{:S(2)}) collective-permute-start(bf16[5,128,128]{2,1,0:T(8,128)(2,1)S(1)} %slice.16.a_ref), channel_id=1, source_target_pairs={{0,1},{1,0},{2,3},{3,2},{4,5},{5,4},{6,7},{7,6},{8,9},{9,8},{10,11... | collective-permute-start | bytes 491528 | tf_op jit(solution)/shard_map/ppermute | solution.py:412
  82.5 1.0 %collective-permute-done.11.b_ref = bf16[5,128,128]{2,1,0:T(8,128)(2,1)S(1)} collective-permute-done((bf16[5,128,128]{2,1,0:T(8,128)(2,1)S(1)}, bf16[5,128,128]{2,1,0:T(8,128)(2,1)S(1)}, u32[]{:S(2)}, u32[]{:S(2)}) %collective-permute-start.11) | collective-permute-done | bytes 163872 | tf_op jit(solution)/shard_map/ppermute | solution.py:412
  83.5 1.2 %shard_map.64 = bf16[128,768]{1,0:T(8,128)(2,1)S(1)} custom-call(bf16[5,128,128]{2,1,0:T(8,128)(2,1)S(1)} %slice.16.a_ref, bf16[5,128,128]{2,1,0:T(8,128)(2,1)S(1)} %collective-permute-done.11.b_ref, bf16[640,1280]{1,0:T(8,128)(2,1)S(1)} %get-tuple-element.117.w_hbm, bf16[640,1280]{1,0:T(8,128)(2,1)S(1)} %collective-permute-done.w2_hbm), custom_call_target="tpu_custom_call" | custom-call | flops 251658240 | bytes 4194304 | tf_op jit(solution)/shard_map/pallas_call | solution.py:291
  84.7 1.2 %collective-permute-start.13 = (bf16[128,768]{1,0:T(8,128)(2,1)S(1)}, bf16[128,768]{1,0:T(8,128)(2,1)S(1)}, u32[]{:S(2)}, u32[]{:S(2)}) collective-permute-start(bf16[128,768]{1,0:T(8,128)(2,1)S(1)} %shard_map.64), channel_id=1, source_target_pairs={{0,2},{2,0},{1,3},{3,1},{4,6},{6,4},{5,7},{7,5},{8,10},{10,8},{9,1... | collective-permute-start | bytes 589832 | tf_op jit(solution)/shard_map/ppermute | solution.py:415
  87.3 2.8 %shard_map.62.near_ref = f32[128,1280]{1,0:T(8,128)S(1)} custom-call(bf16[5,128,128]{2,1,0:T(8,128)(2,1)S(1)} %slice.16.a_ref, bf16[5,128,128]{2,1,0:T(8,128)(2,1)S(1)} %collective-permute-done.11.b_ref, bf16[640,1280]{1,0:T(8,128)(2,1)S(1)} %copy-done, bf16[640,1280]{1,0:T(8,128)(2,1)} %collective-permute-done.1.w2_hbm), custom_call_target="tpu_custom_call" | custom-call | flops 419430400 | bytes 4194304 | tf_op jit(solution)/shard_map/pallas_call | solution.py:291
  90.0 3.7 %collective-permute-done.12.refs_0_ = bf16[128,512]{1,0:T(8,128)(2,1)S(1)} collective-permute-done((bf16[128,512]{1,0:T(8,128)(2,1)S(1)}, bf16[128,512]{1,0:T(8,128)(2,1)S(1)}, u32[]{:S(2)}, u32[]{:S(2)}) %collective-permute-start.12) | collective-permute-done | bytes 131104 | tf_op jit(solution)/shard_map/ppermute | solution.py:415
  (26 shorter events, 5.6 us)
Async XLA Ops:
  1.9 32.7 %all-to-all-start = ((bf16[8,384,128]{2,1,0:T(8,128)(2,1)}), bf16[8,384,128]{2,1,0:T(8,128)(2,1)}, u32[]{:S(2)}, u32[]{:S(2)}) async-start(bf16[8,384,128]{2,1,0:T(8,128)(2,1)} %shard_map.55), calls=%async_computation | async-start | bytes 1572864 | tf_op jit(solution)/shard_map/all_to_all | solution.py:389
  11.0 6.2 %copy-start.1 = (s32[64,64]{1,0:T(8,128)S(1)}, s32[64,64]{1,0:T(8,128)}, u32[]{:S(2)}) copy-start(s32[64,64]{1,0:T(8,128)} %mask_ref) | copy-start | bytes 49156
  16.2 22.4 %collective-permute-start = (bf16[640,1280]{1,0:T(8,128)(2,1)}, bf16[640,1280]{1,0:T(8,128)(2,1)S(1)}, u32[]{:S(2)}, u32[]{:S(2)}) collective-permute-start(bf16[640,1280]{1,0:T(8,128)(2,1)} %get-tuple-element.86), channel_id=1, source_target_pairs={{0,1},{1,0},{2,3},{3,2},{4,5},{5,4},{6,7},{7,6},{8,9},{9,8},{10,11... | collective-permute-start | bytes 4915208 | tf_op jit(solution)/shard_map/ppermute | solution.py:386
  17.2 21.5 %collective-permute-start.1 = (bf16[640,1280]{1,0:T(8,128)(2,1)}, bf16[640,1280]{1,0:T(8,128)(2,1)}, u32[]{:S(2)}, u32[]{:S(2)}) collective-permute-start(bf16[640,1280]{1,0:T(8,128)(2,1)} %get-tuple-element.87), channel_id=1, source_target_pairs={{0,1},{1,0},{2,3},{3,2},{4,5},{5,4},{6,7},{7,6},{8,9},{9,8},{10,11... | collective-permute-start | bytes 4915208 | tf_op jit(solution)/shard_map/ppermute | solution.py:386
  35.7 9.4 %collective-permute-start.2 = (bf16[4,256,128]{2,1,0:T(8,128)(2,1)S(1)}, bf16[4,256,128]{2,1,0:T(8,128)(2,1)S(1)}, u32[]{:S(2)}, u32[]{:S(2)}) collective-permute-start(bf16[4,256,128]{2,1,0:T(8,128)(2,1)S(1)} %get-tuple-element.96.refs_0_), channel_id=1, source_target_pairs={{0,4},{4,8},{8,12},{12,0},{1,5},{5,9},{9,13},{13,1},{2,6},{6,10},{... | collective-permute-start | bytes 786440 | tf_op jit(solution)/shard_map/ppermute | solution.py:393
  37.1 8.0 %collective-permute-start.4 = (bf16[4,256,128]{2,1,0:T(8,128)(2,1)S(1)}, bf16[4,256,128]{2,1,0:T(8,128)(2,1)S(1)}, u32[]{:S(2)}, u32[]{:S(2)}) collective-permute-start(bf16[4,256,128]{2,1,0:T(8,128)(2,1)S(1)} %get-tuple-element.95.refs_1_), channel_id=1, source_target_pairs={{0,12},{4,0},{8,4},{12,8},{1,13},{5,1},{9,5},{13,9},{2,14},{6,2},{... | collective-permute-start | bytes 786440 | tf_op jit(solution)/shard_map/ppermute | solution.py:394
  39.6 8.5 %collective-permute-start.6 = (bf16[8,128,128]{2,1,0:T(8,128)(2,1)S(1)}, bf16[8,128,128]{2,1,0:T(8,128)(2,1)S(1)}, u32[]{:S(2)}, u32[]{:S(2)}) collective-permute-start(bf16[8,128,128]{2,1,0:T(8,128)(2,1)S(1)} %slice.14.own_ref.q_ref), channel_id=1, source_target_pairs={{0,128},{128,0},{1,129},{129,1},{2,130},{130,2},{3,131},{131,3},{4... | collective-permute-start | bytes 786440 | tf_op jit(solution)/shard_map/ppermute | solution.py:397
  42.4 9.1 %collective-permute-start.7 = (bf16[4,256,128]{2,1,0:T(8,128)(2,1)S(1)}, bf16[4,256,128]{2,1,0:T(8,128)(2,1)S(1)}, u32[]{:S(2)}, u32[]{:S(2)}) collective-permute-start(bf16[4,256,128]{2,1,0:T(8,128)(2,1)S(1)} %get-tuple-element.95.refs_1_), channel_id=1, source_target_pairs={{0,4},{4,8},{8,12},{12,0},{1,5},{5,9},{9,13},{13,1},{2,6},{6,10},{... | collective-permute-start | bytes 786440 | tf_op jit(solution)/shard_map/ppermute | solution.py:398
  42.4 9.1 %collective-permute-start.8 = (bf16[4,256,128]{2,1,0:T(8,128)(2,1)S(1)}, bf16[4,256,128]{2,1,0:T(8,128)(2,1)S(1)}, u32[]{:S(2)}, u32[]{:S(2)}) collective-permute-start(bf16[4,256,128]{2,1,0:T(8,128)(2,1)S(1)} %get-tuple-element.96.refs_0_), channel_id=1, source_target_pairs={{0,12},{4,0},{8,4},{12,8},{1,13},{5,1},{9,5},{13,9},{2,14},{6,2},{... | collective-permute-start | bytes 786440 | tf_op jit(solution)/shard_map/ppermute | solution.py:399
  45.1 11.0 %collective-permute-start.3 = (bf16[4,256,128]{2,1,0:T(8,128)(2,1)S(1)}, bf16[4,256,128]{2,1,0:T(8,128)(2,1)S(1)}, u32[]{:S(2)}, u32[]{:S(2)}) collective-permute-start(bf16[4,256,128]{2,1,0:T(8,128)(2,1)S(1)} %collective-permute-done.2.refs_0_), channel_id=1, source_target_pairs={{0,4},{4,8},{8,12},{12,0},{1,5},{5,9},{9,13},{13,1},{2,6},{6,10},{... | collective-permute-start | bytes 786440 | tf_op jit(solution)/shard_map/ppermute | solution.py:400
  45.1 11.0 %collective-permute-start.5 = (bf16[4,256,128]{2,1,0:T(8,128)(2,1)S(1)}, bf16[4,256,128]{2,1,0:T(8,128)(2,1)S(1)}, u32[]{:S(2)}, u32[]{:S(2)}) collective-permute-start(bf16[4,256,128]{2,1,0:T(8,128)(2,1)S(1)} %collective-permute-done.4.refs_3_), channel_id=1, source_target_pairs={{0,12},{4,0},{8,4},{12,8},{1,13},{5,1},{9,5},{13,9},{2,14},{6,2},{... | collective-permute-start | bytes 786440 | tf_op jit(solution)/shard_map/ppermute | solution.py:401
  58.3 6.9 %collective-permute-start.9 = (bf16[8,128,128]{2,1,0:T(8,128)(2,1)S(1)}, bf16[8,128,128]{2,1,0:T(8,128)(2,1)S(1)}, u32[]{:S(2)}, u32[]{:S(2)}) collective-permute-start(bf16[8,128,128]{2,1,0:T(8,128)(2,1)S(1)} %get-tuple-element.113), channel_id=1, source_target_pairs={{0,128},{128,0},{1,129},{129,1},{2,130},{130,2},{3,131},{131,3},{4... | collective-permute-start | bytes 786440 | tf_op jit(solution)/shard_map/ppermute | solution.py:407
  60.7 4.5 %collective-permute-start.10 = (f32[16,128]{1,0:T(8,128)S(1)}, f32[16,128]{1,0:T(8,128)S(1)}, u32[]{:S(2)}, u32[]{:S(2)}) collective-permute-start(f32[16,128]{1,0:T(8,128)S(1)} %get-tuple-element.114), channel_id=1, source_target_pairs={{0,128},{128,0},{1,129},{129,1},{2,130},{130,2},{3,131},{131,3},{4... | collective-permute-start | bytes 24584 | tf_op jit(solution)/shard_map/ppermute | solution.py:408
  77.8 5.7 %collective-permute-start.11 = (bf16[5,128,128]{2,1,0:T(8,128)(2,1)S(1)}, bf16[5,128,128]{2,1,0:T(8,128)(2,1)S(1)}, u32[]{:S(2)}, u32[]{:S(2)}) collective-permute-start(bf16[5,128,128]{2,1,0:T(8,128)(2,1)S(1)} %slice.16.a_ref), channel_id=1, source_target_pairs={{0,1},{1,0},{2,3},{3,2},{4,5},{5,4},{6,7},{7,6},{8,9},{9,8},{10,11... | collective-permute-start | bytes 491528 | tf_op jit(solution)/shard_map/ppermute | solution.py:412
  84.7 2.6 %copy-start = (bf16[640,1280]{1,0:T(8,128)(2,1)S(1)}, bf16[640,1280]{1,0:T(8,128)(2,1)}, u32[]{:S(2)}) copy-start(bf16[640,1280]{1,0:T(8,128)(2,1)} %get-tuple-element.115.w_hbm) | copy-start | bytes 4915204
  84.7 9.0 %collective-permute-start.13 = (bf16[128,768]{1,0:T(8,128)(2,1)S(1)}, bf16[128,768]{1,0:T(8,128)(2,1)S(1)}, u32[]{:S(2)}, u32[]{:S(2)}) collective-permute-start(bf16[128,768]{1,0:T(8,128)(2,1)S(1)} %shard_map.64), channel_id=1, source_target_pairs={{0,2},{2,0},{1,3},{3,1},{4,6},{6,4},{5,7},{7,5},{8,10},{10,8},{9,1... | collective-permute-start | bytes 589832 | tf_op jit(solution)/shard_map/ppermute | solution.py:415
  86.9 6.9 %collective-permute-start.12 = (bf16[128,512]{1,0:T(8,128)(2,1)S(1)}, bf16[128,512]{1,0:T(8,128)(2,1)S(1)}, u32[]{:S(2)}, u32[]{:S(2)}) collective-permute-start(bf16[128,512]{1,0:T(8,128)(2,1)S(1)} %shard_map.63), channel_id=1, source_target_pairs={{0,2},{2,0},{1,3},{3,1},{4,6},{6,4},{5,7},{7,5},{8,10},{10,8},{9,1... | collective-permute-start | bytes 393224 | tf_op jit(solution)/shard_map/ppermute | solution.py:415

commit v15 on v14

--- a/solution.py
+++ b/solution.py
@@ -259,50 +259,49 @@
     )(here, here_stats, there, there_stats)
 
 
-def project(a, b, w_own, w_other, first, width, dtype):
-    deep = w_own.shape[0]
+def project(heads, w, added, first, width, dtype):
+    deep = w.shape[0]
     tiles = width // TILE_N
 
-    def kernel(a_ref, b_ref, w_hbm, w2_hbm, out_ref, rows_ref, w_ref, sems):
+    def kernel(heads_ref, w_hbm, *refs):
+        if added is not None:
+            added_ref, refs = refs[0], refs[1:]
+        out_ref, rows_ref, w_ref, sems = refs
         copies = []
         for tile in range(tiles):
             lanes = pl.ds(first + tile * TILE_N, TILE_N)
-            for which, source in enumerate((w_hbm, w2_hbm)):
-                copies.append(
-                    pltpu.make_async_copy(
-                        source.at[:, lanes], w_ref.at[which, tile], sems.at[which, tile]
-                    )
-                )
-                copies[-1].start()
-        for which, ref in enumerate((a_ref, b_ref)):
-            for head in range(HEADS):
-                at = (which * HEADS + head) * HEAD_DIM
-                rows_ref[:, at : at + HEAD_DIM] = ref[head]
+            copies.append(
+                pltpu.make_async_copy(w_hbm.at[:, lanes], w_ref.at[tile], sems.at[tile])
+            )
+            copies[-1].start()
+        for head in range(HEADS):
+            at = head * HEAD_DIM
+            rows_ref[:, at : at + HEAD_DIM] = heads_ref[head]
         for tile in range(tiles):
-            copies[2 * tile].wait()
-            copies[2 * tile + 1].wait()
-            out = jnp.dot(rows_ref[:, :deep], w_ref[0, tile], preferred_element_type=jnp.float32)
-            out = out + jnp.dot(
-                rows_ref[:, deep:], w_ref[1, tile], preferred_element_type=jnp.float32
-            )
-            out_ref[:, tile * TILE_N : (tile + 1) * TILE_N] = out.astype(out_ref.dtype)
-
-    anywhere = pl.BlockSpec(memory_space=pl.ANY)
+            copies[tile].wait()
+            at = tile * TILE_N
+            out = jnp.dot(rows_ref[...], w_ref[tile], preferred_element_type=jnp.float32)
+            if added is not None:
+                out = out + added_ref[:, first + at : first + at + TILE_N]
+            out_ref[:, at : at + TILE_N] = out.astype(out_ref.dtype)
+
     return pl.pallas_call(
         kernel,
         out_shape=jax.ShapeDtypeStruct((BLOCK, width), dtype),
-        in_specs=in_vmem(2) + [anywhere] * 2,
+        in_specs=in_vmem(1)
+        + [pl.BlockSpec(memory_space=pl.ANY)]
+        + in_vmem(0 if added is None else 1),
         out_specs=in_vmem(1)[0],
         scratch_shapes=[
-            pltpu.VMEM((BLOCK, 2 * deep), jnp.bfloat16),
-            pltpu.VMEM((2, tiles, deep, TILE_N), jnp.bfloat16),
-            pltpu.SemaphoreType.DMA((2, tiles)),
+            pltpu.VMEM((BLOCK, deep), jnp.bfloat16),
+            pltpu.VMEM((tiles, deep, TILE_N), jnp.bfloat16),
+            pltpu.SemaphoreType.DMA((tiles,)),
         ],
-        compiler_params=pltpu.CompilerParams(vmem_limit_bytes=12 * MIB),
+        compiler_params=pltpu.CompilerParams(vmem_limit_bytes=8 * MIB),
         cost_estimate=pl.CostEstimate(
-            flops=2 * BLOCK * 2 * deep * width, bytes_accessed=4 * MIB, transcendentals=0
+            flops=2 * BLOCK * deep * width, bytes_accessed=2 * MIB, transcendentals=0
         ),
-    )(a, b, w_own, w_other)
+    )(heads, w, *(() if added is None else (added,)))
 
 
 def add_kernel(near_ref, *refs):
@@ -410,16 +409,18 @@
     heads = merge(here, here_stats, there, there_stats)
     heads = lax.all_to_all(heads, "z", 0, 0, tiled=True)[:HEADS]
     heads_core = lax.ppermute(heads, "c", shift(NC, 1))
+    far_own = project(heads, w_own[0], None, 0, width, jnp.float32)
     early = width // TILE_N // 2 * TILE_N
     far = [
         lax.ppermute(
-            project(heads, heads_core, w_own[0], w_here[0], first, columns, jnp.bfloat16),
+            project(heads_core, w_here[0], far_own, first, columns, jnp.bfloat16),
             "xl",
             shift(XL, 1),
         )
         for first, columns in ((0, early), (early, width - early))
     ]
-    near = project(heads, heads_core, w_own[1], w_here[1], 0, width, jnp.float32)
+    near = project(heads, w_own[1], None, 0, width, jnp.float32)
+    near = project(heads_core, w_here[1], near, 0, width, jnp.float32)
     return add(near, far)
 
 

time: 95.1 us -> 95.1 us (level)
    pallas_call x3 -> x5, Pallas kernels: 4.85 us -> 6.5 us  [project(): pl.pallas_call(kernel, out_shape=jax.ShapeDtypeStruct((BLOCK, width), dty...]
    pallas_call x2, Pallas kernels: 7.95 us -> 6.83 us  [attend(): pl.pallas_call(kernel, out_shape=(whole, whole, whole), in_specs=in_smem(...]
    ppermute x1, waiting for transfers between devices: 1.03 us -> 0.01 us  [local(): heads_core = lax.ppermute(heads, 'c', shift(NC, 1))]
  transfers between devices with their start and end apart: 15 -> 15, of which waited for: 5 -> 5; matrix products, arithmetic and copies ran while one was open for 8% -> 8% of each run, Pallas kernels for 20% -> 21%
where the time goes in v15:
time: 95.1 us; the launch traced here: 94.6 us
  starting transfers between devices  30 us (32%)
  Pallas kernels  26.2 us (28%)
  waiting for transfers between devices  19.1 us (20%)
  blocking collectives  11.8 us (12%)
  local copies, waits for them, and re-layouts  7.3 us (8%)
    all_to_all x1, waiting for transfers between devices, local(): slots = lax.all_to_all(slots, 'z', 0, 0, tiled=True)  13.1 us
    all_to_all x1, blocking collectives, local(): heads = lax.all_to_all(heads, 'z', 0, 0, tiled=True)[:HEADS]  11.8 us
    all_to_all x1, starting transfers between devices, local(): slots = lax.all_to_all(slots, 'z', 0, 0, tiled=True)  9.03 us
    pallas_call x2, Pallas kernels, attend(): pl.pallas_call(kernel, out_shape=(whole, whole, whole), in_specs=in_smem(...  6.83 us
    pallas_call x5, Pallas kernels, project(): pl.pallas_call(kernel, out_shape=jax.ShapeDtypeStruct((BLOCK, width), dty...  6.5 us
    dynamic_slice x1, local copies, waits for them, and re-layouts, w_columns(): lax.dynamic_slice(w, (0, (to_xl * NC + to_c) * width), (w.shape[0], width))  5.24 us
    pallas_call x2, Pallas kernels, attend_last(): pl.pallas_call(kernel, out_shape=(jax.ShapeDtypeStruct((NZ, BLOCK, HEAD_D...  5.17 us
    pallas_call x1, Pallas kernels, live_tiles(): pl.pallas_call(tiles_kernel, out_shape=tuple(out_shape), in_specs=in_smem...  4.37 us
  transfers between devices with their start and end apart: 15, of which 5 were waited for; matrix products, arithmetic and copies ran while one was open for 8% of the time, Pallas kernels for 21%

profile of v15, /device:TPU:1, one launch (start us, length us, event | category | flops | bytes accessed | tf_op | source)
XLA Modules:
  0.0 94.6 jit_solution(11243544595774988301)
XLA Ops:
  0.0 1.9 %shard_map.55 = bf16[8,384,128]{2,1,0:T(8,128)(2,1)} custom-call(bf16[128,640]{1,0:T(8,128)(2,1)} %q_hbm.1, bf16[128,640]{1,0:T(8,128)(2,1)} %k_hbm.1, bf16[128,640]{1,0:T(8,128)(2,1)} %v_hbm.1), custom_call_target="tpu_custom_call" | custom-call | tf_op jit(solution)/shard_map/pallas_call | solution.py:53
  1.9 9.0 %all-to-all-start = ((bf16[8,384,128]{2,1,0:T(8,128)(2,1)}), bf16[8,384,128]{2,1,0:T(8,128)(2,1)}, u32[]{:S(2)}, u32[]{:S(2)}) async-start(bf16[8,384,128]{2,1,0:T(8,128)(2,1)} %shard_map.55), calls=%async_computation | async-start | bytes 1572864 | tf_op jit(solution)/shard_map/all_to_all | solution.py:388
  11.0 5.2 %constant_dynamic-slice_fusion = (bf16[640,1280]{1,0:T(8,128)(2,1)}, bf16[640,1280]{1,0:T(8,128)(2,1)}, bf16[640,1280]{1,0:T(8,128)(2,1)S(1)}, bf16[640,1280]{1,0:T(8,128)(2,1)}) fusion(bf16[640,5120]{1,0:T(8,128)(2,1)} %param.9, s32[]{:T(128)S(6)} %select_n.15, s32[]{:T(128)S(6)} %select_n.14, s32[]{:T(128)S(6)} %select_n.13, s32[]{:T(128)S(6)} %select_n.12), kind=kLoop, calls=%fused_computation | loop fusion | bytes 13107216 | tf_op jit(solution)/shard_map/dynamic_slice | solution.py:378
  17.2 4.4 %shard_map.56 = (s32[1]{0:T(128)}, s32[256]{0:T(256)S(1)}, s32[256]{0:T(256)S(1)}, s32[1]{0:T(128)}, s32[384]{0:T(512)S(1)}, /*index=5*/s32[384]{0:T(512)S(1)}, ...) custom-call(s32[64,64]{1,0:T(8,128)S(1)} %copy-done.1), custom_call_target="tpu_custom_call" | custom-call | flops 1000000 | bytes 100000 | tf_op jit(solution)/shard_map/pallas_call | solution.py:361
  21.5 13.1 %all-to-all-done = bf16[8,384,128]{2,1,0:T(8,128)(2,1)} async-done(((bf16[8,384,128]{2,1,0:T(8,128)(2,1)}), bf16[8,384,128]{2,1,0:T(8,128)(2,1)}, u32[]{:S(2)}, u32[]{:S(2)}) %all-to-all-start) | async-done | bytes 786464 | tf_op jit(solution)/shard_map/all_to_all | solution.py:388
  34.6 1.1 %fusion = (bf16[4,256,128]{2,1,0:T(8,128)(2,1)S(1)}, bf16[4,256,128]{2,1,0:T(8,128)(2,1)S(1)}) fusion(bf16[8,384,128]{2,1,0:T(8,128)(2,1)} %all-to-all-done), kind=kLoop, calls=%fused_computation.4 | loop fusion | bytes 1048576 | tf_op jit(solution)/shard_map/slice | solution.py:390
  35.7 1.4 %collective-permute-start.2 = (bf16[4,256,128]{2,1,0:T(8,128)(2,1)S(1)}, bf16[4,256,128]{2,1,0:T(8,128)(2,1)S(1)}, u32[]{:S(2)}, u32[]{:S(2)}) collective-permute-start(bf16[4,256,128]{2,1,0:T(8,128)(2,1)S(1)} %get-tuple-element.96.refs_0_), channel_id=1, source_target_pairs={{0,4},{4,8},{8,12},{12,0},{1,5},{5,9},{9,13},{13,1},{2,6},{6,10},{... | collective-permute-start | bytes 786440 | tf_op jit(solution)/shard_map/ppermute | solution.py:392
  37.1 1.5 %collective-permute-start.4 = (bf16[4,256,128]{2,1,0:T(8,128)(2,1)S(1)}, bf16[4,256,128]{2,1,0:T(8,128)(2,1)S(1)}, u32[]{:S(2)}, u32[]{:S(2)}) collective-permute-start(bf16[4,256,128]{2,1,0:T(8,128)(2,1)S(1)} %get-tuple-element.95.refs_1_), channel_id=1, source_target_pairs={{0,12},{4,0},{8,4},{12,8},{1,13},{5,1},{9,5},{13,9},{2,14},{6,2},{... | collective-permute-start | bytes 786440 | tf_op jit(solution)/shard_map/ppermute | solution.py:393
  38.6 1.0 %slice.14.own_ref.q_ref = bf16[8,128,128]{2,1,0:T(8,128)(2,1)S(1)} slice(bf16[8,384,128]{2,1,0:T(8,128)(2,1)} %all-to-all-done), slice={[0:8], [0:128], [0:128]} | slice | bytes 524288 | tf_op jit(solution)/shard_map/slice | solution.py:395
  39.6 2.8 %collective-permute-start.6 = (bf16[8,128,128]{2,1,0:T(8,128)(2,1)S(1)}, bf16[8,128,128]{2,1,0:T(8,128)(2,1)S(1)}, u32[]{:S(2)}, u32[]{:S(2)}) collective-permute-start(bf16[8,128,128]{2,1,0:T(8,128)(2,1)S(1)} %slice.14.own_ref.q_ref), channel_id=1, source_target_pairs={{0,128},{128,0},{1,129},{129,1},{2,130},{130,2},{3,131},{131,3},{4... | collective-permute-start | bytes 786440 | tf_op jit(solution)/shard_map/ppermute | solution.py:396
  42.4 2.7 %collective-permute-start.8 = (bf16[4,256,128]{2,1,0:T(8,128)(2,1)S(1)}, bf16[4,256,128]{2,1,0:T(8,128)(2,1)S(1)}, u32[]{:S(2)}, u32[]{:S(2)}) collective-permute-start(bf16[4,256,128]{2,1,0:T(8,128)(2,1)S(1)} %get-tuple-element.96.refs_0_), channel_id=1, source_target_pairs={{0,12},{4,0},{8,4},{12,8},{1,13},{5,1},{9,5},{13,9},{2,14},{6,2},{... | collective-permute-start | bytes 786440 | tf_op jit(solution)/shard_map/ppermute | solution.py:398
  45.1 2.7 %collective-permute-start.5 = (bf16[4,256,128]{2,1,0:T(8,128)(2,1)S(1)}, bf16[4,256,128]{2,1,0:T(8,128)(2,1)S(1)}, u32[]{:S(2)}, u32[]{:S(2)}) collective-permute-start(bf16[4,256,128]{2,1,0:T(8,128)(2,1)S(1)} %collective-permute-done.4.refs_3_), channel_id=1, source_target_pairs={{0,12},{4,0},{8,4},{12,8},{1,13},{5,1},{9,5},{13,9},{2,14},{6,2},{... | collective-permute-start | bytes 786440 | tf_op jit(solution)/shard_map/ppermute | solution.py:400
  48.1 2.9 %shard_map.57 = (f32[16,128,128]{2,1,0:T(8,128)S(1)}, f32[16,128,128]{2,1,0:T(8,128)S(1)}, f32[16,128,128]{2,1,0:T(8,128)S(1)}) custom-call(s32[1]{0:T(128)} %get-tuple-element.97.count_ref, s32[256]{0:T(256)S(1)} %get-tuple-element.98.block_ref, s32[256]{0:T(256)S(1)} %get-tuple-element.99.slot_ref, bf16[8,128,128]{2,1,0:T(8,128)(2,1)S(1)} %slice.14.own_ref.q_ref, ...), custom_call_target="tpu_custom_call" | custom-call | flops 335544320 | bytes 6291456 | tf_op jit(solution)/shard_map/pallas_call | solution.py:217
  51.0 4.0 %shard_map.58 = (f32[16,128,128]{2,1,0:T(8,128)S(1)}, f32[16,128,128]{2,1,0:T(8,128)S(1)}, f32[16,128,128]{2,1,0:T(8,128)S(1)}) custom-call(s32[1]{0:T(128)} %get-tuple-element.92.count_ref, s32[384]{0:T(512)S(1)} %get-tuple-element.93.block_ref, s32[384]{0:T(512)S(1)} %get-tuple-element.94.slot_ref, bf16[8,128,128]{2,1,0:T(8,128)(2,1)S(1)} %slice.14.own_ref.q_ref, ...), custom_call_target="tpu_custom_call" | custom-call | flops 671088640 | bytes 6291456 | tf_op jit(solution)/shard_map/pallas_call | solution.py:217
  55.9 2.2 %shard_map.59 = (bf16[8,128,128]{2,1,0:T(8,128)(2,1)S(1)}, f32[16,128]{1,0:T(8,128)S(1)}) custom-call(s32[1]{0:T(128)} %get-tuple-element.89.count_ref, s32[192]{0:T(256)S(1)} %get-tuple-element.90.block_ref, s32[192]{0:T(256)S(1)} %get-tuple-element.91.slot_ref, bf16[8,128,128]{2,1,0:T(8,128)(2,1)S(1)} %collective-permute-done.6.other_ref.q_ref, ...), custom_call_target="tpu_custom_call" | custom-call | flops 83886080 | bytes 3145728 | tf_op jit(solution)/shard_map/pallas_call | solution.py:162
  58.1 2.3 %collective-permute-start.9 = (bf16[8,128,128]{2,1,0:T(8,128)(2,1)S(1)}, bf16[8,128,128]{2,1,0:T(8,128)(2,1)S(1)}, u32[]{:S(2)}, u32[]{:S(2)}) collective-permute-start(bf16[8,128,128]{2,1,0:T(8,128)(2,1)S(1)} %get-tuple-element.113), channel_id=1, source_target_pairs={{0,128},{128,0},{1,129},{129,1},{2,130},{130,2},{3,131},{131,3},{4... | collective-permute-start | bytes 786440 | tf_op jit(solution)/shard_map/ppermute | solution.py:406
  61.1 3.0 %shard_map.60 = (f32[8,128,128]{2,1,0:T(8,128)S(1)}, f32[128,128]{1,0:T(8,128)S(1)}) custom-call(s32[1]{0:T(128)} %get-tuple-element.79.count_ref, s32[192]{0:T(256)S(1)} %get-tuple-element.80.block_ref, s32[192]{0:T(256)S(1)} %get-tuple-element.81.slot_ref, bf16[8,128,128]{2,1,0:T(8,128)(2,1)S(1)} %slice.14.own_ref.q_ref, ...), custom_call_target="tpu_custom_call" | custom-call | flops 83886080 | bytes 3145728 | tf_op jit(solution)/shard_map/pallas_call | solution.py:162
  64.1 1.3 %collective-permute-done.10.there_stats_ref = f32[16,128]{1,0:T(8,128)S(1)} collective-permute-done((f32[16,128]{1,0:T(8,128)S(1)}, f32[16,128]{1,0:T(8,128)S(1)}, u32[]{:S(2)}, u32[]{:S(2)}) %collective-permute-start.10) | collective-permute-done | bytes 8224 | tf_op jit(solution)/shard_map/ppermute | solution.py:407
  66.0 11.8 %all_to_all.10 = bf16[8,128,128]{2,1,0:T(8,128)(2,1)S(1)} all-to-all(bf16[8,128,128]{2,1,0:T(8,128)(2,1)S(1)} %shard_map.61), channel_id=1, replica_groups=mesh['xh'=2,'z'=8,'y'=4,'xl'=2,'c'=2] {'z'}, dimensions={0} | all-to-all | bytes 524288 | tf_op jit(solution)/shard_map/all_to_all | solution.py:410
  77.9 4.3 %collective-permute-start.11 = (bf16[5,128,128]{2,1,0:T(8,128)(2,1)S(1)}, bf16[5,128,128]{2,1,0:T(8,128)(2,1)S(1)}, u32[]{:S(2)}, u32[]{:S(2)}) collective-permute-start(bf16[5,128,128]{2,1,0:T(8,128)(2,1)S(1)} %slice.16.heads_ref), channel_id=1, source_target_pairs={{0,1},{1,0},{2,3},{3,2},{4,5},{5,4},{6,7},{7,6},{8,9},{9,8},{10,11... | collective-permute-start | bytes 491528 | tf_op jit(solution)/shard_map/ppermute | solution.py:411
  82.2 1.4 %shard_map.64.refs_0_ = f32[128,1280]{1,0:T(8,128)S(1)} custom-call(bf16[5,128,128]{2,1,0:T(8,128)(2,1)S(1)} %slice.16.heads_ref, bf16[640,1280]{1,0:T(8,128)(2,1)S(1)} %copy-done), custom_call_target="tpu_custom_call" | custom-call | flops 209715200 | bytes 2097152 | tf_op jit(solution)/shard_map/pallas_call | solution.py:288
  86.7 1.4 %shard_map.62.refs_0_ = f32[128,1280]{1,0:T(8,128)S(1)} custom-call(bf16[5,128,128]{2,1,0:T(8,128)(2,1)S(1)} %slice.16.heads_ref, bf16[640,1280]{1,0:T(8,128)(2,1)S(1)} %get-tuple-element.116.w_hbm), custom_call_target="tpu_custom_call" | custom-call | flops 209715200 | bytes 2097152 | tf_op jit(solution)/shard_map/pallas_call | solution.py:288
  88.1 2.2 %shard_map.63.near_ref = f32[128,1280]{1,0:T(8,128)S(1)} custom-call(bf16[5,128,128]{2,1,0:T(8,128)(2,1)S(1)} %collective-permute-done.11.heads_ref, bf16[640,1280]{1,0:T(8,128)(2,1)} %collective-permute-done.1.w_hbm, f32[128,1280]{1,0:T(8,128)S(1)} %shard_map.62.refs_0_), custom_call_target="tpu_custom_call" | custom-call | flops 209715200 | bytes 2097152 | tf_op jit(solution)/shard_map/pallas_call | solution.py:288
  90.4 3.5 %collective-permute-done.12.refs_0_ = bf16[128,512]{1,0:T(8,128)(2,1)S(1)} collective-permute-done((bf16[128,512]{1,0:T(8,128)(2,1)S(1)}, bf16[128,512]{1,0:T(8,128)(2,1)S(1)}, u32[]{:S(2)}, u32[]{:S(2)}) %collective-permute-start.12) | collective-permute-done | bytes 131104 | tf_op jit(solution)/shard_map/ppermute | solution.py:415
  (28 shorter events, 7.5 us)
Async XLA Ops:
  1.9 32.7 %all-to-all-start = ((bf16[8,384,128]{2,1,0:T(8,128)(2,1)}), bf16[8,384,128]{2,1,0:T(8,128)(2,1)}, u32[]{:S(2)}, u32[]{:S(2)}) async-start(bf16[8,384,128]{2,1,0:T(8,128)(2,1)} %shard_map.55), calls=%async_computation | async-start | bytes 1572864 | tf_op jit(solution)/shard_map/all_to_all | solution.py:388
  11.0 6.2 %copy-start.1 = (s32[64,64]{1,0:T(8,128)S(1)}, s32[64,64]{1,0:T(8,128)}, u32[]{:S(2)}) copy-start(s32[64,64]{1,0:T(8,128)} %mask_ref) | copy-start | bytes 49156
  16.2 22.4 %collective-permute-start = (bf16[640,1280]{1,0:T(8,128)(2,1)}, bf16[640,1280]{1,0:T(8,128)(2,1)S(1)}, u32[]{:S(2)}, u32[]{:S(2)}) collective-permute-start(bf16[640,1280]{1,0:T(8,128)(2,1)} %get-tuple-element.86), channel_id=1, source_target_pairs={{0,1},{1,0},{2,3},{3,2},{4,5},{5,4},{6,7},{7,6},{8,9},{9,8},{10,11... | collective-permute-start | bytes 4915208 | tf_op jit(solution)/shard_map/ppermute | solution.py:385
  17.2 21.5 %collective-permute-start.1 = (bf16[640,1280]{1,0:T(8,128)(2,1)}, bf16[640,1280]{1,0:T(8,128)(2,1)}, u32[]{:S(2)}, u32[]{:S(2)}) collective-permute-start(bf16[640,1280]{1,0:T(8,128)(2,1)} %get-tuple-element.87), channel_id=1, source_target_pairs={{0,1},{1,0},{2,3},{3,2},{4,5},{5,4},{6,7},{7,6},{8,9},{9,8},{10,11... | collective-permute-start | bytes 4915208 | tf_op jit(solution)/shard_map/ppermute | solution.py:385
  35.7 9.4 %collective-permute-start.2 = (bf16[4,256,128]{2,1,0:T(8,128)(2,1)S(1)}, bf16[4,256,128]{2,1,0:T(8,128)(2,1)S(1)}, u32[]{:S(2)}, u32[]{:S(2)}) collective-permute-start(bf16[4,256,128]{2,1,0:T(8,128)(2,1)S(1)} %get-tuple-element.96.refs_0_), channel_id=1, source_target_pairs={{0,4},{4,8},{8,12},{12,0},{1,5},{5,9},{9,13},{13,1},{2,6},{6,10},{... | collective-permute-start | bytes 786440 | tf_op jit(solution)/shard_map/ppermute | solution.py:392
  37.1 8.0 %collective-permute-start.4 = (bf16[4,256,128]{2,1,0:T(8,128)(2,1)S(1)}, bf16[4,256,128]{2,1,0:T(8,128)(2,1)S(1)}, u32[]{:S(2)}, u32[]{:S(2)}) collective-permute-start(bf16[4,256,128]{2,1,0:T(8,128)(2,1)S(1)} %get-tuple-element.95.refs_1_), channel_id=1, source_target_pairs={{0,12},{4,0},{8,4},{12,8},{1,13},{5,1},{9,5},{13,9},{2,14},{6,2},{... | collective-permute-start | bytes 786440 | tf_op jit(solution)/shard_map/ppermute | solution.py:393
  39.6 8.5 %collective-permute-start.6 = (bf16[8,128,128]{2,1,0:T(8,128)(2,1)S(1)}, bf16[8,128,128]{2,1,0:T(8,128)(2,1)S(1)}, u32[]{:S(2)}, u32[]{:S(2)}) collective-permute-start(bf16[8,128,128]{2,1,0:T(8,128)(2,1)S(1)} %slice.14.own_ref.q_ref), channel_id=1, source_target_pairs={{0,128},{128,0},{1,129},{129,1},{2,130},{130,2},{3,131},{131,3},{4... | collective-permute-start | bytes 786440 | tf_op jit(solution)/shard_map/ppermute | solution.py:396
  42.4 8.5 %collective-permute-start.7 = (bf16[4,256,128]{2,1,0:T(8,128)(2,1)S(1)}, bf16[4,256,128]{2,1,0:T(8,128)(2,1)S(1)}, u32[]{:S(2)}, u32[]{:S(2)}) collective-permute-start(bf16[4,256,128]{2,1,0:T(8,128)(2,1)S(1)} %get-tuple-element.95.refs_1_), channel_id=1, source_target_pairs={{0,4},{4,8},{8,12},{12,0},{1,5},{5,9},{9,13},{13,1},{2,6},{6,10},{... | collective-permute-start | bytes 786440 | tf_op jit(solution)/shard_map/ppermute | solution.py:397
  42.4 8.6 %collective-permute-start.8 = (bf16[4,256,128]{2,1,0:T(8,128)(2,1)S(1)}, bf16[4,256,128]{2,1,0:T(8,128)(2,1)S(1)}, u32[]{:S(2)}, u32[]{:S(2)}) collective-permute-start(bf16[4,256,128]{2,1,0:T(8,128)(2,1)S(1)} %get-tuple-element.96.refs_0_), channel_id=1, source_target_pairs={{0,12},{4,0},{8,4},{12,8},{1,13},{5,1},{9,5},{13,9},{2,14},{6,2},{... | collective-permute-start | bytes 786440 | tf_op jit(solution)/shard_map/ppermute | solution.py:398
  45.1 10.8 %collective-permute-start.3 = (bf16[4,256,128]{2,1,0:T(8,128)(2,1)S(1)}, bf16[4,256,128]{2,1,0:T(8,128)(2,1)S(1)}, u32[]{:S(2)}, u32[]{:S(2)}) collective-permute-start(bf16[4,256,128]{2,1,0:T(8,128)(2,1)S(1)} %collective-permute-done.2.refs_0_), channel_id=1, source_target_pairs={{0,4},{4,8},{8,12},{12,0},{1,5},{5,9},{9,13},{13,1},{2,6},{6,10},{... | collective-permute-start | bytes 786440 | tf_op jit(solution)/shard_map/ppermute | solution.py:399
  45.1 10.8 %collective-permute-start.5 = (bf16[4,256,128]{2,1,0:T(8,128)(2,1)S(1)}, bf16[4,256,128]{2,1,0:T(8,128)(2,1)S(1)}, u32[]{:S(2)}, u32[]{:S(2)}) collective-permute-start(bf16[4,256,128]{2,1,0:T(8,128)(2,1)S(1)} %collective-permute-done.4.refs_3_), channel_id=1, source_target_pairs={{0,12},{4,0},{8,4},{12,8},{1,13},{5,1},{9,5},{13,9},{2,14},{6,2},{... | collective-permute-start | bytes 786440 | tf_op jit(solution)/shard_map/ppermute | solution.py:400
  58.1 7.3 %collective-permute-start.9 = (bf16[8,128,128]{2,1,0:T(8,128)(2,1)S(1)}, bf16[8,128,128]{2,1,0:T(8,128)(2,1)S(1)}, u32[]{:S(2)}, u32[]{:S(2)}) collective-permute-start(bf16[8,128,128]{2,1,0:T(8,128)(2,1)S(1)} %get-tuple-element.113), channel_id=1, source_target_pairs={{0,128},{128,0},{1,129},{129,1},{2,130},{130,2},{3,131},{131,3},{4... | collective-permute-start | bytes 786440 | tf_op jit(solution)/shard_map/ppermute | solution.py:406
  60.3 5.1 %collective-permute-start.10 = (f32[16,128]{1,0:T(8,128)S(1)}, f32[16,128]{1,0:T(8,128)S(1)}, u32[]{:S(2)}, u32[]{:S(2)}) collective-permute-start(f32[16,128]{1,0:T(8,128)S(1)} %get-tuple-element.114), channel_id=1, source_target_pairs={{0,128},{128,0},{1,129},{129,1},{2,130},{130,2},{3,131},{131,3},{4... | collective-permute-start | bytes 24584 | tf_op jit(solution)/shard_map/ppermute | solution.py:407
  64.1 18.1 %copy-start = (bf16[640,1280]{1,0:T(8,128)(2,1)S(1)}, bf16[640,1280]{1,0:T(8,128)(2,1)}, u32[]{:S(2)}) copy-start(bf16[640,1280]{1,0:T(8,128)(2,1)} %get-tuple-element.118.w_hbm) | copy-start | bytes 4915204
  77.9 5.7 %collective-permute-start.11 = (bf16[5,128,128]{2,1,0:T(8,128)(2,1)S(1)}, bf16[5,128,128]{2,1,0:T(8,128)(2,1)S(1)}, u32[]{:S(2)}, u32[]{:S(2)}) collective-permute-start(bf16[5,128,128]{2,1,0:T(8,128)(2,1)S(1)} %slice.16.heads_ref), channel_id=1, source_target_pairs={{0,1},{1,0},{2,3},{3,2},{4,5},{5,4},{6,7},{7,6},{8,9},{9,8},{10,11... | collective-permute-start | bytes 491528 | tf_op jit(solution)/shard_map/ppermute | solution.py:411
  84.4 9.4 %collective-permute-start.13 = (bf16[128,768]{1,0:T(8,128)(2,1)S(1)}, bf16[128,768]{1,0:T(8,128)(2,1)S(1)}, u32[]{:S(2)}, u32[]{:S(2)}) collective-permute-start(bf16[128,768]{1,0:T(8,128)(2,1)S(1)} %shard_map.66), channel_id=1, source_target_pairs={{0,2},{2,0},{1,3},{3,1},{4,6},{6,4},{5,7},{7,5},{8,10},{10,8},{9,1... | collective-permute-start | bytes 589832 | tf_op jit(solution)/shard_map/ppermute | solution.py:415
  86.0 7.8 %collective-permute-start.12 = (bf16[128,512]{1,0:T(8,128)(2,1)S(1)}, bf16[128,512]{1,0:T(8,128)(2,1)S(1)}, u32[]{:S(2)}, u32[]{:S(2)}) collective-permute-start(bf16[128,512]{1,0:T(8,128)(2,1)S(1)} %shard_map.65), channel_id=1, source_target_pairs={{0,2},{2,0},{1,3},{3,1},{4,6},{6,4},{5,7},{7,5},{8,10},{10,8},{9,1... | collective-permute-start | bytes 393224 | tf_op jit(solution)/shard_map/ppermute | solution.py:415

commit v16 on v15

--- a/solution.py
+++ b/solution.py
@@ -37,14 +37,19 @@
     ]
     for load in loads:
         load.start()
+    stores = []
     for t, load in enumerate(loads):
         load.wait()
         for head in range(HEADS):
             lanes = slice(head * HEAD_DIM, (head + 1) * HEAD_DIM)
-            out_ref[head, t * BLOCK : (t + 1) * BLOCK, :] = whole_ref[t, :, lanes]
-    out = pltpu.make_async_copy(out_ref, slots_hbm.at[:HEADS], sems.at[3])
-    out.start()
-    out.wait()
+            out_ref[t, head] = whole_ref[t, :, lanes]
+        rows = pl.ds(t * BLOCK, BLOCK)
+        stores.append(
+            pltpu.make_async_copy(out_ref.at[t], slots_hbm.at[:HEADS, rows], sems.at[3 + t])
+        )
+        stores[-1].start()
+    for store in stores:
+        store.wait()
 
 
 def split(queries, keys, values):
@@ -57,8 +62,8 @@
         out_specs=anywhere,
         scratch_shapes=[
             pltpu.VMEM((3,) + queries.shape, jnp.bfloat16),
-            pltpu.VMEM((HEADS,) + part, jnp.bfloat16),
-            pltpu.SemaphoreType.DMA((4,)),
+            pltpu.VMEM((3, HEADS, BLOCK, HEAD_DIM), jnp.bfloat16),
+            pltpu.SemaphoreType.DMA((6,)),
         ],
         compiler_params=pltpu.CompilerParams(vmem_limit_bytes=56 * MIB),
     )(queries, keys, values)

time: 95.1 us -> 94.9 us (level)
  transfers between devices with their start and end apart: 15 -> 15, of which waited for: 5 -> 5; matrix products, arithmetic and copies ran while one was open for 8% -> 8% of each run, Pallas kernels for 21% -> 22%
where the time goes in v16:
time: 94.9 us; the launch traced here: 94.6 us
  starting transfers between devices  30 us (32%)
  Pallas kernels  26.7 us (28%)
  waiting for transfers between devices  18.5 us (19%)
  blocking collectives  11.8 us (12%)
  local copies, waits for them, and re-layouts  7.3 us (8%)
    all_to_all x1, waiting for transfers between devices, local(): slots = lax.all_to_all(slots, 'z', 0, 0, tiled=True)  13.1 us
    all_to_all x1, blocking collectives, local(): heads = lax.all_to_all(heads, 'z', 0, 0, tiled=True)[:HEADS]  11.8 us
    all_to_all x1, starting transfers between devices, local(): slots = lax.all_to_all(slots, 'z', 0, 0, tiled=True)  9.03 us
    pallas_call x2, Pallas kernels, attend(): pl.pallas_call(kernel, out_shape=(whole, whole, whole), in_specs=in_smem(...  7.41 us
    pallas_call x5, Pallas kernels, project(): pl.pallas_call(kernel, out_shape=jax.ShapeDtypeStruct((BLOCK, width), dty...  6.51 us
    dynamic_slice x1, local copies, waits for them, and re-layouts, w_columns(): lax.dynamic_slice(w, (0, (to_xl * NC + to_c) * width), (w.shape[0], width))  5.24 us
    pallas_call x2, Pallas kernels, attend_last(): pl.pallas_call(kernel, out_shape=(jax.ShapeDtypeStruct((NZ, BLOCK, HEAD_D...  5.17 us
    pallas_call x1, Pallas kernels, live_tiles(): pl.pallas_call(tiles_kernel, out_shape=tuple(out_shape), in_specs=in_smem...  4.37 us
  transfers between devices with their start and end apart: 15, of which 5 were waited for; matrix products, arithmetic and copies ran while one was open for 8% of the time, Pallas kernels for 22%

profile of v16, /device:TPU:1, one launch (start us, length us, event | category | flops | bytes accessed | tf_op | source)
XLA Modules:
  0.0 94.6 jit_solution(11391346176106486213)
XLA Ops:
  0.0 1.8 %shard_map.55 = bf16[8,384,128]{2,1,0:T(8,128)(2,1)} custom-call(bf16[128,640]{1,0:T(8,128)(2,1)} %q_hbm.1, bf16[128,640]{1,0:T(8,128)(2,1)} %k_hbm.1, bf16[128,640]{1,0:T(8,128)(2,1)} %v_hbm.1), custom_call_target="tpu_custom_call" | custom-call | tf_op jit(solution)/shard_map/pallas_call | solution.py:58
  1.8 9.0 %all-to-all-start = ((bf16[8,384,128]{2,1,0:T(8,128)(2,1)}), bf16[8,384,128]{2,1,0:T(8,128)(2,1)}, u32[]{:S(2)}, u32[]{:S(2)}) async-start(bf16[8,384,128]{2,1,0:T(8,128)(2,1)} %shard_map.55), calls=%async_computation | async-start | bytes 1572864 | tf_op jit(solution)/shard_map/all_to_all | solution.py:393
  10.9 5.2 %constant_dynamic-slice_fusion = (bf16[640,1280]{1,0:T(8,128)(2,1)}, bf16[640,1280]{1,0:T(8,128)(2,1)}, bf16[640,1280]{1,0:T(8,128)(2,1)S(1)}, bf16[640,1280]{1,0:T(8,128)(2,1)}) fusion(bf16[640,5120]{1,0:T(8,128)(2,1)} %param.9, s32[]{:T(128)S(6)} %select_n.15, s32[]{:T(128)S(6)} %select_n.14, s32[]{:T(128)S(6)} %select_n.13, s32[]{:T(128)S(6)} %select_n.12), kind=kLoop, calls=%fused_computation | loop fusion | bytes 13107216 | tf_op jit(solution)/shard_map/dynamic_slice | solution.py:383
  17.1 4.4 %shard_map.56 = (s32[1]{0:T(128)}, s32[256]{0:T(256)S(1)}, s32[256]{0:T(256)S(1)}, s32[1]{0:T(128)}, s32[384]{0:T(512)S(1)}, /*index=5*/s32[384]{0:T(512)S(1)}, ...) custom-call(s32[64,64]{1,0:T(8,128)S(1)} %copy-done.1), custom_call_target="tpu_custom_call" | custom-call | flops 1000000 | bytes 100000 | tf_op jit(solution)/shard_map/pallas_call | solution.py:366
  21.5 13.1 %all-to-all-done = bf16[8,384,128]{2,1,0:T(8,128)(2,1)} async-done(((bf16[8,384,128]{2,1,0:T(8,128)(2,1)}), bf16[8,384,128]{2,1,0:T(8,128)(2,1)}, u32[]{:S(2)}, u32[]{:S(2)}) %all-to-all-start) | async-done | bytes 786464 | tf_op jit(solution)/shard_map/all_to_all | solution.py:393
  34.6 1.1 %fusion = (bf16[4,256,128]{2,1,0:T(8,128)(2,1)S(1)}, bf16[4,256,128]{2,1,0:T(8,128)(2,1)S(1)}) fusion(bf16[8,384,128]{2,1,0:T(8,128)(2,1)} %all-to-all-done), kind=kLoop, calls=%fused_computation.4 | loop fusion | bytes 1048576 | tf_op jit(solution)/shard_map/slice | solution.py:395
  35.6 1.4 %collective-permute-start.2 = (bf16[4,256,128]{2,1,0:T(8,128)(2,1)S(1)}, bf16[4,256,128]{2,1,0:T(8,128)(2,1)S(1)}, u32[]{:S(2)}, u32[]{:S(2)}) collective-permute-start(bf16[4,256,128]{2,1,0:T(8,128)(2,1)S(1)} %get-tuple-element.96.refs_0_), channel_id=1, source_target_pairs={{0,4},{4,8},{8,12},{12,0},{1,5},{5,9},{9,13},{13,1},{2,6},{6,10},{... | collective-permute-start | bytes 786440 | tf_op jit(solution)/shard_map/ppermute | solution.py:397
  37.0 1.5 %collective-permute-start.4 = (bf16[4,256,128]{2,1,0:T(8,128)(2,1)S(1)}, bf16[4,256,128]{2,1,0:T(8,128)(2,1)S(1)}, u32[]{:S(2)}, u32[]{:S(2)}) collective-permute-start(bf16[4,256,128]{2,1,0:T(8,128)(2,1)S(1)} %get-tuple-element.95.refs_1_), channel_id=1, source_target_pairs={{0,12},{4,0},{8,4},{12,8},{1,13},{5,1},{9,5},{13,9},{2,14},{6,2},{... | collective-permute-start | bytes 786440 | tf_op jit(solution)/shard_map/ppermute | solution.py:398
  39.5 2.8 %collective-permute-start.6 = (bf16[8,128,128]{2,1,0:T(8,128)(2,1)S(1)}, bf16[8,128,128]{2,1,0:T(8,128)(2,1)S(1)}, u32[]{:S(2)}, u32[]{:S(2)}) collective-permute-start(bf16[8,128,128]{2,1,0:T(8,128)(2,1)S(1)} %slice.14.own_ref.q_ref), channel_id=1, source_target_pairs={{0,128},{128,0},{1,129},{129,1},{2,130},{130,2},{3,131},{131,3},{4... | collective-permute-start | bytes 786440 | tf_op jit(solution)/shard_map/ppermute | solution.py:401
  42.3 2.7 %collective-permute-start.8 = (bf16[4,256,128]{2,1,0:T(8,128)(2,1)S(1)}, bf16[4,256,128]{2,1,0:T(8,128)(2,1)S(1)}, u32[]{:S(2)}, u32[]{:S(2)}) collective-permute-start(bf16[4,256,128]{2,1,0:T(8,128)(2,1)S(1)} %get-tuple-element.96.refs_0_), channel_id=1, source_target_pairs={{0,12},{4,0},{8,4},{12,8},{1,13},{5,1},{9,5},{13,9},{2,14},{6,2},{... | collective-permute-start | bytes 786440 | tf_op jit(solution)/shard_map/ppermute | solution.py:403
  45.0 2.7 %collective-permute-start.5 = (bf16[4,256,128]{2,1,0:T(8,128)(2,1)S(1)}, bf16[4,256,128]{2,1,0:T(8,128)(2,1)S(1)}, u32[]{:S(2)}, u32[]{:S(2)}) collective-permute-start(bf16[4,256,128]{2,1,0:T(8,128)(2,1)S(1)} %collective-permute-done.4.refs_3_), channel_id=1, source_target_pairs={{0,12},{4,0},{8,4},{12,8},{1,13},{5,1},{9,5},{13,9},{2,14},{6,2},{... | collective-permute-start | bytes 786440 | tf_op jit(solution)/shard_map/ppermute | solution.py:405
  48.0 3.4 %shard_map.57 = (f32[16,128,128]{2,1,0:T(8,128)S(1)}, f32[16,128,128]{2,1,0:T(8,128)S(1)}, f32[16,128,128]{2,1,0:T(8,128)S(1)}) custom-call(s32[1]{0:T(128)} %get-tuple-element.97.count_ref, s32[256]{0:T(256)S(1)} %get-tuple-element.98.block_ref, s32[256]{0:T(256)S(1)} %get-tuple-element.99.slot_ref, bf16[8,128,128]{2,1,0:T(8,128)(2,1)S(1)} %slice.14.own_ref.q_ref, ...), custom_call_target="tpu_custom_call" | custom-call | flops 335544320 | bytes 6291456 | tf_op jit(solution)/shard_map/pallas_call | solution.py:222
  51.5 4.0 %shard_map.58 = (f32[16,128,128]{2,1,0:T(8,128)S(1)}, f32[16,128,128]{2,1,0:T(8,128)S(1)}, f32[16,128,128]{2,1,0:T(8,128)S(1)}) custom-call(s32[1]{0:T(128)} %get-tuple-element.92.count_ref, s32[384]{0:T(512)S(1)} %get-tuple-element.93.block_ref, s32[384]{0:T(512)S(1)} %get-tuple-element.94.slot_ref, bf16[8,128,128]{2,1,0:T(8,128)(2,1)S(1)} %slice.14.own_ref.q_ref, ...), custom_call_target="tpu_custom_call" | custom-call | flops 671088640 | bytes 6291456 | tf_op jit(solution)/shard_map/pallas_call | solution.py:222
  55.8 2.2 %shard_map.59 = (bf16[8,128,128]{2,1,0:T(8,128)(2,1)S(1)}, f32[16,128]{1,0:T(8,128)S(1)}) custom-call(s32[1]{0:T(128)} %get-tuple-element.89.count_ref, s32[192]{0:T(256)S(1)} %get-tuple-element.90.block_ref, s32[192]{0:T(256)S(1)} %get-tuple-element.91.slot_ref, bf16[8,128,128]{2,1,0:T(8,128)(2,1)S(1)} %collective-permute-done.6.other_ref.q_ref, ...), custom_call_target="tpu_custom_call" | custom-call | flops 83886080 | bytes 3145728 | tf_op jit(solution)/shard_map/pallas_call | solution.py:167
  58.0 3.0 %collective-permute-start.9 = (bf16[8,128,128]{2,1,0:T(8,128)(2,1)S(1)}, bf16[8,128,128]{2,1,0:T(8,128)(2,1)S(1)}, u32[]{:S(2)}, u32[]{:S(2)}) collective-permute-start(bf16[8,128,128]{2,1,0:T(8,128)(2,1)S(1)} %get-tuple-element.113), channel_id=1, source_target_pairs={{0,128},{128,0},{1,129},{129,1},{2,130},{130,2},{3,131},{131,3},{4... | collective-permute-start | bytes 786440 | tf_op jit(solution)/shard_map/ppermute | solution.py:411
  61.1 3.0 %shard_map.60 = (f32[8,128,128]{2,1,0:T(8,128)S(1)}, f32[128,128]{1,0:T(8,128)S(1)}) custom-call(s32[1]{0:T(128)} %get-tuple-element.79.count_ref, s32[192]{0:T(256)S(1)} %get-tuple-element.80.block_ref, s32[192]{0:T(256)S(1)} %get-tuple-element.81.slot_ref, bf16[8,128,128]{2,1,0:T(8,128)(2,1)S(1)} %slice.14.own_ref.q_ref, ...), custom_call_target="tpu_custom_call" | custom-call | flops 83886080 | bytes 3145728 | tf_op jit(solution)/shard_map/pallas_call | solution.py:167
  64.1 1.3 %collective-permute-done.10.there_stats_ref = f32[16,128]{1,0:T(8,128)S(1)} collective-permute-done((f32[16,128]{1,0:T(8,128)S(1)}, f32[16,128]{1,0:T(8,128)S(1)}, u32[]{:S(2)}, u32[]{:S(2)}) %collective-permute-start.10) | collective-permute-done | bytes 8224 | tf_op jit(solution)/shard_map/ppermute | solution.py:412
  66.1 11.8 %all_to_all.10 = bf16[8,128,128]{2,1,0:T(8,128)(2,1)S(1)} all-to-all(bf16[8,128,128]{2,1,0:T(8,128)(2,1)S(1)} %shard_map.61), channel_id=1, replica_groups=mesh['xh'=2,'z'=8,'y'=4,'xl'=2,'c'=2] {'z'}, dimensions={0} | all-to-all | bytes 524288 | tf_op jit(solution)/shard_map/all_to_all | solution.py:415
  77.9 4.2 %collective-permute-start.11 = (bf16[5,128,128]{2,1,0:T(8,128)(2,1)S(1)}, bf16[5,128,128]{2,1,0:T(8,128)(2,1)S(1)}, u32[]{:S(2)}, u32[]{:S(2)}) collective-permute-start(bf16[5,128,128]{2,1,0:T(8,128)(2,1)S(1)} %slice.16.heads_ref), channel_id=1, source_target_pairs={{0,1},{1,0},{2,3},{3,2},{4,5},{5,4},{6,7},{7,6},{8,9},{9,8},{10,11... | collective-permute-start | bytes 491528 | tf_op jit(solution)/shard_map/ppermute | solution.py:416
  82.1 1.4 %shard_map.64.refs_0_ = f32[128,1280]{1,0:T(8,128)S(1)} custom-call(bf16[5,128,128]{2,1,0:T(8,128)(2,1)S(1)} %slice.16.heads_ref, bf16[640,1280]{1,0:T(8,128)(2,1)S(1)} %copy-done), custom_call_target="tpu_custom_call" | custom-call | flops 209715200 | bytes 2097152 | tf_op jit(solution)/shard_map/pallas_call | solution.py:293
  84.4 1.0 %collective-permute-start.13 = (bf16[128,768]{1,0:T(8,128)(2,1)S(1)}, bf16[128,768]{1,0:T(8,128)(2,1)S(1)}, u32[]{:S(2)}, u32[]{:S(2)}) collective-permute-start(bf16[128,768]{1,0:T(8,128)(2,1)S(1)} %shard_map.66), channel_id=1, source_target_pairs={{0,2},{2,0},{1,3},{3,1},{4,6},{6,4},{5,7},{7,5},{8,10},{10,8},{9,1... | collective-permute-start | bytes 589832 | tf_op jit(solution)/shard_map/ppermute | solution.py:420
  86.6 1.4 %shard_map.62.refs_0_ = f32[128,1280]{1,0:T(8,128)S(1)} custom-call(bf16[5,128,128]{2,1,0:T(8,128)(2,1)S(1)} %slice.16.heads_ref, bf16[640,1280]{1,0:T(8,128)(2,1)S(1)} %get-tuple-element.116.w_hbm), custom_call_target="tpu_custom_call" | custom-call | flops 209715200 | bytes 2097152 | tf_op jit(solution)/shard_map/pallas_call | solution.py:293
  88.1 2.2 %shard_map.63.near_ref = f32[128,1280]{1,0:T(8,128)S(1)} custom-call(bf16[5,128,128]{2,1,0:T(8,128)(2,1)S(1)} %collective-permute-done.11.heads_ref, bf16[640,1280]{1,0:T(8,128)(2,1)} %collective-permute-done.1.w_hbm, f32[128,1280]{1,0:T(8,128)S(1)} %shard_map.62.refs_0_), custom_call_target="tpu_custom_call" | custom-call | flops 209715200 | bytes 2097152 | tf_op jit(solution)/shard_map/pallas_call | solution.py:293
  90.3 3.5 %collective-permute-done.12.refs_0_ = bf16[128,512]{1,0:T(8,128)(2,1)S(1)} collective-permute-done((bf16[128,512]{1,0:T(8,128)(2,1)S(1)}, bf16[128,512]{1,0:T(8,128)(2,1)S(1)}, u32[]{:S(2)}, u32[]{:S(2)}) %collective-permute-start.12) | collective-permute-done | bytes 131104 | tf_op jit(solution)/shard_map/ppermute | solution.py:420
  (28 shorter events, 6.3 us)
Async XLA Ops:
  1.8 32.7 %all-to-all-start = ((bf16[8,384,128]{2,1,0:T(8,128)(2,1)}), bf16[8,384,128]{2,1,0:T(8,128)(2,1)}, u32[]{:S(2)}, u32[]{:S(2)}) async-start(bf16[8,384,128]{2,1,0:T(8,128)(2,1)} %shard_map.55), calls=%async_computation | async-start | bytes 1572864 | tf_op jit(solution)/shard_map/all_to_all | solution.py:393
  10.9 6.2 %copy-start.1 = (s32[64,64]{1,0:T(8,128)S(1)}, s32[64,64]{1,0:T(8,128)}, u32[]{:S(2)}) copy-start(s32[64,64]{1,0:T(8,128)} %mask_ref) | copy-start | bytes 49156
  16.1 22.4 %collective-permute-start = (bf16[640,1280]{1,0:T(8,128)(2,1)}, bf16[640,1280]{1,0:T(8,128)(2,1)S(1)}, u32[]{:S(2)}, u32[]{:S(2)}) collective-permute-start(bf16[640,1280]{1,0:T(8,128)(2,1)} %get-tuple-element.86), channel_id=1, source_target_pairs={{0,1},{1,0},{2,3},{3,2},{4,5},{5,4},{6,7},{7,6},{8,9},{9,8},{10,11... | collective-permute-start | bytes 4915208 | tf_op jit(solution)/shard_map/ppermute | solution.py:390
  17.1 21.5 %collective-permute-start.1 = (bf16[640,1280]{1,0:T(8,128)(2,1)}, bf16[640,1280]{1,0:T(8,128)(2,1)}, u32[]{:S(2)}, u32[]{:S(2)}) collective-permute-start(bf16[640,1280]{1,0:T(8,128)(2,1)} %get-tuple-element.87), channel_id=1, source_target_pairs={{0,1},{1,0},{2,3},{3,2},{4,5},{5,4},{6,7},{7,6},{8,9},{9,8},{10,11... | collective-permute-start | bytes 4915208 | tf_op jit(solution)/shard_map/ppermute | solution.py:390
  35.6 9.4 %collective-permute-start.2 = (bf16[4,256,128]{2,1,0:T(8,128)(2,1)S(1)}, bf16[4,256,128]{2,1,0:T(8,128)(2,1)S(1)}, u32[]{:S(2)}, u32[]{:S(2)}) collective-permute-start(bf16[4,256,128]{2,1,0:T(8,128)(2,1)S(1)} %get-tuple-element.96.refs_0_), channel_id=1, source_target_pairs={{0,4},{4,8},{8,12},{12,0},{1,5},{5,9},{9,13},{13,1},{2,6},{6,10},{... | collective-permute-start | bytes 786440 | tf_op jit(solution)/shard_map/ppermute | solution.py:397
  37.0 8.0 %collective-permute-start.4 = (bf16[4,256,128]{2,1,0:T(8,128)(2,1)S(1)}, bf16[4,256,128]{2,1,0:T(8,128)(2,1)S(1)}, u32[]{:S(2)}, u32[]{:S(2)}) collective-permute-start(bf16[4,256,128]{2,1,0:T(8,128)(2,1)S(1)} %get-tuple-element.95.refs_1_), channel_id=1, source_target_pairs={{0,12},{4,0},{8,4},{12,8},{1,13},{5,1},{9,5},{13,9},{2,14},{6,2},{... | collective-permute-start | bytes 786440 | tf_op jit(solution)/shard_map/ppermute | solution.py:398
  39.5 8.5 %collective-permute-start.6 = (bf16[8,128,128]{2,1,0:T(8,128)(2,1)S(1)}, bf16[8,128,128]{2,1,0:T(8,128)(2,1)S(1)}, u32[]{:S(2)}, u32[]{:S(2)}) collective-permute-start(bf16[8,128,128]{2,1,0:T(8,128)(2,1)S(1)} %slice.14.own_ref.q_ref), channel_id=1, source_target_pairs={{0,128},{128,0},{1,129},{129,1},{2,130},{130,2},{3,131},{131,3},{4... | collective-permute-start | bytes 786440 | tf_op jit(solution)/shard_map/ppermute | solution.py:401
  42.3 9.1 %collective-permute-start.7 = (bf16[4,256,128]{2,1,0:T(8,128)(2,1)S(1)}, bf16[4,256,128]{2,1,0:T(8,128)(2,1)S(1)}, u32[]{:S(2)}, u32[]{:S(2)}) collective-permute-start(bf16[4,256,128]{2,1,0:T(8,128)(2,1)S(1)} %get-tuple-element.95.refs_1_), channel_id=1, source_target_pairs={{0,4},{4,8},{8,12},{12,0},{1,5},{5,9},{9,13},{13,1},{2,6},{6,10},{... | collective-permute-start | bytes 786440 | tf_op jit(solution)/shard_map/ppermute | solution.py:402
  42.3 9.1 %collective-permute-start.8 = (bf16[4,256,128]{2,1,0:T(8,128)(2,1)S(1)}, bf16[4,256,128]{2,1,0:T(8,128)(2,1)S(1)}, u32[]{:S(2)}, u32[]{:S(2)}) collective-permute-start(bf16[4,256,128]{2,1,0:T(8,128)(2,1)S(1)} %get-tuple-element.96.refs_0_), channel_id=1, source_target_pairs={{0,12},{4,0},{8,4},{12,8},{1,13},{5,1},{9,5},{13,9},{2,14},{6,2},{... | collective-permute-start | bytes 786440 | tf_op jit(solution)/shard_map/ppermute | solution.py:403
  45.0 10.8 %collective-permute-start.3 = (bf16[4,256,128]{2,1,0:T(8,128)(2,1)S(1)}, bf16[4,256,128]{2,1,0:T(8,128)(2,1)S(1)}, u32[]{:S(2)}, u32[]{:S(2)}) collective-permute-start(bf16[4,256,128]{2,1,0:T(8,128)(2,1)S(1)} %collective-permute-done.2.refs_0_), channel_id=1, source_target_pairs={{0,4},{4,8},{8,12},{12,0},{1,5},{5,9},{9,13},{13,1},{2,6},{6,10},{... | collective-permute-start | bytes 786440 | tf_op jit(solution)/shard_map/ppermute | solution.py:404
  45.0 10.8 %collective-permute-start.5 = (bf16[4,256,128]{2,1,0:T(8,128)(2,1)S(1)}, bf16[4,256,128]{2,1,0:T(8,128)(2,1)S(1)}, u32[]{:S(2)}, u32[]{:S(2)}) collective-permute-start(bf16[4,256,128]{2,1,0:T(8,128)(2,1)S(1)} %collective-permute-done.4.refs_3_), channel_id=1, source_target_pairs={{0,12},{4,0},{8,4},{12,8},{1,13},{5,1},{9,5},{13,9},{2,14},{6,2},{... | collective-permute-start | bytes 786440 | tf_op jit(solution)/shard_map/ppermute | solution.py:405
  58.0 7.4 %collective-permute-start.9 = (bf16[8,128,128]{2,1,0:T(8,128)(2,1)S(1)}, bf16[8,128,128]{2,1,0:T(8,128)(2,1)S(1)}, u32[]{:S(2)}, u32[]{:S(2)}) collective-permute-start(bf16[8,128,128]{2,1,0:T(8,128)(2,1)S(1)} %get-tuple-element.113), channel_id=1, source_target_pairs={{0,128},{128,0},{1,129},{129,1},{2,130},{130,2},{3,131},{131,3},{4... | collective-permute-start | bytes 786440 | tf_op jit(solution)/shard_map/ppermute | solution.py:411
  61.0 4.4 %collective-permute-start.10 = (f32[16,128]{1,0:T(8,128)S(1)}, f32[16,128]{1,0:T(8,128)S(1)}, u32[]{:S(2)}, u32[]{:S(2)}) collective-permute-start(f32[16,128]{1,0:T(8,128)S(1)} %get-tuple-element.114), channel_id=1, source_target_pairs={{0,128},{128,0},{1,129},{129,1},{2,130},{130,2},{3,131},{131,3},{4... | collective-permute-start | bytes 24584 | tf_op jit(solution)/shard_map/ppermute | solution.py:412
  64.1 18.0 %copy-start = (bf16[640,1280]{1,0:T(8,128)(2,1)S(1)}, bf16[640,1280]{1,0:T(8,128)(2,1)}, u32[]{:S(2)}) copy-start(bf16[640,1280]{1,0:T(8,128)(2,1)} %get-tuple-element.118.w_hbm) | copy-start | bytes 4915204
  77.9 5.6 %collective-permute-start.11 = (bf16[5,128,128]{2,1,0:T(8,128)(2,1)S(1)}, bf16[5,128,128]{2,1,0:T(8,128)(2,1)S(1)}, u32[]{:S(2)}, u32[]{:S(2)}) collective-permute-start(bf16[5,128,128]{2,1,0:T(8,128)(2,1)S(1)} %slice.16.heads_ref), channel_id=1, source_target_pairs={{0,1},{1,0},{2,3},{3,2},{4,5},{5,4},{6,7},{7,6},{8,9},{9,8},{10,11... | collective-permute-start | bytes 491528 | tf_op jit(solution)/shard_map/ppermute | solution.py:416
  84.4 9.4 %collective-permute-start.13 = (bf16[128,768]{1,0:T(8,128)(2,1)S(1)}, bf16[128,768]{1,0:T(8,128)(2,1)S(1)}, u32[]{:S(2)}, u32[]{:S(2)}) collective-permute-start(bf16[128,768]{1,0:T(8,128)(2,1)S(1)} %shard_map.66), channel_id=1, source_target_pairs={{0,2},{2,0},{1,3},{3,1},{4,6},{6,4},{5,7},{7,5},{8,10},{10,8},{9,1... | collective-permute-start | bytes 589832 | tf_op jit(solution)/shard_map/ppermute | solution.py:420
  86.0 7.8 %collective-permute-start.12 = (bf16[128,512]{1,0:T(8,128)(2,1)S(1)}, bf16[128,512]{1,0:T(8,128)(2,1)S(1)}, u32[]{:S(2)}, u32[]{:S(2)}) collective-permute-start(bf16[128,512]{1,0:T(8,128)(2,1)S(1)} %shard_map.65), channel_id=1, source_target_pairs={{0,2},{2,0},{1,3},{3,1},{4,6},{6,4},{5,7},{7,5},{8,10},{10,8},{9,1... | collective-permute-start | bytes 393224 | tf_op jit(solution)/shard_map/ppermute | solution.py:420

commit v17 on v15

--- a/solution.py
+++ b/solution.py
@@ -184,6 +184,7 @@
 
 def attend(tables, query, parts, state):
     first = state is None
+    unroll = UNROLL if first else 2 * UNROLL
     slots = sum(part.shape[0] for part in parts)
     whole = jax.ShapeDtypeStruct((ROWS, BLOCK, BLOCK), jnp.float32)
 
@@ -199,7 +200,7 @@
         hold_parts(part_refs, kv_ref)
         count = count_ref[0]
         top_ref[...] = jnp.full(top_ref.shape, LOW, jnp.float32)
-        score_tiles(UNROLL, count, tables, q_ref, kv_ref, s_ref, top_ref)
+        score_tiles(unroll, count, tables, q_ref, kv_ref, s_ref, top_ref)
         for block in range(ROWS):
             top = jnp.max(top_ref[block], axis=1, keepdims=True)
             if first:
@@ -212,7 +213,7 @@
                 m_ref[block] = new
                 l_ref[block] = l_in[block] * fade
                 a_ref[block] = a_in[block] * fade
-        mix_tiles(UNROLL, count, tables, kv_ref, s_ref, m_ref, l_ref, a_ref)
+        mix_tiles(unroll, count, tables, kv_ref, s_ref, m_ref, l_ref, a_ref)
 
     return pl.pallas_call(
         kernel,
@@ -348,7 +349,7 @@
 
         total = lax.fori_loop(0, ROWS if on is None else NZ, one_query_block, jnp.int32(0))
         count_ref[0] = total
-        for u in range(UNROLL):
+        for u in range(2 * UNROLL):
             block_ref[total + u] = 0
             slot_ref[total + u] = 0
 

time: 95.1 us -> 95 us (level)
  no operation moved by 1% of the time
where the time goes in v17:
time: 95 us; the launch traced here: 94.8 us
  starting transfers between devices  30.5 us (32%)
  Pallas kernels  26.6 us (28%)
  waiting for transfers between devices  18.3 us (19%)
  blocking collectives  11.9 us (13%)
  local copies, waits for them, and re-layouts  7.3 us (8%)
    all_to_all x1, waiting for transfers between devices, local(): slots = lax.all_to_all(slots, 'z', 0, 0, tiled=True)  13.1 us
    all_to_all x1, blocking collectives, local(): heads = lax.all_to_all(heads, 'z', 0, 0, tiled=True)[:HEADS]  11.9 us
    all_to_all x1, starting transfers between devices, local(): slots = lax.all_to_all(slots, 'z', 0, 0, tiled=True)  9.03 us
    pallas_call x2, Pallas kernels, attend(): pl.pallas_call(kernel, out_shape=(whole, whole, whole), in_specs=in_smem(...  7.22 us
    pallas_call x5, Pallas kernels, project(): pl.pallas_call(kernel, out_shape=jax.ShapeDtypeStruct((BLOCK, width), dty...  6.51 us
    dynamic_slice x1, local copies, waits for them, and re-layouts, w_columns(): lax.dynamic_slice(w, (0, (to_xl * NC + to_c) * width), (w.shape[0], width))  5.24 us
    pallas_call x2, Pallas kernels, attend_last(): pl.pallas_call(kernel, out_shape=(jax.ShapeDtypeStruct((NZ, BLOCK, HEAD_D...  5.17 us
    ppermute x1, starting transfers between devices, local(): heads_core = lax.ppermute(heads, 'c', shift(NC, 1))  4.79 us
  transfers between devices with their start and end apart: 15, of which 5 were waited for; matrix products, arithmetic and copies ran while one was open for 8% of the time, Pallas kernels for 21%

profile of v17, /device:TPU:1, one launch (start us, length us, event | category | flops | bytes accessed | tf_op | source)
XLA Modules:
  0.0 94.8 jit_solution(11222425909336287998)
XLA Ops:
  0.0 1.9 %shard_map.55 = bf16[8,384,128]{2,1,0:T(8,128)(2,1)} custom-call(bf16[128,640]{1,0:T(8,128)(2,1)} %q_hbm.1, bf16[128,640]{1,0:T(8,128)(2,1)} %k_hbm.1, bf16[128,640]{1,0:T(8,128)(2,1)} %v_hbm.1), custom_call_target="tpu_custom_call" | custom-call | tf_op jit(solution)/shard_map/pallas_call | solution.py:53
  1.9 9.0 %all-to-all-start = ((bf16[8,384,128]{2,1,0:T(8,128)(2,1)}), bf16[8,384,128]{2,1,0:T(8,128)(2,1)}, u32[]{:S(2)}, u32[]{:S(2)}) async-start(bf16[8,384,128]{2,1,0:T(8,128)(2,1)} %shard_map.55), calls=%async_computation | async-start | bytes 1572864 | tf_op jit(solution)/shard_map/all_to_all | solution.py:389
  11.0 5.2 %constant_dynamic-slice_fusion = (bf16[640,1280]{1,0:T(8,128)(2,1)}, bf16[640,1280]{1,0:T(8,128)(2,1)}, bf16[640,1280]{1,0:T(8,128)(2,1)S(1)}, bf16[640,1280]{1,0:T(8,128)(2,1)}) fusion(bf16[640,5120]{1,0:T(8,128)(2,1)} %param.9, s32[]{:T(128)S(6)} %select_n.15, s32[]{:T(128)S(6)} %select_n.14, s32[]{:T(128)S(6)} %select_n.13, s32[]{:T(128)S(6)} %select_n.12), kind=kLoop, calls=%fused_computation | loop fusion | bytes 13107216 | tf_op jit(solution)/shard_map/dynamic_slice | solution.py:379
  16.2 1.0 %collective-permute-start = (bf16[640,1280]{1,0:T(8,128)(2,1)}, bf16[640,1280]{1,0:T(8,128)(2,1)S(1)}, u32[]{:S(2)}, u32[]{:S(2)}) collective-permute-start(bf16[640,1280]{1,0:T(8,128)(2,1)} %get-tuple-element.86), channel_id=1, source_target_pairs={{0,1},{1,0},{2,3},{3,2},{4,5},{5,4},{6,7},{7,6},{8,9},{9,8},{10,11... | collective-permute-start | bytes 4915208 | tf_op jit(solution)/shard_map/ppermute | solution.py:386
  17.2 4.4 %shard_map.56 = (s32[1]{0:T(128)}, s32[256]{0:T(256)S(1)}, s32[256]{0:T(256)S(1)}, s32[1]{0:T(128)}, s32[384]{0:T(512)S(1)}, /*index=5*/s32[384]{0:T(512)S(1)}, ...) custom-call(s32[64,64]{1,0:T(8,128)S(1)} %copy-done.1), custom_call_target="tpu_custom_call" | custom-call | flops 1000000 | bytes 100000 | tf_op jit(solution)/shard_map/pallas_call | solution.py:362
  21.6 13.1 %all-to-all-done = bf16[8,384,128]{2,1,0:T(8,128)(2,1)} async-done(((bf16[8,384,128]{2,1,0:T(8,128)(2,1)}), bf16[8,384,128]{2,1,0:T(8,128)(2,1)}, u32[]{:S(2)}, u32[]{:S(2)}) %all-to-all-start) | async-done | bytes 786464 | tf_op jit(solution)/shard_map/all_to_all | solution.py:389
  34.6 1.1 %fusion = (bf16[4,256,128]{2,1,0:T(8,128)(2,1)S(1)}, bf16[4,256,128]{2,1,0:T(8,128)(2,1)S(1)}) fusion(bf16[8,384,128]{2,1,0:T(8,128)(2,1)} %all-to-all-done), kind=kLoop, calls=%fused_computation.4 | loop fusion | bytes 1048576 | tf_op jit(solution)/shard_map/slice | solution.py:391
  35.7 1.4 %collective-permute-start.2 = (bf16[4,256,128]{2,1,0:T(8,128)(2,1)S(1)}, bf16[4,256,128]{2,1,0:T(8,128)(2,1)S(1)}, u32[]{:S(2)}, u32[]{:S(2)}) collective-permute-start(bf16[4,256,128]{2,1,0:T(8,128)(2,1)S(1)} %get-tuple-element.96.refs_0_), channel_id=1, source_target_pairs={{0,4},{4,8},{8,12},{12,0},{1,5},{5,9},{9,13},{13,1},{2,6},{6,10},{... | collective-permute-start | bytes 786440 | tf_op jit(solution)/shard_map/ppermute | solution.py:393
  37.1 1.5 %collective-permute-start.4 = (bf16[4,256,128]{2,1,0:T(8,128)(2,1)S(1)}, bf16[4,256,128]{2,1,0:T(8,128)(2,1)S(1)}, u32[]{:S(2)}, u32[]{:S(2)}) collective-permute-start(bf16[4,256,128]{2,1,0:T(8,128)(2,1)S(1)} %get-tuple-element.95.refs_1_), channel_id=1, source_target_pairs={{0,12},{4,0},{8,4},{12,8},{1,13},{5,1},{9,5},{13,9},{2,14},{6,2},{... | collective-permute-start | bytes 786440 | tf_op jit(solution)/shard_map/ppermute | solution.py:394
  38.6 1.0 %slice.14.own_ref.q_ref = bf16[8,128,128]{2,1,0:T(8,128)(2,1)S(1)} slice(bf16[8,384,128]{2,1,0:T(8,128)(2,1)} %all-to-all-done), slice={[0:8], [0:128], [0:128]} | slice | bytes 524288 | tf_op jit(solution)/shard_map/slice | solution.py:396
  39.6 2.8 %collective-permute-start.6 = (bf16[8,128,128]{2,1,0:T(8,128)(2,1)S(1)}, bf16[8,128,128]{2,1,0:T(8,128)(2,1)S(1)}, u32[]{:S(2)}, u32[]{:S(2)}) collective-permute-start(bf16[8,128,128]{2,1,0:T(8,128)(2,1)S(1)} %slice.14.own_ref.q_ref), channel_id=1, source_target_pairs={{0,128},{128,0},{1,129},{129,1},{2,130},{130,2},{3,131},{131,3},{4... | collective-permute-start | bytes 786440 | tf_op jit(solution)/shard_map/ppermute | solution.py:397
  42.4 2.7 %collective-permute-start.8 = (bf16[4,256,128]{2,1,0:T(8,128)(2,1)S(1)}, bf16[4,256,128]{2,1,0:T(8,128)(2,1)S(1)}, u32[]{:S(2)}, u32[]{:S(2)}) collective-permute-start(bf16[4,256,128]{2,1,0:T(8,128)(2,1)S(1)} %get-tuple-element.96.refs_0_), channel_id=1, source_target_pairs={{0,12},{4,0},{8,4},{12,8},{1,13},{5,1},{9,5},{13,9},{2,14},{6,2},{... | collective-permute-start | bytes 786440 | tf_op jit(solution)/shard_map/ppermute | solution.py:399
  45.1 2.7 %collective-permute-start.5 = (bf16[4,256,128]{2,1,0:T(8,128)(2,1)S(1)}, bf16[4,256,128]{2,1,0:T(8,128)(2,1)S(1)}, u32[]{:S(2)}, u32[]{:S(2)}) collective-permute-start(bf16[4,256,128]{2,1,0:T(8,128)(2,1)S(1)} %collective-permute-done.4.refs_3_), channel_id=1, source_target_pairs={{0,12},{4,0},{8,4},{12,8},{1,13},{5,1},{9,5},{13,9},{2,14},{6,2},{... | collective-permute-start | bytes 786440 | tf_op jit(solution)/shard_map/ppermute | solution.py:401
  48.1 2.9 %shard_map.57 = (f32[16,128,128]{2,1,0:T(8,128)S(1)}, f32[16,128,128]{2,1,0:T(8,128)S(1)}, f32[16,128,128]{2,1,0:T(8,128)S(1)}) custom-call(s32[1]{0:T(128)} %get-tuple-element.97.count_ref, s32[256]{0:T(256)S(1)} %get-tuple-element.98.block_ref, s32[256]{0:T(256)S(1)} %get-tuple-element.99.slot_ref, bf16[8,128,128]{2,1,0:T(8,128)(2,1)S(1)} %slice.14.own_ref.q_ref, ...), custom_call_target="tpu_custom_call" | custom-call | flops 335544320 | bytes 6291456 | tf_op jit(solution)/shard_map/pallas_call | solution.py:218
  51.0 4.4 %shard_map.58 = (f32[16,128,128]{2,1,0:T(8,128)S(1)}, f32[16,128,128]{2,1,0:T(8,128)S(1)}, f32[16,128,128]{2,1,0:T(8,128)S(1)}) custom-call(s32[1]{0:T(128)} %get-tuple-element.92.count_ref, s32[384]{0:T(512)S(1)} %get-tuple-element.93.block_ref, s32[384]{0:T(512)S(1)} %get-tuple-element.94.slot_ref, bf16[8,128,128]{2,1,0:T(8,128)(2,1)S(1)} %slice.14.own_ref.q_ref, ...), custom_call_target="tpu_custom_call" | custom-call | flops 671088640 | bytes 6291456 | tf_op jit(solution)/shard_map/pallas_call | solution.py:218
  55.9 2.2 %shard_map.59 = (bf16[8,128,128]{2,1,0:T(8,128)(2,1)S(1)}, f32[16,128]{1,0:T(8,128)S(1)}) custom-call(s32[1]{0:T(128)} %get-tuple-element.89.count_ref, s32[192]{0:T(256)S(1)} %get-tuple-element.90.block_ref, s32[192]{0:T(256)S(1)} %get-tuple-element.91.slot_ref, bf16[8,128,128]{2,1,0:T(8,128)(2,1)S(1)} %collective-permute-done.6.other_ref.q_ref, ...), custom_call_target="tpu_custom_call" | custom-call | flops 83886080 | bytes 3145728 | tf_op jit(solution)/shard_map/pallas_call | solution.py:162
  58.1 2.9 %collective-permute-start.9 = (bf16[8,128,128]{2,1,0:T(8,128)(2,1)S(1)}, bf16[8,128,128]{2,1,0:T(8,128)(2,1)S(1)}, u32[]{:S(2)}, u32[]{:S(2)}) collective-permute-start(bf16[8,128,128]{2,1,0:T(8,128)(2,1)S(1)} %get-tuple-element.113), channel_id=1, source_target_pairs={{0,128},{128,0},{1,129},{129,1},{2,130},{130,2},{3,131},{131,3},{4... | collective-permute-start | bytes 786440 | tf_op jit(solution)/shard_map/ppermute | solution.py:407
  61.1 3.0 %shard_map.60 = (f32[8,128,128]{2,1,0:T(8,128)S(1)}, f32[128,128]{1,0:T(8,128)S(1)}) custom-call(s32[1]{0:T(128)} %get-tuple-element.79.count_ref, s32[192]{0:T(256)S(1)} %get-tuple-element.80.block_ref, s32[192]{0:T(256)S(1)} %get-tuple-element.81.slot_ref, bf16[8,128,128]{2,1,0:T(8,128)(2,1)S(1)} %slice.14.own_ref.q_ref, ...), custom_call_target="tpu_custom_call" | custom-call | flops 83886080 | bytes 3145728 | tf_op jit(solution)/shard_map/pallas_call | solution.py:162
  65.6 11.9 %all_to_all.10 = bf16[8,128,128]{2,1,0:T(8,128)(2,1)S(1)} all-to-all(bf16[8,128,128]{2,1,0:T(8,128)(2,1)S(1)} %shard_map.61), channel_id=1, replica_groups=mesh['xh'=2,'z'=8,'y'=4,'xl'=2,'c'=2] {'z'}, dimensions={0} | all-to-all | bytes 524288 | tf_op jit(solution)/shard_map/all_to_all | solution.py:411
  77.5 4.8 %collective-permute-start.11 = (bf16[5,128,128]{2,1,0:T(8,128)(2,1)S(1)}, bf16[5,128,128]{2,1,0:T(8,128)(2,1)S(1)}, u32[]{:S(2)}, u32[]{:S(2)}) collective-permute-start(bf16[5,128,128]{2,1,0:T(8,128)(2,1)S(1)} %slice.16.heads_ref), channel_id=1, source_target_pairs={{0,1},{1,0},{2,3},{3,2},{4,5},{5,4},{6,7},{7,6},{8,9},{9,8},{10,11... | collective-permute-start | bytes 491528 | tf_op jit(solution)/shard_map/ppermute | solution.py:412
  82.3 1.4 %shard_map.64.refs_0_ = f32[128,1280]{1,0:T(8,128)S(1)} custom-call(bf16[5,128,128]{2,1,0:T(8,128)(2,1)S(1)} %slice.16.heads_ref, bf16[640,1280]{1,0:T(8,128)(2,1)S(1)} %copy-done), custom_call_target="tpu_custom_call" | custom-call | flops 209715200 | bytes 2097152 | tf_op jit(solution)/shard_map/pallas_call | solution.py:289
  86.8 1.4 %shard_map.62.refs_0_ = f32[128,1280]{1,0:T(8,128)S(1)} custom-call(bf16[5,128,128]{2,1,0:T(8,128)(2,1)S(1)} %slice.16.heads_ref, bf16[640,1280]{1,0:T(8,128)(2,1)S(1)} %get-tuple-element.116.w_hbm), custom_call_target="tpu_custom_call" | custom-call | flops 209715200 | bytes 2097152 | tf_op jit(solution)/shard_map/pallas_call | solution.py:289
  88.2 2.2 %shard_map.63.near_ref = f32[128,1280]{1,0:T(8,128)S(1)} custom-call(bf16[5,128,128]{2,1,0:T(8,128)(2,1)S(1)} %collective-permute-done.11.heads_ref, bf16[640,1280]{1,0:T(8,128)(2,1)} %collective-permute-done.1.w_hbm, f32[128,1280]{1,0:T(8,128)S(1)} %shard_map.62.refs_0_), custom_call_target="tpu_custom_call" | custom-call | flops 209715200 | bytes 2097152 | tf_op jit(solution)/shard_map/pallas_call | solution.py:289
  90.5 3.5 %collective-permute-done.12.refs_0_ = bf16[128,512]{1,0:T(8,128)(2,1)S(1)} collective-permute-done((bf16[128,512]{1,0:T(8,128)(2,1)S(1)}, bf16[128,512]{1,0:T(8,128)(2,1)S(1)}, u32[]{:S(2)}, u32[]{:S(2)}) %collective-permute-start.12) | collective-permute-done | bytes 131104 | tf_op jit(solution)/shard_map/ppermute | solution.py:416
  (28 shorter events, 6.4 us)
Async XLA Ops:
  1.9 32.7 %all-to-all-start = ((bf16[8,384,128]{2,1,0:T(8,128)(2,1)}), bf16[8,384,128]{2,1,0:T(8,128)(2,1)}, u32[]{:S(2)}, u32[]{:S(2)}) async-start(bf16[8,384,128]{2,1,0:T(8,128)(2,1)} %shard_map.55), calls=%async_computation | async-start | bytes 1572864 | tf_op jit(solution)/shard_map/all_to_all | solution.py:389
  11.0 6.2 %copy-start.1 = (s32[64,64]{1,0:T(8,128)S(1)}, s32[64,64]{1,0:T(8,128)}, u32[]{:S(2)}) copy-start(s32[64,64]{1,0:T(8,128)} %mask_ref) | copy-start | bytes 49156
  16.2 22.4 %collective-permute-start = (bf16[640,1280]{1,0:T(8,128)(2,1)}, bf16[640,1280]{1,0:T(8,128)(2,1)S(1)}, u32[]{:S(2)}, u32[]{:S(2)}) collective-permute-start(bf16[640,1280]{1,0:T(8,128)(2,1)} %get-tuple-element.86), channel_id=1, source_target_pairs={{0,1},{1,0},{2,3},{3,2},{4,5},{5,4},{6,7},{7,6},{8,9},{9,8},{10,11... | collective-permute-start | bytes 4915208 | tf_op jit(solution)/shard_map/ppermute | solution.py:386
  17.2 21.5 %collective-permute-start.1 = (bf16[640,1280]{1,0:T(8,128)(2,1)}, bf16[640,1280]{1,0:T(8,128)(2,1)}, u32[]{:S(2)}, u32[]{:S(2)}) collective-permute-start(bf16[640,1280]{1,0:T(8,128)(2,1)} %get-tuple-element.87), channel_id=1, source_target_pairs={{0,1},{1,0},{2,3},{3,2},{4,5},{5,4},{6,7},{7,6},{8,9},{9,8},{10,11... | collective-permute-start | bytes 4915208 | tf_op jit(solution)/shard_map/ppermute | solution.py:386
  35.7 9.4 %collective-permute-start.2 = (bf16[4,256,128]{2,1,0:T(8,128)(2,1)S(1)}, bf16[4,256,128]{2,1,0:T(8,128)(2,1)S(1)}, u32[]{:S(2)}, u32[]{:S(2)}) collective-permute-start(bf16[4,256,128]{2,1,0:T(8,128)(2,1)S(1)} %get-tuple-element.96.refs_0_), channel_id=1, source_target_pairs={{0,4},{4,8},{8,12},{12,0},{1,5},{5,9},{9,13},{13,1},{2,6},{6,10},{... | collective-permute-start | bytes 786440 | tf_op jit(solution)/shard_map/ppermute | solution.py:393
  37.1 8.0 %collective-permute-start.4 = (bf16[4,256,128]{2,1,0:T(8,128)(2,1)S(1)}, bf16[4,256,128]{2,1,0:T(8,128)(2,1)S(1)}, u32[]{:S(2)}, u32[]{:S(2)}) collective-permute-start(bf16[4,256,128]{2,1,0:T(8,128)(2,1)S(1)} %get-tuple-element.95.refs_1_), channel_id=1, source_target_pairs={{0,12},{4,0},{8,4},{12,8},{1,13},{5,1},{9,5},{13,9},{2,14},{6,2},{... | collective-permute-start | bytes 786440 | tf_op jit(solution)/shard_map/ppermute | solution.py:394
  39.6 8.5 %collective-permute-start.6 = (bf16[8,128,128]{2,1,0:T(8,128)(2,1)S(1)}, bf16[8,128,128]{2,1,0:T(8,128)(2,1)S(1)}, u32[]{:S(2)}, u32[]{:S(2)}) collective-permute-start(bf16[8,128,128]{2,1,0:T(8,128)(2,1)S(1)} %slice.14.own_ref.q_ref), channel_id=1, source_target_pairs={{0,128},{128,0},{1,129},{129,1},{2,130},{130,2},{3,131},{131,3},{4... | collective-permute-start | bytes 786440 | tf_op jit(solution)/shard_map/ppermute | solution.py:397
  42.4 8.5 %collective-permute-start.7 = (bf16[4,256,128]{2,1,0:T(8,128)(2,1)S(1)}, bf16[4,256,128]{2,1,0:T(8,128)(2,1)S(1)}, u32[]{:S(2)}, u32[]{:S(2)}) collective-permute-start(bf16[4,256,128]{2,1,0:T(8,128)(2,1)S(1)} %get-tuple-element.95.refs_1_), channel_id=1, source_target_pairs={{0,4},{4,8},{8,12},{12,0},{1,5},{5,9},{9,13},{13,1},{2,6},{6,10},{... | collective-permute-start | bytes 786440 | tf_op jit(solution)/shard_map/ppermute | solution.py:398
  42.4 8.5 %collective-permute-start.8 = (bf16[4,256,128]{2,1,0:T(8,128)(2,1)S(1)}, bf16[4,256,128]{2,1,0:T(8,128)(2,1)S(1)}, u32[]{:S(2)}, u32[]{:S(2)}) collective-permute-start(bf16[4,256,128]{2,1,0:T(8,128)(2,1)S(1)} %get-tuple-element.96.refs_0_), channel_id=1, source_target_pairs={{0,12},{4,0},{8,4},{12,8},{1,13},{5,1},{9,5},{13,9},{2,14},{6,2},{... | collective-permute-start | bytes 786440 | tf_op jit(solution)/shard_map/ppermute | solution.py:399
  45.1 10.8 %collective-permute-start.3 = (bf16[4,256,128]{2,1,0:T(8,128)(2,1)S(1)}, bf16[4,256,128]{2,1,0:T(8,128)(2,1)S(1)}, u32[]{:S(2)}, u32[]{:S(2)}) collective-permute-start(bf16[4,256,128]{2,1,0:T(8,128)(2,1)S(1)} %collective-permute-done.2.refs_0_), channel_id=1, source_target_pairs={{0,4},{4,8},{8,12},{12,0},{1,5},{5,9},{9,13},{13,1},{2,6},{6,10},{... | collective-permute-start | bytes 786440 | tf_op jit(solution)/shard_map/ppermute | solution.py:400
  45.1 10.8 %collective-permute-start.5 = (bf16[4,256,128]{2,1,0:T(8,128)(2,1)S(1)}, bf16[4,256,128]{2,1,0:T(8,128)(2,1)S(1)}, u32[]{:S(2)}, u32[]{:S(2)}) collective-permute-start(bf16[4,256,128]{2,1,0:T(8,128)(2,1)S(1)} %collective-permute-done.4.refs_3_), channel_id=1, source_target_pairs={{0,12},{4,0},{8,4},{12,8},{1,13},{5,1},{9,5},{13,9},{2,14},{6,2},{... | collective-permute-start | bytes 786440 | tf_op jit(solution)/shard_map/ppermute | solution.py:401
  58.1 6.9 %collective-permute-start.9 = (bf16[8,128,128]{2,1,0:T(8,128)(2,1)S(1)}, bf16[8,128,128]{2,1,0:T(8,128)(2,1)S(1)}, u32[]{:S(2)}, u32[]{:S(2)}) collective-permute-start(bf16[8,128,128]{2,1,0:T(8,128)(2,1)S(1)} %get-tuple-element.113), channel_id=1, source_target_pairs={{0,128},{128,0},{1,129},{129,1},{2,130},{130,2},{3,131},{131,3},{4... | collective-permute-start | bytes 786440 | tf_op jit(solution)/shard_map/ppermute | solution.py:407
  60.9 4.0 %collective-permute-start.10 = (f32[16,128]{1,0:T(8,128)S(1)}, f32[16,128]{1,0:T(8,128)S(1)}, u32[]{:S(2)}, u32[]{:S(2)}) collective-permute-start(f32[16,128]{1,0:T(8,128)S(1)} %get-tuple-element.114), channel_id=1, source_target_pairs={{0,128},{128,0},{1,129},{129,1},{2,130},{130,2},{3,131},{131,3},{4... | collective-permute-start | bytes 24584 | tf_op jit(solution)/shard_map/ppermute | solution.py:408
  64.1 18.2 %copy-start = (bf16[640,1280]{1,0:T(8,128)(2,1)S(1)}, bf16[640,1280]{1,0:T(8,128)(2,1)}, u32[]{:S(2)}) copy-start(bf16[640,1280]{1,0:T(8,128)(2,1)} %get-tuple-element.118.w_hbm) | copy-start | bytes 4915204
  77.5 6.2 %collective-permute-start.11 = (bf16[5,128,128]{2,1,0:T(8,128)(2,1)S(1)}, bf16[5,128,128]{2,1,0:T(8,128)(2,1)S(1)}, u32[]{:S(2)}, u32[]{:S(2)}) collective-permute-start(bf16[5,128,128]{2,1,0:T(8,128)(2,1)S(1)} %slice.16.heads_ref), channel_id=1, source_target_pairs={{0,1},{1,0},{2,3},{3,2},{4,5},{5,4},{6,7},{7,6},{8,9},{9,8},{10,11... | collective-permute-start | bytes 491528 | tf_op jit(solution)/shard_map/ppermute | solution.py:412
  84.6 9.4 %collective-permute-start.13 = (bf16[128,768]{1,0:T(8,128)(2,1)S(1)}, bf16[128,768]{1,0:T(8,128)(2,1)S(1)}, u32[]{:S(2)}, u32[]{:S(2)}) collective-permute-start(bf16[128,768]{1,0:T(8,128)(2,1)S(1)} %shard_map.66), channel_id=1, source_target_pairs={{0,2},{2,0},{1,3},{3,1},{4,6},{6,4},{5,7},{7,5},{8,10},{10,8},{9,1... | collective-permute-start | bytes 589832 | tf_op jit(solution)/shard_map/ppermute | solution.py:416
  86.0 8.0 %collective-permute-start.12 = (bf16[128,512]{1,0:T(8,128)(2,1)S(1)}, bf16[128,512]{1,0:T(8,128)(2,1)S(1)}, u32[]{:S(2)}, u32[]{:S(2)}) collective-permute-start(bf16[128,512]{1,0:T(8,128)(2,1)S(1)} %shard_map.65), channel_id=1, source_target_pairs={{0,2},{2,0},{1,3},{3,1},{4,6},{6,4},{5,7},{7,5},{8,10},{10,8},{9,1... | collective-permute-start | bytes 393224 | tf_op jit(solution)/shard_map/ppermute | solution.py:416
